TPU v7x, 32 devices: a whole 2x2x4 slice. The times are simulated.
32 devices in a mesh: dp: 4 (over x, core), fsdp: 8 (over z, y).
Axes of the slice: x: 2, y: 2, z: 4, core: 2. Of those that a mesh axis runs over, the one named last changes fastest.
Arguments:
- content: bfloat16 [16384, 768], P(('dp', 'fsdp')), may hold values from -6 to 6
- query: bfloat16 [16384, 768], P(('dp', 'fsdp')), may hold values from -6 to 6
- lengths: int32 [32], P(('dp', 'fsdp')), may hold values from 32 to 512, as said below
- predicted: int32 [16384], P(('dp', 'fsdp')), may hold values 0 or 1
- content_cot: bfloat16 [16384, 768], P(('dp', 'fsdp')), may hold values from -6 to 6
- query_cot: bfloat16 [16384, 768], P(('dp', 'fsdp')), may hold values from -6 to 6
- attn_master: float32 [2, 4, 768, 768], P(None, None, 'fsdp')
- attn_first: float32 [2, 4, 768, 768], P(None, None, 'fsdp')
- attn_second: float32 [2, 4, 768, 768], P(None, None, 'fsdp')
- inner_master: float32 [2, 768, 3072], P(None, 'fsdp'), may hold values from -0.21875 to 0.21875
- inner_first: float32 [2, 768, 3072], P(None, 'fsdp')
- inner_second: float32 [2, 768, 3072], P(None, 'fsdp')
- outer_master: float32 [2, 3072, 768], P(None, 'fsdp'), may hold values from -0.109375 to 0.109375
- outer_first: float32 [2, 3072, 768], P(None, 'fsdp')
- outer_second: float32 [2, 3072, 768], P(None, 'fsdp')
- small_master: float32 [2, 9600], P(None, 'fsdp')
- small_first: float32 [2, 9600], P(None, 'fsdp')
- small_second: float32 [2, 9600], P(None, 'fsdp')
Outputs:
- content_out: bfloat16 [16384, 768], P(('dp', 'fsdp'))
- query_out: bfloat16 [16384, 768], P(('dp', 'fsdp'))
- content_grad: float32 [16384, 768], P(('dp', 'fsdp'))
- query_grad: float32 [16384, 768], P(('dp', 'fsdp'))
- attn_master_new: float32 [2, 4, 768, 768], P(None, None, 'fsdp')
- attn_first_new: float32 [2, 4, 768, 768], P(None, None, 'fsdp')
- attn_second_new: float32 [2, 4, 768, 768], P(None, None, 'fsdp')
- inner_master_new: float32 [2, 768, 3072], P(None, 'fsdp')
- inner_first_new: float32 [2, 768, 3072], P(None, 'fsdp')
- inner_second_new: float32 [2, 768, 3072], P(None, 'fsdp')
- outer_master_new: float32 [2, 3072, 768], P(None, 'fsdp')
- outer_first_new: float32 [2, 3072, 768], P(None, 'fsdp')
- outer_second_new: float32 [2, 3072, 768], P(None, 'fsdp')
- small_master_new: float32 [2, 9600], P(None, 'fsdp')
- small_first_new: float32 [2, 9600], P(None, 'fsdp')
- small_second_new: float32 [2, 9600], P(None, 'fsdp')
Inputs may be any that keep to these rules, and one draw needn't show every extreme that they name: lengths: heavy-tailed; one sequence of the batch has exactly 512.
All inputs are finite; a program needn't handle non-finite values. No bound on the sum of `predicted` on one device may be relied on, other than what follows from the above.
Results may differ from a plain program's by a relative error of at most 0.02.
Values may be sent and summed in bfloat16 or wider, within the bound.
No kernel may reach another device: no remote copies, remote signals or barrier semaphores. Data moves between devices by JAX's collectives and lax.ppermute only.
A program may use at most 320 MiB of HBM per device.

v0:
```python
from functools import partial

import jax
import jax.numpy as jnp
from jax import lax
from jax.sharding import PartitionSpec as P

D = 768
H = 12
DH = 64
FF = 3072
LEN = 512
NB = 32
LAYERS = 2
STEP = 10


NORM_EPS = 1e-05
MASKED = -1000000000.0
BETA_ONE = 0.9
BETA_TWO = 0.999
ATTENTION_RATE = 0.1
FEED_RATE = 0.02
SMALL_RATE = 0.4
WEIGHT_DECAY = 0.01
ADAM_EPS = 1e-08
SCORE_SCALE = 0.125


def layer_norm(values, gain, shift):
    centre = values - jnp.mean(values, axis=-1, keepdims=True)
    spread = jnp.mean(centre * centre, axis=-1, keepdims=True)
    return centre * lax.rsqrt(spread + NORM_EPS) * gain + shift


def unpack(vectors):
    pieces = [vectors[piece_index * D : (piece_index + 1) * D] for piece_index in range(8)]
    hidden_bias = vectors[8 * D : 8 * D + FF]
    bias_table = vectors[8 * D + FF :].reshape(H, NB)
    return (pieces, hidden_bias, bias_table)


def bucket_ids():
    position = jnp.arange(LEN, dtype=jnp.int32)
    offset = position[None, :] - position[:, None]
    distance = jnp.abs(offset)
    far_bucket = jnp.full(distance.shape, 8, jnp.int32)
    for exponent in range(1, 8):
        far_bucket = far_bucket + (distance * distance >= 64 * 2**exponent).astype(jnp.int32)
    near_or_far = jnp.where(distance < 8, distance, far_bucket)
    return near_or_far + NB // 2 * (offset > 0).astype(jnp.int32)


def bucket_onehot():
    return (bucket_ids()[:, :, None] == jnp.arange(NB, dtype=jnp.int32)[None, None, :]).astype(
        jnp.bfloat16
    )


def allowed_pairs(length, pred_flags):
    position = jnp.arange(LEN, dtype=jnp.int32)
    valid_key = (position < length)[None, :]
    row_pos = position[:, None]
    col_pos = position[None, :]
    free_key = (pred_flags == 0)[None, :]
    content_ok = valid_key & (free_key | (pred_flags[:, None] == 1) & (col_pos <= row_pos))
    query_ok = valid_key & (col_pos != row_pos) & (free_key | (col_pos < row_pos))
    return (content_ok, query_ok)


def masked_scores(query_rows, key_rows, position_bias, allowed):
    scores = (
        jnp.einsum("qhd,khd->hqk", query_rows, key_rows, preferred_element_type=jnp.float32)
        * SCORE_SCALE
        + position_bias
    )
    return jnp.where(allowed[None], scores, MASKED)


def table_bias(onehot, table_low):
    return jnp.einsum("qkb,hb->hqk", onehot, table_low, preferred_element_type=jnp.float32)


def attend_slot(onehot, table_low, slot_item):
    query_c, query_q, key_rows, value_rows, length, pred_flags = slot_item
    position_bias = table_bias(onehot, table_low)
    content_ok, query_ok = allowed_pairs(length, pred_flags)
    results = []
    for query_rows, allowed in ((query_c, content_ok), (query_q, query_ok)):
        scores = masked_scores(query_rows, key_rows, position_bias, allowed)
        peak = jnp.max(scores, axis=-1, keepdims=True)
        expos = jnp.exp(scores - peak)
        totals = jnp.sum(expos, axis=-1, keepdims=True)
        probs = (expos / totals).astype(jnp.bfloat16)
        mixed = jnp.einsum(
            "hqk,khd->qhd", probs, value_rows, preferred_element_type=jnp.float32
        ).astype(jnp.bfloat16)
        results.append((mixed, peak[..., 0] + jnp.log(totals[..., 0])))
    return (results[0][0], results[1][0], results[0][1], results[1][1])


def attend_back(onehot, table_low, slot_item):
    (
        query_c,
        query_q,
        key_rows,
        value_rows,
        length,
        pred_flags,
        lse_c,
        lse_q,
        grad_mix_c,
        grad_mix_q,
    ) = slot_item
    position_bias = table_bias(onehot, table_low)
    content_ok, query_ok = allowed_pairs(length, pred_flags)
    grad_keys = jnp.zeros(key_rows.shape, jnp.float32)
    grad_values = jnp.zeros(value_rows.shape, jnp.float32)
    grad_table = jnp.zeros((H, NB), jnp.float32)
    grads_query = []
    for query_rows, allowed, log_total, grad_mix in (
        (query_c, content_ok, lse_c, grad_mix_c),
        (query_q, query_ok, lse_q, grad_mix_q),
    ):
        scores = masked_scores(query_rows, key_rows, position_bias, allowed)
        probs = jnp.exp(scores - log_total[..., None])
        grad_values = grad_values + jnp.einsum(
            "hqk,qhd->khd", probs.astype(jnp.bfloat16), grad_mix, preferred_element_type=jnp.float32
        )
        grad_probs = jnp.einsum(
            "qhd,khd->hqk", grad_mix, value_rows, preferred_element_type=jnp.float32
        )
        grad_scores = probs * (grad_probs - jnp.sum(probs * grad_probs, axis=-1, keepdims=True))
        grad_scores = jnp.where(allowed[None], grad_scores, 0.0).astype(jnp.bfloat16)
        grad_table = grad_table + jnp.einsum(
            "hqk,qkb->hb", grad_scores, onehot, preferred_element_type=jnp.float32
        )
        grads_query.append(
            jnp.einsum("hqk,khd->qhd", grad_scores, key_rows, preferred_element_type=jnp.float32)
            * SCORE_SCALE
        )
        grad_keys = (
            grad_keys
            + jnp.einsum(
                "hqk,qhd->khd", grad_scores, query_rows, preferred_element_type=jnp.float32
            )
            * SCORE_SCALE
        )
    return (grads_query[0], grads_query[1], grad_keys, grad_values, grad_table)


def to_heads(values):
    return values.reshape(-1, LEN, H, DH)


def fetch_forward(shards):
    return (
        lax.all_gather(shards[0], "fsdp", axis=1, tiled=True),
        lax.all_gather(shards[1], "fsdp", axis=0, tiled=True),
        lax.all_gather(shards[2], "fsdp", axis=0, tiled=True),
        lax.all_gather(shards[3], "fsdp", axis=0, tiled=True),
    )


def fetch_backward(shards):
    return (
        lax.all_gather(shards[0], "fsdp", axis=1, tiled=True),
        lax.all_gather(shards[1], "fsdp", axis=0, tiled=True),
        lax.all_gather(shards[2], "fsdp", axis=0, tiled=True),
        lax.all_gather(shards[3], "fsdp", axis=0, tiled=True),
    )


def reduce_layer(grads):
    owned = (
        lax.psum_scatter(
            grads[0].astype(jnp.bfloat16), "fsdp", scatter_dimension=1, tiled=True
        ).astype(jnp.float32),
        lax.psum_scatter(
            grads[1].astype(jnp.bfloat16), "fsdp", scatter_dimension=0, tiled=True
        ).astype(jnp.float32),
        lax.psum_scatter(
            grads[2].astype(jnp.bfloat16), "fsdp", scatter_dimension=0, tiled=True
        ).astype(jnp.float32),
        lax.psum_scatter(
            grads[3].astype(jnp.bfloat16), "fsdp", scatter_dimension=0, tiled=True
        ).astype(jnp.float32),
    )
    return lax.psum((owned[0], owned[1], owned[2], owned[3]), "dp")


def forward_layer(hidden_c, hidden_q, weights, lengths, flag_rows, onehot):
    attn_w, inner_w, outer_w, small_w = weights
    pieces, hidden_bias, bias_table = unpack(small_w.astype(jnp.float32))
    bias_q, bias_v, bias_o, gain_one, shift_one, bias_two, gain_two, shift_two = pieces
    table_low = bias_table.astype(jnp.bfloat16)
    low_c = hidden_c.astype(jnp.bfloat16)
    low_q = hidden_q.astype(jnp.bfloat16)
    projected = jnp.einsum("td,sde->ste", low_c, attn_w[:3], preferred_element_type=jnp.float32)
    query_c = (projected[0] + bias_q).astype(jnp.bfloat16)
    key_rows = projected[1].astype(jnp.bfloat16)
    value_rows = (projected[2] + bias_v).astype(jnp.bfloat16)
    query_q = (jnp.dot(low_q, attn_w[0], preferred_element_type=jnp.float32) + bias_q).astype(
        jnp.bfloat16
    )
    mixed_c, mixed_q, lse_c, lse_q = lax.map(
        partial(attend_slot, onehot, table_low),
        (
            to_heads(query_c),
            to_heads(query_q),
            to_heads(key_rows),
            to_heads(value_rows),
            lengths,
            flag_rows,
        ),
    )
    mixed_c = mixed_c.reshape(-1, D)
    mixed_q = mixed_q.reshape(-1, D)
    outputs = []
    kept = []
    for hidden_in, mixed in ((hidden_c, mixed_c), (hidden_q, mixed_q)):
        resid = hidden_in + jnp.dot(mixed, attn_w[3], preferred_element_type=jnp.float32) + bias_o
        normed = layer_norm(resid, gain_one, shift_one)
        pre_act = (
            jnp.dot(normed.astype(jnp.bfloat16), inner_w, preferred_element_type=jnp.float32)
            + hidden_bias
        )
        active = jax.nn.gelu(pre_act, approximate=True).astype(jnp.bfloat16)
        summed = normed + jnp.dot(active, outer_w, preferred_element_type=jnp.float32) + bias_two
        outputs.append(layer_norm(summed, gain_two, shift_two))
        kept.append((resid, summed, pre_act))
    saved = (
        hidden_c,
        hidden_q,
        query_c,
        query_q,
        key_rows,
        value_rows,
        lse_c,
        lse_q,
        mixed_c,
        mixed_q,
        kept[0],
        kept[1],
    )
    return (outputs[0], outputs[1], saved)


def backward_layer(saved, weights, grad_c, grad_q, lengths, flag_rows, onehot):
    attn_w, inner_w, outer_w, small_w = weights
    pieces, hidden_bias, bias_table = unpack(small_w.astype(jnp.float32))
    bias_q, bias_v, bias_o, gain_one, shift_one, bias_two, gain_two, shift_two = pieces
    table_low = bias_table.astype(jnp.bfloat16)
    (
        hidden_c,
        hidden_q,
        query_c,
        query_q,
        key_rows,
        value_rows,
        lse_c,
        lse_q,
        mixed_c,
        mixed_q,
        kept_c,
        kept_q,
    ) = saved
    gelu_tanh = partial(jax.nn.gelu, approximate=True)
    grad_outer = jnp.zeros(outer_w.shape, jnp.float32)
    grad_inner = jnp.zeros(inner_w.shape, jnp.float32)
    grad_attn_out = jnp.zeros((D, D), jnp.float32)
    grad_bias_two = jnp.zeros((D,), jnp.float32)
    grad_hidden_bias = jnp.zeros((FF,), jnp.float32)
    grad_bias_o = jnp.zeros((D,), jnp.float32)
    grad_gain_one = jnp.zeros((D,), jnp.float32)
    grad_shift_one = jnp.zeros((D,), jnp.float32)
    grad_gain_two = jnp.zeros((D,), jnp.float32)
    grad_shift_two = jnp.zeros((D,), jnp.float32)
    residual_grads = []
    mix_grads = []
    for kept_rows, grad_out, mixed in ((kept_c, grad_c, mixed_c), (kept_q, grad_q, mixed_q)):
        resid, summed, pre_act = kept_rows
        normed, norm_one_back = jax.vjp(layer_norm, resid, gain_one, shift_one)
        unused_out, norm_two_back = jax.vjp(layer_norm, summed, gain_two, shift_two)
        grad_summed, grad_g2, grad_s2 = norm_two_back(grad_out)
        grad_gain_two = grad_gain_two + grad_g2
        grad_shift_two = grad_shift_two + grad_s2
        grad_branch = grad_summed.astype(jnp.bfloat16)
        grad_bias_two = grad_bias_two + jnp.sum(grad_branch.astype(jnp.float32), axis=0)
        active, gelu_back = jax.vjp(gelu_tanh, pre_act)
        grad_outer = grad_outer + jnp.einsum(
            "tf,td->fd",
            active.astype(jnp.bfloat16),
            grad_branch,
            preferred_element_type=jnp.float32,
        )
        grad_active = jnp.einsum(
            "td,fd->tf", grad_branch, outer_w, preferred_element_type=jnp.float32
        )
        grad_pre = gelu_back(grad_active)[0].astype(jnp.bfloat16)
        grad_hidden_bias = grad_hidden_bias + jnp.sum(grad_pre.astype(jnp.float32), axis=0)
        grad_inner = grad_inner + jnp.einsum(
            "td,tf->df", normed.astype(jnp.bfloat16), grad_pre, preferred_element_type=jnp.float32
        )
        grad_normed = grad_summed + jnp.einsum(
            "tf,df->td", grad_pre, inner_w, preferred_element_type=jnp.float32
        )
        grad_resid, grad_g1, grad_s1 = norm_one_back(grad_normed)
        grad_gain_one = grad_gain_one + grad_g1
        grad_shift_one = grad_shift_one + grad_s1
        grad_proj = grad_resid.astype(jnp.bfloat16)
        grad_bias_o = grad_bias_o + jnp.sum(grad_proj.astype(jnp.float32), axis=0)
        grad_attn_out = grad_attn_out + jnp.einsum(
            "td,te->de", mixed, grad_proj, preferred_element_type=jnp.float32
        )
        mix_grads.append(
            jnp.einsum(
                "te,de->td", grad_proj, attn_w[3], preferred_element_type=jnp.float32
            ).astype(jnp.bfloat16)
        )
        residual_grads.append(grad_resid)
    grad_query_c, grad_query_q, grad_keys, grad_values, grad_table = lax.map(
        partial(attend_back, onehot, table_low),
        (
            to_heads(query_c),
            to_heads(query_q),
            to_heads(key_rows),
            to_heads(value_rows),
            lengths,
            flag_rows,
            lse_c,
            lse_q,
            to_heads(mix_grads[0]),
            to_heads(mix_grads[1]),
        ),
    )
    grad_table = jnp.sum(grad_table, axis=0)
    low_query_c = grad_query_c.reshape(-1, D).astype(jnp.bfloat16)
    low_query_q = grad_query_q.reshape(-1, D).astype(jnp.bfloat16)
    low_keys = grad_keys.reshape(-1, D).astype(jnp.bfloat16)
    low_values = grad_values.reshape(-1, D).astype(jnp.bfloat16)
    low_c = hidden_c.astype(jnp.bfloat16)
    low_q = hidden_q.astype(jnp.bfloat16)
    stacked_grads = jnp.stack([low_query_c, low_keys, low_values])
    grad_qkv = jnp.einsum("td,ste->sde", low_c, stacked_grads, preferred_element_type=jnp.float32)
    grad_wq = grad_qkv[0] + jnp.einsum(
        "td,te->de", low_q, low_query_q, preferred_element_type=jnp.float32
    )
    grad_attn = jnp.stack([grad_wq, grad_qkv[1], grad_qkv[2], grad_attn_out])
    grad_bias_q = jnp.sum(low_query_c.astype(jnp.float32), axis=0) + jnp.sum(
        low_query_q.astype(jnp.float32), axis=0
    )
    grad_bias_v = jnp.sum(low_values.astype(jnp.float32), axis=0)
    grad_content = residual_grads[0] + jnp.einsum(
        "ste,sde->td", stacked_grads, attn_w[:3], preferred_element_type=jnp.float32
    )
    grad_query_in = residual_grads[1] + jnp.einsum(
        "te,de->td", low_query_q, attn_w[0], preferred_element_type=jnp.float32
    )
    grad_small = jnp.concatenate(
        [
            grad_bias_q,
            grad_bias_v,
            grad_bias_o,
            grad_gain_one,
            grad_shift_one,
            grad_bias_two,
            grad_gain_two,
            grad_shift_two,
            grad_hidden_bias,
            grad_table.reshape(-1),
        ]
    )
    return (grad_content, grad_query_in, (grad_attn, grad_inner, grad_outer, grad_small))


def adam_update(master, first, second, grad, rate):
    first_new = BETA_ONE * first + (1.0 - BETA_ONE) * grad
    second_new = BETA_TWO * second + (1.0 - BETA_TWO) * grad * grad
    first_hat = first_new / (1.0 - BETA_ONE**STEP)
    second_hat = second_new / (1.0 - BETA_TWO**STEP)
    master_new = master - rate * (
        first_hat / (jnp.sqrt(second_hat) + ADAM_EPS) + WEIGHT_DECAY * master
    )
    return (master_new, first_new, second_new)


def per_device(
    content,
    query,
    lengths,
    predicted,
    content_cot,
    query_cot,
    attn_master,
    attn_first,
    attn_second,
    inner_master,
    inner_first,
    inner_second,
    outer_master,
    outer_first,
    outer_second,
    small_master,
    small_first,
    small_second,
):
    masters = (attn_master, inner_master, outer_master, small_master)
    slot_count = lengths.shape[0]
    flag_rows = predicted.reshape(slot_count, LEN)
    onehot = bucket_onehot()
    hidden_c = content.astype(jnp.float32)
    hidden_q = query.astype(jnp.float32)
    kept_weights = []
    saved_layers = []
    for layer_index in range(LAYERS):
        shards = tuple((master[layer_index].astype(jnp.bfloat16) for master in masters))
        gathered = fetch_forward(shards)
        kept_weights.append(gathered)
        hidden_c, hidden_q, saved = forward_layer(
            hidden_c, hidden_q, gathered, lengths, flag_rows, onehot
        )
        saved_layers.append(saved)
    position = jnp.arange(LEN, dtype=jnp.int32)
    valid_rows = (position[None, :] < lengths[:, None]).reshape(-1, 1).astype(jnp.float32)
    grad_c = content_cot.astype(jnp.float32) * valid_rows
    grad_q = query_cot.astype(jnp.float32) * valid_rows
    layer_grads = [None] * LAYERS
    for layer_index in reversed(range(LAYERS)):
        weights = fetch_backward(
            tuple((master[layer_index].astype(jnp.bfloat16) for master in masters))
        )
        grad_c, grad_q, local_grads = backward_layer(
            saved_layers[layer_index], weights, grad_c, grad_q, lengths, flag_rows, onehot
        )
        layer_grads[layer_index] = reduce_layer(local_grads)
    reduced = tuple(
        (
            jnp.stack([layer_grads[layer_index][member] for layer_index in range(LAYERS)])
            for member in range(4)
        )
    )
    attn_new = adam_update(attn_master, attn_first, attn_second, reduced[0], ATTENTION_RATE)
    inner_new = adam_update(inner_master, inner_first, inner_second, reduced[1], FEED_RATE)
    outer_new = adam_update(outer_master, outer_first, outer_second, reduced[2], FEED_RATE)
    small_new = adam_update(small_master, small_first, small_second, reduced[3], SMALL_RATE)
    return (
        hidden_c.astype(jnp.bfloat16),
        hidden_q.astype(jnp.bfloat16),
        grad_c,
        grad_q,
        attn_new[0],
        attn_new[1],
        attn_new[2],
        inner_new[0],
        inner_new[1],
        inner_new[2],
        outer_new[0],
        outer_new[1],
        outer_new[2],
        small_new[0],
        small_new[1],
        small_new[2],
    )


def solution(mesh):
    placed = (
        P(("dp", "fsdp"), None),
        P(("dp", "fsdp"), None),
        P(("dp", "fsdp")),
        P(("dp", "fsdp")),
        P(("dp", "fsdp"), None),
        P(("dp", "fsdp"), None),
        P(None, None, "fsdp", None),
        P(None, None, "fsdp", None),
        P(None, None, "fsdp", None),
        P(None, "fsdp", None),
        P(None, "fsdp", None),
        P(None, "fsdp", None),
        P(None, "fsdp", None),
        P(None, "fsdp", None),
        P(None, "fsdp", None),
        P(None, "fsdp"),
        P(None, "fsdp"),
        P(None, "fsdp"),
    )
    return jax.shard_map(
        per_device,
        mesh=mesh,
        in_specs=placed,
        out_specs=(
            P(("dp", "fsdp"), None),
            P(("dp", "fsdp"), None),
            P(("dp", "fsdp"), None),
            P(("dp", "fsdp"), None),
            P(None, None, "fsdp", None),
            P(None, None, "fsdp", None),
            P(None, None, "fsdp", None),
            P(None, "fsdp", None),
            P(None, "fsdp", None),
            P(None, "fsdp", None),
            P(None, "fsdp", None),
            P(None, "fsdp", None),
            P(None, "fsdp", None),
            P(None, "fsdp"),
            P(None, "fsdp"),
            P(None, "fsdp"),
        ),
        check_vma=False,
    )
```

profile of v0, /device:TPU:0, one launch (start us, length us, event | category | flops | bytes accessed | tf_op | source)
XLA Modules:
  0.0 1623.3 jit_solution(3103809449391144961)
XLA Ops:
  19.8 41.1 %all-reduce.9 = (bf16[9600]{0:T(1024)(128)(2,1)S(1)}, bf16[9600]{0:T(1024)(128)(2,1)S(1)}) all-reduce(bf16[9600]{0:T(1024)(128)(2,1)S(1)} %dynamic-update-slice, bf16[9600]{0:T(1024)(128)(2,1)S(1)} %dynamic-update-slice.1), channel_id=3, replica_groups=mesh['dp'=4,'fsdp'=8] {'fsdp'}, use_global_device_ids=true, to_apply=%add | all-reduce | flops 19200 | bytes 76800
  76.0 46.2 %copy.289 = pred[512,512,32]{1,2,0:T(32,128)(4,1)} copy(pred[512,512,32]{0,2,1:T(32,128)(4,1)} %iota_compare_fusion) | data formatting | bytes 16777216 | tf_op jit(solution)/shard_map/eq | solution.py:55
  122.2 13.4 fusion.301
  135.6 17.8 %copy.298 = f32[12,512,512]{1,2,0:T(8,128)} copy(f32[12,512,512]{2,0,1:T(8,128)} %fusion.301) | data formatting | bytes 25165824 | tf_op jit(solution)/shard_map/while/body/eval_jaxpr/qkb,hb->hqk/dot_general | solution.py:81
  153.4 13.1 fusion.300
  166.5 17.8 %copy.290 = f32[12,512,512]{1,2,0:T(8,128)} copy(f32[12,512,512]{2,0,1:T(8,128)} %fusion.300) | data formatting | bytes 25165824 | tf_op jit(solution)/shard_map/while/body/eval_jaxpr/qkb,hb->hqk/dot_general | solution.py:81
  229.8 27.8 %all-gather.19.cloned.1.call-done = bf16[1,3072,768]{2,1,0:T(8,128)(2,1)} async-done(((bf16[1,384,768]{2,1,0:T(8,128)(2,1)}), bf16[1,3072,768]{2,1,0:T(8,128)(2,1)}) %all-gather.19.cloned.1.call-update) | async-done | bytes 4718608 | tf_op jit(solution)/shard_map/all_gather | solution.py:160
  266.7 71.6 %all-gather.21.cloned.1.call-done = bf16[1,4,768,768]{3,1,0,2:T(4,128)(2,1)} async-done(((bf16[1,4,96,768]{3,1,0,2:T(4,128)(2,1)}), bf16[1,4,768,768]{3,1,0,2:T(4,128)(2,1)}) %all-gather.21.cloned.1.call-update) | async-done | bytes 4718608 | tf_op jit(solution)/shard_map/all_gather | solution.py:158
  447.5 52.1 %all-gather.25.cloned.1.call-done = bf16[1,3072,768]{2,1,0:T(8,128)(2,1)} async-done(((bf16[1,384,768]{2,1,0:T(8,128)(2,1)}), bf16[1,3072,768]{2,1,0:T(8,128)(2,1)}) %all-gather.25.cloned.1.call-update) | async-done | bytes 4718608 | tf_op jit(solution)/shard_map/all_gather | solution.py:160
  567.2 17.3 %select_convert_fusion.2 = bf16[12,512,512]{1,2,0:T(8,128)(2,1)} fusion(f32[12,512,512]{1,2,0:T(8,128)} %copy-done.1, f32[12,512]{1,0:T(8,128)S(1)} %log_add_fusion.2, pred[512,512]{0,1:T(8,128)(4,1)} %get-tuple-element.405, bf16[512,12,64]{0,2,1:T(8,128)(2,1)S(1)} %bitcast.389, bf16[512,12,64]{0,2,1:T(8,128)(2,1)} %add_convert_fusion.13), kind=kOutput, calls=%fused_computation.21 | convolution fusion | flops 827333120 | bytes 20733952 | tf_op jit(solution)/shard_map/while/body/eval_jaxpr/sub | solution.py:133
  585.9 17.0 %select_convert_fusion.3 = bf16[12,512,512]{1,2,0:T(8,128)(2,1)} fusion(f32[12,512,512]{1,2,0:T(8,128)} %copy-done.3, f32[12,512]{1,0:T(8,128)S(1)} %log_add_fusion.3, pred[512,512]{0,1:T(8,128)(4,1)S(1)} %copy-done.66, bf16[512,12,64]{0,2,1:T(8,128)(2,1)S(1)} %bitcast.384, bf16[512,12,64]{0,2,1:T(8,128)(2,1)} %add_convert_fusion.13), kind=kOutput, calls=%fused_computation.25 | convolution fusion | flops 827333120 | bytes 20733952 | tf_op jit(solution)/shard_map/while/body/eval_jaxpr/sub | solution.py:133
  682.8 13.2 select_convert_fusion
  697.2 13.2 select_convert_fusion.1
  832.6 10.3 fusion.192
  843.0 11.9 fusion.210
  854.9 11.5 fusion.207
  866.4 197.0 %all-reduce.16.cloned.1.call-done = (bf16[4,768,768]{2,0,1:T(4,128)(2,1)}, bf16[4,768,768]{2,0,1:T(4,128)(2,1)}) async-done(((bf16[4,768,768]{2,0,1:T(4,128)(2,1)}, bf16[4,768,768]{2,0,1:T(4,128)(2,1)}), (bf16[4,768,768]{2,0,1:T(4,128)(2,1)}, bf16[4,768,768]{2,0,1:T(4,128)(2,1)})) %all-reduce.16.cloned.1.call-update) | async-done | bytes 9437200
  1068.1 93.2 %reduce-scatter.11.cloned.1.call-done = bf16[384,768]{1,0:T(8,128)(2,1)} async-done(((bf16[3072,768]{1,0:T(8,128)(2,1)}), bf16[384,768]{1,0:T(8,128)(2,1)}) %reduce-scatter.11.cloned.1.call-update) | async-done | bytes 589840 | tf_op jit(solution)/shard_map/reduce_scatter | solution.py:182
  1163.4 96.6 %reduce-scatter.9.cloned.1.call-done = bf16[384,768]{1,0:T(8,128)(2,1)} async-done(((bf16[3072,768]{1,0:T(8,128)(2,1)}), bf16[384,768]{1,0:T(8,128)(2,1)}) %reduce-scatter.9.cloned.1.call-update) | async-done | bytes 589840 | tf_op jit(solution)/shard_map/reduce_scatter | solution.py:182
  1262.2 96.4 %reduce-scatter.5.cloned.1.call-done = bf16[96,3072]{1,0:T(8,128)(2,1)} async-done(((bf16[768,3072]{1,0:T(8,128)(2,1)}), bf16[96,3072]{1,0:T(8,128)(2,1)}) %reduce-scatter.5.cloned.1.call-update) | async-done | bytes 589840 | tf_op jit(solution)/shard_map/reduce_scatter | solution.py:179
  1360.7 96.7 %reduce-scatter.7.cloned.1.call-done = bf16[96,3072]{1,0:T(8,128)(2,1)} async-done(((bf16[768,3072]{1,0:T(8,128)(2,1)}), bf16[96,3072]{1,0:T(8,128)(2,1)}) %reduce-scatter.7.cloned.1.call-update) | async-done | bytes 589840 | tf_op jit(solution)/shard_map/reduce_scatter | solution.py:179
  1464.6 36.3 %all-reduce.8 = (bf16[9600]{0:T(1024)(128)(2,1)S(1)}, bf16[9600]{0:T(1024)(128)(2,1)S(1)}) all-reduce(bf16[9600]{0:T(1024)(128)(2,1)S(1)} %constant_dynamic-update-slice_fusion.7, bf16[9600]{0:T(1024)(128)(2,1)S(1)} %constant_dynamic-update-slice_fusion.6), channel_id=17, replica_groups=mesh['dp'=4,'fsdp'=8] {'fsdp'}, use_global_device_ids=true, to_apply=%region_92.93.clone | all-reduce | flops 19200 | bytes 76800
  1501.1 11.9 all-reduce.6
  1522.2 72.4 %all-reduce.14.cloned.1.call-done = (f32[1,4,96,768]{3,2,1,0:T(8,128)}, f32[1,4,96,768]{3,2,1,0:T(8,128)}, f32[1,96,3072]{2,1,0:T(8,128)}, f32[1,96,3072]{2,1,0:...) async-done(((f32[1,4,96,768]{3,2,1,0:T(8,128)}, f32[1,4,96,768]{3,2,1,0:T(8,128)}, f32[1,96,3072]{2,1,0:T(8,128)}, f32[1,96,3072]{2,1,0:T(8,128)}, ...) | async-done | bytes 7077904 | tf_op jit(solution)/shard_map/psum | solution.py:189
  (833 shorter events, 506.9 us)
Async XLA Ops:
  7.2 178.2 %all-gather.15.cloned.1.call-start = ((), (), s32[]{:S(2)}) async-start(), calls=%async_computation.8 | async-start | bytes 5308416 | tf_op jit(solution)/shard_map/all_gather | solution.py:158
  11.9 210.3 %all-gather.17.cloned.1.call-start = ((), (), s32[]{:S(2)}) async-start(), calls=%async_computation.9 | async-start | bytes 5308416 | tf_op jit(solution)/shard_map/all_gather | solution.py:159
  13.8 243.8 %all-gather.19.cloned.1.call-start = ((), (), s32[]{:S(2)}) async-start(), calls=%async_computation.10 | async-start | bytes 5308416 | tf_op jit(solution)/shard_map/all_gather | solution.py:160
  16.0 322.2 %all-gather.21.cloned.1.call-start = ((), (), s32[]{:S(2)}) async-start(), calls=%async_computation.11 | async-start | bytes 5308416 | tf_op jit(solution)/shard_map/all_gather | solution.py:158
  16.6 422.6 %all-gather.23.cloned.1.call-start = ((), (), s32[]{:S(2)}) async-start(), calls=%async_computation.12 | async-start | bytes 5308416 | tf_op jit(solution)/shard_map/all_gather | solution.py:159
  17.2 482.4 %all-gather.25.cloned.1.call-start = ((), (), s32[]{:S(2)}) async-start(), calls=%async_computation.13 | async-start | bytes 5308416 | tf_op jit(solution)/shard_map/all_gather | solution.py:160
  17.8 1045.6 %all-reduce.16.cloned.1.call-start = ((), (), s32[]{:S(2)}) async-start(), calls=%async_computation.15 | async-start | bytes 18874368
  67.3 140.0 %copy-start.121 = (f32[12,64]{1,0:T(8,128)}, f32[12,64]{1,0:T(8,128)S(1)}, u32[]{:S(2)}) copy-start(f32[12,64]{1,0:T(8,128)S(1)} %slice.232) | copy-start | bytes 9220
  197.4 163.1 %copy-start.5 = (bf16[1,512,768]{1,2,0:T(8,128)(2,1)}, bf16[1,512,768]{1,2,0:T(8,128)(2,1)S(1)}, u32[]{:S(2)}) copy-start(bf16[1,512,768]{1,2,0:T(8,128)(2,1)S(1)} %slice.383) | copy-start | bytes 2359300
  257.6 80.7 %copy-start.163 = (f32[768]{0:T(1024)S(1)}, f32[768]{0:T(1024)}, u32[]{:S(2)}) copy-start(f32[768]{0:T(1024)} %get-tuple-element.298) | copy-start | bytes 9220
  257.6 80.7 %copy-start.221 = (f32[768]{0:T(1024)S(1)}, f32[768]{0:T(1024)}, u32[]{:S(2)}) copy-start(f32[768]{0:T(1024)} %get-tuple-element.305) | copy-start | bytes 9220
  265.2 78.0 %copy-start.139 = (f32[512]{0:T(512)}, f32[512]{0:T(512)S(1)}, u32[]{:S(2)}) copy-start(f32[512]{0:T(512)S(1)} %broadcast_multiply_fusion.6) | copy-start | bytes 6148
  266.7 76.6 %copy-start.149 = (f32[512]{0:T(512)}, f32[512]{0:T(512)S(1)}, u32[]{:S(2)}) copy-start(f32[512]{0:T(512)S(1)} %multiply_reduce_fusion.26) | copy-start | bytes 6148
  266.7 76.6 %copy-start.206 = (f32[512]{0:T(512)}, f32[512]{0:T(512)S(1)}, u32[]{:S(2)}) copy-start(f32[512]{0:T(512)S(1)} %fusion.238) | copy-start | bytes 6148
  419.4 127.7 %copy-start.135 = (f32[512]{0:T(512)}, f32[512]{0:T(512)S(1)}, u32[]{:S(2)}) copy-start(f32[512]{0:T(512)S(1)} %broadcast_multiply_fusion.1) | copy-start | bytes 6148
  436.4 110.7 %copy-start.137 = (f32[512]{0:T(512)}, f32[512]{0:T(512)S(1)}, u32[]{:S(2)}) copy-start(f32[512]{0:T(512)S(1)} %broadcast_multiply_fusion.5) | copy-start | bytes 6148
  437.9 73.7 %copy-start.200 = (f32[512]{0:T(512)}, f32[512]{0:T(512)S(1)}, u32[]{:S(2)}) copy-start(f32[512]{0:T(512)S(1)} %fusion.243) | copy-start | bytes 6148
  437.9 61.7 %copy-start.203 = (f32[512]{0:T(512)}, f32[512]{0:T(512)S(1)}, u32[]{:S(2)}) copy-start(f32[512]{0:T(512)S(1)} %fusion.239) | copy-start | bytes 6148
  439.2 60.4 %copy-start.188 = (f32[1,3072]{1,0:T(1,128)S(1)}, f32[1,3072]{1,0:T(1,128)}, u32[]{:S(2)}) copy-start(f32[1,3072]{1,0:T(1,128)} %slice.331) | copy-start | bytes 36868
  766.2 395.1 %reduce-scatter.11.cloned.1.call-start = ((), (), s32[]{:S(2)}) async-start(), calls=%async_computation.7 | async-start | bytes 5308416 | tf_op jit(solution)/shard_map/reduce_scatter | solution.py:182
  782.3 477.7 %reduce-scatter.9.cloned.1.call-start = ((), (), s32[]{:S(2)}) async-start(), calls=%async_computation.6 | async-start | bytes 5308416 | tf_op jit(solution)/shard_map/reduce_scatter | solution.py:182
  798.5 560.0 %reduce-scatter.5.cloned.1.call-start = ((), (), s32[]{:S(2)}) async-start(), calls=%async_computation.4 | async-start | bytes 5308416 | tf_op jit(solution)/shard_map/reduce_scatter | solution.py:179
  809.7 647.7 %reduce-scatter.7.cloned.1.call-start = ((), (), s32[]{:S(2)}) async-start(), calls=%async_computation.5 | async-start | bytes 5308416 | tf_op jit(solution)/shard_map/reduce_scatter | solution.py:179
  820.7 773.9 %all-reduce.14.cloned.1.call-start = ((), (), s32[]{:S(2)}) async-start(), calls=%async_computation.14 | async-start | bytes 14155776 | tf_op jit(solution)/shard_map/psum | solution.py:189
  (257 other events, 1452.0 us)
Sparse Core Ops, SparseCore 0:
  12.0 83.7 all-gather.14
  98.5 78.1 all-gather.16
  179.5 77.9 all-gather.18
  260.2 78.0 all-gather.20
  340.9 78.0 all-gather.22
  421.5 78.0 all-gather.24
  766.3 296.9 all-reduce.15
  1067.0 94.2 reduce-scatter.10
  1164.9 95.0 reduce-scatter.8
  1263.5 95.0 reduce-scatter.4
  1362.2 95.1 reduce-scatter.6
  1461.2 133.3 all-reduce.13
where the time goes:
time: 1630 us; the launch traced here: 1620 us
  waiting for transfers between devices  805 us (49%)
  matrix products  425 us (26%)
  local copies, waits for them, and re-layouts  209 us (13%)
  blocking collectives  89.3 us (5%)
  other arithmetic  73.1 us (4%)
  between operations  20.4 us (1%)
    unnamed x13, waiting for transfers between devices  199 us
    reduce_scatter x2, waiting for transfers between devices, reduce_layer(): lax.psum_scatter(grads[1].astype(jnp.bfloat16), 'fsdp', scatter_dimension...  193 us
    reduce_scatter x2, waiting for transfers between devices, reduce_layer(): lax.psum_scatter(grads[2].astype(jnp.bfloat16), 'fsdp', scatter_dimension...  190 us
    all_gather x2, waiting for transfers between devices, fetch_forward(): lax.all_gather(shards[2], 'fsdp', axis=0, tiled=True)  79.9 us
    unnamed x2, blocking collectives  77.4 us
    psum x1, waiting for transfers between devices, reduce_layer(): return lax.psum((owned[0], owned[1], owned[2], owned[3]), 'dp')  72.4 us
    all_gather x2, waiting for transfers between devices, fetch_forward(): lax.all_gather(shards[0], 'fsdp', axis=1, tiled=True)  71.6 us
    unnamed x570, local copies, waits for them, and re-layouts  63.3 us
  transfers between devices with their start and end apart: 12, of which 9 were waited for; matrix products, arithmetic and copies ran while one was open for 24% of the time, Pallas kernels for 0%

commit v1 on v0

--- a/solution.py
+++ b/solution.py
@@ -3,6 +3,8 @@
 import jax
 import jax.numpy as jnp
 from jax import lax
+from jax.experimental import pallas as pl
+from jax.experimental.pallas import tpu as pltpu
 from jax.sharding import PartitionSpec as P
 
 D = 768
@@ -153,40 +155,211 @@
     return values.reshape(-1, LEN, H, DH)
 
 
+AXES = ("dp", "fsdp")
+GRID = (2, 2, 4, 2)
+ROWS = 96
+
+
+def places():
+    return [
+        (x, c, z, y) for x in range(2) for c in range(2) for z in range(4) for y in range(2)
+    ]
+
+
+def flat(x, c, z, y):
+    return ((x * 2 + c) * 4 + z) * 2 + y
+
+
+def move(value, shift):
+    pairs = [(flat(*place), flat(*shift(*place))) for place in places()]
+    return lax.ppermute(value, AXES, pairs)
+
+
+def swap_core(value):
+    return move(value, lambda x, c, z, y: (x, 1 - c, z, y))
+
+
+def swap_x(value):
+    return move(value, lambda x, c, z, y: (1 - x, c, z, y))
+
+
+def swap_y(value):
+    return move(value, lambda x, c, z, y: (x, c, z, 1 - y))
+
+
+def shift_z(value, step):
+    return move(value, lambda x, c, z, y: (x, c, (z + step) % 4, y))
+
+
+def my_place():
+    dp = lax.axis_index("dp")
+    fsdp = lax.axis_index("fsdp")
+    return (dp // 2, dp % 2, fsdp // 2, fsdp % 2)
+
+
+def spread_blocks(own):
+    column = jnp.stack([own] + [shift_z(own, step) for step in (1, 2, 3)])
+    from_x = swap_x(column)
+    from_y = swap_y(column)
+    corner_low = swap_x(from_y[:2])
+    corner_high = swap_y(from_x[2:])
+    mine = (column, from_x, from_y, corner_low, corner_high)
+    return mine + tuple(swap_core(piece) for piece in mine)
+
+
+PIECES = ((0, 0, 0, 4), (1, 0, 0, 4), (0, 1, 0, 4), (1, 1, 0, 2), (1, 1, 2, 4))
+
+
+def assemble_kernel(kinds, place_ref, *refs):
+    x, c, z, y = (place_ref[index] for index in range(4))
+    pieces = refs[:10]
+    outs = refs[10 : 10 + len(kinds)]
+    sems = refs[10 + len(kinds)]
+    copies = []
+    for other in range(2):
+        for piece, (dx, dy, first, last) in enumerate(PIECES):
+            for k in range(first, last):
+                quarter = (x ^ dx) * 2 + (c ^ other)
+                owner = ((z - k) & 3) * 2 + (y ^ dy)
+                for member, kind in enumerate(kinds):
+                    if kind == "attn":
+                        target = outs[member].at[quarter, pl.ds(owner * 96, 96), :]
+                    elif kind == "inner":
+                        target = outs[member].at[pl.ds(owner * 96, 96), pl.ds(quarter * 768, 768)]
+                    else:
+                        target = outs[member].at[pl.ds(owner * 384 + quarter * 96, 96), :]
+                    copy = pltpu.make_async_copy(
+                        pieces[other * 5 + piece].at[k - first, member],
+                        target,
+                        sems.at[len(copies)],
+                    )
+                    copy.start()
+                    copies.append(copy)
+    for copy in copies:
+        copy.wait()
+
+
+SHAPES = {"attn": (4, D, D), "inner": (D, FF), "outer": (FF, D)}
+
+
+def assemble(kinds, place, pieces):
+    any_spec = pl.BlockSpec(memory_space=pl.ANY)
+    return pl.pallas_call(
+        partial(assemble_kernel, kinds),
+        out_shape=[jax.ShapeDtypeStruct(SHAPES[kind], jnp.bfloat16) for kind in kinds],
+        in_specs=[pl.BlockSpec(memory_space=pltpu.SMEM)] + [any_spec] * 10,
+        out_specs=[any_spec] * len(kinds),
+        scratch_shapes=[pltpu.SemaphoreType.DMA((32 * len(kinds),))],
+        name="assemble",
+    )(place, *pieces)
+
+
+def own_quarter(kind, shard, quarter):
+    if kind == "attn":
+        part = lax.dynamic_index_in_dim(shard, quarter, 0, keepdims=False)
+    elif kind == "inner":
+        part = lax.dynamic_slice_in_dim(shard, quarter * D, D, 1)
+    else:
+        part = lax.dynamic_slice_in_dim(shard, quarter * ROWS, ROWS, 0)
+    return part.astype(jnp.bfloat16)
+
+
+def gather_group(kinds, shards):
+    x, c, z, y = my_place()
+    own = jnp.stack([own_quarter(kind, shard, x * 2 + c) for kind, shard in zip(kinds, shards)])
+    place = jnp.stack([x, c, z, y]).astype(jnp.int32)
+    return assemble(kinds, place, spread_blocks(own))
+
+
+def to_blocks(kind, grad):
+    low = grad.astype(jnp.bfloat16)
+    if kind == "attn":
+        return low.reshape(2, 2, 4, 2, ROWS, D)
+    if kind == "inner":
+        return low.reshape(4, 2, ROWS, 2, 2, D).transpose(3, 4, 0, 1, 2, 5)
+    return low.reshape(4, 2, 2, 2, ROWS, D).transpose(2, 3, 0, 1, 4, 5)
+
+
+def add_low(*values):
+    total = values[0].astype(jnp.float32)
+    for value in values[1:]:
+        total = total + value.astype(jnp.float32)
+    return total.astype(jnp.bfloat16)
+
+
+def pick(value, axis, index):
+    return lax.dynamic_index_in_dim(value, index, axis, keepdims=False)
+
+
+def reduce_group(kinds, grads):
+    x, c, z, y = my_place()
+    blocks = jnp.stack([to_blocks(kind, grad) for kind, grad in zip(kinds, grads)], axis=4)
+    both = add_low(pick(blocks, 1, c), swap_core(pick(blocks, 1, 1 - c)))
+    parts = {}
+    for dx in range(2):
+        for dy in range(2):
+            parts[dx, dy] = pick(pick(both, 2, y ^ dy), 0, x ^ dx)
+    corner = parts[1, 1]
+    by_x = swap_x(corner[:2])
+    by_y = swap_y(corner[2:])
+    for_y = jnp.concatenate([add_low(parts[0, 1][:2], by_x), parts[0, 1][2:]])
+    for_x = jnp.concatenate([parts[1, 0][:2], add_low(parts[1, 0][2:], by_y)])
+    column = add_low(parts[0, 0], swap_x(for_x), swap_y(for_y))
+    total = pick(column, 0, z).astype(jnp.float32)
+    for step in (1, 2, 3):
+        total = total + shift_z(pick(column, 0, (z + step) % 4), step).astype(jnp.float32)
+    low = total.astype(jnp.bfloat16)
+    pair = jnp.stack([low, swap_x(low)])
+    both_pairs = jnp.stack([pair, swap_core(pair)], axis=1)
+    quarters = jnp.stack(
+        [
+            jnp.stack([pick(pick(both_pairs, 1, c ^ core), 0, x ^ side) for core in range(2)])
+            for side in range(2)
+        ]
+    )
+    results = []
+    for member, kind in enumerate(kinds):
+        four = quarters[:, :, member].reshape(4, ROWS, D).astype(jnp.float32)
+        if kind == "attn":
+            results.append(four)
+        elif kind == "inner":
+            results.append(four.transpose(1, 0, 2).reshape(ROWS, FF))
+        else:
+            results.append(four.reshape(4 * ROWS, D))
+    return results
+
+
+def fetch_layer(fast, shards):
+    if not fast:
+        return fetch_forward(shards)
+    (attn,) = gather_group(("attn",), shards[:1])
+    inner, outer = gather_group(("inner", "outer"), shards[1:3])
+    return (attn, inner, outer)
+
+
+def reduce_fast(grads):
+    inner, outer = reduce_group(("inner", "outer"), grads[1:3])
+    (attn,) = reduce_group(("attn",), grads[:1])
+    return (attn, inner, outer)
+
+
 def fetch_forward(shards):
+    low = tuple(shard.astype(jnp.bfloat16) for shard in shards)
     return (
-        lax.all_gather(shards[0], "fsdp", axis=1, tiled=True),
-        lax.all_gather(shards[1], "fsdp", axis=0, tiled=True),
-        lax.all_gather(shards[2], "fsdp", axis=0, tiled=True),
-        lax.all_gather(shards[3], "fsdp", axis=0, tiled=True),
-    )
-
-
-def fetch_backward(shards):
-    return (
-        lax.all_gather(shards[0], "fsdp", axis=1, tiled=True),
-        lax.all_gather(shards[1], "fsdp", axis=0, tiled=True),
-        lax.all_gather(shards[2], "fsdp", axis=0, tiled=True),
-        lax.all_gather(shards[3], "fsdp", axis=0, tiled=True),
+        lax.all_gather(low[0], "fsdp", axis=1, tiled=True),
+        lax.all_gather(low[1], "fsdp", axis=0, tiled=True),
+        lax.all_gather(low[2], "fsdp", axis=0, tiled=True),
     )
 
 
 def reduce_layer(grads):
-    owned = (
+    owned = tuple(
         lax.psum_scatter(
-            grads[0].astype(jnp.bfloat16), "fsdp", scatter_dimension=1, tiled=True
-        ).astype(jnp.float32),
-        lax.psum_scatter(
-            grads[1].astype(jnp.bfloat16), "fsdp", scatter_dimension=0, tiled=True
-        ).astype(jnp.float32),
-        lax.psum_scatter(
-            grads[2].astype(jnp.bfloat16), "fsdp", scatter_dimension=0, tiled=True
-        ).astype(jnp.float32),
-        lax.psum_scatter(
-            grads[3].astype(jnp.bfloat16), "fsdp", scatter_dimension=0, tiled=True
-        ).astype(jnp.float32),
-    )
-    return lax.psum((owned[0], owned[1], owned[2], owned[3]), "dp")
+            grad.astype(jnp.bfloat16), "fsdp", scatter_dimension=axis, tiled=True
+        ).astype(jnp.float32)
+        for grad, axis in zip(grads, (1, 0, 0))
+    )
+    return lax.psum(owned, "dp")
 
 
 def forward_layer(hidden_c, hidden_q, weights, lengths, flag_rows, onehot):
@@ -386,6 +559,7 @@
 
 
 def per_device(
+    fast,
     content,
     query,
     lengths,
@@ -413,9 +587,12 @@
     hidden_q = query.astype(jnp.float32)
     kept_weights = []
     saved_layers = []
+    small_all = lax.all_gather(
+        small_master.astype(jnp.bfloat16), "fsdp", axis=1, tiled=True
+    )
     for layer_index in range(LAYERS):
-        shards = tuple((master[layer_index].astype(jnp.bfloat16) for master in masters))
-        gathered = fetch_forward(shards)
+        shards = tuple((master[layer_index] for master in masters[:3]))
+        gathered = fetch_layer(fast, shards) + (small_all[layer_index],)
         kept_weights.append(gathered)
         hidden_c, hidden_q, saved = forward_layer(
             hidden_c, hidden_q, gathered, lengths, flag_rows, onehot
@@ -426,20 +603,32 @@
     grad_c = content_cot.astype(jnp.float32) * valid_rows
     grad_q = query_cot.astype(jnp.float32) * valid_rows
     layer_grads = [None] * LAYERS
+    small_grads = [None] * LAYERS
     for layer_index in reversed(range(LAYERS)):
-        weights = fetch_backward(
-            tuple((master[layer_index].astype(jnp.bfloat16) for master in masters))
-        )
         grad_c, grad_q, local_grads = backward_layer(
-            saved_layers[layer_index], weights, grad_c, grad_q, lengths, flag_rows, onehot
-        )
-        layer_grads[layer_index] = reduce_layer(local_grads)
+            saved_layers[layer_index],
+            kept_weights[layer_index],
+            grad_c,
+            grad_q,
+            lengths,
+            flag_rows,
+            onehot,
+        )
+        small_grads[layer_index] = local_grads[3]
+        layer_grads[layer_index] = (
+            reduce_fast(local_grads[:3]) if fast else reduce_layer(local_grads[:3])
+        )
+    small_sum = lax.psum(jnp.stack(small_grads), ("dp", "fsdp"))
+    owned = small_master.shape[1]
+    small_own = lax.dynamic_slice_in_dim(
+        small_sum, lax.axis_index("fsdp") * owned, owned, 1
+    )
     reduced = tuple(
         (
             jnp.stack([layer_grads[layer_index][member] for layer_index in range(LAYERS)])
-            for member in range(4)
-        )
-    )
+            for member in range(3)
+        )
+    ) + (small_own,)
     attn_new = adam_update(attn_master, attn_first, attn_second, reduced[0], ATTENTION_RATE)
     inner_new = adam_update(inner_master, inner_first, inner_second, reduced[1], FEED_RATE)
     outer_new = adam_update(outer_master, outer_first, outer_second, reduced[2], FEED_RATE)
@@ -485,8 +674,9 @@
         P(None, "fsdp"),
         P(None, "fsdp"),
     )
+    fast = tuple(mesh.shape.values()) == (4, 8)
     return jax.shard_map(
-        per_device,
+        partial(per_device, fast),
         mesh=mesh,
         in_specs=placed,
         out_specs=(

time: 1630 us -> 1950 us (1.20)
  Pallas kernels: 0 us -> 866 us
  waiting for transfers between devices: 805 us -> 221 us
  local copies, waits for them, and re-layouts: 209 us -> 117 us
  starting transfers between devices: 1.06 us -> 84.7 us
  blocking collectives: 89.3 us -> 38.2 us
  other arithmetic: 73.1 us -> 122 us
  matrix products: 425 us -> 468 us
    pallas_call x0 -> x4, Pallas kernels: none -> 866 us  [assemble(): pl.pallas_call(partial(assemble_kernel, kinds), out_shape=[jax.ShapeDtype...]
    reduce_scatter x4 -> x0, waiting for transfers between devices: 383 us -> none  [the longest x2 193 us: reduce_layer(): lax.psum_scatter(grads[1].astype(jnp.bfloat16), 'fsdp', scatter_dimension...]
    unnamed x13 -> x1, waiting for transfers between devices: 199 us -> 0.02 us
    ppermute x0 -> x88, waiting for transfers between devices: none -> 190 us  [move(): return lax.ppermute(value, AXES, pairs)]
    all_gather x6 -> x0, waiting for transfers between devices: 152 us -> none  [the longest x2 79.9 us: fetch_forward(): lax.all_gather(shards[2], 'fsdp', axis=0, tiled=True)]
    ppermute x0 -> x88, starting transfers between devices: none -> 84.6 us  [move(): return lax.ppermute(value, AXES, pairs)]
    unnamed x2 -> x0, blocking collectives: 77.4 us -> none
    eq x1 -> x0, local copies, waits for them, and re-layouts: 46.2 us -> none  [bucket_onehot(): bucket_ids()[:, :, None] == jnp.arange(NB, dtype=jnp.int32)[None, None, :]]
  transfers between devices with their start and end apart: 12 -> 89, of which waited for: 9 -> 28; matrix products, arithmetic and copies ran while one was open for 24% -> 17% of each run, Pallas kernels for 0% -> 30%
where the time goes in v1:
time: 1950 us; the launch traced here: 1940 us
  Pallas kernels  866 us (44%)
  matrix products  468 us (24%)
  waiting for transfers between devices  221 us (11%)
  other arithmetic  122 us (6%)
  local copies, waits for them, and re-layouts  117 us (6%)
  starting transfers between devices  84.7 us (4%)
  blocking collectives  38.2 us (2%)
    pallas_call x4, Pallas kernels, assemble(): pl.pallas_call(partial(assemble_kernel, kinds), out_shape=[jax.ShapeDtype...  866 us
    ppermute x88, waiting for transfers between devices, move(): return lax.ppermute(value, AXES, pairs)  190 us
    ppermute x88, starting transfers between devices, move(): return lax.ppermute(value, AXES, pairs)  84.6 us
    sub x4, matrix products, attend_back(): grad_probs - jnp.sum(probs * grad_probs, axis=-1, keepdims=True)  69.1 us
    dot_general x4, matrix products, masked_scores(): jnp.einsum('qhd,khd->hqk', query_rows, key_rows, preferred_element_type=j...  63.3 us
    dot_general x4, matrix products, attend_back(): jnp.einsum('hqk,qkb->hb', grad_scores, onehot, preferred_element_type=jnp...  42.5 us
    dot_general x4, matrix products, backward_layer(): jnp.einsum('td,fd->tf', grad_branch, outer_w, preferred_element_type=jnp....  41.1 us
    dot_general x4, matrix products, backward_layer(): jnp.einsum('tf,td->fd', active.astype(jnp.bfloat16), grad_branch, preferr...  40.5 us
  transfers between devices with their start and end apart: 89, of which 28 were waited for; matrix products, arithmetic and copies ran while one was open for 17% of the time, Pallas kernels for 30%

profile of v1, /device:TPU:0, one launch (start us, length us, event | category | flops | bytes accessed | tf_op | source)
XLA Modules:
  0.0 1936.6 jit_solution(2937748270153814950)
XLA Ops:
  22.3 38.2 %all-gather = bf16[8,1200,2]{1,2,0:T(2,128)(2,1)S(1)} all-gather(bf16[1,1200,2]{1,2,0:T(2,128)(2,1)S(1)} %convert_bitcast_fusion), channel_id=1, replica_groups=mesh['dp'=4,'fsdp'=8] {'fsdp'}, dimensions={0}, use_global_device_ids=true | all-gather | bytes 43200 | tf_op jit(solution)/shard_map/all_gather | solution.py:590
  111.5 12.2 collective-permute-done.13
  147.1 145.0 %assemble.4 = bf16[4,768,768]{2,1,0:T(8,128)(2,1)} custom-call(s32[4]{0:T(128)} %pad_add_fusion.place_ref, bf16[4,1,96,768]{3,2,1,0:T(8,128)(2,1)} %copy-done.77, bf16[4,1,96,768]{3,2,1,0:T(8,128)(2,1)} %copy-done.89, bf16[4,1,96,768]{3,2,1,0:T(8,128)(2,1)} %copy-done.88, bf16[2,1,96,768]{3,2,1,0:T(8,128)(2,1)} %collective-permute-done.5.refs_3_, ...), custom_call_target="tpu_custom_call" | custom-call | tf_op jit(solution)/shard_map/assemble/pallas_call | solution.py:247
  301.5 18.0 fusion.323
  319.6 13.7 fusion.317
  363.0 18.1 collective-permute-done.16.refs_2_
  383.0 23.2 %collective-permute-done.40.refs_2_ = bf16[4,2,96,768]{3,2,1,0:T(8,128)(2,1)} collective-permute-done((bf16[4,2,96,768]{3,2,1,0:T(8,128)(2,1)}, bf16[4,2,96,768]{3,2,1,0:T(8,128)(2,1)}, u32[]{:S(2)}, u32[]{:S(2)}) %collective-permute-start.40) | collective-permute-done | bytes 1179680 | tf_op jit(solution)/shard_map/ppermute | solution.py:175
  415.5 145.0 %assemble.6 = bf16[4,768,768]{2,1,0:T(8,128)(2,1)} custom-call(s32[4]{0:T(128)} %pad_add_fusion.place_ref, bf16[4,1,96,768]{3,2,1,0:T(8,128)(2,1)} %pad_maximum_fusion.20.refs_0_, bf16[4,1,96,768]{3,2,1,0:T(8,128)(2,1)} %copy-done.86, bf16[4,1,96,768]{3,2,1,0:T(8,128)(2,1)} %collective-permute-done.28.refs_2_, ...), custom_call_target="tpu_custom_call" | custom-call | tf_op jit(solution)/shard_map/assemble/pallas_call | solution.py:247
  565.0 13.4 collective-permute-done.42.refs_4_
  580.3 288.2 %assemble.5 = (bf16[768,3072]{1,0:T(8,128)(2,1)}, bf16[3072,768]{1,0:T(8,128)(2,1)}) custom-call(s32[4]{0:T(128)} %pad_add_fusion.place_ref, bf16[4,2,96,768]{3,2,1,0:T(8,128)(2,1)} %pad_maximum_fusion.4.refs_0_, bf16[4,2,96,768]{3,2,1,0:T(8,128)(2,1)} %copy-done.69, bf16[4,2,96,768]{3,2,1,0:T(8,128)(2,1)} %copy-done.68, ...), custom_call_target="tpu_custom_call" | custom-call | tf_op jit(solution)/shard_map/assemble/pallas_call | solution.py:247
  896.8 17.0 fusion.326
  913.9 14.6 fusion.320
  955.6 288.2 %assemble.7 = (bf16[768,3072]{1,0:T(8,128)(2,1)}, bf16[3072,768]{1,0:T(8,128)(2,1)}) custom-call(s32[4]{0:T(128)} %pad_add_fusion.place_ref, bf16[4,2,96,768]{3,2,1,0:T(8,128)(2,1)} %pad_maximum_fusion.5.refs_0_, bf16[4,2,96,768]{3,2,1,0:T(8,128)(2,1)} %collective-permute-done.39.refs_1_, bf16[4,2,96,768]{3,2,1,0:T(8,128)(2,1)} %collective-permute-done.40.refs_2_, ...), custom_call_target="tpu_custom_call" | custom-call | tf_op jit(solution)/shard_map/assemble/pallas_call | solution.py:247
  1272.6 15.3 convert_reduce_fusion
  1317.8 16.9 select_convert_fusion.2
  1336.1 17.4 select_convert_fusion.3
  1423.1 16.6 convert_reduce_fusion.2
  1467.1 17.4 select_convert_fusion
  1484.9 17.4 select_convert_fusion.1
  1582.6 11.7 reshape.1071
  1659.9 11.8 reshape.1069
  1720.0 31.5 %all-reduce.2.cloned.1.call-done = f32[2,9600]{1,0:T(2,128)} async-done(((f32[2,9600]{1,0:T(2,128)}), f32[2,9600]{1,0:T(2,128)}) %all-reduce.2.cloned.1.call-update) | async-done | bytes 76816 | tf_op jit(solution)/shard_map/psum | solution.py:621
  1831.5 20.4 %collective-permute-done.82 = bf16[4,2,96,768]{3,2,1,0:T(8,128)(2,1)S(1)} collective-permute-done((bf16[4,2,96,768]{3,2,1,0:T(8,128)(2,1)S(1)}, bf16[4,2,96,768]{3,2,1,0:T(8,128)(2,1)S(1)}, u32[]{:S(2)}, u32[]{:S(2)}) %collective-permute-start.82) | collective-permute-done | bytes 1179680 | tf_op jit(solution)/shard_map/ppermute | solution.py:175
  1860.0 15.1 collective-permute-done.72
  (1084 shorter events, 691.0 us)
Async XLA Ops:
  7.2 1744.2 %all-reduce.2.cloned.1.call-start = ((), (), s32[]{:S(2)}) async-start(), calls=%async_computation | async-start | bytes 153600 | tf_op jit(solution)/shard_map/psum | solution.py:621
  10.7 70.4 %collective-permute-start.26 = (bf16[1,96,768]{2,1,0:T(8,128)(2,1)}, bf16[1,96,768]{2,1,0:T(8,128)(2,1)}, u32[]{:S(2)}, u32[]{:S(2)}) collective-permute-start(bf16[1,96,768]{2,1,0:T(8,128)(2,1)} %fusion.436), channel_id=1, source_target_pairs={{0,6},{1,7},{2,0},{3,1},{4,2},{5,3},{6,4},{7,5},{8,14},{9,15},{10,... | collective-permute-start | bytes 442376 | tf_op jit(solution)/shard_map/ppermute | solution.py:175
  15.8 74.0 %collective-permute-start.25 = (bf16[1,96,768]{2,1,0:T(8,128)(2,1)}, bf16[1,96,768]{2,1,0:T(8,128)(2,1)}, u32[]{:S(2)}, u32[]{:S(2)}) collective-permute-start(bf16[1,96,768]{2,1,0:T(8,128)(2,1)} %fusion.436), channel_id=1, source_target_pairs={{0,4},{1,5},{2,6},{3,7},{4,0},{5,1},{6,2},{7,3},{8,12},{9,13},{10,... | collective-permute-start | bytes 442376 | tf_op jit(solution)/shard_map/ppermute | solution.py:175
  17.3 58.2 %collective-permute-start.2 = (bf16[1,96,768]{2,1,0:T(8,128)(2,1)}, bf16[1,96,768]{2,1,0:T(8,128)(2,1)}, u32[]{:S(2)}, u32[]{:S(2)}) collective-permute-start(bf16[1,96,768]{2,1,0:T(8,128)(2,1)} %fusion.435), channel_id=1, source_target_pairs={{0,6},{1,7},{2,0},{3,1},{4,2},{5,3},{6,4},{7,5},{8,14},{9,15},{10,... | collective-permute-start | bytes 442376 | tf_op jit(solution)/shard_map/ppermute | solution.py:175
  17.8 57.8 %collective-permute-start.1 = (bf16[1,96,768]{2,1,0:T(8,128)(2,1)}, bf16[1,96,768]{2,1,0:T(8,128)(2,1)}, u32[]{:S(2)}, u32[]{:S(2)}) collective-permute-start(bf16[1,96,768]{2,1,0:T(8,128)(2,1)} %fusion.435), channel_id=1, source_target_pairs={{0,4},{1,5},{2,6},{3,7},{4,0},{5,1},{6,2},{7,3},{8,12},{9,13},{10,... | collective-permute-start | bytes 442376 | tf_op jit(solution)/shard_map/ppermute | solution.py:175
  20.3 56.4 %collective-permute-start = (bf16[1,96,768]{2,1,0:T(8,128)(2,1)}, bf16[1,96,768]{2,1,0:T(8,128)(2,1)}, u32[]{:S(2)}, u32[]{:S(2)}) collective-permute-start(bf16[1,96,768]{2,1,0:T(8,128)(2,1)} %fusion.435), channel_id=1, source_target_pairs={{0,2},{1,3},{2,4},{3,5},{4,6},{5,7},{6,0},{7,1},{8,10},{9,11},{10,... | collective-permute-start | bytes 442376 | tf_op jit(solution)/shard_map/ppermute | solution.py:175
  145.7 206.3 %collective-permute-start.31 = (bf16[4,1,96,768]{3,2,1,0:T(8,128)(2,1)}, bf16[4,1,96,768]{3,2,1,0:T(8,128)(2,1)}, u32[]{:S(2)}, u32[]{:S(2)}) collective-permute-start(bf16[4,1,96,768]{3,2,1,0:T(8,128)(2,1)} %pad_maximum_fusion.20.refs_0_), channel_id=1, source_target_pairs={{0,8},{1,9},{2,10},{3,11},{4,12},{5,13},{6,14},{7,15},{8,0},{9,1},... | collective-permute-start | bytes 1769480 | tf_op jit(solution)/shard_map/ppermute | solution.py:175
  146.3 414.3 %collective-permute-start.19 = (bf16[4,2,96,768]{3,2,1,0:T(8,128)(2,1)}, bf16[4,2,96,768]{3,2,1,0:T(8,128)(2,1)}, u32[]{:S(2)}, u32[]{:S(2)}) collective-permute-start(bf16[4,2,96,768]{3,2,1,0:T(8,128)(2,1)} %pad_maximum_fusion.4.refs_0_), channel_id=1, source_target_pairs={{0,8},{1,9},{2,10},{3,11},{4,12},{5,13},{6,14},{7,15},{8,0},{9,1},... | collective-permute-start | bytes 3538952 | tf_op jit(solution)/shard_map/ppermute | solution.py:175
  146.3 207.7 %collective-permute-start.29 = (bf16[2,1,96,768]{3,2,1,0:T(8,128)(2,1)}, bf16[2,1,96,768]{3,2,1,0:T(8,128)(2,1)}, u32[]{:S(2)}, u32[]{:S(2)}) collective-permute-start(bf16[2,1,96,768]{3,2,1,0:T(8,128)(2,1)} %slice.529), channel_id=1, source_target_pairs={{0,16},{1,17},{2,18},{3,19},{4,20},{5,21},{6,22},{7,23},{8,24},{9,... | collective-permute-start | bytes 884744 | tf_op jit(solution)/shard_map/ppermute | solution.py:175
  147.1 208.3 %collective-permute-start.30 = (bf16[2,1,96,768]{3,2,1,0:T(8,128)(2,1)}, bf16[2,1,96,768]{3,2,1,0:T(8,128)(2,1)}, u32[]{:S(2)}, u32[]{:S(2)}) collective-permute-start(bf16[2,1,96,768]{3,2,1,0:T(8,128)(2,1)} %slice.530), channel_id=1, source_target_pairs={{0,1},{1,0},{2,3},{3,2},{4,5},{5,4},{6,7},{7,6},{8,9},{9,8},{10,11... | collective-permute-start | bytes 884744 | tf_op jit(solution)/shard_map/ppermute | solution.py:175
  147.1 208.6 %collective-permute-start.33 = (bf16[4,1,96,768]{3,2,1,0:T(8,128)(2,1)}, bf16[4,1,96,768]{3,2,1,0:T(8,128)(2,1)}, u32[]{:S(2)}, u32[]{:S(2)}) collective-permute-start(bf16[4,1,96,768]{3,2,1,0:T(8,128)(2,1)} %collective-permute-done.28.refs_2_), channel_id=1, source_target_pairs={{0,8},{1,9},{2,10},{3,11},{4,12},{5,13},{6,14},{7,15},{8,0},{9,1},... | collective-permute-start | bytes 1769480 | tf_op jit(solution)/shard_map/ppermute | solution.py:175
  355.6 205.0 %collective-permute-start.39 = (bf16[4,2,96,768]{3,2,1,0:T(8,128)(2,1)}, bf16[4,2,96,768]{3,2,1,0:T(8,128)(2,1)}, u32[]{:S(2)}, u32[]{:S(2)}) collective-permute-start(bf16[4,2,96,768]{3,2,1,0:T(8,128)(2,1)} %pad_maximum_fusion.5.refs_0_), channel_id=1, source_target_pairs={{0,16},{1,17},{2,18},{3,19},{4,20},{5,21},{6,22},{7,23},{8,24},{9,... | collective-permute-start | bytes 3538952 | tf_op jit(solution)/shard_map/ppermute | solution.py:175
  411.8 151.1 %collective-permute-start.17 = (bf16[2,2,96,768]{3,2,1,0:T(8,128)(2,1)}, bf16[2,2,96,768]{3,2,1,0:T(8,128)(2,1)}, u32[]{:S(2)}, u32[]{:S(2)}) collective-permute-start(bf16[2,2,96,768]{3,2,1,0:T(8,128)(2,1)} %slice.523), channel_id=1, source_target_pairs={{0,16},{1,17},{2,18},{3,19},{4,20},{5,21},{6,22},{7,23},{8,24},{9,... | collective-permute-start | bytes 1769480 | tf_op jit(solution)/shard_map/ppermute | solution.py:175
  413.1 150.2 %collective-permute-start.18 = (bf16[2,2,96,768]{3,2,1,0:T(8,128)(2,1)}, bf16[2,2,96,768]{3,2,1,0:T(8,128)(2,1)}, u32[]{:S(2)}, u32[]{:S(2)}) collective-permute-start(bf16[2,2,96,768]{3,2,1,0:T(8,128)(2,1)} %slice.524), channel_id=1, source_target_pairs={{0,1},{1,0},{2,3},{3,2},{4,5},{5,4},{6,7},{7,6},{8,9},{9,8},{10,11... | collective-permute-start | bytes 1769480 | tf_op jit(solution)/shard_map/ppermute | solution.py:175
  414.8 148.4 %collective-permute-start.41 = (bf16[2,2,96,768]{3,2,1,0:T(8,128)(2,1)}, bf16[2,2,96,768]{3,2,1,0:T(8,128)(2,1)}, u32[]{:S(2)}, u32[]{:S(2)}) collective-permute-start(bf16[2,2,96,768]{3,2,1,0:T(8,128)(2,1)} %slice.542), channel_id=1, source_target_pairs={{0,16},{1,17},{2,18},{3,19},{4,20},{5,21},{6,22},{7,23},{8,24},{9,... | collective-permute-start | bytes 1769480 | tf_op jit(solution)/shard_map/ppermute | solution.py:175
  578.4 377.2 %collective-permute-start.43 = (bf16[4,2,96,768]{3,2,1,0:T(8,128)(2,1)}, bf16[4,2,96,768]{3,2,1,0:T(8,128)(2,1)}, u32[]{:S(2)}, u32[]{:S(2)}) collective-permute-start(bf16[4,2,96,768]{3,2,1,0:T(8,128)(2,1)} %pad_maximum_fusion.5.refs_0_), channel_id=1, source_target_pairs={{0,8},{1,9},{2,10},{3,11},{4,12},{5,13},{6,14},{7,15},{8,0},{9,1},... | collective-permute-start | bytes 3538952 | tf_op jit(solution)/shard_map/ppermute | solution.py:175
  578.4 377.2 %collective-permute-start.45 = (bf16[4,2,96,768]{3,2,1,0:T(8,128)(2,1)}, bf16[4,2,96,768]{3,2,1,0:T(8,128)(2,1)}, u32[]{:S(2)}, u32[]{:S(2)}) collective-permute-start(bf16[4,2,96,768]{3,2,1,0:T(8,128)(2,1)} %collective-permute-done.40.refs_2_), channel_id=1, source_target_pairs={{0,8},{1,9},{2,10},{3,11},{4,12},{5,13},{6,14},{7,15},{8,0},{9,1},... | collective-permute-start | bytes 3538952 | tf_op jit(solution)/shard_map/ppermute | solution.py:175
  578.9 376.7 %collective-permute-start.44 = (bf16[4,2,96,768]{3,2,1,0:T(8,128)(2,1)}, bf16[4,2,96,768]{3,2,1,0:T(8,128)(2,1)}, u32[]{:S(2)}, u32[]{:S(2)}) collective-permute-start(bf16[4,2,96,768]{3,2,1,0:T(8,128)(2,1)} %collective-permute-done.39.refs_1_), channel_id=1, source_target_pairs={{0,8},{1,9},{2,10},{3,11},{4,12},{5,13},{6,14},{7,15},{8,0},{9,1},... | collective-permute-start | bytes 3538952 | tf_op jit(solution)/shard_map/ppermute | solution.py:175
  579.0 376.6 %collective-permute-start.46 = (bf16[2,2,96,768]{3,2,1,0:T(8,128)(2,1)}, bf16[2,2,96,768]{3,2,1,0:T(8,128)(2,1)}, u32[]{:S(2)}, u32[]{:S(2)}) collective-permute-start(bf16[2,2,96,768]{3,2,1,0:T(8,128)(2,1)} %collective-permute-done.41.refs_3_), channel_id=1, source_target_pairs={{0,8},{1,9},{2,10},{3,11},{4,12},{5,13},{6,14},{7,15},{8,0},{9,1},... | collective-permute-start | bytes 1769480 | tf_op jit(solution)/shard_map/ppermute | solution.py:175
  579.4 376.2 %collective-permute-start.47 = (bf16[2,2,96,768]{3,2,1,0:T(8,128)(2,1)}, bf16[2,2,96,768]{3,2,1,0:T(8,128)(2,1)}, u32[]{:S(2)}, u32[]{:S(2)}) collective-permute-start(bf16[2,2,96,768]{3,2,1,0:T(8,128)(2,1)} %collective-permute-done.42.refs_4_), channel_id=1, source_target_pairs={{0,8},{1,9},{2,10},{3,11},{4,12},{5,13},{6,14},{7,15},{8,0},{9,1},... | collective-permute-start | bytes 1769480 | tf_op jit(solution)/shard_map/ppermute | solution.py:175
  1574.9 111.4 %collective-permute-start.58 = (bf16[2,4,2,1,96,768]{5,4,2,1,0,3:T(8,128)(2,1)}, bf16[2,4,2,1,96,768]{5,4,2,1,0,3:T(8,128)(2,1)}, u32[]{:S(2)}, u32[]{:S(2)}) collective-permute-start(bf16[2,4,2,1,96,768]{5,4,2,1,0,3:T(8,128)(2,1)} %dynamic-slice_bitcast_fusion), channel_id=1, source_target_pairs={{0,8},{1,9},{2,10},{3,11},{4,12},{5,13},{6,14},{7,15},{8,0},{9,1},... | collective-permute-start | bytes 7077896 | tf_op jit(solution)/shard_map/ppermute | solution.py:175
  1603.9 182.7 %collective-permute-start.78 = (bf16[2,4,2,2,96,768]{5,4,3,2,1,0:T(8,128)(2,1)}, bf16[2,4,2,2,96,768]{5,4,3,2,1,0:T(8,128)(2,1)}, u32[]{:S(2)}, u32[]{:S(2)}) collective-permute-start(bf16[2,4,2,2,96,768]{5,4,3,2,1,0:T(8,128)(2,1)} %fusion.95), channel_id=1, source_target_pairs={{0,8},{1,9},{2,10},{3,11},{4,12},{5,13},{6,14},{7,15},{8,0},{9,1},... | collective-permute-start | bytes 14155784 | tf_op jit(solution)/shard_map/ppermute | solution.py:175
  1679.7 119.9 %collective-permute-start.68 = (bf16[2,4,2,2,96,768]{5,4,3,2,1,0:T(8,128)(2,1)}, bf16[2,4,2,2,96,768]{5,4,3,2,1,0:T(8,128)(2,1)}, u32[]{:S(2)}, u32[]{:S(2)}) collective-permute-start(bf16[2,4,2,2,96,768]{5,4,3,2,1,0:T(8,128)(2,1)} %fusion.99), channel_id=1, source_target_pairs={{0,8},{1,9},{2,10},{3,11},{4,12},{5,13},{6,14},{7,15},{8,0},{9,1},... | collective-permute-start | bytes 14155784 | tf_op jit(solution)/shard_map/ppermute | solution.py:175
  1707.8 51.4 %collective-permute-start.52 = (bf16[4,1,96,768]{3,2,0,1:T(8,128)(2,1)S(1)}, bf16[4,1,96,768]{3,2,0,1:T(8,128)(2,1)}, u32[]{:S(2)}, u32[]{:S(2)}) collective-permute-start(bf16[4,1,96,768]{3,2,0,1:T(8,128)(2,1)S(1)} %pad_maximum_fusion.22), channel_id=1, source_target_pairs={{0,1},{1,0},{2,3},{3,2},{4,5},{5,4},{6,7},{7,6},{8,9},{9,8},{10,11... | collective-permute-start | bytes 1769480 | tf_op jit(solution)/shard_map/ppermute | solution.py:175
  (360 other events, 10735.6 us)
Sparse Core Ops, SparseCore 0:
  1631.0 120.3 all-reduce.1

commit v2 on v1

--- a/solution.py
+++ b/solution.py
@@ -210,11 +210,48 @@
 PIECES = ((0, 0, 0, 4), (1, 0, 0, 4), (0, 1, 0, 4), (1, 1, 0, 2), (1, 1, 2, 4))
 
 
-def assemble_kernel(kinds, place_ref, *refs):
+def dot_nn(left, right):
+    return jnp.dot(left, right, preferred_element_type=jnp.float32)
+
+
+def dot_nt(left, right):
+    return lax.dot_general(
+        left, right, (((1,), (1,)), ((), ())), preferred_element_type=jnp.float32
+    )
+
+
+def dot_tn(left, right):
+    return lax.dot_general(
+        left, right, (((0,), (0,)), ((), ())), preferred_element_type=jnp.float32
+    )
+
+
+ANY_SPEC = pl.BlockSpec(memory_space=pl.ANY)
+VMEM_SPEC = pl.BlockSpec(memory_space=pltpu.VMEM)
+SMEM_SPEC = pl.BlockSpec(memory_space=pltpu.SMEM)
+TALL = 2 * LEN
+HALF = 256
+PARAMS = pltpu.CompilerParams(vmem_limit_bytes=60 * 1024 * 1024)
+
+
+def norm_parts(values):
+    centre = values - jnp.mean(values, axis=-1, keepdims=True)
+    spread = jnp.mean(centre * centre, axis=-1, keepdims=True)
+    scale = lax.rsqrt(spread + NORM_EPS)
+    return (centre * scale, scale)
+
+
+def norm_back(unit, scale, grad, gain):
+    scaled = grad * gain
+    return scale * (
+        scaled
+        - jnp.mean(scaled, axis=-1, keepdims=True)
+        - unit * jnp.mean(scaled * unit, axis=-1, keepdims=True)
+    )
+
+
+def start_fetch(kinds, place_ref, pieces, targets, sems):
     x, c, z, y = (place_ref[index] for index in range(4))
-    pieces = refs[:10]
-    outs = refs[10 : 10 + len(kinds)]
-    sems = refs[10 + len(kinds)]
     copies = []
     for other in range(2):
         for piece, (dx, dy, first, last) in enumerate(PIECES):
@@ -223,11 +260,18 @@
                 owner = ((z - k) & 3) * 2 + (y ^ dy)
                 for member, kind in enumerate(kinds):
                     if kind == "attn":
-                        target = outs[member].at[quarter, pl.ds(owner * 96, 96), :]
+                        target = targets[member].at[
+                            quarter, pl.ds(pl.multiple_of(owner * ROWS, ROWS), ROWS), :
+                        ]
                     elif kind == "inner":
-                        target = outs[member].at[pl.ds(owner * 96, 96), pl.ds(quarter * 768, 768)]
+                        target = targets[member].at[
+                            pl.ds(pl.multiple_of(owner * ROWS, ROWS), ROWS),
+                            pl.ds(pl.multiple_of(quarter * D, D), D),
+                        ]
                     else:
-                        target = outs[member].at[pl.ds(owner * 384 + quarter * 96, 96), :]
+                        target = targets[member].at[
+                            pl.ds(pl.multiple_of(owner * 384 + quarter * ROWS, ROWS), ROWS), :
+                        ]
                     copy = pltpu.make_async_copy(
                         pieces[other * 5 + piece].at[k - first, member],
                         target,
@@ -235,113 +279,662 @@
                     )
                     copy.start()
                     copies.append(copy)
-    for copy in copies:
+    return copies
+
+
+def project_kernel(place_ref, low_ref, small_ref, *refs):
+    pieces = refs[:10]
+    q_ref, k_ref, v_ref, w_out, w_ref, sems, out_sem = refs[10:]
+    for copy in start_fetch(("attn",), place_ref, pieces, (w_ref,), sems):
         copy.wait()
-
-
-SHAPES = {"attn": (4, D, D), "inner": (D, FF), "outer": (FF, D)}
-
-
-def assemble(kinds, place, pieces):
-    any_spec = pl.BlockSpec(memory_space=pl.ANY)
+    keep = pltpu.make_async_copy(w_ref, w_out, out_sem)
+    keep.start()
+    bias_q = small_ref[0:1, :]
+    bias_v = small_ref[1:2, :]
+    for row in range(0, TALL, HALF):
+        rows = low_ref[row : row + HALF, :]
+        q_ref[row : row + HALF, :] = (dot_nn(rows, w_ref[0]) + bias_q).astype(jnp.bfloat16)
+        if row < LEN:
+            k_ref[row : row + HALF, :] = dot_nn(rows, w_ref[1]).astype(jnp.bfloat16)
+            v_ref[row : row + HALF, :] = (dot_nn(rows, w_ref[2]) + bias_v).astype(jnp.bfloat16)
+    keep.wait()
+
+
+def project(place, low, small, pieces):
     return pl.pallas_call(
-        partial(assemble_kernel, kinds),
-        out_shape=[jax.ShapeDtypeStruct(SHAPES[kind], jnp.bfloat16) for kind in kinds],
-        in_specs=[pl.BlockSpec(memory_space=pltpu.SMEM)] + [any_spec] * 10,
-        out_specs=[any_spec] * len(kinds),
-        scratch_shapes=[pltpu.SemaphoreType.DMA((32 * len(kinds),))],
-        name="assemble",
-    )(place, *pieces)
-
-
-def own_quarter(kind, shard, quarter):
-    if kind == "attn":
-        part = lax.dynamic_index_in_dim(shard, quarter, 0, keepdims=False)
-    elif kind == "inner":
-        part = lax.dynamic_slice_in_dim(shard, quarter * D, D, 1)
-    else:
-        part = lax.dynamic_slice_in_dim(shard, quarter * ROWS, ROWS, 0)
-    return part.astype(jnp.bfloat16)
-
-
-def gather_group(kinds, shards):
-    x, c, z, y = my_place()
-    own = jnp.stack([own_quarter(kind, shard, x * 2 + c) for kind, shard in zip(kinds, shards)])
-    place = jnp.stack([x, c, z, y]).astype(jnp.int32)
-    return assemble(kinds, place, spread_blocks(own))
-
-
-def to_blocks(kind, grad):
-    low = grad.astype(jnp.bfloat16)
-    if kind == "attn":
-        return low.reshape(2, 2, 4, 2, ROWS, D)
-    if kind == "inner":
-        return low.reshape(4, 2, ROWS, 2, 2, D).transpose(3, 4, 0, 1, 2, 5)
-    return low.reshape(4, 2, 2, 2, ROWS, D).transpose(2, 3, 0, 1, 4, 5)
-
-
-def add_low(*values):
-    total = values[0].astype(jnp.float32)
-    for value in values[1:]:
-        total = total + value.astype(jnp.float32)
-    return total.astype(jnp.bfloat16)
-
-
-def pick(value, axis, index):
-    return lax.dynamic_index_in_dim(value, index, axis, keepdims=False)
-
-
-def reduce_group(kinds, grads):
-    x, c, z, y = my_place()
-    blocks = jnp.stack([to_blocks(kind, grad) for kind, grad in zip(kinds, grads)], axis=4)
-    both = add_low(pick(blocks, 1, c), swap_core(pick(blocks, 1, 1 - c)))
-    parts = {}
-    for dx in range(2):
-        for dy in range(2):
-            parts[dx, dy] = pick(pick(both, 2, y ^ dy), 0, x ^ dx)
-    corner = parts[1, 1]
-    by_x = swap_x(corner[:2])
-    by_y = swap_y(corner[2:])
-    for_y = jnp.concatenate([add_low(parts[0, 1][:2], by_x), parts[0, 1][2:]])
-    for_x = jnp.concatenate([parts[1, 0][:2], add_low(parts[1, 0][2:], by_y)])
-    column = add_low(parts[0, 0], swap_x(for_x), swap_y(for_y))
-    total = pick(column, 0, z).astype(jnp.float32)
-    for step in (1, 2, 3):
-        total = total + shift_z(pick(column, 0, (z + step) % 4), step).astype(jnp.float32)
-    low = total.astype(jnp.bfloat16)
-    pair = jnp.stack([low, swap_x(low)])
-    both_pairs = jnp.stack([pair, swap_core(pair)], axis=1)
-    quarters = jnp.stack(
-        [
-            jnp.stack([pick(pick(both_pairs, 1, c ^ core), 0, x ^ side) for core in range(2)])
-            for side in range(2)
-        ]
-    )
-    results = []
-    for member, kind in enumerate(kinds):
-        four = quarters[:, :, member].reshape(4, ROWS, D).astype(jnp.float32)
-        if kind == "attn":
-            results.append(four)
-        elif kind == "inner":
-            results.append(four.transpose(1, 0, 2).reshape(ROWS, FF))
-        else:
-            results.append(four.reshape(4 * ROWS, D))
-    return results
-
-
-def fetch_layer(fast, shards):
-    if not fast:
-        return fetch_forward(shards)
-    (attn,) = gather_group(("attn",), shards[:1])
-    inner, outer = gather_group(("inner", "outer"), shards[1:3])
-    return (attn, inner, outer)
-
-
-def reduce_fast(grads):
-    inner, outer = reduce_group(("inner", "outer"), grads[1:3])
-    (attn,) = reduce_group(("attn",), grads[:1])
-    return (attn, inner, outer)
-
+        project_kernel,
+        out_shape=[
+            jax.ShapeDtypeStruct((TALL, D), jnp.bfloat16),
+            jax.ShapeDtypeStruct((LEN, D), jnp.bfloat16),
+            jax.ShapeDtypeStruct((LEN, D), jnp.bfloat16),
+            jax.ShapeDtypeStruct((4, D, D), jnp.bfloat16),
+        ],
+        in_specs=[SMEM_SPEC, VMEM_SPEC, VMEM_SPEC] + [ANY_SPEC] * 10,
+        out_specs=[VMEM_SPEC] * 3 + [ANY_SPEC],
+        scratch_shapes=[
+            pltpu.VMEM((4, D, D), jnp.bfloat16),
+            pltpu.SemaphoreType.DMA((32,)),
+            pltpu.SemaphoreType.DMA,
+        ],
+        compiler_params=PARAMS,
+        cost_estimate=pl.CostEstimate(flops=2 * 2048 * D * D, bytes_accessed=16000000, transcendentals=0),
+        name="project",
+    )(place, low, small, *pieces)
+
+
+def build_masks(length, row_flags, col_flags, mask_ref, alive_ref):
+    flags = row_flags[...]
+
+    def body(step, carry):
+        start = pl.multiple_of(step * 64, 64)
+        key = lax.broadcasted_iota(jnp.int32, (64, LEN), 0) + start
+        query = lax.broadcasted_iota(jnp.int32, (64, LEN), 1)
+        valid = key < length
+        free = jnp.broadcast_to(col_flags[pl.ds(start, 64), :], (64, LEN)) == 0.0
+        marked = jnp.broadcast_to(flags, (64, LEN)) == 1.0
+        content_ok = valid & (free | (marked & (key <= query)))
+        query_ok = valid & (key != query) & (free | (key < query))
+        mask_ref[pl.ds(start, 64), :LEN] = content_ok.astype(jnp.float32)
+        mask_ref[pl.ds(start, 64), LEN:] = query_ok.astype(jnp.float32)
+        return carry
+
+    lax.fori_loop(0, 8, body, 0)
+    alive_ref[...] = jnp.max(mask_ref[...], axis=0, keepdims=True)
+
+
+def build_tiles(t_row, tile_ref):
+    spread = jnp.broadcast_to(t_row, (128, 512))
+    rolled = pltpu.roll(spread, 0, 1, stride=1, stride_axis=0)
+    tile_ref[...] = rolled[:, :384]
+
+
+def position_bias(tile_ref, far_ref, head, query_block, key_block):
+    apart = query_block - key_block
+    if apart >= 2:
+        return far_ref[head, 0]
+    if apart <= -2:
+        return far_ref[head, 1]
+    return tile_ref[:, 128 * (apart + 1) : 128 * (apart + 2)]
+
+
+def head_lanes(shape, head):
+    lane = lax.broadcasted_iota(jnp.int32, shape, 1)
+    return (lane >= 64) if head else (lane < 64)
+
+
+def mix_kernel(
+    length_ref, far_ref, q_ref, k_ref, v_ref, row_flags, col_flags, t_ref,
+    a_ref, lse_ref, mask_ref, alive_ref, tile_ref, p_ref, o_ref,
+):
+    pair = pl.program_id(0)
+
+    @pl.when(pair == 0)
+    def _():
+        build_masks(length_ref[0], row_flags, col_flags, mask_ref, alive_ref)
+
+    keys = k_ref[...].astype(jnp.float32) * SCORE_SCALE
+    values_t = v_ref[...].astype(jnp.float32).T.astype(jnp.bfloat16)
+    for head in range(2):
+        build_tiles(t_ref[head], tile_ref.at[head])
+        keys_own = jnp.where(head_lanes(keys.shape, head), keys, 0.0).astype(jnp.bfloat16)
+        for chunk in range(4):
+            at = chunk * HALF
+            scores = dot_nt(keys_own, q_ref[at : at + HALF, :])
+            for side in range(2):
+                lanes = slice(at + side * 128, at + side * 128 + 128)
+                blocks = []
+                peak = None
+                for key_block in range(4):
+                    rows = slice(key_block * 128, key_block * 128 + 128)
+                    block = scores[rows, side * 128 : side * 128 + 128] + position_bias(
+                        tile_ref.at[head], far_ref, pair * 2 + head, (chunk % 2) * 2 + side, key_block
+                    )
+                    block = jnp.where(mask_ref[rows, lanes] > 0.0, block, MASKED)
+                    blocks.append(block)
+                    high = jnp.max(block, axis=0, keepdims=True)
+                    peak = high if peak is None else jnp.maximum(peak, high)
+                total = None
+                for key_block in range(4):
+                    rows = slice(key_block * 128, key_block * 128 + 128)
+                    expo = jnp.exp(blocks[key_block] - peak)
+                    part = jnp.sum(expo, axis=0, keepdims=True)
+                    total = part if total is None else total + part
+                    p_ref[head, rows, lanes] = expo.astype(jnp.bfloat16)
+                lse_ref[head, :, lanes] = jnp.where(
+                    alive_ref[:, lanes] > 0.0, peak + jnp.log(total), 1e30
+                )
+                o_ref[head : head + 1, lanes] = 1.0 / total
+        mixed = dot_nn(values_t[head * 64 : head * 64 + 64, :], p_ref[head])
+        o_ref[8 + head * 64 : 8 + head * 64 + 64, :] = mixed * o_ref[head : head + 1, :]
+    a_ref[...] = o_ref[8:, :].T.astype(jnp.bfloat16)
+
+
+def mix(length, far, tvec, q, k, v, row_flags, col_flags):
+    tall = pl.BlockSpec((TALL, 128), lambda p: (0, p))
+    short = pl.BlockSpec((LEN, 128), lambda p: (0, p))
+    return pl.pallas_call(
+        mix_kernel,
+        grid=(H // 2,),
+        out_shape=[
+            jax.ShapeDtypeStruct((TALL, D), jnp.bfloat16),
+            jax.ShapeDtypeStruct((H, 1, TALL), jnp.float32),
+        ],
+        in_specs=[
+            SMEM_SPEC, SMEM_SPEC, tall, short, short,
+            pl.BlockSpec((1, LEN), lambda p: (0, 0)),
+            pl.BlockSpec((LEN, 1), lambda p: (0, 0)),
+            pl.BlockSpec((2, 1, 512), lambda p: (p, 0, 0)),
+        ],
+        out_specs=[tall, pl.BlockSpec((2, 1, TALL), lambda p: (p, 0, 0))],
+        scratch_shapes=[
+            pltpu.VMEM((LEN, TALL), jnp.float32),
+            pltpu.VMEM((1, TALL), jnp.float32),
+            pltpu.VMEM((2, 128, 384), jnp.float32),
+            pltpu.VMEM((2, LEN, TALL), jnp.bfloat16),
+            pltpu.VMEM((136, TALL), jnp.float32),
+        ],
+        compiler_params=PARAMS,
+        cost_estimate=pl.CostEstimate(flops=6500000000, bytes_accessed=8000000, transcendentals=6300000),
+        name="mix",
+    )(length, far, q, k, v, row_flags, col_flags, tvec)
+
+
+def mix_back_kernel(
+    length_ref, far_ref, q_ref, k_ref, v_ref, da_ref, a_ref, lse_ref, row_flags, col_flags, t_ref,
+    dq_ref, dk_ref, dv_ref, table_ref,
+    mask_ref, alive_ref, tile_ref, p_ref, s_ref, near_ref, d_ref,
+):
+    pair = pl.program_id(0)
+
+    @pl.when(pair == 0)
+    def _():
+        build_masks(length_ref[0], row_flags, col_flags, mask_ref, alive_ref)
+
+    keys = k_ref[...].astype(jnp.float32) * SCORE_SCALE
+    keys_t = keys.T.astype(jnp.bfloat16)
+    product = da_ref[...].astype(jnp.float32) * a_ref[...].astype(jnp.float32)
+    d_ref[...] = product.T
+    values = v_ref[...]
+    grads_k = []
+    grads_v = []
+    near_ref[...] = jnp.zeros(near_ref.shape, jnp.float32)
+    turn = (
+        lax.broadcasted_iota(jnp.int32, (128, 128), 0)
+        + lax.broadcasted_iota(jnp.int32, (128, 128), 1)
+        == 127
+    ).astype(jnp.float32)
+    for head in range(2):
+        build_tiles(t_ref[head], tile_ref.at[head])
+        mine = head_lanes(keys.shape, head)
+        keys_own = jnp.where(mine, keys, 0.0).astype(jnp.bfloat16)
+        values_own = jnp.where(mine, values.astype(jnp.float32), 0.0).astype(jnp.bfloat16)
+        delta = jnp.sum(d_ref[head * 64 : head * 64 + 64, :], axis=0, keepdims=True)
+        far_low = jnp.zeros((8, 128), jnp.float32)
+        far_high = jnp.zeros((8, 128), jnp.float32)
+        for chunk in range(4):
+            at = chunk * HALF
+            scores = dot_nt(keys_own, q_ref[at : at + HALF, :])
+            pulls = dot_nt(values_own, da_ref[at : at + HALF, :])
+            for side in range(2):
+                lanes = slice(at + side * 128, at + side * 128 + 128)
+                log_total = lse_ref[head, :, lanes]
+                shift = delta[:, lanes]
+                for key_block in range(4):
+                    rows = slice(key_block * 128, key_block * 128 + 128)
+                    cols = slice(side * 128, side * 128 + 128)
+                    query_block = (chunk % 2) * 2 + side
+                    block = scores[rows, cols] + position_bias(
+                        tile_ref.at[head], far_ref, pair * 2 + head, query_block, key_block
+                    )
+                    block = jnp.where(mask_ref[rows, lanes] > 0.0, block, MASKED)
+                    prob = jnp.exp(block - log_total)
+                    p_ref[head, rows, lanes] = prob.astype(jnp.bfloat16)
+                    grad = prob * (pulls[rows, cols] - shift)
+                    s_ref[head, rows, lanes] = grad.astype(jnp.bfloat16)
+                    apart = query_block - key_block
+                    if apart >= 2:
+                        far_low = far_low + jnp.sum(grad.reshape(16, 8, 128), axis=0)
+                    elif apart <= -2:
+                        far_high = far_high + jnp.sum(grad.reshape(16, 8, 128), axis=0)
+                    else:
+                        near_ref[head, :, 128 * (apart + 1) : 128 * (apart + 2)] += grad
+        grads_v.append(dot_nn(p_ref[head], da_ref[...]))
+        grads_k.append(dot_nn(s_ref[head], q_ref[...]))
+        d_ref[head * 64 : head * 64 + 64, :] = dot_nn(
+            keys_t[head * 64 : head * 64 + 64, :], s_ref[head]
+        )
+        turned = jnp.dot(
+            turn, near_ref[head], precision=lax.Precision.HIGHEST, preferred_element_type=jnp.float32
+        )
+        aligned = pltpu.roll(turned, 0, 1, stride=1, stride_axis=0)
+        table_ref[head, :, :512] = jnp.sum(aligned, axis=0, keepdims=True)
+        table_ref[head, :, 512:640] = jnp.sum(far_low, axis=0, keepdims=True)
+        table_ref[head, :, 640:] = jnp.sum(far_high, axis=0, keepdims=True)
+    dead = (1.0 - alive_ref[...]) * (1.0 / LEN)
+    uniform = dot_nn(dead.astype(jnp.bfloat16), da_ref[...])
+    first = head_lanes((LEN, 128), 0)
+    dv_ref[...] = (jnp.where(first, grads_v[0], grads_v[1]) + uniform).astype(jnp.bfloat16)
+    dk_ref[...] = (jnp.where(first, grads_k[0], grads_k[1]) * SCORE_SCALE).astype(jnp.bfloat16)
+    dq_ref[...] = d_ref[...].T.astype(jnp.bfloat16)
+
+
+def mix_back(length, far, tvec, q, k, v, da, a, lse, row_flags, col_flags):
+    tall = pl.BlockSpec((TALL, 128), lambda p: (0, p))
+    short = pl.BlockSpec((LEN, 128), lambda p: (0, p))
+    return pl.pallas_call(
+        mix_back_kernel,
+        grid=(H // 2,),
+        out_shape=[
+            jax.ShapeDtypeStruct((TALL, D), jnp.bfloat16),
+            jax.ShapeDtypeStruct((LEN, D), jnp.bfloat16),
+            jax.ShapeDtypeStruct((LEN, D), jnp.bfloat16),
+            jax.ShapeDtypeStruct((H, 1, 768), jnp.float32),
+        ],
+        in_specs=[
+            SMEM_SPEC, SMEM_SPEC, tall, short, short, tall, tall,
+            pl.BlockSpec((2, 1, TALL), lambda p: (p, 0, 0)),
+            pl.BlockSpec((1, LEN), lambda p: (0, 0)),
+            pl.BlockSpec((LEN, 1), lambda p: (0, 0)),
+            pl.BlockSpec((2, 1, 512), lambda p: (p, 0, 0)),
+        ],
+        out_specs=[tall, short, short, pl.BlockSpec((2, 1, 768), lambda p: (p, 0, 0))],
+        scratch_shapes=[
+            pltpu.VMEM((LEN, TALL), jnp.float32),
+            pltpu.VMEM((1, TALL), jnp.float32),
+            pltpu.VMEM((2, 128, 384), jnp.float32),
+            pltpu.VMEM((2, LEN, TALL), jnp.bfloat16),
+            pltpu.VMEM((2, LEN, TALL), jnp.bfloat16),
+            pltpu.VMEM((2, 128, 512), jnp.float32),
+            pltpu.VMEM((128, TALL), jnp.float32),
+        ],
+        compiler_params=PARAMS,
+        cost_estimate=pl.CostEstimate(flops=16000000000, bytes_accessed=12000000, transcendentals=6300000),
+        name="mix_back",
+    )(length, far, q, k, v, da, a, lse, row_flags, col_flags, tvec)
+
+
+GELU_SCALE = 0.7978845608028654
+GELU_CUBE = 0.044715
+
+
+def feed_kernel(place_ref, small_ref, hidden_bias_ref, mix_any, hidden_any, attn_any, *refs):
+    pieces = refs[:10]
+    (
+        resid_out, summed_out, pre_out, next_out, low_out,
+        mix_ref, hidden_ref, wo_ref, inner_ref, outer_ref, resid_ref, total_ref, normed_ref,
+        pre_ref, next_ref, low_ref, sems, load_sems, store_sems,
+    ) = refs[10:]
+    loads = [
+        pltpu.make_async_copy(mix_any, mix_ref, load_sems.at[0]),
+        pltpu.make_async_copy(attn_any.at[3], wo_ref, load_sems.at[1]),
+        pltpu.make_async_copy(hidden_any, hidden_ref, load_sems.at[2]),
+    ]
+    for load in loads:
+        load.start()
+    fetches = start_fetch(("inner", "outer"), place_ref, pieces, (inner_ref, outer_ref), sems)
+    for load in loads:
+        load.wait()
+    for row in range(0, TALL, HALF):
+        rows = slice(row, row + HALF)
+        resid = hidden_ref[rows, :] + dot_nn(mix_ref[rows, :], wo_ref[...]) + small_ref[2:3, :]
+        resid_ref[rows, :] = resid
+        unit, scale = norm_parts(resid)
+        normed = unit * small_ref[3:4, :] + small_ref[4:5, :]
+        normed_ref[rows, :] = normed.astype(jnp.bfloat16)
+        total_ref[rows, :] = normed + small_ref[5:6, :]
+    stores = [pltpu.make_async_copy(resid_ref, resid_out, store_sems.at[0])]
+    stores[0].start()
+    for fetch in fetches:
+        fetch.wait()
+    for chunk in range(4):
+        cols = slice(chunk * D, chunk * D + D)
+
+        def body(step, carry):
+            rows = pl.ds(pl.multiple_of(step * HALF, HALF), HALF)
+            pre = dot_nn(normed_ref[rows, :], inner_ref[:, cols]) + hidden_bias_ref[:, cols]
+            pre_ref[rows, cols] = pre.astype(jnp.bfloat16)
+            tanh = jnp.tanh(GELU_SCALE * (pre + GELU_CUBE * (pre * pre * pre)))
+            active = (pre * (0.5 + 0.5 * tanh)).astype(jnp.bfloat16)
+            total_ref[rows, :] += dot_nn(active, outer_ref[cols, :])
+            return carry
+
+        for step in range(4):
+            body(step, 0)
+        store = pltpu.make_async_copy(
+            pre_ref.at[:, cols], pre_out.at[:, cols], store_sems.at[1 + chunk]
+        )
+        store.start()
+        stores.append(store)
+    store = pltpu.make_async_copy(total_ref, summed_out, store_sems.at[5])
+    store.start()
+    stores.append(store)
+    for row in range(0, TALL, HALF):
+        rows = slice(row, row + HALF)
+        unit, scale = norm_parts(total_ref[rows, :])
+        following = unit * small_ref[6:7, :] + small_ref[7:8, :]
+        next_ref[rows, :] = following
+        low_ref[rows, :] = following.astype(jnp.bfloat16)
+    for index, (source, target) in enumerate(((next_ref, next_out), (low_ref, low_out))):
+        store = pltpu.make_async_copy(source, target, store_sems.at[6 + index])
+        store.start()
+        stores.append(store)
+    for store in stores:
+        store.wait()
+
+
+def feed(place, small, hidden_bias, mixed, hidden, attn, pieces):
+    return pl.pallas_call(
+        feed_kernel,
+        out_shape=[
+            jax.ShapeDtypeStruct((TALL, D), jnp.float32),
+            jax.ShapeDtypeStruct((TALL, D), jnp.float32),
+            jax.ShapeDtypeStruct((TALL, FF), jnp.bfloat16),
+            jax.ShapeDtypeStruct((TALL, D), jnp.float32),
+            jax.ShapeDtypeStruct((TALL, D), jnp.bfloat16),
+        ],
+        in_specs=[SMEM_SPEC, VMEM_SPEC, VMEM_SPEC] + [ANY_SPEC] * 13,
+        out_specs=[ANY_SPEC] * 5,
+        scratch_shapes=[
+            pltpu.VMEM((TALL, D), jnp.bfloat16),
+            pltpu.VMEM((TALL, D), jnp.float32),
+            pltpu.VMEM((D, D), jnp.bfloat16),
+            pltpu.VMEM((D, FF), jnp.bfloat16),
+            pltpu.VMEM((FF, D), jnp.bfloat16),
+            pltpu.VMEM((TALL, D), jnp.float32),
+            pltpu.VMEM((TALL, D), jnp.float32),
+            pltpu.VMEM((TALL, D), jnp.bfloat16),
+            pltpu.VMEM((TALL, FF), jnp.bfloat16),
+            pltpu.VMEM((TALL, D), jnp.float32),
+            pltpu.VMEM((TALL, D), jnp.bfloat16),
+            pltpu.SemaphoreType.DMA((64,)),
+            pltpu.SemaphoreType.DMA((3,)),
+            pltpu.SemaphoreType.DMA((8,)),
+        ],
+        compiler_params=PARAMS,
+        cost_estimate=pl.CostEstimate(flops=2 * TALL * D * (D + 2 * FF), bytes_accessed=40000000, transcendentals=3000000),
+        name="feed",
+    )(place, small, hidden_bias, mixed, hidden, attn, *pieces)
+
+
+def feed_back_kernel(place_ref, small_ref, grad_any, summed_any, resid_any, pre_any, mix_any, attn_any, *refs):
+    pieces = refs[:10]
+    (
+        dresid_out, dmix_out, dwo_out, keep_out, send_out, vec_ref, dhidden_ref,
+        grad_ref, summed_ref, resid_ref, pre_ref, mix_ref, wo_ref, inner_ref, outer_ref,
+        total_ref, branch_ref, normed_ref, active_ref, dpre_ref, dinner_ref, douter_ref,
+        dwo_ref, sems, load_sems, store_sems, block_sems,
+    ) = refs[10:]
+    proj_ref = branch_ref
+    dmix_ref = active_ref
+    x, c, z, y = (place_ref[index] for index in range(4))
+    load = [
+        pltpu.make_async_copy(source, target, load_sems.at[index])
+        for index, (source, target) in enumerate(
+            (
+                (grad_any, grad_ref), (summed_any, summed_ref), (resid_any, resid_ref),
+                (pre_any, pre_ref), (mix_any, mix_ref), (attn_any.at[3], wo_ref),
+            )
+        )
+    ]
+    for copy in load[:3]:
+        copy.start()
+    fetches = start_fetch(("inner", "outer"), place_ref, pieces, (inner_ref, outer_ref), sems)
+    for copy in load[3:]:
+        copy.start()
+    for copy in load[:3]:
+        copy.wait()
+    gain_two_grad = jnp.zeros((1, D), jnp.float32)
+    shift_two_grad = jnp.zeros((1, D), jnp.float32)
+    bias_two_grad = jnp.zeros((1, D), jnp.float32)
+    for row in range(0, TALL, HALF):
+        rows = slice(row, row + HALF)
+        grad = grad_ref[rows, :]
+        unit, scale = norm_parts(summed_ref[rows, :])
+        gain_two_grad += jnp.sum(grad * unit, axis=0, keepdims=True)
+        shift_two_grad += jnp.sum(grad, axis=0, keepdims=True)
+        back = norm_back(unit, scale, grad, small_ref[6:7, :])
+        total_ref[rows, :] = back
+        low = back.astype(jnp.bfloat16)
+        branch_ref[rows, :] = low
+        bias_two_grad += jnp.sum(low.astype(jnp.float32), axis=0, keepdims=True)
+        unit, scale = norm_parts(resid_ref[rows, :])
+        normed_ref[rows, :] = (unit * small_ref[3:4, :] + small_ref[4:5, :]).astype(jnp.bfloat16)
+    vec_ref[5:6, :] = bias_two_grad
+    vec_ref[6:7, :] = gain_two_grad
+    vec_ref[7:8, :] = shift_two_grad
+    for copy in fetches + load[3:]:
+        copy.wait()
+    blocks = []
+
+    def place_block(core, source, target_index):
+        sem = block_sems.at[len(blocks)]
+        keep = pltpu.make_async_copy(source, keep_out.at[target_index], sem)
+        send = pltpu.make_async_copy(source, send_out.at[target_index], sem)
+
+        @pl.when(c == core)
+        def _():
+            keep.start()
+
+        @pl.when(c != core)
+        def _():
+            send.start()
+
+        blocks.append(keep)
+
+    for chunk in range(4):
+        cols = slice(chunk * D, chunk * D + D)
+        bias_grad = jnp.zeros((1, D), jnp.float32)
+        for row in range(0, TALL, HALF):
+            rows = slice(row, row + HALF)
+            pull = dot_nt(branch_ref[rows, :], outer_ref[cols, :])
+            pre = pre_ref[rows, cols].astype(jnp.float32)
+            square = pre * pre
+            tanh = jnp.tanh(GELU_SCALE * pre * (1.0 + GELU_CUBE * square))
+            half = 0.5 + 0.5 * tanh
+            active_ref[rows, :] = (pre * half).astype(jnp.bfloat16)
+            slope = half + (0.5 * GELU_SCALE) * pre * (1.0 - tanh * tanh) * (
+                1.0 + (3.0 * GELU_CUBE) * square
+            )
+            dpre = (pull * slope).astype(jnp.bfloat16)
+            dpre_ref[rows, :] = dpre
+            bias_grad += jnp.sum(dpre.astype(jnp.float32), axis=0, keepdims=True)
+            total_ref[rows, :] += dot_nt(dpre, inner_ref[:, cols])
+        dhidden_ref[:, cols] = bias_grad
+        douter_ref[cols, :] = dot_tn(active_ref[...], branch_ref[...]).astype(jnp.bfloat16)
+        dinner_ref[:, cols] = dot_tn(normed_ref[...], dpre_ref[...]).astype(jnp.bfloat16)
+        for owner in range(8):
+            place_block(
+                chunk % 2,
+                dinner_ref.at[owner * ROWS : owner * ROWS + ROWS, cols],
+                ((chunk // 2) ^ x, (owner % 2) ^ y, ((owner // 2) - z) & 3, 0),
+            )
+        for strip in range(8):
+            quarter = strip % 4
+            start = chunk * D + strip * ROWS
+            place_block(
+                quarter % 2,
+                douter_ref.at[start : start + ROWS, :],
+                ((quarter // 2) ^ x, (strip // 4) ^ y, (chunk - z) & 3, 1),
+            )
+    gain_one_grad = jnp.zeros((1, D), jnp.float32)
+    shift_one_grad = jnp.zeros((1, D), jnp.float32)
+    bias_o_grad = jnp.zeros((1, D), jnp.float32)
+    for row in range(0, TALL, HALF):
+        rows = slice(row, row + HALF)
+        grad = total_ref[rows, :]
+        unit, scale = norm_parts(resid_ref[rows, :])
+        gain_one_grad += jnp.sum(grad * unit, axis=0, keepdims=True)
+        shift_one_grad += jnp.sum(grad, axis=0, keepdims=True)
+        back = norm_back(unit, scale, grad, small_ref[3:4, :])
+        grad_ref[rows, :] = back
+        low = back.astype(jnp.bfloat16)
+        proj_ref[rows, :] = low
+        bias_o_grad += jnp.sum(low.astype(jnp.float32), axis=0, keepdims=True)
+        dmix_ref[rows, :] = dot_nt(low, wo_ref[...]).astype(jnp.bfloat16)
+    dwo_ref[...] = dot_tn(mix_ref[...], proj_ref[...]).astype(jnp.bfloat16)
+    vec_ref[0:2, :] = jnp.zeros((2, D), jnp.float32)
+    vec_ref[2:3, :] = bias_o_grad
+    vec_ref[3:4, :] = gain_one_grad
+    vec_ref[4:5, :] = shift_one_grad
+    stores = [
+        pltpu.make_async_copy(source, target, store_sems.at[index])
+        for index, (source, target) in enumerate(
+            ((grad_ref, dresid_out), (dmix_ref, dmix_out), (dwo_ref, dwo_out))
+        )
+    ]
+    for store in stores:
+        store.start()
+    for copy in blocks + stores:
+        copy.wait()
+
+
+def feed_back(place, small, grad, summed, resid, pre, mixed, attn, pieces):
+    blocks = jax.ShapeDtypeStruct((2, 2, 4, 2, ROWS, D), jnp.bfloat16)
+    return pl.pallas_call(
+        feed_back_kernel,
+        out_shape=[
+            jax.ShapeDtypeStruct((TALL, D), jnp.float32),
+            jax.ShapeDtypeStruct((TALL, D), jnp.bfloat16),
+            jax.ShapeDtypeStruct((D, D), jnp.bfloat16),
+            blocks,
+            blocks,
+            jax.ShapeDtypeStruct((8, D), jnp.float32),
+            jax.ShapeDtypeStruct((1, FF), jnp.float32),
+        ],
+        in_specs=[SMEM_SPEC, VMEM_SPEC] + [ANY_SPEC] * 16,
+        out_specs=[ANY_SPEC] * 5 + [VMEM_SPEC] * 2,
+        scratch_shapes=[
+            pltpu.VMEM((TALL, D), jnp.float32),
+            pltpu.VMEM((TALL, D), jnp.float32),
+            pltpu.VMEM((TALL, D), jnp.float32),
+            pltpu.VMEM((TALL, FF), jnp.bfloat16),
+            pltpu.VMEM((TALL, D), jnp.bfloat16),
+            pltpu.VMEM((D, D), jnp.bfloat16),
+            pltpu.VMEM((D, FF), jnp.bfloat16),
+            pltpu.VMEM((FF, D), jnp.bfloat16),
+            pltpu.VMEM((TALL, D), jnp.float32),
+            pltpu.VMEM((TALL, D), jnp.bfloat16),
+            pltpu.VMEM((TALL, D), jnp.bfloat16),
+            pltpu.VMEM((TALL, D), jnp.bfloat16),
+            pltpu.VMEM((TALL, D), jnp.bfloat16),
+            pltpu.VMEM((D, FF), jnp.bfloat16),
+            pltpu.VMEM((FF, D), jnp.bfloat16),
+            pltpu.VMEM((D, D), jnp.bfloat16),
+            pltpu.SemaphoreType.DMA((64,)),
+            pltpu.SemaphoreType.DMA((6,)),
+            pltpu.SemaphoreType.DMA((3,)),
+            pltpu.SemaphoreType.DMA((64,)),
+        ],
+        compiler_params=PARAMS,
+        cost_estimate=pl.CostEstimate(flops=4 * TALL * D * (D + 2 * FF), bytes_accessed=60000000, transcendentals=3000000),
+        name="feed_back",
+    )(place, small, grad, summed, resid, pre, mixed, attn, *pieces)
+
+
+def weight_back_kernel(place_ref, low_ref, dq_ref, dk_ref, dv_ref, dwo_ref, keep_out, send_out, vec_ref, grads_ref, sems):
+    x, c, z, y = (place_ref[index] for index in range(4))
+    blocks = []
+
+    def place_matrix(source, quarter):
+        for owner in range(8):
+            index = ((quarter // 2) ^ x, (owner % 2) ^ y, ((owner // 2) - z) & 3, 0)
+            part = source.at[owner * ROWS : owner * ROWS + ROWS, :]
+            sem = sems.at[len(blocks)]
+            keep = pltpu.make_async_copy(part, keep_out.at[index], sem)
+            send = pltpu.make_async_copy(part, send_out.at[index], sem)
+
+            @pl.when(c == quarter % 2)
+            def _():
+                keep.start()
+
+            @pl.when(c != quarter % 2)
+            def _():
+                send.start()
+
+            blocks.append(keep)
+
+    place_matrix(dwo_ref, 3)
+    grads_ref[0] = dot_tn(low_ref[...], dq_ref[...]).astype(jnp.bfloat16)
+    place_matrix(grads_ref.at[0], 0)
+    grads_ref[1] = dot_tn(low_ref[:LEN, :], dk_ref[...]).astype(jnp.bfloat16)
+    place_matrix(grads_ref.at[1], 1)
+    grads_ref[2] = dot_tn(low_ref[:LEN, :], dv_ref[...]).astype(jnp.bfloat16)
+    place_matrix(grads_ref.at[2], 2)
+    vec_ref[0:1, :] = jnp.sum(dq_ref[...].astype(jnp.float32), axis=0, keepdims=True)
+    vec_ref[1:2, :] = jnp.sum(dv_ref[...].astype(jnp.float32), axis=0, keepdims=True)
+    for block in blocks:
+        block.wait()
+
+
+def weight_back(place, low, dq, dk, dv, dwo):
+    blocks = jax.ShapeDtypeStruct((2, 2, 4, 1, ROWS, D), jnp.bfloat16)
+    return pl.pallas_call(
+        weight_back_kernel,
+        out_shape=[blocks, blocks, jax.ShapeDtypeStruct((2, D), jnp.float32)],
+        in_specs=[SMEM_SPEC] + [VMEM_SPEC] * 5,
+        out_specs=[ANY_SPEC] * 2 + [VMEM_SPEC],
+        scratch_shapes=[
+            pltpu.VMEM((3, D, D), jnp.bfloat16),
+            pltpu.SemaphoreType.DMA((32,)),
+        ],
+        compiler_params=PARAMS,
+        cost_estimate=pl.CostEstimate(flops=2 * 2048 * D * D, bytes_accessed=12000000, transcendentals=0),
+        name="weight_back",
+    )(place, low, dq, dk, dv, dwo)
+
+
+def input_back_kernel(dq_ref, dk_ref, dv_ref, w_ref, dresid_ref, first_ref, second_ref):
+    for row in range(0, LEN, HALF):
+        rows = slice(row, row + HALF)
+        first_ref[rows, :] = (
+            dresid_ref[rows, :]
+            + dot_nt(dq_ref[rows, :], w_ref[0])
+            + dot_nt(dk_ref[rows, :], w_ref[1])
+            + dot_nt(dv_ref[rows, :], w_ref[2])
+        )
+        rest = slice(LEN + row, LEN + row + HALF)
+        second_ref[rows, :] = dresid_ref[rest, :] + dot_nt(dq_ref[rest, :], w_ref[0])
+
+
+def input_back(dq, dk, dv, attn, dresid):
+    half = jax.ShapeDtypeStruct((LEN, D), jnp.float32)
+    return pl.pallas_call(
+        input_back_kernel,
+        out_shape=[half, half],
+        in_specs=[VMEM_SPEC] * 5,
+        out_specs=[VMEM_SPEC] * 2,
+        compiler_params=PARAMS,
+        cost_estimate=pl.CostEstimate(flops=2 * 2048 * D * D, bytes_accessed=16000000, transcendentals=0),
+        name="input_back",
+    )(dq, dk, dv, attn, dresid)
+
+
+def bias_vectors(table):
+    lane = jnp.arange(512, dtype=jnp.int32)
+    offset = jnp.where(lane < 384, 128 - lane, 640 - lane)
+    onehot = bucket_of(offset)[:, None] == jnp.arange(NB, dtype=jnp.int32)[None, :]
+    near = jnp.dot(table, onehot.astype(jnp.float32).T, precision=lax.Precision.HIGHEST)
+    return (near[:, None, :], jnp.stack([table[:, 15], table[:, 31]], axis=1), onehot)
+
+
+def bucket_of(offset):
+    distance = jnp.abs(offset)
+    far_bucket = jnp.full(distance.shape, 8, jnp.int32)
+    for exponent in range(1, 8):
+        far_bucket = far_bucket + (distance * distance >= 64 * 2**exponent).astype(jnp.int32)
+    near_or_far = jnp.where(distance < 8, distance, far_bucket)
+    return near_or_far + NB // 2 * (offset > 0).astype(jnp.int32)
+
+
+def table_grad(sums, onehot):
+    near = jnp.dot(
+        sums[:, 0, :512],
+        jnp.roll(onehot.astype(jnp.float32), 127, axis=0),
+        precision=lax.Precision.HIGHEST,
+    )
+    low = jnp.sum(sums[:, 0, 512:640], axis=1)
+    high = jnp.sum(sums[:, 0, 640:], axis=1)
+    return near.at[:, 15].add(low).at[:, 31].add(high)
 
 def fetch_forward(shards):
     low = tuple(shard.astype(jnp.bfloat16) for shard in shards)
@@ -559,7 +1152,6 @@
 
 
 def per_device(
-    fast,
     content,
     query,
     lengths,
@@ -592,7 +1184,7 @@
     )
     for layer_index in range(LAYERS):
         shards = tuple((master[layer_index] for master in masters[:3]))
-        gathered = fetch_layer(fast, shards) + (small_all[layer_index],)
+        gathered = fetch_forward(shards) + (small_all[layer_index],)
         kept_weights.append(gathered)
         hidden_c, hidden_q, saved = forward_layer(
             hidden_c, hidden_q, gathered, lengths, flag_rows, onehot
@@ -615,9 +1207,7 @@
             onehot,
         )
         small_grads[layer_index] = local_grads[3]
-        layer_grads[layer_index] = (
-            reduce_fast(local_grads[:3]) if fast else reduce_layer(local_grads[:3])
-        )
+        layer_grads[layer_index] = reduce_layer(local_grads[:3])
     small_sum = lax.psum(jnp.stack(small_grads), ("dp", "fsdp"))
     owned = small_master.shape[1]
     small_own = lax.dynamic_slice_in_dim(
@@ -653,6 +1243,183 @@
     )
 
 
+def own_quarter(kind, shard, quarter):
+    if kind == "attn":
+        part = lax.dynamic_index_in_dim(shard, quarter, 0, keepdims=False)
+    elif kind == "inner":
+        part = lax.dynamic_slice_in_dim(shard, quarter * D, D, 1)
+    else:
+        part = lax.dynamic_slice_in_dim(shard, quarter * ROWS, ROWS, 0)
+    return part.astype(jnp.bfloat16)
+
+
+def gather_group(kinds, shards, place):
+    quarter = place[0] * 2 + place[1]
+    own = jnp.stack([own_quarter(kind, shard, quarter) for kind, shard in zip(kinds, shards)])
+    return spread_blocks(own)
+
+
+def gather_small(shard, place):
+    z, y = place[2], place[3]
+    column = jnp.stack([shift_z(shard, step) for step in (3, 2, 1)] + [shard])
+    other = swap_y(column)
+    pairs = jnp.where(y == 0, jnp.stack([column, other], 1), jnp.stack([other, column], 1))
+    twice = jnp.concatenate([pairs, pairs])
+    whole = lax.dynamic_slice_in_dim(twice, 3 - z, 4, 0)
+    return whole.transpose(2, 0, 1, 3).reshape(shard.shape[0], -1)
+
+
+def sum_small(value):
+    value = value + swap_core(value)
+    value = value + swap_x(value)
+    value = value + swap_y(value)
+    return value + shift_z(value, 1) + shift_z(value, 2) + shift_z(value, 3)
+
+
+def add_low(*values):
+    total = values[0].astype(jnp.float32)
+    for value in values[1:]:
+        total = total + value.astype(jnp.float32)
+    return total.astype(jnp.bfloat16)
+
+
+def reduce_blocks(keep, send):
+    both = add_low(keep, swap_core(send))
+    corner = both[1, 1]
+    by_x = swap_x(corner[:2])
+    by_y = swap_y(corner[2:])
+    for_y = jnp.concatenate([add_low(both[0, 1, :2], by_x), both[0, 1, 2:]])
+    for_x = jnp.concatenate([both[1, 0, :2], add_low(both[1, 0, 2:], by_y)])
+    column = add_low(both[0, 0], swap_x(for_x), swap_y(for_y))
+    total = column[0].astype(jnp.float32)
+    for step in (1, 2, 3):
+        total = total + shift_z(column[step], step).astype(jnp.float32)
+    return total.astype(jnp.bfloat16)
+
+
+def share_quarters(own, place):
+    x, c = place[0], place[1]
+    pair = jnp.stack([own, swap_x(own)])
+    other = swap_core(pair)
+    cores = jnp.where(c == 0, jnp.stack([pair, other], 1), jnp.stack([other, pair], 1))
+    sides = jnp.where(x == 0, cores, cores[::-1])
+    return sides.reshape((4,) + own.shape)
+
+
+def shard_grad(kind, quarters):
+    four = quarters.astype(jnp.float32)
+    if kind == "attn":
+        return four
+    if kind == "inner":
+        return four.transpose(1, 0, 2).reshape(ROWS, FF)
+    return four.reshape(4 * ROWS, D)
+
+
+def small_parts(vectors):
+    values = vectors.astype(jnp.float32)
+    return (
+        values[: 8 * D].reshape(8, D),
+        values[8 * D : 8 * D + FF].reshape(1, FF),
+        bias_vectors(values[8 * D + FF :].reshape(H, NB)),
+    )
+
+
+def per_device_fast(
+    content,
+    query,
+    lengths,
+    predicted,
+    content_cot,
+    query_cot,
+    attn_master,
+    attn_first,
+    attn_second,
+    inner_master,
+    inner_first,
+    inner_second,
+    outer_master,
+    outer_first,
+    outer_second,
+    small_master,
+    small_first,
+    small_second,
+):
+    place_parts = my_place()
+    place = jnp.stack(place_parts).astype(jnp.int32)
+    small_all = gather_small(small_master.astype(jnp.bfloat16), place_parts)
+    attn_pieces = []
+    feed_pieces = []
+    for layer in range(LAYERS):
+        attn_pieces.append(gather_group(("attn",), (attn_master[layer],), place_parts))
+        feed_pieces.append(
+            gather_group(
+                ("inner", "outer"), (inner_master[layer], outer_master[layer]), place_parts
+            )
+        )
+    row_flags = predicted.reshape(1, LEN).astype(jnp.float32)
+    col_flags = predicted.reshape(LEN, 1).astype(jnp.float32)
+    low = jnp.concatenate([content, query])
+    hidden = low.astype(jnp.float32)
+    kept = []
+    for layer in range(LAYERS):
+        small, hidden_bias, (tvec, far, onehot) = small_parts(small_all[layer])
+        q, k, v, attn = project(place, low, small, attn_pieces[layer])
+        mixed, lse = mix(lengths, far, tvec, q, k, v, row_flags, col_flags)
+        resid, summed, pre, hidden, next_low = feed(
+            place, small, hidden_bias, mixed, hidden, attn, feed_pieces[layer]
+        )
+        kept.append((small, far, tvec, onehot, low, q, k, v, attn, mixed, lse, resid, summed, pre))
+        low = next_low
+    valid = (jnp.arange(LEN, dtype=jnp.int32) < lengths[0])[:, None].astype(jnp.float32)
+    grad = jnp.concatenate(
+        [content_cot.astype(jnp.float32) * valid, query_cot.astype(jnp.float32) * valid]
+    )
+    owned = [None] * LAYERS
+    small_grads = [None] * LAYERS
+    for layer in reversed(range(LAYERS)):
+        small, far, tvec, onehot, low_in, q, k, v, attn, mixed, lse, resid, summed, pre = kept[layer]
+        dresid, dmix, dwo, feed_keep, feed_send, feed_vec, dhidden = feed_back(
+            place, small, grad, summed, resid, pre, mixed, attn, feed_pieces[layer]
+        )
+        feed_own = reduce_blocks(feed_keep, feed_send)
+        dq, dk, dv, table_sums = mix_back(
+            lengths, far, tvec, q, k, v, dmix, mixed, lse, row_flags, col_flags
+        )
+        attn_keep, attn_send, attn_vec = weight_back(place, low_in, dq, dk, dv, dwo)
+        attn_own = reduce_blocks(attn_keep, attn_send)
+        grad_c, grad_q = input_back(dq, dk, dv, attn, dresid)
+        if layer:
+            grad = jnp.concatenate([grad_c, grad_q])
+        small_grads[layer] = jnp.concatenate(
+            [
+                attn_vec.reshape(-1),
+                feed_vec[2:].reshape(-1),
+                dhidden.reshape(-1),
+                table_grad(table_sums, onehot).reshape(-1),
+            ]
+        )
+        feed_four = share_quarters(feed_own, place_parts)
+        attn_four = share_quarters(attn_own, place_parts)
+        owned[layer] = (
+            shard_grad("attn", attn_four[:, 0]),
+            shard_grad("inner", feed_four[:, 0]),
+            shard_grad("outer", feed_four[:, 1]),
+        )
+    small_sum = sum_small(jnp.stack(small_grads))
+    size = small_master.shape[1]
+    small_own = lax.dynamic_slice_in_dim(small_sum, lax.axis_index("fsdp") * size, size, 1)
+    reduced = tuple(
+        jnp.stack([owned[layer][member] for layer in range(LAYERS)]) for member in range(3)
+    )
+    attn_new = adam_update(attn_master, attn_first, attn_second, reduced[0], ATTENTION_RATE)
+    inner_new = adam_update(inner_master, inner_first, inner_second, reduced[1], FEED_RATE)
+    outer_new = adam_update(outer_master, outer_first, outer_second, reduced[2], FEED_RATE)
+    small_new = adam_update(small_master, small_first, small_second, small_own, SMALL_RATE)
+    return (
+        (low[:LEN], low[LEN:], grad_c, grad_q) + attn_new + inner_new + outer_new + small_new
+    )
+
+
 def solution(mesh):
     placed = (
         P(("dp", "fsdp"), None),
@@ -676,7 +1443,7 @@
     )
     fast = tuple(mesh.shape.values()) == (4, 8)
     return jax.shard_map(
-        partial(per_device, fast),
+        per_device_fast if fast else per_device,
         mesh=mesh,
         in_specs=placed,
         out_specs=(

time: 1950 us -> 680 us (0.35)
  Pallas kernels: 866 us -> 273 us
  matrix products: 468 us -> 0.71 us
  local copies, waits for them, and re-layouts: 117 us -> 47 us
  other arithmetic: 122 us -> 60.9 us
  blocking collectives: 38.2 us -> 0 us
  waiting for transfers between devices: 221 us -> 198 us
    pallas_call x4 -> x14, Pallas kernels: 866 us -> 273 us  [the longest x2 83.8 us: feed_back(): pl.pallas_call(feed_back_kernel, out_shape=[jax.ShapeDtypeStruct((TALL, D...]
    dot_general x74 -> x4, matrix products: 399 us -> 0.71 us  [the longest x2 0.45 us: table_grad(): jnp.dot(sums[:, 0, :512], jnp.roll(onehot.astype(jnp.float32), 127, axis=...]
    sub x4 -> x0, matrix products: 69.1 us -> none  [attend_back(): grad_probs - jnp.sum(probs * grad_probs, axis=-1, keepdims=True)]
    reduce_sum x25 -> x2, other arithmetic: 43.3 us -> 1.75 us  [table_grad(): high = jnp.sum(sums[:, 0, 640:], axis=1)]
    all_gather x1 -> x0, blocking collectives: 38.2 us -> none  [per_device(): lax.all_gather(small_master.astype(jnp.bfloat16), 'fsdp', axis=1, tiled=T...]
    reshape x8, local copies, waits for them, and re-layouts: 36.4 us -> 2.94 us  [the longest x2 1.56 us: per_device_fast(): attn_vec.reshape(-1)]
    psum x1 -> x0, waiting for transfers between devices: 31.5 us -> none  [per_device(): small_sum = lax.psum(jnp.stack(small_grads), ('dp', 'fsdp'))]
    unnamed x595 -> x113, local copies, waits for them, and re-layouts: 29.6 us -> 5.06 us
  transfers between devices with their start and end apart: 89 -> 98, of which waited for: 28 -> 34; matrix products, arithmetic and copies ran while one was open for 17% -> 12% of each run, Pallas kernels for 30% -> 13%
where the time goes in v2:
time: 680 us; the launch traced here: 674 us
  Pallas kernels  273 us (40%)
  waiting for transfers between devices  198 us (29%)
  starting transfers between devices  91.6 us (13%)
  other arithmetic  60.9 us (9%)
  local copies, waits for them, and re-layouts  47 us (7%)
    ppermute x98, waiting for transfers between devices, move(): return lax.ppermute(value, AXES, pairs)  198 us
    ppermute x98, starting transfers between devices, move(): return lax.ppermute(value, AXES, pairs)  91.6 us
    pallas_call x2, Pallas kernels, feed_back(): pl.pallas_call(feed_back_kernel, out_shape=[jax.ShapeDtypeStruct((TALL, D...  83.8 us
    pallas_call x2, Pallas kernels, mix_back(): pl.pallas_call(mix_back_kernel, grid=(H // 2,), out_shape=[jax.ShapeDtype...  54 us
    pallas_call x2, Pallas kernels, feed(): pl.pallas_call(feed_kernel, out_shape=[jax.ShapeDtypeStruct((TALL, D), jn...  48.2 us
    pallas_call x2, Pallas kernels, mix(): pl.pallas_call(mix_kernel, grid=(H // 2,), out_shape=[jax.ShapeDtypeStruc...  37.9 us
    pallas_call x2, Pallas kernels, input_back(): pl.pallas_call(input_back_kernel, out_shape=[half, half], in_specs=[VMEM_...  17 us
    pallas_call x2, Pallas kernels, project(): pl.pallas_call(project_kernel, out_shape=[jax.ShapeDtypeStruct((TALL, D),...  16.9 us
  transfers between devices with their start and end apart: 98, of which 34 were waited for; matrix products, arithmetic and copies ran while one was open for 12% of the time, Pallas kernels for 13%

profile of v2, /device:TPU:0, one launch (start us, length us, event | category | flops | bytes accessed | tf_op | source)
XLA Modules:
  0.0 673.6 jit_solution(368487930247436068)
XLA Ops:
  46.8 7.5 %collective-permute-start.42 = (bf16[2,96,768]{2,1,0:T(8,128)(2,1)}, bf16[2,96,768]{2,1,0:T(8,128)(2,1)S(1)}, u32[]{:S(2)}, u32[]{:S(2)}) collective-permute-start(bf16[2,96,768]{2,1,0:T(8,128)(2,1)} %get-tuple-element.241), channel_id=1, source_target_pairs={{0,6},{1,7},{2,0},{3,1},{4,2},{5,3},{6,4},{7,5},{8,14},{9,15},{10,... | collective-permute-start | bytes 884744 | tf_op jit(solution)/shard_map/ppermute | solution.py:175
  58.2 13.5 %collective-permute-done.17 = bf16[2,96,768]{2,1,0:T(8,128)(2,1)S(1)} collective-permute-done((bf16[2,96,768]{2,1,0:T(8,128)(2,1)S(1)}, bf16[2,96,768]{2,1,0:T(8,128)(2,1)S(1)}, u32[]{:S(2)}, u32[]{:S(2)}) %collective-permute-start.17) | collective-permute-done | bytes 294944 | tf_op jit(solution)/shard_map/ppermute | solution.py:175
  77.3 12.2 %collective-permute-done.41 = bf16[2,96,768]{2,1,0:T(8,128)(2,1)S(1)} collective-permute-done((bf16[2,96,768]{2,1,0:T(8,128)(2,1)}, bf16[2,96,768]{2,1,0:T(8,128)(2,1)S(1)}, u32[]{:S(2)}, u32[]{:S(2)}) %collective-permute-start.41) | collective-permute-done | bytes 294944 | tf_op jit(solution)/shard_map/ppermute | solution.py:175
  114.6 7.6 %collective-permute-done.33.refs_3_ = bf16[2,1,96,768]{3,2,1,0:T(8,128)(2,1)S(1)} collective-permute-done((bf16[2,1,96,768]{3,2,1,0:T(8,128)(2,1)S(1)}, bf16[2,1,96,768]{3,2,1,0:T(8,128)(2,1)S(1)}, u32[]{:S(2)}, u32[]{:S(2)}) %collective-permute-start.33) | collective-permute-done | bytes 294944 | tf_op jit(solution)/shard_map/ppermute | solution.py:175
  129.7 21.4 %collective-permute-done.19.refs_1_ = bf16[4,2,96,768]{3,2,1,0:T(8,128)(2,1)} collective-permute-done((bf16[4,2,96,768]{3,2,1,0:T(8,128)(2,1)S(1)}, bf16[4,2,96,768]{3,2,1,0:T(8,128)(2,1)}, u32[]{:S(2)}, u32[]{:S(2)}) %collective-permute-start.19) | collective-permute-done | bytes 1179680 | tf_op jit(solution)/shard_map/ppermute | solution.py:175
  157.7 18.7 %collective-permute-done.43.refs_1_ = bf16[4,2,96,768]{3,2,1,0:T(8,128)(2,1)} collective-permute-done((bf16[4,2,96,768]{3,2,1,0:T(8,128)(2,1)S(1)}, bf16[4,2,96,768]{3,2,1,0:T(8,128)(2,1)}, u32[]{:S(2)}, u32[]{:S(2)}) %collective-permute-start.43) | collective-permute-done | bytes 1179680 | tf_op jit(solution)/shard_map/ppermute | solution.py:175
  182.4 8.4 %project.2 = (bf16[1024,768]{1,0:T(8,128)(2,1)}, bf16[512,768]{1,0:T(8,128)(2,1)}, bf16[512,768]{1,0:T(8,128)(2,1)}, bf16[4,768,768]{2,1,0:T(8,128)(2,1)}) custom-call(s32[4]{0:T(128)} %pad_add_fusion.place_ref, bf16[1024,768]{1,0:T(8,128)(2,1)} %constant_dynamic-update-slice_fusion.low_ref, f32[8,768]{1,0:T(8,128)} %reshape.595.small_ref, ...), custom_call_target="tpu_custom_call" | custom-call | flops 2415919104 | bytes 16000000 | tf_op jit(solution)/shard_map/project/pallas_call | solution.py:304
  191.5 19.1 %mix.2 = (bf16[1024,768]{1,0:T(8,128)(2,1)}, f32[12,1,1024]{2,1,0:T(1,128)}) custom-call(s32[1]{0:T(128)} %copy.381.length_ref, f32[12,2]{1,0:T(8,128)} %pad_maximum_fusion.31.far_ref, bf16[1024,768]{1,0:T(8,128)(2,1)} %get-tuple-element.117.q_ref, bf16[512,768]{1,0:T(8,128)(2,1)} %get-tuple-element.118.k_ref, bf16[512,768]{1,0:T(8,128)(2,1)} %get-tuple-element.119.v_ref, ...), custom_call_target="tpu_custom_call" | custom-call | flops 6499999744 | bytes 8000000 | tf_op jit(solution)/shard_map/mix/pallas_call | solution.py:415
  216.7 24.0 %feed.2 = (f32[1024,768]{1,0:T(8,128)}, f32[1024,768]{1,0:T(8,128)}, bf16[1024,3072]{1,0:T(8,128)(2,1)}, f32[1024,768]{1,0:T(8,128)}, bf16[1024,768]{1,0:T(8,128)(2,1)}) custom-call(s32[4]{0:T(128)} %pad_add_fusion.place_ref, f32[8,768]{1,0:T(8,128)} %reshape.595.small_ref, f32[1,3072]{1,0:T(1,128)} %bitcast.285, ...), custom_call_target="tpu_custom_call" | custom-call | flops 10871635968 | bytes 40000000 | tf_op jit(solution)/shard_map/feed/pallas_call | solution.py:626
  241.3 8.5 %project.3 = (bf16[1024,768]{1,0:T(8,128)(2,1)}, bf16[512,768]{1,0:T(8,128)(2,1)}, bf16[512,768]{1,0:T(8,128)(2,1)}, bf16[4,768,768]{2,1,0:T(8,128)(2,1)}) custom-call(s32[4]{0:T(128)} %pad_add_fusion.place_ref, bf16[1024,768]{1,0:T(8,128)(2,1)} %get-tuple-element.122.low_ref, f32[8,768]{1,0:T(8,128)} %reshape.593.small_ref, ...), custom_call_target="tpu_custom_call" | custom-call | flops 2415919104 | bytes 16000000 | tf_op jit(solution)/shard_map/project/pallas_call | solution.py:304
  249.7 18.8 %mix.3 = (bf16[1024,768]{1,0:T(8,128)(2,1)}, f32[12,1,1024]{2,1,0:T(1,128)}) custom-call(s32[1]{0:T(128)} %copy.381.length_ref, f32[12,2]{1,0:T(8,128)} %pad_maximum_fusion.30.far_ref, bf16[1024,768]{1,0:T(8,128)(2,1)} %get-tuple-element.123.q_ref, bf16[512,768]{1,0:T(8,128)(2,1)} %get-tuple-element.124.k_ref, bf16[512,768]{1,0:T(8,128)(2,1)} %get-tuple-element.125.v_ref, ...), custom_call_target="tpu_custom_call" | custom-call | flops 6499999744 | bytes 8000000 | tf_op jit(solution)/shard_map/mix/pallas_call | solution.py:415
  269.7 24.2 %feed.3 = (f32[1024,768]{1,0:T(8,128)}, f32[1024,768]{1,0:T(8,128)}, bf16[1024,3072]{1,0:T(8,128)(2,1)}, f32[1024,768]{1,0:T(8,128)}, bf16[1024,768]{1,0:T(8,128)(2,1)}) custom-call(s32[4]{0:T(128)} %pad_add_fusion.place_ref, f32[8,768]{1,0:T(8,128)} %reshape.593.small_ref, f32[1,3072]{1,0:T(1,128)} %bitcast.284, ...), custom_call_target="tpu_custom_call" | custom-call | flops 10871635968 | bytes 40000000 | tf_op jit(solution)/shard_map/feed/pallas_call | solution.py:626
  293.9 41.8 %feed_back.2 = (f32[1024,768]{1,0:T(8,128)}, bf16[1024,768]{1,0:T(8,128)(2,1)}, bf16[768,768]{1,0:T(8,128)(2,1)}, bf16[2,2,4,2,96,768]{5,4,3,2,1,0:T(8,128)(2,1)...) custom-call(s32[4]{0:T(128)} %pad_add_fusion.place_ref, ...), custom_call_target="tpu_custom_call" | custom-call | flops 21743271936 | bytes 60000000 | tf_op jit(solution)/shard_map/feed_back/pallas_call | solution.py:793
  335.8 27.1 %mix_back.2 = (bf16[1024,768]{1,0:T(8,128)(2,1)}, bf16[512,768]{1,0:T(8,128)(2,1)}, bf16[512,768]{1,0:T(8,128)(2,1)}, f32[12,1,768]{2,1,0:T(1,128)}) custom-call(s32[1]{0:T(128)} %copy.381.length_ref, f32[12,2]{1,0:T(8,128)} %pad_maximum_fusion.30.far_ref, bf16[1024,768]{1,0:T(8,128)(2,1)} %get-tuple-element.123.q_ref, ...), custom_call_target="tpu_custom_call" | custom-call | flops 16000000000 | bytes 12000000 | tf_op jit(solution)/shard_map/mix_back/pallas_call | solution.py:524
  364.5 8.5 %input_back.2 = (f32[512,768]{1,0:T(8,128)}, f32[512,768]{1,0:T(8,128)}) custom-call(bf16[1024,768]{1,0:T(8,128)(2,1)} %get-tuple-element.135.dq_ref, bf16[512,768]{1,0:T(8,128)(2,1)} %get-tuple-element.136.dk_ref, bf16[512,768]{1,0:T(8,128)(2,1)} %get-tuple-element.137.dv_ref, bf16[4,768,768]{2,1,0:T(8,128)(2,1)} %get-tuple-element.128.attn_any.w_ref, ...), custom_call_target="tpu_custom_call" | custom-call | flops 2415919104 | bytes 16000000 | tf_op jit(solution)/shard_map/input_back/pallas_call | solution.py:901
  376.8 42.0 %feed_back.3 = (f32[1024,768]{1,0:T(8,128)}, bf16[1024,768]{1,0:T(8,128)(2,1)}, bf16[768,768]{1,0:T(8,128)(2,1)}, bf16[2,2,4,2,96,768]{5,4,3,2,1,0:T(8,128)(2,1)...) custom-call(s32[4]{0:T(128)} %pad_add_fusion.place_ref, ...), custom_call_target="tpu_custom_call" | custom-call | flops 21743271936 | bytes 60000000 | tf_op jit(solution)/shard_map/feed_back/pallas_call | solution.py:793
  418.9 26.9 %mix_back.3 = (bf16[1024,768]{1,0:T(8,128)(2,1)}, bf16[512,768]{1,0:T(8,128)(2,1)}, bf16[512,768]{1,0:T(8,128)(2,1)}, f32[12,1,768]{2,1,0:T(1,128)}) custom-call(s32[1]{0:T(128)} %copy.381.length_ref, f32[12,2]{1,0:T(8,128)} %pad_maximum_fusion.31.far_ref, bf16[1024,768]{1,0:T(8,128)(2,1)} %get-tuple-element.117.q_ref, ...), custom_call_target="tpu_custom_call" | custom-call | flops 16000000000 | bytes 12000000 | tf_op jit(solution)/shard_map/mix_back/pallas_call | solution.py:524
  447.4 7.4 %weight_back.3 = (bf16[2,2,4,1,96,768]{5,4,3,2,1,0:T(8,128)(2,1)}, bf16[2,2,4,1,96,768]{5,4,3,2,1,0:T(8,128)(2,1)}, f32[2,768]{1,0:T(2,128)}) custom-call(s32[4]{0:T(128)} %pad_add_fusion.place_ref, bf16[1024,768]{1,0:T(8,128)(2,1)} %get-tuple-element.122.low_ref, bf16[1024,768]{1,0:T(8,128)(2,1)} %get-tuple-element.135.dq_ref, ...), custom_call_target="tpu_custom_call" | custom-call | flops 2415919104 | bytes 12000000 | tf_op jit(solution)/shard_map/weight_back/pallas_call | solution.py:871
  494.5 8.5 %input_back.3 = (f32[512,768]{1,0:T(8,128)}, f32[512,768]{1,0:T(8,128)}) custom-call(bf16[1024,768]{1,0:T(8,128)(2,1)} %get-tuple-element.146.dq_ref, bf16[512,768]{1,0:T(8,128)(2,1)} %get-tuple-element.147.dk_ref, bf16[512,768]{1,0:T(8,128)(2,1)} %get-tuple-element.148.dv_ref, bf16[4,768,768]{2,1,0:T(8,128)(2,1)} %get-tuple-element.121.attn_any.w_ref, ...), custom_call_target="tpu_custom_call" | custom-call | flops 2415919104 | bytes 16000000 | tf_op jit(solution)/shard_map/input_back/pallas_call | solution.py:901
  559.8 7.8 %collective-permute-done.83 = bf16[2,2,96,768]{3,2,1,0:T(8,128)(2,1)S(1)} collective-permute-done((bf16[2,2,96,768]{3,2,1,0:T(8,128)(2,1)S(1)}, bf16[2,2,96,768]{3,2,1,0:T(8,128)(2,1)S(1)}, u32[]{:S(2)}, u32[]{:S(2)}) %collective-permute-start.83) | collective-permute-done | bytes 589856 | tf_op jit(solution)/shard_map/ppermute | solution.py:175
  569.4 8.1 %collective-permute-done.73 = bf16[2,2,96,768]{3,2,1,0:T(8,128)(2,1)S(1)} collective-permute-done((bf16[2,2,96,768]{3,2,1,0:T(8,128)(2,1)S(1)}, bf16[2,2,96,768]{3,2,1,0:T(8,128)(2,1)S(1)}, u32[]{:S(2)}, u32[]{:S(2)}) %collective-permute-start.73) | collective-permute-done | bytes 589856 | tf_op jit(solution)/shard_map/ppermute | solution.py:175
  590.3 16.1 %collective-permute-done.86 = bf16[4,2,96,768]{3,2,1,0:T(8,128)(2,1)S(1)} collective-permute-done((bf16[4,2,96,768]{3,2,1,0:T(8,128)(2,1)S(1)}, bf16[4,2,96,768]{3,2,1,0:T(8,128)(2,1)S(1)}, u32[]{:S(2)}, u32[]{:S(2)}) %collective-permute-start.86) | collective-permute-done | bytes 1179680 | tf_op jit(solution)/shard_map/ppermute | solution.py:175
  610.3 16.2 %collective-permute-done.76 = bf16[4,2,96,768]{3,2,1,0:T(8,128)(2,1)S(1)} collective-permute-done((bf16[4,2,96,768]{3,2,1,0:T(8,128)(2,1)S(1)}, bf16[4,2,96,768]{3,2,1,0:T(8,128)(2,1)S(1)}, u32[]{:S(2)}, u32[]{:S(2)}) %collective-permute-start.76) | collective-permute-done | bytes 1179680 | tf_op jit(solution)/shard_map/ppermute | solution.py:175
  639.4 10.3 %collective-permute-done.78 = bf16[2,96,768]{2,1,0:T(8,128)(2,1)S(1)} collective-permute-done((bf16[2,96,768]{2,1,0:T(8,128)(2,1)S(1)}, bf16[2,96,768]{2,1,0:T(8,128)(2,1)S(1)}, u32[]{:S(2)}, u32[]{:S(2)}) %collective-permute-start.78) | collective-permute-done | bytes 294944 | tf_op jit(solution)/shard_map/ppermute | solution.py:175
  (465 shorter events, 265.7 us)
Async XLA Ops:
  40.5 31.2 %collective-permute-start.17 = (bf16[2,96,768]{2,1,0:T(8,128)(2,1)S(1)}, bf16[2,96,768]{2,1,0:T(8,128)(2,1)S(1)}, u32[]{:S(2)}, u32[]{:S(2)}) collective-permute-start(bf16[2,96,768]{2,1,0:T(8,128)(2,1)S(1)} %get-tuple-element.243), channel_id=1, source_target_pairs={{0,4},{1,5},{2,6},{3,7},{4,0},{5,1},{6,2},{7,3},{8,12},{9,13},{10,... | collective-permute-start | bytes 884744 | tf_op jit(solution)/shard_map/ppermute | solution.py:175
  41.7 30.1 %collective-permute-start.16 = (bf16[2,96,768]{2,1,0:T(8,128)(2,1)S(1)}, bf16[2,96,768]{2,1,0:T(8,128)(2,1)S(1)}, u32[]{:S(2)}, u32[]{:S(2)}) collective-permute-start(bf16[2,96,768]{2,1,0:T(8,128)(2,1)S(1)} %get-tuple-element.243), channel_id=1, source_target_pairs={{0,2},{1,3},{2,4},{3,5},{4,6},{5,7},{6,0},{7,1},{8,10},{9,11},{10,... | collective-permute-start | bytes 884744 | tf_op jit(solution)/shard_map/ppermute | solution.py:175
  54.3 35.3 %collective-permute-start.7 = (bf16[4,1,96,768]{3,2,1,0:T(8,128)(2,1)}, bf16[4,1,96,768]{3,2,1,0:T(8,128)(2,1)}, u32[]{:S(2)}, u32[]{:S(2)}) collective-permute-start(bf16[4,1,96,768]{3,2,1,0:T(8,128)(2,1)} %pad_maximum_fusion.11.refs_0_), channel_id=1, source_target_pairs={{0,16},{1,17},{2,18},{3,19},{4,20},{5,21},{6,22},{7,23},{8,24},{9,... | collective-permute-start | bytes 1769480 | tf_op jit(solution)/shard_map/ppermute | solution.py:175
  55.8 33.9 %collective-permute-start.8 = (bf16[4,1,96,768]{3,2,1,0:T(8,128)(2,1)}, bf16[4,1,96,768]{3,2,1,0:T(8,128)(2,1)}, u32[]{:S(2)}, u32[]{:S(2)}) collective-permute-start(bf16[4,1,96,768]{3,2,1,0:T(8,128)(2,1)} %pad_maximum_fusion.11.refs_0_), channel_id=1, source_target_pairs={{0,1},{1,0},{2,3},{3,2},{4,5},{5,4},{6,7},{7,6},{8,9},{9,8},{10,11... | collective-permute-start | bytes 1769480 | tf_op jit(solution)/shard_map/ppermute | solution.py:175
  71.8 29.1 %collective-permute-start.31 = (bf16[4,1,96,768]{3,2,1,0:T(8,128)(2,1)}, bf16[4,1,96,768]{3,2,1,0:T(8,128)(2,1)}, u32[]{:S(2)}, u32[]{:S(2)}) collective-permute-start(bf16[4,1,96,768]{3,2,1,0:T(8,128)(2,1)} %pad_maximum_fusion.12.refs_0_), channel_id=1, source_target_pairs={{0,16},{1,17},{2,18},{3,19},{4,20},{5,21},{6,22},{7,23},{8,24},{9,... | collective-permute-start | bytes 1769480 | tf_op jit(solution)/shard_map/ppermute | solution.py:175
  122.2 29.0 %collective-permute-start.19 = (bf16[4,2,96,768]{3,2,1,0:T(8,128)(2,1)S(1)}, bf16[4,2,96,768]{3,2,1,0:T(8,128)(2,1)}, u32[]{:S(2)}, u32[]{:S(2)}) collective-permute-start(bf16[4,2,96,768]{3,2,1,0:T(8,128)(2,1)S(1)} %pad_maximum_fusion.2.refs_0_), channel_id=1, source_target_pairs={{0,16},{1,17},{2,18},{3,19},{4,20},{5,21},{6,22},{7,23},{8,24},{9,... | collective-permute-start | bytes 3538952 | tf_op jit(solution)/shard_map/ppermute | solution.py:175
  122.7 29.0 %collective-permute-start.20 = (bf16[4,2,96,768]{3,2,1,0:T(8,128)(2,1)S(1)}, bf16[4,2,96,768]{3,2,1,0:T(8,128)(2,1)}, u32[]{:S(2)}, u32[]{:S(2)}) collective-permute-start(bf16[4,2,96,768]{3,2,1,0:T(8,128)(2,1)S(1)} %pad_maximum_fusion.2.refs_0_), channel_id=1, source_target_pairs={{0,1},{1,0},{2,3},{3,2},{4,5},{5,4},{6,7},{7,6},{8,9},{9,8},{10,11... | collective-permute-start | bytes 3538952 | tf_op jit(solution)/shard_map/ppermute | solution.py:175
  124.7 51.8 %collective-permute-start.43 = (bf16[4,2,96,768]{3,2,1,0:T(8,128)(2,1)S(1)}, bf16[4,2,96,768]{3,2,1,0:T(8,128)(2,1)}, u32[]{:S(2)}, u32[]{:S(2)}) collective-permute-start(bf16[4,2,96,768]{3,2,1,0:T(8,128)(2,1)S(1)} %pad_maximum_fusion.3.refs_0_), channel_id=1, source_target_pairs={{0,16},{1,17},{2,18},{3,19},{4,20},{5,21},{6,22},{7,23},{8,24},{9,... | collective-permute-start | bytes 3538952 | tf_op jit(solution)/shard_map/ppermute | solution.py:175
  126.2 50.8 %collective-permute-start.44 = (bf16[4,2,96,768]{3,2,1,0:T(8,128)(2,1)S(1)}, bf16[4,2,96,768]{3,2,1,0:T(8,128)(2,1)}, u32[]{:S(2)}, u32[]{:S(2)}) collective-permute-start(bf16[4,2,96,768]{3,2,1,0:T(8,128)(2,1)S(1)} %pad_maximum_fusion.3.refs_0_), channel_id=1, source_target_pairs={{0,1},{1,0},{2,3},{3,2},{4,5},{5,4},{6,7},{7,6},{8,9},{9,8},{10,11... | collective-permute-start | bytes 3538952 | tf_op jit(solution)/shard_map/ppermute | solution.py:175
  155.1 58.5 %collective-permute-start.23 = (bf16[4,2,96,768]{3,2,1,0:T(8,128)(2,1)S(1)}, bf16[4,2,96,768]{3,2,1,0:T(8,128)(2,1)}, u32[]{:S(2)}, u32[]{:S(2)}) collective-permute-start(bf16[4,2,96,768]{3,2,1,0:T(8,128)(2,1)S(1)} %pad_maximum_fusion.2.refs_0_), channel_id=1, source_target_pairs={{0,8},{1,9},{2,10},{3,11},{4,12},{5,13},{6,14},{7,15},{8,0},{9,1},... | collective-permute-start | bytes 3538952 | tf_op jit(solution)/shard_map/ppermute | solution.py:175
  155.7 35.1 %collective-permute-start.21 = (bf16[2,2,96,768]{3,2,1,0:T(8,128)(2,1)}, bf16[2,2,96,768]{3,2,1,0:T(8,128)(2,1)}, u32[]{:S(2)}, u32[]{:S(2)}) collective-permute-start(bf16[2,2,96,768]{3,2,1,0:T(8,128)(2,1)} %slice.487), channel_id=1, source_target_pairs={{0,16},{1,17},{2,18},{3,19},{4,20},{5,21},{6,22},{7,23},{8,24},{9,... | collective-permute-start | bytes 1769480 | tf_op jit(solution)/shard_map/ppermute | solution.py:175
  157.2 34.2 %collective-permute-start.22 = (bf16[2,2,96,768]{3,2,1,0:T(8,128)(2,1)S(1)}, bf16[2,2,96,768]{3,2,1,0:T(8,128)(2,1)}, u32[]{:S(2)}, u32[]{:S(2)}) collective-permute-start(bf16[2,2,96,768]{3,2,1,0:T(8,128)(2,1)S(1)} %slice.488), channel_id=1, source_target_pairs={{0,1},{1,0},{2,3},{3,2},{4,5},{5,4},{6,7},{7,6},{8,9},{9,8},{10,11... | collective-permute-start | bytes 1769480 | tf_op jit(solution)/shard_map/ppermute | solution.py:175
  176.4 37.7 %collective-permute-start.24 = (bf16[4,2,96,768]{3,2,1,0:T(8,128)(2,1)}, bf16[4,2,96,768]{3,2,1,0:T(8,128)(2,1)}, u32[]{:S(2)}, u32[]{:S(2)}) collective-permute-start(bf16[4,2,96,768]{3,2,1,0:T(8,128)(2,1)} %collective-permute-done.19.refs_1_), channel_id=1, source_target_pairs={{0,8},{1,9},{2,10},{3,11},{4,12},{5,13},{6,14},{7,15},{8,0},{9,1},... | collective-permute-start | bytes 3538952 | tf_op jit(solution)/shard_map/ppermute | solution.py:175
  177.0 38.6 %collective-permute-start.25 = (bf16[4,2,96,768]{3,2,1,0:T(8,128)(2,1)}, bf16[4,2,96,768]{3,2,1,0:T(8,128)(2,1)}, u32[]{:S(2)}, u32[]{:S(2)}) collective-permute-start(bf16[4,2,96,768]{3,2,1,0:T(8,128)(2,1)} %collective-permute-done.20.refs_2_), channel_id=1, source_target_pairs={{0,8},{1,9},{2,10},{3,11},{4,12},{5,13},{6,14},{7,15},{8,0},{9,1},... | collective-permute-start | bytes 3538952 | tf_op jit(solution)/shard_map/ppermute | solution.py:175
  213.6 54.9 %collective-permute-start.47 = (bf16[4,2,96,768]{3,2,1,0:T(8,128)(2,1)S(1)}, bf16[4,2,96,768]{3,2,1,0:T(8,128)(2,1)S(1)}, u32[]{:S(2)}, u32[]{:S(2)}) collective-permute-start(bf16[4,2,96,768]{3,2,1,0:T(8,128)(2,1)S(1)} %pad_maximum_fusion.3.refs_0_), channel_id=1, source_target_pairs={{0,8},{1,9},{2,10},{3,11},{4,12},{5,13},{6,14},{7,15},{8,0},{9,1},... | collective-permute-start | bytes 3538952 | tf_op jit(solution)/shard_map/ppermute | solution.py:175
  216.1 52.4 %collective-permute-start.48 = (bf16[4,2,96,768]{3,2,1,0:T(8,128)(2,1)}, bf16[4,2,96,768]{3,2,1,0:T(8,128)(2,1)}, u32[]{:S(2)}, u32[]{:S(2)}) collective-permute-start(bf16[4,2,96,768]{3,2,1,0:T(8,128)(2,1)} %collective-permute-done.43.refs_1_), channel_id=1, source_target_pairs={{0,8},{1,9},{2,10},{3,11},{4,12},{5,13},{6,14},{7,15},{8,0},{9,1},... | collective-permute-start | bytes 3538952 | tf_op jit(solution)/shard_map/ppermute | solution.py:175
  216.2 52.4 %collective-permute-start.49 = (bf16[4,2,96,768]{3,2,1,0:T(8,128)(2,1)}, bf16[4,2,96,768]{3,2,1,0:T(8,128)(2,1)}, u32[]{:S(2)}, u32[]{:S(2)}) collective-permute-start(bf16[4,2,96,768]{3,2,1,0:T(8,128)(2,1)} %collective-permute-done.44.refs_2_), channel_id=1, source_target_pairs={{0,8},{1,9},{2,10},{3,11},{4,12},{5,13},{6,14},{7,15},{8,0},{9,1},... | collective-permute-start | bytes 3538952 | tf_op jit(solution)/shard_map/ppermute | solution.py:175
  471.6 75.2 %collective-permute-start.82 = (bf16[2,2,4,2,96,768]{5,4,3,2,1,0:T(8,128)(2,1)}, bf16[2,2,4,2,96,768]{5,4,3,2,1,0:T(8,128)(2,1)}, u32[]{:S(2)}, u32[]{:S(2)}) collective-permute-start(bf16[2,2,4,2,96,768]{5,4,3,2,1,0:T(8,128)(2,1)} %get-tuple-element.161), channel_id=1, source_target_pairs={{0,8},{1,9},{2,10},{3,11},{4,12},{5,13},{6,14},{7,15},{8,0},{9,1},... | collective-permute-start | bytes 14155784 | tf_op jit(solution)/shard_map/ppermute | solution.py:175
  472.1 81.9 %collective-permute-start.72 = (bf16[2,2,4,2,96,768]{5,4,3,2,1,0:T(8,128)(2,1)}, bf16[2,2,4,2,96,768]{5,4,3,2,1,0:T(8,128)(2,1)}, u32[]{:S(2)}, u32[]{:S(2)}) collective-permute-start(bf16[2,2,4,2,96,768]{5,4,3,2,1,0:T(8,128)(2,1)} %get-tuple-element.159), channel_id=1, source_target_pairs={{0,8},{1,9},{2,10},{3,11},{4,12},{5,13},{6,14},{7,15},{8,0},{9,1},... | collective-permute-start | bytes 14155784 | tf_op jit(solution)/shard_map/ppermute | solution.py:175
  535.9 44.8 %collective-permute-start.97 = (f32[2,9600]{1,0:T(2,128)}, f32[2,9600]{1,0:T(2,128)S(1)}, u32[]{:S(2)}, u32[]{:S(2)}) collective-permute-start(f32[2,9600]{1,0:T(2,128)} %add.402), channel_id=1, source_target_pairs={{0,6},{1,7},{2,0},{3,1},{4,2},{5,3},{6,4},{7,5},{8,14},{9,15},{10,... | collective-permute-start | bytes 230408 | tf_op jit(solution)/shard_map/ppermute | solution.py:175
  577.5 28.9 %collective-permute-start.86 = (bf16[4,2,96,768]{3,2,1,0:T(8,128)(2,1)S(1)}, bf16[4,2,96,768]{3,2,1,0:T(8,128)(2,1)S(1)}, u32[]{:S(2)}, u32[]{:S(2)}) collective-permute-start(bf16[4,2,96,768]{3,2,1,0:T(8,128)(2,1)S(1)} %pad_maximum_fusion.8), channel_id=1, source_target_pairs={{0,1},{1,0},{2,3},{3,2},{4,5},{5,4},{6,7},{7,6},{8,9},{9,8},{10,11... | collective-permute-start | bytes 3538952 | tf_op jit(solution)/shard_map/ppermute | solution.py:175
  578.7 28.9 %collective-permute-start.84 = (bf16[4,2,96,768]{3,2,1,0:T(8,128)(2,1)S(1)}, bf16[4,2,96,768]{3,2,1,0:T(8,128)(2,1)S(1)}, u32[]{:S(2)}, u32[]{:S(2)}) collective-permute-start(bf16[4,2,96,768]{3,2,1,0:T(8,128)(2,1)S(1)} %pad_maximum_fusion.7), channel_id=1, source_target_pairs={{0,16},{1,17},{2,18},{3,19},{4,20},{5,21},{6,22},{7,23},{8,24},{9,... | collective-permute-start | bytes 3538952 | tf_op jit(solution)/shard_map/ppermute | solution.py:175
  587.1 39.3 %collective-permute-start.76 = (bf16[4,2,96,768]{3,2,1,0:T(8,128)(2,1)S(1)}, bf16[4,2,96,768]{3,2,1,0:T(8,128)(2,1)S(1)}, u32[]{:S(2)}, u32[]{:S(2)}) collective-permute-start(bf16[4,2,96,768]{3,2,1,0:T(8,128)(2,1)S(1)} %pad_maximum_fusion.6), channel_id=1, source_target_pairs={{0,1},{1,0},{2,3},{3,2},{4,5},{5,4},{6,7},{7,6},{8,9},{9,8},{10,11... | collective-permute-start | bytes 3538952 | tf_op jit(solution)/shard_map/ppermute | solution.py:175
  587.7 39.7 %collective-permute-start.74 = (bf16[4,2,96,768]{3,2,1,0:T(8,128)(2,1)S(1)}, bf16[4,2,96,768]{3,2,1,0:T(8,128)(2,1)S(1)}, u32[]{:S(2)}, u32[]{:S(2)}) collective-permute-start(bf16[4,2,96,768]{3,2,1,0:T(8,128)(2,1)S(1)} %pad_maximum_fusion.5), channel_id=1, source_target_pairs={{0,16},{1,17},{2,18},{3,19},{4,20},{5,21},{6,22},{7,23},{8,24},{9,... | collective-permute-start | bytes 3538952 | tf_op jit(solution)/shard_map/ppermute | solution.py:175
  (130 other events, 1811.1 us)

commit v3 on v2

--- a/solution.py
+++ b/solution.py
@@ -195,16 +195,6 @@
     dp = lax.axis_index("dp")
     fsdp = lax.axis_index("fsdp")
     return (dp // 2, dp % 2, fsdp // 2, fsdp % 2)
-
-
-def spread_blocks(own):
-    column = jnp.stack([own] + [shift_z(own, step) for step in (1, 2, 3)])
-    from_x = swap_x(column)
-    from_y = swap_y(column)
-    corner_low = swap_x(from_y[:2])
-    corner_high = swap_y(from_x[2:])
-    mine = (column, from_x, from_y, corner_low, corner_high)
-    return mine + tuple(swap_core(piece) for piece in mine)
 
 
 PIECES = ((0, 0, 0, 4), (1, 0, 0, 4), (0, 1, 0, 4), (1, 1, 0, 2), (1, 1, 2, 4))
@@ -1253,10 +1243,25 @@
     return part.astype(jnp.bfloat16)
 
 
-def gather_group(kinds, shards, place):
+def after(value, *others):
+    return lax.optimization_barrier((value, others))[0]
+
+
+def own_group(kinds, shards, place):
     quarter = place[0] * 2 + place[1]
-    own = jnp.stack([own_quarter(kind, shard, quarter) for kind, shard in zip(kinds, shards)])
-    return spread_blocks(own)
+    return jnp.stack([own_quarter(kind, shard, quarter) for kind, shard in zip(kinds, shards)])
+
+
+def gather_column(own):
+    return jnp.stack([own] + [shift_z(own, step) for step in (1, 2, 3)])
+
+
+def gather_sides(column):
+    return (swap_x(column), swap_y(column))
+
+
+def gather_corners(from_x, from_y):
+    return (swap_x(from_y[:2]), swap_y(from_x[2:]))
 
 
 def gather_small(shard, place):
@@ -1283,17 +1288,34 @@
     return total.astype(jnp.bfloat16)
 
 
-def reduce_blocks(keep, send):
-    both = add_low(keep, swap_core(send))
+def reduce_core(keep, got):
+    return add_low(keep, got)
+
+
+def reduce_corners(both):
     corner = both[1, 1]
-    by_x = swap_x(corner[:2])
-    by_y = swap_y(corner[2:])
+    return (swap_x(corner[:2]), swap_y(corner[2:]))
+
+
+def reduce_sides(both, corners):
+    by_x, by_y = corners
     for_y = jnp.concatenate([add_low(both[0, 1, :2], by_x), both[0, 1, 2:]])
     for_x = jnp.concatenate([both[1, 0, :2], add_low(both[1, 0, 2:], by_y)])
-    column = add_low(both[0, 0], swap_x(for_x), swap_y(for_y))
+    return (swap_x(for_x), swap_y(for_y))
+
+
+def reduce_column(both, sides):
+    return add_low(both[0, 0], *sides)
+
+
+def reduce_shifts(column):
+    return tuple(shift_z(column[step], step) for step in (1, 2, 3))
+
+
+def reduce_total(column, shifts):
     total = column[0].astype(jnp.float32)
-    for step in (1, 2, 3):
-        total = total + shift_z(column[step], step).astype(jnp.float32)
+    for value in shifts:
+        total = total + value.astype(jnp.float32)
     return total.astype(jnp.bfloat16)
 
 
@@ -1347,50 +1369,113 @@
     place_parts = my_place()
     place = jnp.stack(place_parts).astype(jnp.int32)
     small_all = gather_small(small_master.astype(jnp.bfloat16), place_parts)
-    attn_pieces = []
-    feed_pieces = []
-    for layer in range(LAYERS):
-        attn_pieces.append(gather_group(("attn",), (attn_master[layer],), place_parts))
-        feed_pieces.append(
-            gather_group(
-                ("inner", "outer"), (inner_master[layer], outer_master[layer]), place_parts
-            )
-        )
+    own_a0, own_a1 = (own_group(("attn",), (attn_master[l],), place_parts) for l in range(2))
+    own_f0, own_f1 = (
+        own_group(("inner", "outer"), (inner_master[l], outer_master[l]), place_parts)
+        for l in range(2)
+    )
+    col_a0 = gather_column(own_a0)
+    sides_a0 = gather_sides(col_a0)
+    col_f0 = gather_column(after(own_f0, col_a0))
+    corners_a0 = gather_corners(*sides_a0)
+    sides_f0 = gather_sides(after(col_f0, *sides_a0))
+    mine_a0 = (col_a0,) + sides_a0 + corners_a0
+    pieces_a0 = mine_a0 + tuple(swap_core(piece) for piece in mine_a0)
+    col_a1 = gather_column(after(own_a1, col_f0))
     row_flags = predicted.reshape(1, LEN).astype(jnp.float32)
     col_flags = predicted.reshape(LEN, 1).astype(jnp.float32)
     low = jnp.concatenate([content, query])
     hidden = low.astype(jnp.float32)
     kept = []
-    for layer in range(LAYERS):
-        small, hidden_bias, (tvec, far, onehot) = small_parts(small_all[layer])
-        q, k, v, attn = project(place, low, small, attn_pieces[layer])
-        mixed, lse = mix(lengths, far, tvec, q, k, v, row_flags, col_flags)
-        resid, summed, pre, hidden, next_low = feed(
-            place, small, hidden_bias, mixed, hidden, attn, feed_pieces[layer]
-        )
-        kept.append((small, far, tvec, onehot, low, q, k, v, attn, mixed, lse, resid, summed, pre))
-        low = next_low
+    small0, hidden_bias0, (tvec0, far0, onehot) = small_parts(small_all[0])
+    small1, hidden_bias1, (tvec1, far1, onehot) = small_parts(small_all[1])
+    q0, k0, v0, attn0 = project(place, low, small0, pieces_a0)
+    col_f1 = gather_column(after(own_f1, col_a1, q0))
+    corners_f0 = gather_corners(*sides_f0)
+    sides_a1 = gather_sides(after(col_a1, q0, *sides_f0))
+    q0_late = after(q0, *sides_f0)
+    mixed0, lse0 = mix(lengths, far0, tvec0, q0_late, k0, v0, row_flags, col_flags)
+    mine_f0 = (col_f0,) + sides_f0 + corners_f0
+    pieces_f0 = mine_f0 + tuple(swap_core(piece) for piece in mine_f0)
+    corners_a1 = gather_corners(*sides_a1)
+    sides_f1 = gather_sides(after(col_f1, mixed0, *sides_a1))
+    mixed0_late = after(mixed0, *sides_a1)
+    resid0, summed0, pre0, hidden1, low1 = feed(
+        place, small0, hidden_bias0, mixed0_late, hidden, attn0, pieces_f0
+    )
+    mine_a1 = (col_a1,) + sides_a1 + corners_a1
+    pieces_a1 = mine_a1 + tuple(swap_core(piece) for piece in mine_a1)
+    q1, k1, v1, attn1 = project(place, low1, small1, pieces_a1)
+    corners_f1 = gather_corners(*sides_f1)
+    q1_late = after(q1, *sides_f1)
+    mixed1, lse1 = mix(lengths, far1, tvec1, q1_late, k1, v1, row_flags, col_flags)
+    mine_f1 = (col_f1,) + sides_f1 + corners_f1
+    pieces_f1 = mine_f1 + tuple(swap_core(piece) for piece in mine_f1)
+    resid1, summed1, pre1, unused, low_out = feed(
+        place, small1, hidden_bias1, mixed1, hidden1, attn1, pieces_f1
+    )
     valid = (jnp.arange(LEN, dtype=jnp.int32) < lengths[0])[:, None].astype(jnp.float32)
     grad = jnp.concatenate(
         [content_cot.astype(jnp.float32) * valid, query_cot.astype(jnp.float32) * valid]
     )
-    owned = [None] * LAYERS
-    small_grads = [None] * LAYERS
-    for layer in reversed(range(LAYERS)):
-        small, far, tvec, onehot, low_in, q, k, v, attn, mixed, lse, resid, summed, pre = kept[layer]
-        dresid, dmix, dwo, feed_keep, feed_send, feed_vec, dhidden = feed_back(
-            place, small, grad, summed, resid, pre, mixed, attn, feed_pieces[layer]
-        )
-        feed_own = reduce_blocks(feed_keep, feed_send)
-        dq, dk, dv, table_sums = mix_back(
-            lengths, far, tvec, q, k, v, dmix, mixed, lse, row_flags, col_flags
-        )
-        attn_keep, attn_send, attn_vec = weight_back(place, low_in, dq, dk, dv, dwo)
-        attn_own = reduce_blocks(attn_keep, attn_send)
-        grad_c, grad_q = input_back(dq, dk, dv, attn, dresid)
-        if layer:
-            grad = jnp.concatenate([grad_c, grad_q])
-        small_grads[layer] = jnp.concatenate(
+    dresid1, dmix1, dwo1, keep_f1, send_f1, vec_f1, dhidden1 = feed_back(
+        place, small1, grad, summed1, resid1, pre1, mixed1, attn1, pieces_f1
+    )
+    get_f1 = swap_core(send_f1)
+    dq1, dk1, dv1, table1 = mix_back(
+        lengths, far1, tvec1, q1, k1, v1, dmix1, mixed1, lse1, row_flags, col_flags
+    )
+    both_f1 = reduce_core(keep_f1, after(get_f1, dq1))
+    by_f1 = reduce_corners(both_f1)
+    keep_a1, send_a1, vec_a1 = weight_back(place, low1, after(dq1, get_f1), dk1, dv1, dwo1)
+    get_a1 = swap_core(send_a1)
+    grad_c1, grad_q1 = input_back(after(dq1, keep_a1), dk1, dv1, attn1, dresid1)
+    both_a1 = reduce_core(keep_a1, after(get_a1, grad_c1))
+    by_a1 = reduce_corners(both_a1)
+    sides_rf1 = reduce_sides(both_f1, after(by_f1, grad_c1))
+    grad = after(jnp.concatenate([grad_c1, grad_q1]), by_f1, get_a1)
+    dresid0, dmix0, dwo0, keep_f0, send_f0, vec_f0, dhidden0 = feed_back(
+        place, small0, grad, summed0, resid0, pre0, mixed0, attn0, pieces_f0
+    )
+    get_f0 = swap_core(send_f0)
+    column_f1 = reduce_column(both_f1, after(sides_rf1, dmix0))
+    shifts_f1 = reduce_shifts(column_f1)
+    sides_ra1 = reduce_sides(both_a1, after(by_a1, dmix0))
+    dmix0_late = after(dmix0, by_a1, sides_rf1)
+    dq0, dk0, dv0, table0 = mix_back(
+        lengths, far0, tvec0, q0, k0, v0, dmix0_late, mixed0, lse0, row_flags, col_flags
+    )
+    both_f0 = reduce_core(keep_f0, after(get_f0, dq0))
+    by_f0 = reduce_corners(both_f0)
+    column_a1 = reduce_column(both_a1, after(sides_ra1, dq0))
+    keep_a0, send_a0, vec_a0 = weight_back(
+        place, low, after(dq0, shifts_f1, get_f0, sides_ra1), dk0, dv0, dwo0
+    )
+    get_a0 = swap_core(send_a0)
+    shifts_a1 = reduce_shifts(after(column_a1, keep_a0))
+    own_gf1 = reduce_total(column_f1, shifts_f1)
+    four_f1 = share_quarters(after(own_gf1, keep_a0), place_parts)
+    sides_rf0 = reduce_sides(both_f0, after(by_f0, keep_a0))
+    grad_c, grad_q = input_back(after(dq0, keep_a0), dk0, dv0, attn0, dresid0)
+    both_a0 = reduce_core(keep_a0, get_a0)
+    by_a0 = reduce_corners(both_a0)
+    own_ga1 = reduce_total(column_a1, shifts_a1)
+    four_a1 = share_quarters(own_ga1, place_parts)
+    sides_ra0 = reduce_sides(both_a0, by_a0)
+    column_f0 = reduce_column(both_f0, sides_rf0)
+    four_f0 = share_quarters(reduce_total(column_f0, reduce_shifts(column_f0)), place_parts)
+    column_a0 = reduce_column(both_a0, sides_ra0)
+    four_a0 = share_quarters(reduce_total(column_a0, reduce_shifts(column_a0)), place_parts)
+    owned = [
+        (
+            shard_grad("attn", attn_four[:, 0]),
+            shard_grad("inner", feed_four[:, 0]),
+            shard_grad("outer", feed_four[:, 1]),
+        )
+        for attn_four, feed_four in ((four_a0, four_f0), (four_a1, four_f1))
+    ]
+    small_grads = [
+        jnp.concatenate(
             [
                 attn_vec.reshape(-1),
                 feed_vec[2:].reshape(-1),
@@ -1398,13 +1483,11 @@
                 table_grad(table_sums, onehot).reshape(-1),
             ]
         )
-        feed_four = share_quarters(feed_own, place_parts)
-        attn_four = share_quarters(attn_own, place_parts)
-        owned[layer] = (
-            shard_grad("attn", attn_four[:, 0]),
-            shard_grad("inner", feed_four[:, 0]),
-            shard_grad("outer", feed_four[:, 1]),
-        )
+        for attn_vec, feed_vec, dhidden, table_sums in (
+            (vec_a0, vec_f0, dhidden0, table0),
+            (vec_a1, vec_f1, dhidden1, table1),
+        )
+    ]
     small_sum = sum_small(jnp.stack(small_grads))
     size = small_master.shape[1]
     small_own = lax.dynamic_slice_in_dim(small_sum, lax.axis_index("fsdp") * size, size, 1)
@@ -1416,7 +1499,7 @@
     outer_new = adam_update(outer_master, outer_first, outer_second, reduced[2], FEED_RATE)
     small_new = adam_update(small_master, small_first, small_second, small_own, SMALL_RATE)
     return (
-        (low[:LEN], low[LEN:], grad_c, grad_q) + attn_new + inner_new + outer_new + small_new
+        (low_out[:LEN], low_out[LEN:], grad_c, grad_q) + attn_new + inner_new + outer_new + small_new
     )
 
 

time: 680 us -> 715 us (1.051)
  other arithmetic: 60.9 us -> 85.3 us
  waiting for transfers between devices: 198 us -> 182 us
  local copies, waits for them, and re-layouts: 47 us -> 62 us
    ppermute x98, waiting for transfers between devices: 198 us -> 182 us  [move(): return lax.ppermute(value, AXES, pairs)]
    convert_element_type x12, other arithmetic: 14.4 us -> 26.4 us  [add_low(): return total.astype(jnp.bfloat16)]
    concatenate x9, other arithmetic: 4.44 us -> 11.7 us  [the longest x4 4.01 us: reduce_sides(): for_y = jnp.concatenate([add_low(both[0, 1, :2], by_x), both[0, 1, 2:]])]
  transfers between devices with their start and end apart: 98 -> 98, of which waited for: 34 -> 24; matrix products, arithmetic and copies ran while one was open for 12% -> 19% of each run, Pallas kernels for 13% -> 27%
where the time goes in v3:
time: 715 us; the launch traced here: 705 us
  Pallas kernels  272 us (38%)
  waiting for transfers between devices  182 us (25%)
  starting transfers between devices  98.7 us (14%)
  other arithmetic  85.3 us (12%)
  local copies, waits for them, and re-layouts  62 us (9%)
    ppermute x98, waiting for transfers between devices, move(): return lax.ppermute(value, AXES, pairs)  182 us
    ppermute x98, starting transfers between devices, move(): return lax.ppermute(value, AXES, pairs)  98.7 us
    pallas_call x2, Pallas kernels, feed_back(): pl.pallas_call(feed_back_kernel, out_shape=[jax.ShapeDtypeStruct((TALL, D...  84 us
    pallas_call x2, Pallas kernels, mix_back(): pl.pallas_call(mix_back_kernel, grid=(H // 2,), out_shape=[jax.ShapeDtype...  53.5 us
    pallas_call x2, Pallas kernels, feed(): pl.pallas_call(feed_kernel, out_shape=[jax.ShapeDtypeStruct((TALL, D), jn...  48 us
    pallas_call x2, Pallas kernels, mix(): pl.pallas_call(mix_kernel, grid=(H // 2,), out_shape=[jax.ShapeDtypeStruc...  38.1 us
    convert_element_type x12, other arithmetic, add_low(): return total.astype(jnp.bfloat16)  26.4 us
    pallas_call x2, Pallas kernels, input_back(): pl.pallas_call(input_back_kernel, out_shape=[half, half], in_specs=[VMEM_...  17 us
  transfers between devices with their start and end apart: 98, of which 24 were waited for; matrix products, arithmetic and copies ran while one was open for 19% of the time, Pallas kernels for 27%

profile of v3, /device:TPU:0, one launch (start us, length us, event | category | flops | bytes accessed | tf_op | source)
XLA Modules:
  0.0 705.2 jit_solution(14862277766112519979)
XLA Ops:
  34.0 10.6 %collective-permute-done = bf16[2,1200]{1,0:T(2,128)(2,1)S(1)} collective-permute-done((bf16[2,1200]{1,0:T(2,128)(2,1)}, bf16[2,1200]{1,0:T(2,128)(2,1)S(1)}, u32[]{:S(2)}, u32[]{:S(2)}) %collective-permute-start) | collective-permute-done | bytes 4832 | tf_op jit(solution)/shard_map/ppermute | solution.py:175
  59.0 7.9 %collective-permute-start.22 = (bf16[1,96,768]{2,1,0:T(8,128)(2,1)S(1)}, bf16[1,96,768]{2,1,0:T(8,128)(2,1)S(1)}, u32[]{:S(2)}, u32[]{:S(2)}) collective-permute-start(bf16[1,96,768]{2,1,0:T(8,128)(2,1)S(1)} %fusion.36), channel_id=1, source_target_pairs={{0,4},{1,5},{2,6},{3,7},{4,0},{5,1},{6,2},{7,3},{8,12},{9,13},{10,... | collective-permute-start | bytes 442376 | tf_op jit(solution)/shard_map/ppermute | solution.py:175
  80.1 25.9 %collective-permute-done.10.refs_4_ = bf16[2,1,96,768]{3,2,1,0:T(8,128)(2,1)S(1)} collective-permute-done((bf16[2,1,96,768]{3,2,1,0:T(8,128)(2,1)S(1)}, bf16[2,1,96,768]{3,2,1,0:T(8,128)(2,1)S(1)}, u32[]{:S(2)}, u32[]{:S(2)}) %collective-permute-start.10) | collective-permute-done | bytes 294944 | tf_op jit(solution)/shard_map/ppermute | solution.py:175
  108.5 8.5 %project.2 = (bf16[1024,768]{1,0:T(8,128)(2,1)}, bf16[512,768]{1,0:T(8,128)(2,1)}, bf16[512,768]{1,0:T(8,128)(2,1)}, bf16[4,768,768]{2,1,0:T(8,128)(2,1)}) custom-call(s32[4]{0:T(128)} %pad_add_fusion.place_ref, bf16[1024,768]{1,0:T(8,128)(2,1)} %constant_dynamic-update-slice_fusion.low_ref, f32[8,768]{1,0:T(8,128)} %reshape.595.small_ref, ...), custom_call_target="tpu_custom_call" | custom-call | flops 2415919104 | bytes 16000000 | tf_op jit(solution)/shard_map/project/pallas_call | solution.py:294
  129.9 18.5 %collective-permute-done.41 = bf16[2,96,768]{2,1,0:T(8,128)(2,1)S(1)} collective-permute-done((bf16[2,96,768]{2,1,0:T(8,128)(2,1)S(1)}, bf16[2,96,768]{2,1,0:T(8,128)(2,1)S(1)}, u32[]{:S(2)}, u32[]{:S(2)}) %collective-permute-start.41) | collective-permute-done | bytes 294944 | tf_op jit(solution)/shard_map/ppermute | solution.py:175
  155.4 19.0 %mix.2 = (bf16[1024,768]{1,0:T(8,128)(2,1)}, f32[12,1,1024]{2,1,0:T(1,128)}) custom-call(s32[1]{0:T(128)} %copy.381.length_ref, f32[12,2]{1,0:T(8,128)} %pad_maximum_fusion.31.far_ref, bf16[1024,768]{1,0:T(8,128)(2,1)} %get-tuple-element.150.q_ref, bf16[512,768]{1,0:T(8,128)(2,1)} %get-tuple-element.151.k_ref, bf16[512,768]{1,0:T(8,128)(2,1)} %get-tuple-element.152.v_ref, ...), custom_call_target="tpu_custom_call" | custom-call | flops 6499999744 | bytes 8000000 | tf_op jit(solution)/shard_map/mix/pallas_call | solution.py:405
  180.2 29.0 %collective-permute-done.33.refs_3_ = bf16[2,1,96,768]{3,2,1,0:T(8,128)(2,1)S(1)} collective-permute-done((bf16[2,1,96,768]{3,2,1,0:T(8,128)(2,1)S(1)}, bf16[2,1,96,768]{3,2,1,0:T(8,128)(2,1)S(1)}, u32[]{:S(2)}, u32[]{:S(2)}) %collective-permute-start.33) | collective-permute-done | bytes 294944 | tf_op jit(solution)/shard_map/ppermute | solution.py:175
  210.4 7.0 collective-permute-done.34.refs_4_
  234.8 24.0 %feed.2 = (f32[1024,768]{1,0:T(8,128)}, f32[1024,768]{1,0:T(8,128)}, bf16[1024,3072]{1,0:T(8,128)(2,1)}, f32[1024,768]{1,0:T(8,128)}, bf16[1024,768]{1,0:T(8,128)(2,1)}) custom-call(s32[4]{0:T(128)} %pad_add_fusion.place_ref, f32[8,768]{1,0:T(8,128)} %reshape.595.small_ref, f32[1,3072]{1,0:T(1,128)} %bitcast.279, ...), custom_call_target="tpu_custom_call" | custom-call | flops 10871635968 | bytes 40000000 | tf_op jit(solution)/shard_map/feed/pallas_call | solution.py:616
  258.9 8.4 %project.3 = (bf16[1024,768]{1,0:T(8,128)(2,1)}, bf16[512,768]{1,0:T(8,128)(2,1)}, bf16[512,768]{1,0:T(8,128)(2,1)}, bf16[4,768,768]{2,1,0:T(8,128)(2,1)}) custom-call(s32[4]{0:T(128)} %pad_add_fusion.place_ref, bf16[1024,768]{1,0:T(8,128)(2,1)} %get-tuple-element.158.low_ref, f32[8,768]{1,0:T(8,128)} %reshape.593.small_ref, ...), custom_call_target="tpu_custom_call" | custom-call | flops 2415919104 | bytes 16000000 | tf_op jit(solution)/shard_map/project/pallas_call | solution.py:294
  267.9 19.1 %mix.3 = (bf16[1024,768]{1,0:T(8,128)(2,1)}, f32[12,1,1024]{2,1,0:T(1,128)}) custom-call(s32[1]{0:T(128)} %copy.381.length_ref, f32[12,2]{1,0:T(8,128)} %pad_maximum_fusion.30.far_ref, bf16[1024,768]{1,0:T(8,128)(2,1)} %get-tuple-element.162.q_ref, bf16[512,768]{1,0:T(8,128)(2,1)} %get-tuple-element.163.k_ref, bf16[512,768]{1,0:T(8,128)(2,1)} %get-tuple-element.164.v_ref, ...), custom_call_target="tpu_custom_call" | custom-call | flops 6499999744 | bytes 8000000 | tf_op jit(solution)/shard_map/mix/pallas_call | solution.py:405
  288.1 24.0 %feed.3 = (f32[1024,768]{1,0:T(8,128)}, f32[1024,768]{1,0:T(8,128)}, bf16[1024,3072]{1,0:T(8,128)(2,1)}, f32[1024,768]{1,0:T(8,128)}, bf16[1024,768]{1,0:T(8,128)(2,1)}) custom-call(s32[4]{0:T(128)} %pad_add_fusion.place_ref, f32[8,768]{1,0:T(8,128)} %reshape.593.small_ref, f32[1,3072]{1,0:T(1,128)} %bitcast.278, ...), custom_call_target="tpu_custom_call" | custom-call | flops 10871635968 | bytes 40000000 | tf_op jit(solution)/shard_map/feed/pallas_call | solution.py:616
  312.1 42.1 %feed_back.2 = (f32[1024,768]{1,0:T(8,128)}, bf16[1024,768]{1,0:T(8,128)(2,1)}, bf16[768,768]{1,0:T(8,128)(2,1)}, bf16[2,2,4,2,96,768]{5,4,3,2,1,0:T(8,128)(2,1)...) custom-call(s32[4]{0:T(128)} %pad_add_fusion.place_ref, ...), custom_call_target="tpu_custom_call" | custom-call | flops 21743271936 | bytes 60000000 | tf_op jit(solution)/shard_map/feed_back/pallas_call | solution.py:783
  355.1 26.8 %mix_back.2 = (bf16[1024,768]{1,0:T(8,128)(2,1)}, bf16[512,768]{1,0:T(8,128)(2,1)}, bf16[512,768]{1,0:T(8,128)(2,1)}, f32[12,1,768]{2,1,0:T(1,128)}) custom-call(s32[1]{0:T(128)} %copy.381.length_ref, f32[12,2]{1,0:T(8,128)} %pad_maximum_fusion.30.far_ref, bf16[1024,768]{1,0:T(8,128)(2,1)} %get-tuple-element.162.q_ref, ...), custom_call_target="tpu_custom_call" | custom-call | flops 16000000000 | bytes 12000000 | tf_op jit(solution)/shard_map/mix_back/pallas_call | solution.py:514
  384.7 7.4 %weight_back.2 = (bf16[2,2,4,1,96,768]{5,4,3,2,1,0:T(8,128)(2,1)}, bf16[2,2,4,1,96,768]{5,4,3,2,1,0:T(8,128)(2,1)}, f32[2,768]{1,0:T(2,128)}) custom-call(s32[4]{0:T(128)} %pad_add_fusion.place_ref, bf16[1024,768]{1,0:T(8,128)(2,1)} %get-tuple-element.158.low_ref, bf16[1024,768]{1,0:T(8,128)(2,1)} %get-tuple-element.181.dq_ref, ...), custom_call_target="tpu_custom_call" | custom-call | flops 2415919104 | bytes 12000000 | tf_op jit(solution)/shard_map/weight_back/pallas_call | solution.py:861
  406.3 8.5 %input_back.2 = (f32[512,768]{1,0:T(8,128)}, f32[512,768]{1,0:T(8,128)}) custom-call(bf16[1024,768]{1,0:T(8,128)(2,1)} %get-tuple-element.181.dq_ref, bf16[512,768]{1,0:T(8,128)(2,1)} %get-tuple-element.177.dk_ref, bf16[512,768]{1,0:T(8,128)(2,1)} %get-tuple-element.178.dv_ref, bf16[4,768,768]{2,1,0:T(8,128)(2,1)} %get-tuple-element.167.attn_any.w_ref, ...), custom_call_target="tpu_custom_call" | custom-call | flops 2415919104 | bytes 16000000 | tf_op jit(solution)/shard_map/input_back/pallas_call | solution.py:891
  425.5 41.9 %feed_back.3 = (f32[1024,768]{1,0:T(8,128)}, bf16[1024,768]{1,0:T(8,128)(2,1)}, bf16[768,768]{1,0:T(8,128)(2,1)}, bf16[2,2,4,2,96,768]{5,4,3,2,1,0:T(8,128)(2,1)...) custom-call(s32[4]{0:T(128)} %pad_add_fusion.place_ref, ...), custom_call_target="tpu_custom_call" | custom-call | flops 21743271936 | bytes 60000000 | tf_op jit(solution)/shard_map/feed_back/pallas_call | solution.py:783
  491.4 26.7 %mix_back.3 = (bf16[1024,768]{1,0:T(8,128)(2,1)}, bf16[512,768]{1,0:T(8,128)(2,1)}, bf16[512,768]{1,0:T(8,128)(2,1)}, f32[12,1,768]{2,1,0:T(1,128)}) custom-call(s32[1]{0:T(128)} %copy.381.length_ref, f32[12,2]{1,0:T(8,128)} %pad_maximum_fusion.31.far_ref, bf16[1024,768]{1,0:T(8,128)(2,1)} %get-tuple-element.150.q_ref, ...), custom_call_target="tpu_custom_call" | custom-call | flops 16000000000 | bytes 12000000 | tf_op jit(solution)/shard_map/mix_back/pallas_call | solution.py:514
  541.1 7.4 %weight_back.3 = (bf16[2,2,4,1,96,768]{5,4,3,2,1,0:T(8,128)(2,1)}, bf16[2,2,4,1,96,768]{5,4,3,2,1,0:T(8,128)(2,1)}, f32[2,768]{1,0:T(2,128)}) custom-call(s32[4]{0:T(128)} %pad_add_fusion.place_ref, bf16[1024,768]{1,0:T(8,128)(2,1)} %constant_dynamic-update-slice_fusion.low_ref, bf16[1024,768]{1,0:T(8,128)(2,1)} %get-tuple-element.209.dq_ref, ...), custom_call_target="tpu_custom_call" | custom-call | flops 2415919104 | bytes 12000000 | tf_op jit(solution)/shard_map/weight_back/pallas_call | solution.py:861
  582.0 8.5 %input_back.3 = (f32[512,768]{1,0:T(8,128)}, f32[512,768]{1,0:T(8,128)}) custom-call(bf16[1024,768]{1,0:T(8,128)(2,1)} %get-tuple-element.209.dq_ref, bf16[512,768]{1,0:T(8,128)(2,1)} %get-tuple-element.205.dk_ref, bf16[512,768]{1,0:T(8,128)(2,1)} %get-tuple-element.206.dv_ref, bf16[4,768,768]{2,1,0:T(8,128)(2,1)} %get-tuple-element.157.attn_any.w_ref, ...), custom_call_target="tpu_custom_call" | custom-call | flops 2415919104 | bytes 16000000 | tf_op jit(solution)/shard_map/input_back/pallas_call | solution.py:891
  614.7 6.3 collective-permute-done.87
  620.9 17.5 %collective-permute-done.86 = bf16[2,96,768]{2,1,0:T(8,128)(2,1)S(1)} collective-permute-done((bf16[2,96,768]{2,1,0:T(8,128)(2,1)S(1)}, bf16[2,96,768]{2,1,0:T(8,128)(2,1)S(1)}, u32[]{:S(2)}, u32[]{:S(2)}) %collective-permute-start.86) | collective-permute-done | bytes 294944 | tf_op jit(solution)/shard_map/ppermute | solution.py:175
  660.9 8.0 %collective-permute-done.70 = bf16[4,1,96,768]{3,2,0,1:T(8,128)(2,1)} collective-permute-done((bf16[4,1,96,768]{3,2,0,1:T(8,128)(2,1)}, bf16[4,1,96,768]{3,2,0,1:T(8,128)(2,1)}, u32[]{:S(2)}, u32[]{:S(2)}) %collective-permute-start.70) | collective-permute-done | bytes 589856 | tf_op jit(solution)/shard_map/ppermute | solution.py:175
  687.6 7.1 %multiply_subtract_fusion.1 = (f32[2,96,3072]{2,1,0:T(8,128)}, f32[2,96,3072]{2,1,0:T(8,128)}, f32[2,96,3072]{2,1,0:T(8,128)}) fusion(f32[2,96,3072]{2,1,0:T(8,128)S(1)} %copy-done.3, bf16[1,96,3072]{2,1,0:T(8,128)(2,1)} %stack_reshape.11, bf16[1,96,3072]{2,1,0:T(8,128)(2,1)} %stack_reshape.10, f32[2,96,3072]{2,1,0:T(8,128)} %param.36, f32[2,96,3072]{2,1,0:T(8,128)} %param.37), kind=kLoop, calls=%fused_computation.25 | loop fusion | flops 10027008 | bytes 15335424 | tf_op jit(solution)/shard_map/sub | solution.py:1138
  (474 shorter events, 292.0 us)
Async XLA Ops:
  32.4 37.8 %collective-permute-start.7 = (bf16[4,1,96,768]{3,2,1,0:T(8,128)(2,1)S(1)}, bf16[4,1,96,768]{3,2,1,0:T(8,128)(2,1)S(1)}, u32[]{:S(2)}, u32[]{:S(2)}) collective-permute-start(bf16[4,1,96,768]{3,2,1,0:T(8,128)(2,1)S(1)} %pad_maximum_fusion.11.refs_0_), channel_id=1, source_target_pairs={{0,16},{1,17},{2,18},{3,19},{4,20},{5,21},{6,22},{7,23},{8,24},{9,... | collective-permute-start | bytes 1769480 | tf_op jit(solution)/shard_map/ppermute | solution.py:175
  70.2 35.9 %collective-permute-start.12 = (bf16[4,1,96,768]{3,2,1,0:T(8,128)(2,1)S(1)}, bf16[4,1,96,768]{3,2,1,0:T(8,128)(2,1)S(1)}, u32[]{:S(2)}, u32[]{:S(2)}) collective-permute-start(bf16[4,1,96,768]{3,2,1,0:T(8,128)(2,1)S(1)} %collective-permute-done.7.refs_1_), channel_id=1, source_target_pairs={{0,8},{1,9},{2,10},{3,11},{4,12},{5,13},{6,14},{7,15},{8,0},{9,1},... | collective-permute-start | bytes 1769480 | tf_op jit(solution)/shard_map/ppermute | solution.py:175
  75.6 41.4 %collective-permute-start.19 = (bf16[4,2,96,768]{3,2,1,0:T(8,128)(2,1)S(1)}, bf16[4,2,96,768]{3,2,1,0:T(8,128)(2,1)}, u32[]{:S(2)}, u32[]{:S(2)}) collective-permute-start(bf16[4,2,96,768]{3,2,1,0:T(8,128)(2,1)S(1)} %pad_maximum_fusion.2.refs_0_), channel_id=1, source_target_pairs={{0,16},{1,17},{2,18},{3,19},{4,20},{5,21},{6,22},{7,23},{8,24},{9,... | collective-permute-start | bytes 3538952 | tf_op jit(solution)/shard_map/ppermute | solution.py:175
  77.1 40.0 %collective-permute-start.20 = (bf16[4,2,96,768]{3,2,1,0:T(8,128)(2,1)S(1)}, bf16[4,2,96,768]{3,2,1,0:T(8,128)(2,1)}, u32[]{:S(2)}, u32[]{:S(2)}) collective-permute-start(bf16[4,2,96,768]{3,2,1,0:T(8,128)(2,1)S(1)} %pad_maximum_fusion.2.refs_0_), channel_id=1, source_target_pairs={{0,1},{1,0},{2,3},{3,2},{4,5},{5,4},{6,7},{7,6},{8,9},{9,8},{10,11... | collective-permute-start | bytes 3538952 | tf_op jit(solution)/shard_map/ppermute | solution.py:175
  108.3 66.7 %collective-permute-start.28 = (bf16[4,2,96,768]{3,2,1,0:T(8,128)(2,1)S(1)}, bf16[4,2,96,768]{3,2,1,0:T(8,128)(2,1)}, u32[]{:S(2)}, u32[]{:S(2)}) collective-permute-start(bf16[4,2,96,768]{3,2,1,0:T(8,128)(2,1)S(1)} %pad_maximum_fusion.2.refs_0_), channel_id=1, source_target_pairs={{0,8},{1,9},{2,10},{3,11},{4,12},{5,13},{6,14},{7,15},{8,0},{9,1},... | collective-permute-start | bytes 3538952 | tf_op jit(solution)/shard_map/ppermute | solution.py:175
  117.0 37.6 %collective-permute-start.24 = (bf16[4,1,96,768]{3,2,1,0:T(8,128)(2,1)S(1)}, bf16[4,1,96,768]{3,2,1,0:T(8,128)(2,1)S(1)}, u32[]{:S(2)}, u32[]{:S(2)}) collective-permute-start(bf16[4,1,96,768]{3,2,1,0:T(8,128)(2,1)S(1)} %pad_maximum_fusion.12.refs_0_), channel_id=1, source_target_pairs={{0,16},{1,17},{2,18},{3,19},{4,20},{5,21},{6,22},{7,23},{8,24},{9,... | collective-permute-start | bytes 1769480 | tf_op jit(solution)/shard_map/ppermute | solution.py:175
  129.9 44.6 %collective-permute-start.35 = (bf16[4,1,96,768]{3,2,1,0:T(8,128)(2,1)S(1)}, bf16[4,1,96,768]{3,2,1,0:T(8,128)(2,1)}, u32[]{:S(2)}, u32[]{:S(2)}) collective-permute-start(bf16[4,1,96,768]{3,2,1,0:T(8,128)(2,1)S(1)} %pad_maximum_fusion.12.refs_0_), channel_id=1, source_target_pairs={{0,8},{1,9},{2,10},{3,11},{4,12},{5,13},{6,14},{7,15},{8,0},{9,1},... | collective-permute-start | bytes 1769480 | tf_op jit(solution)/shard_map/ppermute | solution.py:175
  174.4 44.6 %collective-permute-start.29 = (bf16[4,2,96,768]{3,2,1,0:T(8,128)(2,1)}, bf16[4,2,96,768]{3,2,1,0:T(8,128)(2,1)S(1)}, u32[]{:S(2)}, u32[]{:S(2)}) collective-permute-start(bf16[4,2,96,768]{3,2,1,0:T(8,128)(2,1)} %collective-permute-done.19.refs_1_), channel_id=1, source_target_pairs={{0,8},{1,9},{2,10},{3,11},{4,12},{5,13},{6,14},{7,15},{8,0},{9,1},... | collective-permute-start | bytes 3538952 | tf_op jit(solution)/shard_map/ppermute | solution.py:175
  174.5 45.1 %collective-permute-start.30 = (bf16[4,2,96,768]{3,2,1,0:T(8,128)(2,1)}, bf16[4,2,96,768]{3,2,1,0:T(8,128)(2,1)S(1)}, u32[]{:S(2)}, u32[]{:S(2)}) collective-permute-start(bf16[4,2,96,768]{3,2,1,0:T(8,128)(2,1)} %collective-permute-done.20.refs_2_), channel_id=1, source_target_pairs={{0,8},{1,9},{2,10},{3,11},{4,12},{5,13},{6,14},{7,15},{8,0},{9,1},... | collective-permute-start | bytes 3538952 | tf_op jit(solution)/shard_map/ppermute | solution.py:175
  175.0 45.1 %collective-permute-start.43 = (bf16[4,2,96,768]{3,2,1,0:T(8,128)(2,1)S(1)}, bf16[4,2,96,768]{3,2,1,0:T(8,128)(2,1)}, u32[]{:S(2)}, u32[]{:S(2)}) collective-permute-start(bf16[4,2,96,768]{3,2,1,0:T(8,128)(2,1)S(1)} %pad_maximum_fusion.3.refs_0_), channel_id=1, source_target_pairs={{0,16},{1,17},{2,18},{3,19},{4,20},{5,21},{6,22},{7,23},{8,24},{9,... | collective-permute-start | bytes 3538952 | tf_op jit(solution)/shard_map/ppermute | solution.py:175
  178.0 50.0 %collective-permute-start.44 = (bf16[4,2,96,768]{3,2,1,0:T(8,128)(2,1)S(1)}, bf16[4,2,96,768]{3,2,1,0:T(8,128)(2,1)}, u32[]{:S(2)}, u32[]{:S(2)}) collective-permute-start(bf16[4,2,96,768]{3,2,1,0:T(8,128)(2,1)S(1)} %pad_maximum_fusion.3.refs_0_), channel_id=1, source_target_pairs={{0,1},{1,0},{2,3},{3,2},{4,5},{5,4},{6,7},{7,6},{8,9},{9,8},{10,11... | collective-permute-start | bytes 3538952 | tf_op jit(solution)/shard_map/ppermute | solution.py:175
  231.3 55.7 %collective-permute-start.47 = (bf16[4,2,96,768]{3,2,1,0:T(8,128)(2,1)S(1)}, bf16[4,2,96,768]{3,2,1,0:T(8,128)(2,1)}, u32[]{:S(2)}, u32[]{:S(2)}) collective-permute-start(bf16[4,2,96,768]{3,2,1,0:T(8,128)(2,1)S(1)} %pad_maximum_fusion.3.refs_0_), channel_id=1, source_target_pairs={{0,8},{1,9},{2,10},{3,11},{4,12},{5,13},{6,14},{7,15},{8,0},{9,1},... | collective-permute-start | bytes 3538952 | tf_op jit(solution)/shard_map/ppermute | solution.py:175
  231.6 35.7 %collective-permute-start.45 = (bf16[2,2,96,768]{3,2,1,0:T(8,128)(2,1)S(1)}, bf16[2,2,96,768]{3,2,1,0:T(8,128)(2,1)}, u32[]{:S(2)}, u32[]{:S(2)}) collective-permute-start(bf16[2,2,96,768]{3,2,1,0:T(8,128)(2,1)S(1)} %slice.492), channel_id=1, source_target_pairs={{0,16},{1,17},{2,18},{3,19},{4,20},{5,21},{6,22},{7,23},{8,24},{9,... | collective-permute-start | bytes 1769480 | tf_op jit(solution)/shard_map/ppermute | solution.py:175
  234.3 52.8 %collective-permute-start.48 = (bf16[4,2,96,768]{3,2,1,0:T(8,128)(2,1)}, bf16[4,2,96,768]{3,2,1,0:T(8,128)(2,1)}, u32[]{:S(2)}, u32[]{:S(2)}) collective-permute-start(bf16[4,2,96,768]{3,2,1,0:T(8,128)(2,1)} %collective-permute-done.43.refs_1_), channel_id=1, source_target_pairs={{0,8},{1,9},{2,10},{3,11},{4,12},{5,13},{6,14},{7,15},{8,0},{9,1},... | collective-permute-start | bytes 3538952 | tf_op jit(solution)/shard_map/ppermute | solution.py:175
  234.3 52.8 %collective-permute-start.49 = (bf16[4,2,96,768]{3,2,1,0:T(8,128)(2,1)}, bf16[4,2,96,768]{3,2,1,0:T(8,128)(2,1)}, u32[]{:S(2)}, u32[]{:S(2)}) collective-permute-start(bf16[4,2,96,768]{3,2,1,0:T(8,128)(2,1)} %collective-permute-done.44.refs_2_), channel_id=1, source_target_pairs={{0,8},{1,9},{2,10},{3,11},{4,12},{5,13},{6,14},{7,15},{8,0},{9,1},... | collective-permute-start | bytes 3538952 | tf_op jit(solution)/shard_map/ppermute | solution.py:175
  421.6 52.4 %collective-permute-start.58 = (bf16[4,2,96,768]{3,2,1,0:T(8,128)(2,1)}, bf16[4,2,96,768]{3,2,1,0:T(8,128)(2,1)}, u32[]{:S(2)}, u32[]{:S(2)}) collective-permute-start(bf16[4,2,96,768]{3,2,1,0:T(8,128)(2,1)} %pad_maximum_fusion.4), channel_id=1, source_target_pairs={{0,16},{1,17},{2,18},{3,19},{4,20},{5,21},{6,22},{7,23},{8,24},{9,... | collective-permute-start | bytes 3538952 | tf_op jit(solution)/shard_map/ppermute | solution.py:175
  424.2 49.8 %collective-permute-start.59 = (bf16[4,2,96,768]{3,2,1,0:T(8,128)(2,1)}, bf16[4,2,96,768]{3,2,1,0:T(8,128)(2,1)S(1)}, u32[]{:S(2)}, u32[]{:S(2)}) collective-permute-start(bf16[4,2,96,768]{3,2,1,0:T(8,128)(2,1)} %pad_maximum_fusion.5), channel_id=1, source_target_pairs={{0,1},{1,0},{2,3},{3,2},{4,5},{5,4},{6,7},{7,6},{8,9},{9,8},{10,11... | collective-permute-start | bytes 3538952 | tf_op jit(solution)/shard_map/ppermute | solution.py:175
  467.4 73.7 %collective-permute-start.63 = (bf16[2,2,4,2,96,768]{5,4,3,2,1,0:T(8,128)(2,1)}, bf16[2,2,4,2,96,768]{5,4,3,2,1,0:T(8,128)(2,1)}, u32[]{:S(2)}, u32[]{:S(2)}) collective-permute-start(bf16[2,2,4,2,96,768]{5,4,3,2,1,0:T(8,128)(2,1)} %get-tuple-element.201), channel_id=1, source_target_pairs={{0,8},{1,9},{2,10},{3,11},{4,12},{5,13},{6,14},{7,15},{8,0},{9,1},... | collective-permute-start | bytes 14155784 | tf_op jit(solution)/shard_map/ppermute | solution.py:175
  478.4 46.8 %collective-permute-start.60 = (bf16[2,96,768]{2,1,0:T(8,128)(2,1)}, bf16[2,96,768]{2,1,0:T(8,128)(2,1)}, u32[]{:S(2)}, u32[]{:S(2)}) collective-permute-start(bf16[2,96,768]{2,1,0:T(8,128)(2,1)} %get-tuple-element.286), channel_id=1, source_target_pairs={{0,2},{1,3},{2,4},{3,5},{4,6},{5,7},{6,0},{7,1},{8,10},{9,11},{10,... | collective-permute-start | bytes 884744 | tf_op jit(solution)/shard_map/ppermute | solution.py:175
  479.4 53.6 %collective-permute-start.61 = (bf16[2,96,768]{2,1,0:T(8,128)(2,1)}, bf16[2,96,768]{2,1,0:T(8,128)(2,1)}, u32[]{:S(2)}, u32[]{:S(2)}) collective-permute-start(bf16[2,96,768]{2,1,0:T(8,128)(2,1)} %get-tuple-element.285), channel_id=1, source_target_pairs={{0,4},{1,5},{2,6},{3,7},{4,0},{5,1},{6,2},{7,3},{8,12},{9,13},{10,... | collective-permute-start | bytes 884744 | tf_op jit(solution)/shard_map/ppermute | solution.py:175
  483.3 49.7 %collective-permute-start.62 = (bf16[2,96,768]{2,1,0:T(8,128)(2,1)}, bf16[2,96,768]{2,1,0:T(8,128)(2,1)}, u32[]{:S(2)}, u32[]{:S(2)}) collective-permute-start(bf16[2,96,768]{2,1,0:T(8,128)(2,1)} %get-tuple-element.284), channel_id=1, source_target_pairs={{0,6},{1,7},{2,0},{3,1},{4,2},{5,3},{6,4},{7,5},{8,14},{9,15},{10,... | collective-permute-start | bytes 884744 | tf_op jit(solution)/shard_map/ppermute | solution.py:175
  489.9 45.1 %collective-permute-start.64 = (bf16[4,1,96,768]{3,2,0,1:T(8,128)(2,1)}, bf16[4,1,96,768]{3,2,0,1:T(8,128)(2,1)}, u32[]{:S(2)}, u32[]{:S(2)}) collective-permute-start(bf16[4,1,96,768]{3,2,0,1:T(8,128)(2,1)} %pad_maximum_fusion.13), channel_id=1, source_target_pairs={{0,16},{1,17},{2,18},{3,19},{4,20},{5,21},{6,22},{7,23},{8,24},{9,... | collective-permute-start | bytes 1769480 | tf_op jit(solution)/shard_map/ppermute | solution.py:175
  548.7 42.9 %collective-permute-start.90 = (bf16[2,96,768]{2,1,0:T(8,128)(2,1)}, bf16[2,96,768]{2,1,0:T(8,128)(2,1)S(1)}, u32[]{:S(2)}, u32[]{:S(2)}) collective-permute-start(bf16[2,96,768]{2,1,0:T(8,128)(2,1)} %fusion.21), channel_id=1, source_target_pairs={{0,16},{1,17},{2,18},{3,19},{4,20},{5,21},{6,22},{7,23},{8,24},{9,... | collective-permute-start | bytes 884744 | tf_op jit(solution)/shard_map/ppermute | solution.py:175
  590.6 48.6 %collective-permute-start.66 = (bf16[2,2,4,1,96,768]{5,4,3,2,1,0:T(8,128)(2,1)}, bf16[2,2,4,1,96,768]{5,4,3,2,1,0:T(8,128)(2,1)S(1)}, u32[]{:S(2)}, u32[]{:S(2)}) collective-permute-start(bf16[2,2,4,1,96,768]{5,4,3,2,1,0:T(8,128)(2,1)} %get-tuple-element.213), channel_id=1, source_target_pairs={{0,8},{1,9},{2,10},{3,11},{4,12},{5,13},{6,14},{7,15},{8,0},{9,1},... | collective-permute-start | bytes 7077896 | tf_op jit(solution)/shard_map/ppermute | solution.py:175
  (136 other events, 2152.0 us)

commit v4 on v2

--- a/solution.py
+++ b/solution.py
@@ -187,27 +187,14 @@
     return move(value, lambda x, c, z, y: (x, c, z, 1 - y))
 
 
-def shift_z(value, step):
-    return move(value, lambda x, c, z, y: (x, c, (z + step) % 4, y))
+def swap_z(value, apart):
+    return move(value, lambda x, c, z, y: (x, c, z ^ apart, y))
 
 
 def my_place():
     dp = lax.axis_index("dp")
     fsdp = lax.axis_index("fsdp")
     return (dp // 2, dp % 2, fsdp // 2, fsdp % 2)
-
-
-def spread_blocks(own):
-    column = jnp.stack([own] + [shift_z(own, step) for step in (1, 2, 3)])
-    from_x = swap_x(column)
-    from_y = swap_y(column)
-    corner_low = swap_x(from_y[:2])
-    corner_high = swap_y(from_x[2:])
-    mine = (column, from_x, from_y, corner_low, corner_high)
-    return mine + tuple(swap_core(piece) for piece in mine)
-
-
-PIECES = ((0, 0, 0, 4), (1, 0, 0, 4), (0, 1, 0, 4), (1, 1, 0, 2), (1, 1, 2, 4))
 
 
 def dot_nn(left, right):
@@ -250,42 +237,45 @@
     )
 
 
-def start_fetch(kinds, place_ref, pieces, targets, sems):
+def start_fetch(kinds, plan, place_ref, refs, targets, sems):
     x, c, z, y = (place_ref[index] for index in range(4))
+    mine = z * 2 + y
     copies = []
-    for other in range(2):
-        for piece, (dx, dy, first, last) in enumerate(PIECES):
-            for k in range(first, last):
-                quarter = (x ^ dx) * 2 + (c ^ other)
-                owner = ((z - k) & 3) * 2 + (y ^ dy)
-                for member, kind in enumerate(kinds):
-                    if kind == "attn":
-                        target = targets[member].at[
-                            quarter, pl.ds(pl.multiple_of(owner * ROWS, ROWS), ROWS), :
-                        ]
-                    elif kind == "inner":
-                        target = targets[member].at[
-                            pl.ds(pl.multiple_of(owner * ROWS, ROWS), ROWS),
-                            pl.ds(pl.multiple_of(quarter * D, D), D),
-                        ]
-                    else:
-                        target = targets[member].at[
-                            pl.ds(pl.multiple_of(owner * 384 + quarter * ROWS, ROWS), ROWS), :
-                        ]
-                    copy = pltpu.make_async_copy(
-                        pieces[other * 5 + piece].at[k - first, member],
-                        target,
-                        sems.at[len(copies)],
-                    )
-                    copy.start()
-                    copies.append(copy)
+
+    def start(source, target):
+        copy = pltpu.make_async_copy(source, target, sems.at[len(copies)])
+        copy.start()
+        copies.append(copy)
+
+    for member, kind in enumerate(kinds):
+        target = targets[member]
+        if kind == "attn":
+            start(refs[member], target.at[:, pl.ds(pl.multiple_of(mine * ROWS, ROWS), ROWS), :])
+        elif kind == "inner":
+            for quarter in range(4):
+                start(
+                    refs[member].at[:, quarter * D : quarter * D + D],
+                    target.at[quarter, pl.ds(pl.multiple_of(mine * ROWS, ROWS), ROWS), :],
+                )
+        else:
+            start(refs[member], target.at[z, pl.ds(pl.multiple_of(y * 384, ROWS), 384), :])
+    for array, index, dx, dy, dc, dz, member in plan:
+        quarter = (x ^ dx) * 2 + (c ^ dc)
+        if kinds[member] == "outer":
+            lead, row = z ^ dz, (y ^ dy) * 384 + quarter * ROWS
+        else:
+            lead, row = quarter, ((z ^ dz) * 2 + (y ^ dy)) * ROWS
+        start(
+            refs[len(kinds) + array].at[index],
+            targets[member].at[lead, pl.ds(pl.multiple_of(row, ROWS), ROWS), :],
+        )
     return copies
 
 
-def project_kernel(place_ref, low_ref, small_ref, *refs):
-    pieces = refs[:10]
-    q_ref, k_ref, v_ref, w_out, w_ref, sems, out_sem = refs[10:]
-    for copy in start_fetch(("attn",), place_ref, pieces, (w_ref,), sems):
+def project_kernel(plan, place_ref, low_ref, small_ref, *refs):
+    pieces = refs[:-7]
+    q_ref, k_ref, v_ref, w_out, w_ref, sems, out_sem = refs[-7:]
+    for copy in start_fetch(("attn",), plan, place_ref, pieces, (w_ref,), sems):
         copy.wait()
     keep = pltpu.make_async_copy(w_ref, w_out, out_sem)
     keep.start()
@@ -300,16 +290,17 @@
     keep.wait()
 
 
-def project(place, low, small, pieces):
+def project(place, low, small, group):
+    plan, pieces = group
     return pl.pallas_call(
-        project_kernel,
+        partial(project_kernel, plan),
         out_shape=[
             jax.ShapeDtypeStruct((TALL, D), jnp.bfloat16),
             jax.ShapeDtypeStruct((LEN, D), jnp.bfloat16),
             jax.ShapeDtypeStruct((LEN, D), jnp.bfloat16),
             jax.ShapeDtypeStruct((4, D, D), jnp.bfloat16),
         ],
-        in_specs=[SMEM_SPEC, VMEM_SPEC, VMEM_SPEC] + [ANY_SPEC] * 10,
+        in_specs=[SMEM_SPEC, VMEM_SPEC, VMEM_SPEC] + [ANY_SPEC] * len(pieces),
         out_specs=[VMEM_SPEC] * 3 + [ANY_SPEC],
         scratch_shapes=[
             pltpu.VMEM((4, D, D), jnp.bfloat16),
@@ -364,13 +355,14 @@
 
 def mix_kernel(
     length_ref, far_ref, q_ref, k_ref, v_ref, row_flags, col_flags, t_ref,
-    a_ref, lse_ref, mask_ref, alive_ref, tile_ref, p_ref, o_ref,
+    a_ref, p_ref, inverse_ref, dead_ref, mask_ref, alive_ref, tile_ref, o_ref,
 ):
     pair = pl.program_id(0)
 
     @pl.when(pair == 0)
     def _():
         build_masks(length_ref[0], row_flags, col_flags, mask_ref, alive_ref)
+        dead_ref[...] = (1.0 - alive_ref[...]) * (1.0 / LEN)
 
     keys = k_ref[...].astype(jnp.float32) * SCORE_SCALE
     values_t = v_ref[...].astype(jnp.float32).T.astype(jnp.bfloat16)
@@ -400,10 +392,9 @@
                     part = jnp.sum(expo, axis=0, keepdims=True)
                     total = part if total is None else total + part
                     p_ref[head, rows, lanes] = expo.astype(jnp.bfloat16)
-                lse_ref[head, :, lanes] = jnp.where(
-                    alive_ref[:, lanes] > 0.0, peak + jnp.log(total), 1e30
-                )
-                o_ref[head : head + 1, lanes] = 1.0 / total
+                inverse = 1.0 / total
+                inverse_ref[head, :, lanes] = inverse * alive_ref[:, lanes]
+                o_ref[head : head + 1, lanes] = inverse
         mixed = dot_nn(values_t[head * 64 : head * 64 + 64, :], p_ref[head])
         o_ref[8 + head * 64 : 8 + head * 64 + 64, :] = mixed * o_ref[head : head + 1, :]
     a_ref[...] = o_ref[8:, :].T.astype(jnp.bfloat16)
@@ -417,7 +408,9 @@
         grid=(H // 2,),
         out_shape=[
             jax.ShapeDtypeStruct((TALL, D), jnp.bfloat16),
+            jax.ShapeDtypeStruct((H, LEN, TALL), jnp.bfloat16),
             jax.ShapeDtypeStruct((H, 1, TALL), jnp.float32),
+            jax.ShapeDtypeStruct((1, TALL), jnp.float32),
         ],
         in_specs=[
             SMEM_SPEC, SMEM_SPEC, tall, short, short,
@@ -425,12 +418,16 @@
             pl.BlockSpec((LEN, 1), lambda p: (0, 0)),
             pl.BlockSpec((2, 1, 512), lambda p: (p, 0, 0)),
         ],
-        out_specs=[tall, pl.BlockSpec((2, 1, TALL), lambda p: (p, 0, 0))],
+        out_specs=[
+            tall,
+            pl.BlockSpec((2, LEN, TALL), lambda p: (p, 0, 0)),
+            pl.BlockSpec((2, 1, TALL), lambda p: (p, 0, 0)),
+            pl.BlockSpec((1, TALL), lambda p: (0, 0)),
+        ],
         scratch_shapes=[
             pltpu.VMEM((LEN, TALL), jnp.float32),
             pltpu.VMEM((1, TALL), jnp.float32),
             pltpu.VMEM((2, 128, 384), jnp.float32),
-            pltpu.VMEM((2, LEN, TALL), jnp.bfloat16),
             pltpu.VMEM((136, TALL), jnp.float32),
         ],
         compiler_params=PARAMS,
@@ -440,56 +437,47 @@
 
 
 def mix_back_kernel(
-    length_ref, far_ref, q_ref, k_ref, v_ref, da_ref, a_ref, lse_ref, row_flags, col_flags, t_ref,
+    q_ref, k_ref, v_ref, da_ref, a_ref, p_ref, inverse_ref, dead_ref,
     dq_ref, dk_ref, dv_ref, table_ref,
-    mask_ref, alive_ref, tile_ref, p_ref, s_ref, near_ref, d_ref,
+    s_ref, near_ref, da_t, low_t, q_t, g_ref,
 ):
-    pair = pl.program_id(0)
-
-    @pl.when(pair == 0)
-    def _():
-        build_masks(length_ref[0], row_flags, col_flags, mask_ref, alive_ref)
-
     keys = k_ref[...].astype(jnp.float32) * SCORE_SCALE
     keys_t = keys.T.astype(jnp.bfloat16)
-    product = da_ref[...].astype(jnp.float32) * a_ref[...].astype(jnp.float32)
-    d_ref[...] = product.T
-    values = v_ref[...]
-    grads_k = []
-    grads_v = []
+    q_t[...] = q_ref[...].astype(jnp.float32).T.astype(jnp.bfloat16)
+    da_t[...] = da_ref[...].astype(jnp.float32).T
+    product = a_ref[...].astype(jnp.float32).T * da_t[...]
+    values = v_ref[...].astype(jnp.float32)
     near_ref[...] = jnp.zeros(near_ref.shape, jnp.float32)
     turn = (
         lax.broadcasted_iota(jnp.int32, (128, 128), 0)
         + lax.broadcasted_iota(jnp.int32, (128, 128), 1)
         == 127
     ).astype(jnp.float32)
+    deltas = []
     for head in range(2):
-        build_tiles(t_ref[head], tile_ref.at[head])
-        mine = head_lanes(keys.shape, head)
-        keys_own = jnp.where(mine, keys, 0.0).astype(jnp.bfloat16)
-        values_own = jnp.where(mine, values.astype(jnp.float32), 0.0).astype(jnp.bfloat16)
-        delta = jnp.sum(d_ref[head * 64 : head * 64 + 64, :], axis=0, keepdims=True)
+        rows = slice(head * 64, head * 64 + 64)
+        inverse = inverse_ref[head]
+        deltas.append(jnp.sum(product[rows, :], axis=0, keepdims=True) * inverse)
+        low_t[rows, :] = (da_t[rows, :] * inverse).astype(jnp.bfloat16)
+    for head in range(2):
+        own = slice(head * 64, head * 64 + 64)
+        values_own = jnp.where(head_lanes(values.shape, head), values, 0.0).astype(jnp.bfloat16)
+        delta = deltas[head]
         far_low = jnp.zeros((8, 128), jnp.float32)
         far_high = jnp.zeros((8, 128), jnp.float32)
         for chunk in range(4):
             at = chunk * HALF
-            scores = dot_nt(keys_own, q_ref[at : at + HALF, :])
-            pulls = dot_nt(values_own, da_ref[at : at + HALF, :])
+            pulls = dot_nn(values_own, low_t[:, at : at + HALF])
             for side in range(2):
                 lanes = slice(at + side * 128, at + side * 128 + 128)
-                log_total = lse_ref[head, :, lanes]
                 shift = delta[:, lanes]
+                query_block = (chunk % 2) * 2 + side
                 for key_block in range(4):
                     rows = slice(key_block * 128, key_block * 128 + 128)
                     cols = slice(side * 128, side * 128 + 128)
-                    query_block = (chunk % 2) * 2 + side
-                    block = scores[rows, cols] + position_bias(
-                        tile_ref.at[head], far_ref, pair * 2 + head, query_block, key_block
+                    grad = p_ref[head, rows, lanes].astype(jnp.float32) * (
+                        pulls[rows, cols] - shift
                     )
-                    block = jnp.where(mask_ref[rows, lanes] > 0.0, block, MASKED)
-                    prob = jnp.exp(block - log_total)
-                    p_ref[head, rows, lanes] = prob.astype(jnp.bfloat16)
-                    grad = prob * (pulls[rows, cols] - shift)
                     s_ref[head, rows, lanes] = grad.astype(jnp.bfloat16)
                     apart = query_block - key_block
                     if apart >= 2:
@@ -498,11 +486,9 @@
                         far_high = far_high + jnp.sum(grad.reshape(16, 8, 128), axis=0)
                     else:
                         near_ref[head, :, 128 * (apart + 1) : 128 * (apart + 2)] += grad
-        grads_v.append(dot_nn(p_ref[head], da_ref[...]))
-        grads_k.append(dot_nn(s_ref[head], q_ref[...]))
-        d_ref[head * 64 : head * 64 + 64, :] = dot_nn(
-            keys_t[head * 64 : head * 64 + 64, :], s_ref[head]
-        )
+        g_ref[own, :LEN] = dot_nt(low_t[own, :], p_ref[head])
+        g_ref[own, LEN:] = dot_nt(q_t[own, :], s_ref[head]) * SCORE_SCALE
+        da_t[own, :] = dot_nn(keys_t[own, :], s_ref[head])
         turned = jnp.dot(
             turn, near_ref[head], precision=lax.Precision.HIGHEST, preferred_element_type=jnp.float32
         )
@@ -510,60 +496,61 @@
         table_ref[head, :, :512] = jnp.sum(aligned, axis=0, keepdims=True)
         table_ref[head, :, 512:640] = jnp.sum(far_low, axis=0, keepdims=True)
         table_ref[head, :, 640:] = jnp.sum(far_high, axis=0, keepdims=True)
-    dead = (1.0 - alive_ref[...]) * (1.0 / LEN)
-    uniform = dot_nn(dead.astype(jnp.bfloat16), da_ref[...])
-    first = head_lanes((LEN, 128), 0)
-    dv_ref[...] = (jnp.where(first, grads_v[0], grads_v[1]) + uniform).astype(jnp.bfloat16)
-    dk_ref[...] = (jnp.where(first, grads_k[0], grads_k[1]) * SCORE_SCALE).astype(jnp.bfloat16)
-    dq_ref[...] = d_ref[...].T.astype(jnp.bfloat16)
-
-
-def mix_back(length, far, tvec, q, k, v, da, a, lse, row_flags, col_flags):
-    tall = pl.BlockSpec((TALL, 128), lambda p: (0, p))
-    short = pl.BlockSpec((LEN, 128), lambda p: (0, p))
+    uniform = dot_nn(dead_ref[...].astype(jnp.bfloat16), da_ref[...])
+    dv_ref[...] = (g_ref[:, :LEN].T + uniform).astype(jnp.bfloat16)
+    dk_ref[...] = g_ref[:, LEN:].T.astype(jnp.bfloat16)
+    dq_ref[...] = da_t[...].T.astype(jnp.bfloat16)
+
+
+def mix_back(first, q, k, v, da, a, p, inverse, dead):
+    tall = pl.BlockSpec((TALL, 128), lambda i: (0, i + first))
+    short = pl.BlockSpec((LEN, 128), lambda i: (0, i + first))
     return pl.pallas_call(
         mix_back_kernel,
-        grid=(H // 2,),
+        grid=(H // 4,),
         out_shape=[
-            jax.ShapeDtypeStruct((TALL, D), jnp.bfloat16),
-            jax.ShapeDtypeStruct((LEN, D), jnp.bfloat16),
-            jax.ShapeDtypeStruct((LEN, D), jnp.bfloat16),
-            jax.ShapeDtypeStruct((H, 1, 768), jnp.float32),
+            jax.ShapeDtypeStruct((TALL, D // 2), jnp.bfloat16),
+            jax.ShapeDtypeStruct((LEN, D // 2), jnp.bfloat16),
+            jax.ShapeDtypeStruct((LEN, D // 2), jnp.bfloat16),
+            jax.ShapeDtypeStruct((H // 2, 1, 768), jnp.float32),
         ],
         in_specs=[
-            SMEM_SPEC, SMEM_SPEC, tall, short, short, tall, tall,
-            pl.BlockSpec((2, 1, TALL), lambda p: (p, 0, 0)),
-            pl.BlockSpec((1, LEN), lambda p: (0, 0)),
-            pl.BlockSpec((LEN, 1), lambda p: (0, 0)),
-            pl.BlockSpec((2, 1, 512), lambda p: (p, 0, 0)),
+            tall, short, short, tall, tall,
+            pl.BlockSpec((2, LEN, TALL), lambda i: (i + first, 0, 0)),
+            pl.BlockSpec((2, 1, TALL), lambda i: (i + first, 0, 0)),
+            pl.BlockSpec((1, TALL), lambda i: (0, 0)),
         ],
-        out_specs=[tall, short, short, pl.BlockSpec((2, 1, 768), lambda p: (p, 0, 0))],
+        out_specs=[
+            pl.BlockSpec((TALL, 128), lambda i: (0, i)),
+            pl.BlockSpec((LEN, 128), lambda i: (0, i)),
+            pl.BlockSpec((LEN, 128), lambda i: (0, i)),
+            pl.BlockSpec((2, 1, 768), lambda i: (i, 0, 0)),
+        ],
         scratch_shapes=[
-            pltpu.VMEM((LEN, TALL), jnp.float32),
-            pltpu.VMEM((1, TALL), jnp.float32),
-            pltpu.VMEM((2, 128, 384), jnp.float32),
-            pltpu.VMEM((2, LEN, TALL), jnp.bfloat16),
             pltpu.VMEM((2, LEN, TALL), jnp.bfloat16),
             pltpu.VMEM((2, 128, 512), jnp.float32),
             pltpu.VMEM((128, TALL), jnp.float32),
+            pltpu.VMEM((128, TALL), jnp.bfloat16),
+            pltpu.VMEM((128, TALL), jnp.bfloat16),
+            pltpu.VMEM((128, TALL), jnp.float32),
         ],
         compiler_params=PARAMS,
-        cost_estimate=pl.CostEstimate(flops=16000000000, bytes_accessed=12000000, transcendentals=6300000),
+        cost_estimate=pl.CostEstimate(flops=8000000000, bytes_accessed=16000000, transcendentals=0),
         name="mix_back",
-    )(length, far, q, k, v, da, a, lse, row_flags, col_flags, tvec)
+    )(q, k, v, da, a, p, inverse, dead)
 
 
 GELU_SCALE = 0.7978845608028654
 GELU_CUBE = 0.044715
 
 
-def feed_kernel(place_ref, small_ref, hidden_bias_ref, mix_any, hidden_any, attn_any, *refs):
-    pieces = refs[:10]
+def feed_kernel(plan, place_ref, small_ref, hidden_bias_ref, mix_any, hidden_any, attn_any, *refs):
+    pieces = refs[:-20]
     (
-        resid_out, summed_out, pre_out, next_out, low_out,
+        resid_out, summed_out, pre_out, normed_out, next_out, low_out,
         mix_ref, hidden_ref, wo_ref, inner_ref, outer_ref, resid_ref, total_ref, normed_ref,
         pre_ref, next_ref, low_ref, sems, load_sems, store_sems,
-    ) = refs[10:]
+    ) = refs[-20:]
     loads = [
         pltpu.make_async_copy(mix_any, mix_ref, load_sems.at[0]),
         pltpu.make_async_copy(attn_any.at[3], wo_ref, load_sems.at[1]),
@@ -571,7 +558,7 @@
     ]
     for load in loads:
         load.start()
-    fetches = start_fetch(("inner", "outer"), place_ref, pieces, (inner_ref, outer_ref), sems)
+    fetches = start_fetch(("inner", "outer"), plan, place_ref, pieces, (inner_ref, outer_ref), sems)
     for load in loads:
         load.wait()
     for row in range(0, TALL, HALF):
@@ -582,26 +569,26 @@
         normed = unit * small_ref[3:4, :] + small_ref[4:5, :]
         normed_ref[rows, :] = normed.astype(jnp.bfloat16)
         total_ref[rows, :] = normed + small_ref[5:6, :]
-    stores = [pltpu.make_async_copy(resid_ref, resid_out, store_sems.at[0])]
-    stores[0].start()
+    stores = [
+        pltpu.make_async_copy(resid_ref, resid_out, store_sems.at[0]),
+        pltpu.make_async_copy(normed_ref, normed_out, store_sems.at[8]),
+    ]
+    for store in stores:
+        store.start()
     for fetch in fetches:
         fetch.wait()
     for chunk in range(4):
-        cols = slice(chunk * D, chunk * D + D)
-
-        def body(step, carry):
-            rows = pl.ds(pl.multiple_of(step * HALF, HALF), HALF)
-            pre = dot_nn(normed_ref[rows, :], inner_ref[:, cols]) + hidden_bias_ref[:, cols]
-            pre_ref[rows, cols] = pre.astype(jnp.bfloat16)
+        for row in range(0, TALL, HALF):
+            rows = slice(row, row + HALF)
+            pre = dot_nn(normed_ref[rows, :], inner_ref[chunk]) + hidden_bias_ref[
+                :, chunk * D : chunk * D + D
+            ]
+            pre_ref[chunk, rows, :] = pre.astype(jnp.bfloat16)
             tanh = jnp.tanh(GELU_SCALE * (pre + GELU_CUBE * (pre * pre * pre)))
             active = (pre * (0.5 + 0.5 * tanh)).astype(jnp.bfloat16)
-            total_ref[rows, :] += dot_nn(active, outer_ref[cols, :])
-            return carry
-
-        for step in range(4):
-            body(step, 0)
+            total_ref[rows, :] += dot_nn(active, outer_ref[chunk])
         store = pltpu.make_async_copy(
-            pre_ref.at[:, cols], pre_out.at[:, cols], store_sems.at[1 + chunk]
+            pre_ref.at[chunk], pre_out.at[chunk], store_sems.at[1 + chunk]
         )
         store.start()
         stores.append(store)
@@ -622,33 +609,35 @@
         store.wait()
 
 
-def feed(place, small, hidden_bias, mixed, hidden, attn, pieces):
+def feed(place, small, hidden_bias, mixed, hidden, attn, group):
+    plan, pieces = group
     return pl.pallas_call(
-        feed_kernel,
+        partial(feed_kernel, plan),
         out_shape=[
             jax.ShapeDtypeStruct((TALL, D), jnp.float32),
             jax.ShapeDtypeStruct((TALL, D), jnp.float32),
-            jax.ShapeDtypeStruct((TALL, FF), jnp.bfloat16),
+            jax.ShapeDtypeStruct((4, TALL, D), jnp.bfloat16),
+            jax.ShapeDtypeStruct((TALL, D), jnp.bfloat16),
             jax.ShapeDtypeStruct((TALL, D), jnp.float32),
             jax.ShapeDtypeStruct((TALL, D), jnp.bfloat16),
         ],
-        in_specs=[SMEM_SPEC, VMEM_SPEC, VMEM_SPEC] + [ANY_SPEC] * 13,
-        out_specs=[ANY_SPEC] * 5,
+        in_specs=[SMEM_SPEC, VMEM_SPEC, VMEM_SPEC] + [ANY_SPEC] * (3 + len(pieces)),
+        out_specs=[ANY_SPEC] * 6,
         scratch_shapes=[
             pltpu.VMEM((TALL, D), jnp.bfloat16),
             pltpu.VMEM((TALL, D), jnp.float32),
             pltpu.VMEM((D, D), jnp.bfloat16),
-            pltpu.VMEM((D, FF), jnp.bfloat16),
-            pltpu.VMEM((FF, D), jnp.bfloat16),
+            pltpu.VMEM((4, D, D), jnp.bfloat16),
+            pltpu.VMEM((4, D, D), jnp.bfloat16),
             pltpu.VMEM((TALL, D), jnp.float32),
             pltpu.VMEM((TALL, D), jnp.float32),
             pltpu.VMEM((TALL, D), jnp.bfloat16),
-            pltpu.VMEM((TALL, FF), jnp.bfloat16),
+            pltpu.VMEM((4, TALL, D), jnp.bfloat16),
             pltpu.VMEM((TALL, D), jnp.float32),
             pltpu.VMEM((TALL, D), jnp.bfloat16),
             pltpu.SemaphoreType.DMA((64,)),
             pltpu.SemaphoreType.DMA((3,)),
-            pltpu.SemaphoreType.DMA((8,)),
+            pltpu.SemaphoreType.DMA((9,)),
         ],
         compiler_params=PARAMS,
         cost_estimate=pl.CostEstimate(flops=2 * TALL * D * (D + 2 * FF), bytes_accessed=40000000, transcendentals=3000000),
@@ -656,29 +645,37 @@
     )(place, small, hidden_bias, mixed, hidden, attn, *pieces)
 
 
-def feed_back_kernel(place_ref, small_ref, grad_any, summed_any, resid_any, pre_any, mix_any, attn_any, *refs):
-    pieces = refs[:10]
+def feed_back_kernel(
+    plan, place_ref, small_ref, grad_c_any, grad_q_any, summed_any, normed_any, resid_any, pre_any,
+    mix_any, attn_any, *refs
+):
+    pieces = refs[:-26]
     (
         dresid_out, dmix_out, dwo_out, keep_out, send_out, vec_ref, dhidden_ref,
         grad_ref, summed_ref, resid_ref, pre_ref, mix_ref, wo_ref, inner_ref, outer_ref,
-        total_ref, branch_ref, normed_ref, active_ref, dpre_ref, dinner_ref, douter_ref,
+        branch_ref, normed_ref, active_ref, dpre_ref, dinner_ref, douter_ref,
         dwo_ref, sems, load_sems, store_sems, block_sems,
-    ) = refs[10:]
-    proj_ref = branch_ref
-    dmix_ref = active_ref
+    ) = refs[-26:]
     x, c, z, y = (place_ref[index] for index in range(4))
+    total_ref = summed_ref
     load = [
         pltpu.make_async_copy(source, target, load_sems.at[index])
         for index, (source, target) in enumerate(
             (
-                (grad_any, grad_ref), (summed_any, summed_ref), (resid_any, resid_ref),
-                (pre_any, pre_ref), (mix_any, mix_ref), (attn_any.at[3], wo_ref),
+                (summed_any, summed_ref),
+                (grad_c_any, grad_ref.at[:LEN, :]),
+                (grad_q_any, grad_ref.at[LEN:, :]),
+                (pre_any, pre_ref),
+                (normed_any, normed_ref),
+                (resid_any, resid_ref),
+                (mix_any, mix_ref),
+                (attn_any.at[3], wo_ref),
             )
         )
     ]
     for copy in load[:3]:
         copy.start()
-    fetches = start_fetch(("inner", "outer"), place_ref, pieces, (inner_ref, outer_ref), sems)
+    fetches = start_fetch(("inner", "outer"), plan, place_ref, pieces, (inner_ref, outer_ref), sems)
     for copy in load[3:]:
         copy.start()
     for copy in load[:3]:
@@ -697,8 +694,6 @@
         low = back.astype(jnp.bfloat16)
         branch_ref[rows, :] = low
         bias_two_grad += jnp.sum(low.astype(jnp.float32), axis=0, keepdims=True)
-        unit, scale = norm_parts(resid_ref[rows, :])
-        normed_ref[rows, :] = (unit * small_ref[3:4, :] + small_ref[4:5, :]).astype(jnp.bfloat16)
     vec_ref[5:6, :] = bias_two_grad
     vec_ref[6:7, :] = gain_two_grad
     vec_ref[7:8, :] = shift_two_grad
@@ -706,28 +701,19 @@
         copy.wait()
     blocks = []
 
-    def place_block(core, source, target_index):
-        sem = block_sems.at[len(blocks)]
-        keep = pltpu.make_async_copy(source, keep_out.at[target_index], sem)
-        send = pltpu.make_async_copy(source, send_out.at[target_index], sem)
-
-        @pl.when(c == core)
-        def _():
-            keep.start()
-
-        @pl.when(c != core)
-        def _():
-            send.start()
-
-        blocks.append(keep)
-
-    for chunk in range(4):
-        cols = slice(chunk * D, chunk * D + D)
+    def store(source, target):
+        copy = pltpu.make_async_copy(source, target, block_sems.at[len(blocks)])
+        copy.start()
+        blocks.append(copy)
+
+    for step in range(4):
+        apart, side = 1 - step // 2, step % 2
+        chunk = side * 2 + (c ^ apart)
         bias_grad = jnp.zeros((1, D), jnp.float32)
         for row in range(0, TALL, HALF):
             rows = slice(row, row + HALF)
-            pull = dot_nt(branch_ref[rows, :], outer_ref[cols, :])
-            pre = pre_ref[rows, cols].astype(jnp.float32)
+            pull = dot_nt(branch_ref[rows, :], outer_ref[chunk])
+            pre = pre_ref[chunk, rows, :].astype(jnp.float32)
             square = pre * pre
             tanh = jnp.tanh(GELU_SCALE * pre * (1.0 + GELU_CUBE * square))
             half = 0.5 + 0.5 * tanh
@@ -738,24 +724,22 @@
             dpre = (pull * slope).astype(jnp.bfloat16)
             dpre_ref[rows, :] = dpre
             bias_grad += jnp.sum(dpre.astype(jnp.float32), axis=0, keepdims=True)
-            total_ref[rows, :] += dot_nt(dpre, inner_ref[:, cols])
-        dhidden_ref[:, cols] = bias_grad
-        douter_ref[cols, :] = dot_tn(active_ref[...], branch_ref[...]).astype(jnp.bfloat16)
-        dinner_ref[:, cols] = dot_tn(normed_ref[...], dpre_ref[...]).astype(jnp.bfloat16)
-        for owner in range(8):
-            place_block(
-                chunk % 2,
-                dinner_ref.at[owner * ROWS : owner * ROWS + ROWS, cols],
-                ((chunk // 2) ^ x, (owner % 2) ^ y, ((owner // 2) - z) & 3, 0),
-            )
-        for strip in range(8):
-            quarter = strip % 4
-            start = chunk * D + strip * ROWS
-            place_block(
-                quarter % 2,
-                douter_ref.at[start : start + ROWS, :],
-                ((quarter // 2) ^ x, (strip // 4) ^ y, (chunk - z) & 3, 1),
-            )
+            total_ref[rows, :] += dot_nt(dpre, inner_ref[chunk])
+        dhidden_ref[chunk] = bias_grad
+        douter_ref[step] = (
+            dot_tn(active_ref[...], branch_ref[...]).astype(jnp.bfloat16).reshape(2, 2, 2, ROWS, D)
+        )
+        for y_block in range(2):
+            for x_block in range(2):
+                spot = (y_block ^ y, x_block ^ x, chunk, 1)
+                store(douter_ref.at[step, y_block, x_block, c], keep_out.at[spot])
+                store(douter_ref.at[step, y_block, x_block, 1 - c], send_out.at[spot])
+        dinner_ref[step] = (
+            dot_tn(normed_ref[...], dpre_ref[...]).astype(jnp.bfloat16).reshape(4, 2, ROWS, D)
+        )
+        target = send_out if apart else keep_out
+        for y_block in range(2):
+            store(dinner_ref.at[step, :, y_block], target.at[y_block ^ y, side ^ x, :, 0])
     gain_one_grad = jnp.zeros((1, D), jnp.float32)
     shift_one_grad = jnp.zeros((1, D), jnp.float32)
     bias_o_grad = jnp.zeros((1, D), jnp.float32)
@@ -768,30 +752,32 @@
         back = norm_back(unit, scale, grad, small_ref[3:4, :])
         grad_ref[rows, :] = back
         low = back.astype(jnp.bfloat16)
-        proj_ref[rows, :] = low
+        branch_ref[rows, :] = low
         bias_o_grad += jnp.sum(low.astype(jnp.float32), axis=0, keepdims=True)
-        dmix_ref[rows, :] = dot_nt(low, wo_ref[...]).astype(jnp.bfloat16)
-    dwo_ref[...] = dot_tn(mix_ref[...], proj_ref[...]).astype(jnp.bfloat16)
+        active_ref[rows, :] = dot_nt(low, wo_ref[...]).astype(jnp.bfloat16)
+    stores = [
+        pltpu.make_async_copy(source, target, store_sems.at[index])
+        for index, (source, target) in enumerate(
+            ((grad_ref, dresid_out), (active_ref, dmix_out), (dwo_ref, dwo_out))
+        )
+    ]
+    stores[0].start()
+    stores[1].start()
+    dwo_ref[...] = dot_tn(mix_ref[...], branch_ref[...]).astype(jnp.bfloat16)
+    stores[2].start()
     vec_ref[0:2, :] = jnp.zeros((2, D), jnp.float32)
     vec_ref[2:3, :] = bias_o_grad
     vec_ref[3:4, :] = gain_one_grad
     vec_ref[4:5, :] = shift_one_grad
-    stores = [
-        pltpu.make_async_copy(source, target, store_sems.at[index])
-        for index, (source, target) in enumerate(
-            ((grad_ref, dresid_out), (dmix_ref, dmix_out), (dwo_ref, dwo_out))
-        )
-    ]
-    for store in stores:
-        store.start()
     for copy in blocks + stores:
         copy.wait()
 
 
-def feed_back(place, small, grad, summed, resid, pre, mixed, attn, pieces):
+def feed_back(place, small, grads, summed, normed, resid, pre, mixed, attn, group):
+    plan, pieces = group
     blocks = jax.ShapeDtypeStruct((2, 2, 4, 2, ROWS, D), jnp.bfloat16)
     return pl.pallas_call(
-        feed_back_kernel,
+        partial(feed_back_kernel, plan),
         out_shape=[
             jax.ShapeDtypeStruct((TALL, D), jnp.float32),
             jax.ShapeDtypeStruct((TALL, D), jnp.bfloat16),
@@ -799,114 +785,130 @@
             blocks,
             blocks,
             jax.ShapeDtypeStruct((8, D), jnp.float32),
-            jax.ShapeDtypeStruct((1, FF), jnp.float32),
+            jax.ShapeDtypeStruct((4, 1, D), jnp.float32),
         ],
-        in_specs=[SMEM_SPEC, VMEM_SPEC] + [ANY_SPEC] * 16,
+        in_specs=[SMEM_SPEC, VMEM_SPEC] + [ANY_SPEC] * (8 + len(pieces)),
         out_specs=[ANY_SPEC] * 5 + [VMEM_SPEC] * 2,
         scratch_shapes=[
             pltpu.VMEM((TALL, D), jnp.float32),
             pltpu.VMEM((TALL, D), jnp.float32),
             pltpu.VMEM((TALL, D), jnp.float32),
-            pltpu.VMEM((TALL, FF), jnp.bfloat16),
+            pltpu.VMEM((4, TALL, D), jnp.bfloat16),
             pltpu.VMEM((TALL, D), jnp.bfloat16),
             pltpu.VMEM((D, D), jnp.bfloat16),
-            pltpu.VMEM((D, FF), jnp.bfloat16),
-            pltpu.VMEM((FF, D), jnp.bfloat16),
-            pltpu.VMEM((TALL, D), jnp.float32),
+            pltpu.VMEM((4, D, D), jnp.bfloat16),
+            pltpu.VMEM((4, D, D), jnp.bfloat16),
             pltpu.VMEM((TALL, D), jnp.bfloat16),
             pltpu.VMEM((TALL, D), jnp.bfloat16),
             pltpu.VMEM((TALL, D), jnp.bfloat16),
             pltpu.VMEM((TALL, D), jnp.bfloat16),
-            pltpu.VMEM((D, FF), jnp.bfloat16),
-            pltpu.VMEM((FF, D), jnp.bfloat16),
+            pltpu.VMEM((4, 4, 2, ROWS, D), jnp.bfloat16),
+            pltpu.VMEM((4, 2, 2, 2, ROWS, D), jnp.bfloat16),
             pltpu.VMEM((D, D), jnp.bfloat16),
             pltpu.SemaphoreType.DMA((64,)),
-            pltpu.SemaphoreType.DMA((6,)),
+            pltpu.SemaphoreType.DMA((8,)),
             pltpu.SemaphoreType.DMA((3,)),
-            pltpu.SemaphoreType.DMA((64,)),
+            pltpu.SemaphoreType.DMA((40,)),
         ],
         compiler_params=PARAMS,
         cost_estimate=pl.CostEstimate(flops=4 * TALL * D * (D + 2 * FF), bytes_accessed=60000000, transcendentals=3000000),
         name="feed_back",
-    )(place, small, grad, summed, resid, pre, mixed, attn, *pieces)
-
-
-def weight_back_kernel(place_ref, low_ref, dq_ref, dk_ref, dv_ref, dwo_ref, keep_out, send_out, vec_ref, grads_ref, sems):
+    )(place, small, *grads, summed, normed, resid, pre, mixed, attn, *pieces)
+
+
+def weight_back_kernel(
+    place_ref, low_ref, dq_a, dk_a, dv_a, dq_b, dk_b, dv_b, dwo_ref, keep_out, send_out, vec_ref, grads_ref, sems
+):
     x, c, z, y = (place_ref[index] for index in range(4))
+    grads_ref[3] = dwo_ref[...].reshape(4, 2, ROWS, D)
+    for matrix, halves in enumerate(((dq_a, dq_b), (dk_a, dk_b), (dv_a, dv_b))):
+        for half, grad in enumerate(halves):
+            cols = slice(half * 384, half * 384 + 384)
+            grads_ref[matrix, :, :, :, cols] = (
+                dot_tn(low_ref[: grad.shape[0], :], grad[...])
+                .astype(jnp.bfloat16)
+                .reshape(4, 2, ROWS, 384)
+            )
+            if matrix != 1:
+                vec_ref[matrix // 2 : matrix // 2 + 1, cols] = jnp.sum(
+                    grad[...].astype(jnp.float32), axis=0, keepdims=True
+                )
     blocks = []
-
-    def place_matrix(source, quarter):
-        for owner in range(8):
-            index = ((quarter // 2) ^ x, (owner % 2) ^ y, ((owner // 2) - z) & 3, 0)
-            part = source.at[owner * ROWS : owner * ROWS + ROWS, :]
-            sem = sems.at[len(blocks)]
-            keep = pltpu.make_async_copy(part, keep_out.at[index], sem)
-            send = pltpu.make_async_copy(part, send_out.at[index], sem)
-
-            @pl.when(c == quarter % 2)
-            def _():
-                keep.start()
-
-            @pl.when(c != quarter % 2)
-            def _():
-                send.start()
-
-            blocks.append(keep)
-
-    place_matrix(dwo_ref, 3)
-    grads_ref[0] = dot_tn(low_ref[...], dq_ref[...]).astype(jnp.bfloat16)
-    place_matrix(grads_ref.at[0], 0)
-    grads_ref[1] = dot_tn(low_ref[:LEN, :], dk_ref[...]).astype(jnp.bfloat16)
-    place_matrix(grads_ref.at[1], 1)
-    grads_ref[2] = dot_tn(low_ref[:LEN, :], dv_ref[...]).astype(jnp.bfloat16)
-    place_matrix(grads_ref.at[2], 2)
-    vec_ref[0:1, :] = jnp.sum(dq_ref[...].astype(jnp.float32), axis=0, keepdims=True)
-    vec_ref[1:2, :] = jnp.sum(dv_ref[...].astype(jnp.float32), axis=0, keepdims=True)
+    for apart, target in ((1, send_out), (0, keep_out)):
+        for side in range(2):
+            for y_block in range(2):
+                copy = pltpu.make_async_copy(
+                    grads_ref.at[side * 2 + (c ^ apart), :, y_block],
+                    target.at[y_block ^ y, side ^ x, :, 0],
+                    sems.at[len(blocks)],
+                )
+                copy.start()
+                blocks.append(copy)
     for block in blocks:
         block.wait()
 
 
-def weight_back(place, low, dq, dk, dv, dwo):
+def weight_back(place, low, first, second, dwo):
     blocks = jax.ShapeDtypeStruct((2, 2, 4, 1, ROWS, D), jnp.bfloat16)
     return pl.pallas_call(
         weight_back_kernel,
         out_shape=[blocks, blocks, jax.ShapeDtypeStruct((2, D), jnp.float32)],
-        in_specs=[SMEM_SPEC] + [VMEM_SPEC] * 5,
+        in_specs=[SMEM_SPEC] + [VMEM_SPEC] * 8,
         out_specs=[ANY_SPEC] * 2 + [VMEM_SPEC],
         scratch_shapes=[
-            pltpu.VMEM((3, D, D), jnp.bfloat16),
-            pltpu.SemaphoreType.DMA((32,)),
+            pltpu.VMEM((4, 4, 2, ROWS, D), jnp.bfloat16),
+            pltpu.SemaphoreType.DMA((8,)),
         ],
         compiler_params=PARAMS,
         cost_estimate=pl.CostEstimate(flops=2 * 2048 * D * D, bytes_accessed=12000000, transcendentals=0),
         name="weight_back",
-    )(place, low, dq, dk, dv, dwo)
-
-
-def input_back_kernel(dq_ref, dk_ref, dv_ref, w_ref, dresid_ref, first_ref, second_ref):
-    for row in range(0, LEN, HALF):
-        rows = slice(row, row + HALF)
-        first_ref[rows, :] = (
-            dresid_ref[rows, :]
-            + dot_nt(dq_ref[rows, :], w_ref[0])
-            + dot_nt(dk_ref[rows, :], w_ref[1])
-            + dot_nt(dv_ref[rows, :], w_ref[2])
-        )
-        rest = slice(LEN + row, LEN + row + HALF)
-        second_ref[rows, :] = dresid_ref[rest, :] + dot_nt(dq_ref[rest, :], w_ref[0])
-
-
-def input_back(dq, dk, dv, attn, dresid):
+    )(place, low, *first, *second, dwo)
+
+
+def input_back_kernel(
+    dq_a, dk_a, dv_a, dq_b, dk_b, dv_b, w_ref, dresid_ref, first_ref, second_ref
+):
+    step = pl.program_id(0)
+    total = (
+        dresid_ref[...]
+        + dot_nt(dq_a[...], w_ref[0, :, :384])
+        + dot_nt(dq_b[...], w_ref[0, :, 384:])
+    )
+
+    @pl.when(step < 2)
+    def _():
+        content = total
+        for matrix, halves in ((1, (dk_a, dk_b)), (2, (dv_a, dv_b))):
+            for half, grad in enumerate(halves):
+                content += dot_nt(grad[...], w_ref[matrix, :, half * 384 : half * 384 + 384])
+        first_ref[...] = content
+
+    @pl.when(step >= 2)
+    def _():
+        second_ref[...] = total
+
+
+def input_back(first, second, attn, dresid):
     half = jax.ShapeDtypeStruct((LEN, D), jnp.float32)
+    tall = pl.BlockSpec((HALF, D // 2), lambda i: (i, 0))
+    short = pl.BlockSpec((HALF, D // 2), lambda i: (jnp.minimum(i, 1), 0))
     return pl.pallas_call(
         input_back_kernel,
+        grid=(4,),
         out_shape=[half, half],
-        in_specs=[VMEM_SPEC] * 5,
-        out_specs=[VMEM_SPEC] * 2,
+        in_specs=[
+            tall, short, short, tall, short, short,
+            pl.BlockSpec((3, D, D), lambda i: (0, 0, 0)),
+            pl.BlockSpec((HALF, D), lambda i: (i, 0)),
+        ],
+        out_specs=[
+            pl.BlockSpec((HALF, D), lambda i: (jnp.minimum(i, 1), 0)),
+            pl.BlockSpec((HALF, D), lambda i: (jnp.maximum(i - 2, 0), 0)),
+        ],
         compiler_params=PARAMS,
         cost_estimate=pl.CostEstimate(flops=2 * 2048 * D * D, bytes_accessed=16000000, transcendentals=0),
         name="input_back",
-    )(dq, dk, dv, attn, dresid)
+    )(*first, *second, attn, dresid)
 
 
 def bias_vectors(table):
@@ -935,6 +937,38 @@
     low = jnp.sum(sums[:, 0, 512:640], axis=1)
     high = jnp.sum(sums[:, 0, 640:], axis=1)
     return near.at[:, 15].add(low).at[:, 31].add(high)
+
+
+def adam_kernel(rate, master_ref, first_ref, second_ref, grad_ref, *refs):
+    master_out, first_out, second_out = refs[-3:]
+    grad = grad_ref[...].astype(jnp.float32).reshape(master_ref.shape)
+    new = adam_update(master_ref[...], first_ref[...], second_ref[...], grad, rate)
+    for target, value in zip((master_out, first_out, second_out), new):
+        target[...] = value
+
+
+def adam(kind, layer, rate, state, quarters, member, done):
+    if kind == "attn":
+        block = pl.BlockSpec((1, 1, ROWS, D), lambda i: (layer, i, 0, 0))
+    elif kind == "inner":
+        block = pl.BlockSpec((1, ROWS, D), lambda i: (layer, 0, i))
+    else:
+        block = pl.BlockSpec((1, ROWS, D), lambda i: (layer, i, 0))
+    held = done or ()
+    return pl.pallas_call(
+        partial(adam_kernel, rate),
+        grid=(4,),
+        out_shape=[jax.ShapeDtypeStruct(array.shape, jnp.float32) for array in state],
+        in_specs=[block] * 3
+        + [pl.BlockSpec((1, 1, ROWS, D), lambda i: (i, member, 0, 0))]
+        + [ANY_SPEC] * len(held),
+        out_specs=[block] * 3,
+        input_output_aliases={4 + index: index for index in range(len(held))},
+        compiler_params=PARAMS,
+        cost_estimate=pl.CostEstimate(flops=5000000, bytes_accessed=8000000, transcendentals=0),
+        name="adam",
+    )(*state, quarters, *held)
+
 
 def fetch_forward(shards):
     low = tuple(shard.astype(jnp.bfloat16) for shard in shards)
@@ -1243,37 +1277,67 @@
     )
 
 
-def own_quarter(kind, shard, quarter):
+def quarter_of(kind, shard, quarter):
     if kind == "attn":
-        part = lax.dynamic_index_in_dim(shard, quarter, 0, keepdims=False)
-    elif kind == "inner":
-        part = lax.dynamic_slice_in_dim(shard, quarter * D, D, 1)
-    else:
-        part = lax.dynamic_slice_in_dim(shard, quarter * ROWS, ROWS, 0)
-    return part.astype(jnp.bfloat16)
-
-
-def gather_group(kinds, shards, place):
-    quarter = place[0] * 2 + place[1]
-    own = jnp.stack([own_quarter(kind, shard, quarter) for kind, shard in zip(kinds, shards)])
-    return spread_blocks(own)
+        return lax.dynamic_index_in_dim(shard, quarter, 0, keepdims=False)
+    if kind == "inner":
+        return lax.dynamic_slice_in_dim(shard, quarter * D, D, 1)
+    return lax.dynamic_slice_in_dim(shard, quarter * ROWS, ROWS, 0)
+
+
+def after(value, *others):
+    return lax.optimization_barrier((value, others))[0]
+
+
+def own_blocks(kinds, shards, place, side):
+    quarter = (place[0] ^ side) * 2 + place[1]
+    return jnp.stack([quarter_of(kind, shard, quarter) for kind, shard in zip(kinds, shards)])
+
+
+def gather_group(count, shards, plane, column, sides, corners, mine, theirs):
+    plan = []
+    for core, arrays in enumerate((mine, theirs)):
+        base = core * len(mine)
+        for member in range(count):
+            array, first = plane
+            plan += [
+                (base + array, first + side * count + member, side, 1, core, 0, member)
+                for side in range(2)
+            ]
+            for apart in (1, 2, 3):
+                index = (apart - 1) * count + member
+                array, first = column
+                plan.append((base + array, first + index, 0, 0, core, apart, member))
+                for dx, dy, (array, first) in ((1, 0, sides[0]), (0, 1, sides[1])):
+                    plan.append((base + array, first + index, dx, dy, core, apart, member))
+                skipped = 0
+                for array, first, held in corners:
+                    if skipped <= index < skipped + held:
+                        plan.append(
+                            (base + array, first + index - skipped, 1, 1, core, apart, member)
+                        )
+                    skipped += held
+    return (tuple(plan), tuple(shards) + tuple(mine) + tuple(theirs))
 
 
 def gather_small(shard, place):
     z, y = place[2], place[3]
-    column = jnp.stack([shift_z(shard, step) for step in (3, 2, 1)] + [shard])
-    other = swap_y(column)
-    pairs = jnp.where(y == 0, jnp.stack([column, other], 1), jnp.stack([other, column], 1))
-    twice = jnp.concatenate([pairs, pairs])
-    whole = lax.dynamic_slice_in_dim(twice, 3 - z, 4, 0)
-    return whole.transpose(2, 0, 1, 3).reshape(shard.shape[0], -1)
+    pair = jnp.stack([shard, swap_z(shard, 1)])
+    blocks = jnp.concatenate([pair, swap_z(pair, 2)])
+    low, high = z % 2, z // 2
+    blocks = jnp.where(low == 0, blocks, blocks[jnp.array([1, 0, 3, 2])])
+    blocks = jnp.where(high == 0, blocks, blocks[jnp.array([2, 3, 0, 1])])
+    other = swap_y(blocks)
+    pairs = jnp.where(y == 0, jnp.stack([blocks, other], 1), jnp.stack([other, blocks], 1))
+    return pairs.transpose(2, 0, 1, 3).reshape(shard.shape[0], -1)
 
 
 def sum_small(value):
     value = value + swap_core(value)
     value = value + swap_x(value)
     value = value + swap_y(value)
-    return value + shift_z(value, 1) + shift_z(value, 2) + shift_z(value, 3)
+    value = value + swap_z(value, 1)
+    return value + swap_z(value, 2)
 
 
 def add_low(*values):
@@ -1283,18 +1347,44 @@
     return total.astype(jnp.bfloat16)
 
 
-def reduce_blocks(keep, send):
-    both = add_low(keep, swap_core(send))
-    corner = both[1, 1]
-    by_x = swap_x(corner[:2])
-    by_y = swap_y(corner[2:])
-    for_y = jnp.concatenate([add_low(both[0, 1, :2], by_x), both[0, 1, 2:]])
-    for_x = jnp.concatenate([both[1, 0, :2], add_low(both[1, 0, 2:], by_y)])
-    column = add_low(both[0, 0], swap_x(for_x), swap_y(for_y))
-    total = column[0].astype(jnp.float32)
-    for step in (1, 2, 3):
-        total = total + shift_z(column[step], step).astype(jnp.float32)
-    return total.astype(jnp.bfloat16)
+def reduce_corners(keep, get):
+    corner = add_low(keep[1, 1], get[1, 1])
+    return (swap_x(corner[:2]), swap_y(corner[2:]))
+
+
+def reduce_sides(keep, get, corners):
+    by_x, by_y = corners
+    for_y = jnp.concatenate([add_low(keep[1, 0, :2], get[1, 0, :2], by_x), add_low(keep[1, 0, 2:], get[1, 0, 2:])])
+    for_x = jnp.concatenate([add_low(keep[0, 1, :2], get[0, 1, :2]), add_low(keep[0, 1, 2:], get[0, 1, 2:], by_y)])
+    return (swap_x(for_x), swap_y(for_y))
+
+
+def reduce_column(keep, get, sides):
+    return add_low(keep[0, 0], get[0, 0], *sides)
+
+
+def at_z(column, place, apart):
+    return lax.dynamic_index_in_dim(column, place[2] ^ apart, 0, keepdims=False)
+
+
+def reduce_far(column, place):
+    return swap_z(jnp.stack([at_z(column, place, 2), at_z(column, place, 3)]), 2)
+
+
+def reduce_near(column, far, place):
+    return swap_z(add_low(at_z(column, place, 1), far[1]), 1)
+
+
+def reduce_total(column, far, near, place):
+    return add_low(at_z(column, place, 0), far[0], near)
+
+
+def reduce_direct(column, place):
+    return tuple(swap_z(at_z(column, place, apart), apart) for apart in (1, 2, 3))
+
+
+def direct_total(column, shifts, place):
+    return add_low(at_z(column, place, 0), *shifts)
 
 
 def share_quarters(own, place):
@@ -1304,15 +1394,6 @@
     cores = jnp.where(c == 0, jnp.stack([pair, other], 1), jnp.stack([other, pair], 1))
     sides = jnp.where(x == 0, cores, cores[::-1])
     return sides.reshape((4,) + own.shape)
-
-
-def shard_grad(kind, quarters):
-    four = quarters.astype(jnp.float32)
-    if kind == "attn":
-        return four
-    if kind == "inner":
-        return four.transpose(1, 0, 2).reshape(ROWS, FF)
-    return four.reshape(4 * ROWS, D)
 
 
 def small_parts(vectors):
@@ -1347,76 +1428,190 @@
     place_parts = my_place()
     place = jnp.stack(place_parts).astype(jnp.int32)
     small_all = gather_small(small_master.astype(jnp.bfloat16), place_parts)
-    attn_pieces = []
-    feed_pieces = []
-    for layer in range(LAYERS):
-        attn_pieces.append(gather_group(("attn",), (attn_master[layer],), place_parts))
-        feed_pieces.append(
-            gather_group(
-                ("inner", "outer"), (inner_master[layer], outer_master[layer]), place_parts
-            )
-        )
+    attn_kinds, feed_kinds = ("attn",), ("inner", "outer")
+    attn_low = [attn_master[layer].astype(jnp.bfloat16) for layer in range(LAYERS)]
+    feed_low = [
+        (inner_master[layer].astype(jnp.bfloat16), outer_master[layer].astype(jnp.bfloat16))
+        for layer in range(LAYERS)
+    ]
+    own_a0, own_a1 = (own_blocks(attn_kinds, (w,), place_parts, 0) for w in attn_low)
+    own_f0, own_f1 = (own_blocks(feed_kinds, w, place_parts, 0) for w in feed_low)
+    oth_a0, oth_a1 = (own_blocks(attn_kinds, (w,), place_parts, 1) for w in attn_low)
+    oth_f0, oth_f1 = (own_blocks(feed_kinds, w, place_parts, 1) for w in feed_low)
+    near_a0 = swap_z(own_a0, 1)
+    far_a0 = swap_z(jnp.concatenate([own_a0, near_a0]), 2)
+    plane_a0 = swap_y(jnp.concatenate([own_a0, oth_a0]))
+    near_f0 = swap_z(after(own_f0, near_a0), 1)
+    plane_f0 = swap_y(after(jnp.concatenate([own_f0, oth_f0]), plane_a0))
+    col_a0 = jnp.concatenate([near_a0, far_a0])
+    x0 = swap_x(col_a0)
+    y0 = swap_y(after(col_a0, plane_a0))
+    far_f0 = swap_z(jnp.concatenate([own_f0, near_f0]), 2)
+    far_f0_in = after(far_f0, x0, y0)
+    near_a1 = swap_z(after(own_a1, near_f0), 1)
+    near_f1 = swap_z(after(own_f1, near_a1), 1)
+    mine_0 = jnp.concatenate([plane_a0, col_a0, x0, y0])
+    theirs_0 = swap_core(after(mine_0, plane_f0))
+    col_f0 = jnp.concatenate([near_f0, far_f0_in])
+    x1 = swap_x(jnp.concatenate([col_f0, y0[:2]]))
+    y1 = swap_y(jnp.concatenate([col_f0, x0[2:]]))
+    far_a1 = swap_z(after(jnp.concatenate([own_a1, near_a1]), far_f0), 2)
+    col_a1 = jnp.concatenate([near_a1, far_a1])
+    mine_p0 = jnp.concatenate([plane_f0, col_f0])
+    theirs_p0 = swap_core(mine_p0)
+    mine_1 = jnp.concatenate([x1, y1])
+    theirs_1 = swap_core(mine_1)
+    group_a0 = gather_group(
+        1, (attn_low[0],), (0, 0), (0, 2), ((0, 5), (0, 8)), ((1, 6, 2), (1, 14, 1)),
+        (mine_0, mine_1), (theirs_0, theirs_1),
+    )
+    x2 = swap_x(jnp.concatenate([after(col_a1, x1, y1), y1[:4]]))
+    y2 = swap_y(jnp.concatenate([after(col_a1, x1, y1), x1[4:6]]))
+    plane_a1 = swap_y(after(jnp.concatenate([own_a1, oth_a1]), x1, y1))
+    far_f1 = swap_z(after(jnp.concatenate([own_f1, near_f1]), far_a1, x1, y1), 2)
     row_flags = predicted.reshape(1, LEN).astype(jnp.float32)
     col_flags = predicted.reshape(LEN, 1).astype(jnp.float32)
-    low = jnp.concatenate([content, query])
-    hidden = low.astype(jnp.float32)
-    kept = []
-    for layer in range(LAYERS):
-        small, hidden_bias, (tvec, far, onehot) = small_parts(small_all[layer])
-        q, k, v, attn = project(place, low, small, attn_pieces[layer])
-        mixed, lse = mix(lengths, far, tvec, q, k, v, row_flags, col_flags)
-        resid, summed, pre, hidden, next_low = feed(
-            place, small, hidden_bias, mixed, hidden, attn, feed_pieces[layer]
-        )
-        kept.append((small, far, tvec, onehot, low, q, k, v, attn, mixed, lse, resid, summed, pre))
-        low = next_low
+    low0 = jnp.concatenate([content, query])
+    hidden0 = low0.astype(jnp.float32)
+    small0, hidden_bias0, (tvec0, far0, onehot) = small_parts(small_all[0])
+    small1, hidden_bias1, (tvec1, far1, onehot) = small_parts(small_all[1])
     valid = (jnp.arange(LEN, dtype=jnp.int32) < lengths[0])[:, None].astype(jnp.float32)
-    grad = jnp.concatenate(
-        [content_cot.astype(jnp.float32) * valid, query_cot.astype(jnp.float32) * valid]
-    )
-    owned = [None] * LAYERS
-    small_grads = [None] * LAYERS
-    for layer in reversed(range(LAYERS)):
-        small, far, tvec, onehot, low_in, q, k, v, attn, mixed, lse, resid, summed, pre = kept[layer]
-        dresid, dmix, dwo, feed_keep, feed_send, feed_vec, dhidden = feed_back(
-            place, small, grad, summed, resid, pre, mixed, attn, feed_pieces[layer]
-        )
-        feed_own = reduce_blocks(feed_keep, feed_send)
-        dq, dk, dv, table_sums = mix_back(
-            lengths, far, tvec, q, k, v, dmix, mixed, lse, row_flags, col_flags
-        )
-        attn_keep, attn_send, attn_vec = weight_back(place, low_in, dq, dk, dv, dwo)
-        attn_own = reduce_blocks(attn_keep, attn_send)
-        grad_c, grad_q = input_back(dq, dk, dv, attn, dresid)
-        if layer:
-            grad = jnp.concatenate([grad_c, grad_q])
-        small_grads[layer] = jnp.concatenate(
+    grads = (content_cot.astype(jnp.float32) * valid, query_cot.astype(jnp.float32) * valid)
+    q0, k0, v0, attn0 = project(place, low0, small0, group_a0)
+    q0_late = after(q0, far_f1)
+    mixed0, p0, inverse0, dead = mix(
+        lengths, far0, tvec0, q0_late, k0, v0, row_flags, col_flags
+    )
+    x2, y2, plane_a1 = after((x2, y2, plane_a1), mixed0)
+    mine_2 = jnp.concatenate([plane_a1, col_a1, x2, y2])
+    theirs_2 = swap_core(mine_2)
+    group_f0 = gather_group(
+        2, feed_low[0], (0, 0), (0, 4), ((1, 0), (1, 8)), ((2, 8, 4), (2, 15, 2)),
+        (mine_p0, mine_1, mine_2), (theirs_p0, theirs_1, theirs_2),
+    )
+    far_f1 = after(far_f1, x2, y2)
+    col_f1 = jnp.concatenate([near_f1, far_f1])
+    x3 = swap_x(jnp.concatenate([col_f1, y2[:3]]))
+    y3 = swap_y(col_f1)
+    plane_f1 = swap_y(after(jnp.concatenate([own_f1, oth_f1]), x2, y2))
+    resid0, summed0, pre0, normed0, hidden1, low1 = feed(
+        place, small0, hidden_bias0, mixed0, hidden0, attn0, group_f0
+    )
+    x3, y3, plane_f1 = after((x3, y3, plane_f1), low1)
+    x4 = swap_x(y3[:3])
+    y4 = swap_y(x3[3:6])
+    mine_3 = jnp.concatenate([x3[6:], x3[:6], y3])
+    theirs_3 = swap_core(mine_3)
+    group_a1 = gather_group(
+        1, (attn_low[1],), (0, 0), (0, 2), ((0, 5), (0, 12)), ((1, 0, 3),),
+        (mine_2, mine_3), (theirs_2, theirs_3),
+    )
+    q1, k1, v1, attn1 = project(place, low1, small1, group_a1)
+    x4, y4 = after((x4, y4), q1)
+    mine_4 = jnp.concatenate([plane_f1, col_f1, x4, y4])
+    theirs_4 = swap_core(mine_4)
+    group_f1 = gather_group(
+        2, feed_low[1], (0, 0), (0, 4), ((1, 3), (1, 9)), ((0, 10, 3), (0, 13, 3)),
+        (mine_4, mine_3), (theirs_4, theirs_3),
+    )
+    mixed1, p1, inverse1, dead = mix(
+        lengths, far1, tvec1, q1, k1, v1, row_flags, col_flags
+    )
+    resid1, summed1, pre1, normed1, unused, low_out = feed(
+        place, small1, hidden_bias1, mixed1, hidden1, attn1, group_f1
+    )
+    dresid1, dmix1, dwo1, keep_f1, send_f1, vec_f1, dhidden1 = feed_back(
+        place, small1, grads, summed1, normed1, resid1, pre1, mixed1, attn1, group_f1
+    )
+    get_f1 = swap_core(send_f1)
+    first1 = mix_back(0, q1, k1, v1, dmix1, mixed1, p1, inverse1, dead)
+    by_f1 = reduce_corners(keep_f1, after(get_f1, first1[0]))
+    second1 = mix_back(
+        3, after(q1, get_f1, first1[0]), k1, v1, dmix1, mixed1, p1, inverse1, dead
+    )
+    sides_rf1 = reduce_sides(keep_f1, get_f1, after(by_f1, second1[0]))
+    keep_a1, send_a1, vec_a1 = weight_back(
+        place, low1, after(first1[:3], by_f1), second1[:3], dwo1
+    )
+    get_a1 = swap_core(send_a1)
+    grads = input_back(after(first1[:3], keep_a1), second1[:3], attn1, dresid1)
+    by_a1 = reduce_corners(keep_a1, after(get_a1, grads[0]))
+    dresid0, dmix0, dwo0, keep_f0, send_f0, vec_f0, dhidden0 = feed_back(
+        place, small0, after(grads, get_a1), summed0, normed0, resid0, pre0, mixed0, attn0, group_f0
+    )
+    get_f0 = swap_core(after(send_f0, sides_rf1))
+    sides_ra1 = reduce_sides(keep_a1, get_a1, after(by_a1, dmix0))
+    column_f1 = reduce_column(keep_f1, get_f1, after(sides_rf1, dmix0))
+    zfar_f1 = reduce_far(column_f1, place_parts)
+    first0 = mix_back(
+        0, q0, k0, v0, after(dmix0, by_a1, sides_rf1), mixed0, p0, inverse0, dead
+    )
+    by_f0 = reduce_corners(keep_f0, after(get_f0, first0[0]))
+    second0 = mix_back(
+        3, after(q0, get_f0, first0[0]), k0, v0, dmix0, mixed0, p0, inverse0, dead
+    )
+    zfar_f1, sides_ra1 = after((zfar_f1, sides_ra1), second0[0])
+    keep_a0, send_a0, vec_a0 = weight_back(
+        place, low0, after(first0[:3], by_f0), second0[:3], dwo0
+    )
+    sides_rf0 = reduce_sides(keep_f0, get_f0, after(by_f0, second0[0]))
+    get_a0 = swap_core(send_a0)
+    by_a0 = reduce_corners(keep_a0, get_a0)
+    znear_f1 = reduce_near(column_f1, after(zfar_f1, get_a0), place_parts)
+    column_a1 = reduce_column(keep_a1, get_a1, after(sides_ra1, get_a0))
+    zfar_a1 = reduce_far(column_a1, place_parts)
+    content_grad, query_grad = input_back(after(first0[:3], get_a0), second0[:3], attn0, dresid0)
+    column_f0 = reduce_column(keep_f0, get_f0, after(sides_rf0, content_grad))
+    zfar_f0 = reduce_far(column_f0, place_parts)
+    sides_ra0 = reduce_sides(keep_a0, get_a0, after(by_a0, column_f0))
+    znear_a1 = reduce_near(column_a1, after(zfar_a1, column_f0), place_parts)
+    four_f1 = share_quarters(
+        reduce_total(column_f1, zfar_f1, after(znear_f1, column_f0), place_parts), place_parts
+    )
+    column_a0 = reduce_column(keep_a0, get_a0, sides_ra0)
+    shifts_a0 = reduce_direct(after(column_a0, zfar_f0), place_parts)
+    znear_f0 = reduce_near(column_f0, zfar_f0, place_parts)
+    four_a1 = share_quarters(
+        reduce_total(column_a1, zfar_a1, after(znear_a1, column_a0), place_parts), place_parts
+    )
+    four_f0 = share_quarters(
+        reduce_total(column_f0, zfar_f0, znear_f0, place_parts), place_parts
+    )
+    attn_state = (attn_master, attn_first, attn_second)
+    inner_state = (inner_master, inner_first, inner_second)
+    outer_state = (outer_master, outer_first, outer_second)
+    inner_new = adam("inner", 1, FEED_RATE, inner_state, four_f1, 0, None)
+    outer_new = adam("outer", 1, FEED_RATE, outer_state, four_f1, 1, None)
+    attn_new = adam("attn", 1, ATTENTION_RATE, attn_state, four_a1, 0, None)
+    shifts_a0 = after(shifts_a0, inner_new, outer_new, attn_new)
+    four_a0 = share_quarters(direct_total(column_a0, shifts_a0, place_parts), place_parts)
+    small_grads = [
+        jnp.concatenate(
             [
                 attn_vec.reshape(-1),
                 feed_vec[2:].reshape(-1),
                 dhidden.reshape(-1),
-                table_grad(table_sums, onehot).reshape(-1),
+                table_grad(jnp.concatenate([first[3], second[3]]), onehot).reshape(-1),
             ]
         )
-        feed_four = share_quarters(feed_own, place_parts)
-        attn_four = share_quarters(attn_own, place_parts)
-        owned[layer] = (
-            shard_grad("attn", attn_four[:, 0]),
-            shard_grad("inner", feed_four[:, 0]),
-            shard_grad("outer", feed_four[:, 1]),
-        )
-    small_sum = sum_small(jnp.stack(small_grads))
+        for attn_vec, feed_vec, dhidden, first, second in (
+            (vec_a0, vec_f0, dhidden0, first0, second0),
+            (vec_a1, vec_f1, dhidden1, first1, second1),
+        )
+    ]
+    small_sum = sum_small(after(jnp.stack(small_grads), column_a0))
     size = small_master.shape[1]
     small_own = lax.dynamic_slice_in_dim(small_sum, lax.axis_index("fsdp") * size, size, 1)
-    reduced = tuple(
-        jnp.stack([owned[layer][member] for layer in range(LAYERS)]) for member in range(3)
-    )
-    attn_new = adam_update(attn_master, attn_first, attn_second, reduced[0], ATTENTION_RATE)
-    inner_new = adam_update(inner_master, inner_first, inner_second, reduced[1], FEED_RATE)
-    outer_new = adam_update(outer_master, outer_first, outer_second, reduced[2], FEED_RATE)
+    inner_new = adam("inner", 0, FEED_RATE, inner_state, four_f0, 0, tuple(inner_new))
+    outer_new = adam("outer", 0, FEED_RATE, outer_state, four_f0, 1, tuple(outer_new))
+    attn_new = adam("attn", 0, ATTENTION_RATE, attn_state, four_a0, 0, tuple(attn_new))
     small_new = adam_update(small_master, small_first, small_second, small_own, SMALL_RATE)
     return (
-        (low[:LEN], low[LEN:], grad_c, grad_q) + attn_new + inner_new + outer_new + small_new
+        (low_out[:LEN], low_out[LEN:], content_grad, query_grad)
+        + tuple(attn_new)
+        + tuple(inner_new)
+        + tuple(outer_new)
+        + small_new
     )
 
 

time: 680 us -> 670 us (0.985)
  waiting for transfers between devices: 198 us -> 156 us
  starting transfers between devices: 91.6 us -> 61.8 us
  Pallas kernels: 273 us -> 301 us
  local copies, waits for them, and re-layouts: 47 us -> 63.8 us
  other arithmetic: 60.9 us -> 71.8 us
    ppermute x98 -> x73, waiting for transfers between devices: 198 us -> 156 us  [move(): return lax.ppermute(value, AXES, pairs)]
    ppermute x98 -> x73, starting transfers between devices: 91.6 us -> 61.8 us  [move(): return lax.ppermute(value, AXES, pairs)]
    pallas_call x10 -> x18, Pallas kernels: 220 us -> 244 us  [the longest x2 81.5 us: feed_back(): pl.pallas_call(partial(feed_back_kernel, plan), out_shape=[jax.ShapeDtype...]
    convert_element_type x12 -> x24, other arithmetic: 14.4 us -> 32.3 us  [add_low(): return total.astype(jnp.bfloat16)]
    sub x4 -> x1, other arithmetic: 16.7 us -> 1.43 us  [adam_update(): master - rate * (first_hat / (jnp.sqrt(second_hat) + ADAM_EPS) + WEIGHT_D...]
    unnamed x113 -> x105, local copies, waits for them, and re-layouts: 5.06 us -> 16.9 us
    concatenate x10 -> x22, other arithmetic: 6.37 us -> 17.7 us  [the longest x4 3.15 us: reduce_sides(): jnp.concatenate([add_low(keep[1, 0, :2], get[1, 0, :2], by_x), add_low(ke...]
    slice x16, local copies, waits for them, and re-layouts: 21.6 us -> 12.8 us  [the longest x4 2.89 us: reduce_corners(): return (swap_x(corner[:2]), swap_y(corner[2:]))]
  transfers between devices with their start and end apart: 98 -> 73, of which waited for: 34 -> 25; matrix products, arithmetic and copies ran while one was open for 12% -> 18% of each run, Pallas kernels for 13% -> 32%
where the time goes in v4:
time: 670 us; the launch traced here: 659 us
  Pallas kernels  301 us (45%)
  waiting for transfers between devices  156 us (23%)
  other arithmetic  71.8 us (11%)
  local copies, waits for them, and re-layouts  63.8 us (10%)
  starting transfers between devices  61.8 us (9%)
    ppermute x73, waiting for transfers between devices, move(): return lax.ppermute(value, AXES, pairs)  156 us
    pallas_call x2, Pallas kernels, feed_back(): pl.pallas_call(partial(feed_back_kernel, plan), out_shape=[jax.ShapeDtype...  81.5 us
    ppermute x73, starting transfers between devices, move(): return lax.ppermute(value, AXES, pairs)  61.8 us
    pallas_call x4, Pallas kernels, mix_back(): pl.pallas_call(mix_back_kernel, grid=(H // 4,), out_shape=[jax.ShapeDtype...  49.3 us
    pallas_call x2, Pallas kernels, feed(): pl.pallas_call(partial(feed_kernel, plan), out_shape=[jax.ShapeDtypeStruc...  48.5 us
    pallas_call x2, Pallas kernels, mix(): pl.pallas_call(mix_kernel, grid=(H // 2,), out_shape=[jax.ShapeDtypeStruc...  38.9 us
    convert_element_type x24, other arithmetic, add_low(): return total.astype(jnp.bfloat16)  32.3 us
    pallas_call x6, Pallas kernels, adam(): pl.pallas_call(partial(adam_kernel, rate), grid=(4,), out_shape=[jax.Shap...  28.6 us
  transfers between devices with their start and end apart: 73, of which 25 were waited for; matrix products, arithmetic and copies ran while one was open for 18% of the time, Pallas kernels for 32%

profile of v4, /device:TPU:0, one launch (start us, length us, event | category | flops | bytes accessed | tf_op | source)
XLA Modules:
  0.0 659.3 jit_solution(8381292087403558105)
XLA Ops:
  33.3 18.8 %collective-permute-done.5 = bf16[2,96,768]{2,1,0:T(8,128)(2,1)S(1)} collective-permute-done((bf16[2,96,768]{2,1,0:T(8,128)(2,1)S(1)}, bf16[2,96,768]{2,1,0:T(8,128)(2,1)S(1)}, u32[]{:S(2)}, u32[]{:S(2)}) %collective-permute-start.5) | collective-permute-done | bytes 294944 | tf_op jit(solution)/shard_map/ppermute | solution.py:175
  71.7 20.3 %collective-permute-done.10 = bf16[8,96,768]{2,1,0:T(8,128)(2,1)} collective-permute-done((bf16[8,96,768]{2,1,0:T(8,128)(2,1)}, bf16[8,96,768]{2,1,0:T(8,128)(2,1)}, u32[]{:S(2)}, u32[]{:S(2)}) %collective-permute-start.10) | collective-permute-done | bytes 1179680 | tf_op jit(solution)/shard_map/ppermute | solution.py:175
  97.0 7.9 %collective-permute-done.12 = bf16[4,96,768]{2,1,0:T(8,128)(2,1)} collective-permute-done((bf16[4,96,768]{2,1,0:T(8,128)(2,1)}, bf16[4,96,768]{2,1,0:T(8,128)(2,1)}, u32[]{:S(2)}, u32[]{:S(2)}) %collective-permute-start.12) | collective-permute-done | bytes 589856 | tf_op jit(solution)/shard_map/ppermute | solution.py:175
  117.4 8.7 %collective-permute-done.16 = bf16[2,96,768]{2,1,0:T(8,128)(2,1)S(1)} collective-permute-done((bf16[2,96,768]{2,1,0:T(8,128)(2,1)}, bf16[2,96,768]{2,1,0:T(8,128)(2,1)S(1)}, u32[]{:S(2)}, u32[]{:S(2)}) %collective-permute-start.16) | collective-permute-done | bytes 294944 | tf_op jit(solution)/shard_map/ppermute | solution.py:175
  135.9 8.3 %project.2 = (bf16[1024,768]{1,0:T(8,128)(2,1)}, bf16[512,768]{1,0:T(8,128)(2,1)}, bf16[512,768]{1,0:T(8,128)(2,1)}, bf16[4,768,768]{2,1,0:T(8,128)(2,1)}) custom-call(s32[4]{0:T(128)} %pad_add_fusion.place_ref, bf16[1024,768]{1,0:T(8,128)(2,1)} %copy-done.2, f32[8,768]{1,0:T(8,128)} %reshape.1011.small_ref, bf16[4,96,768]{2,1,0:T(8,128)(2,1)} %get-tuple-element.412.refs_0_, ...), custom_call_target="tpu_custom_call" | custom-call | flops 2415919104 | bytes 16000000 | tf_op jit(solution)/shard_map/project/pallas_call | solution.py:295
  144.2 14.0 %collective-permute-done.18 = bf16[4,96,768]{2,1,0:T(8,128)(2,1)S(1)} collective-permute-done((bf16[4,96,768]{2,1,0:T(8,128)(2,1)}, bf16[4,96,768]{2,1,0:T(8,128)(2,1)S(1)}, u32[]{:S(2)}, u32[]{:S(2)}) %collective-permute-start.18) | collective-permute-done | bytes 589856 | tf_op jit(solution)/shard_map/ppermute | solution.py:175
  158.2 19.5 %mix.2 = (bf16[1024,768]{1,0:T(8,128)(2,1)}, bf16[12,512,1024]{2,1,0:T(8,128)(2,1)}, f32[12,1,1024]{2,1,0:T(1,128)}, f32[1,1024]{1,0:T(1,128)}) custom-call(s32[1]{0:T(128)} %copy.406.length_ref, f32[12,2]{1,0:T(8,128)} %pad_maximum_fusion.44.far_ref, bf16[1024,768]{1,0:T(8,128)(2,1)} %get-tuple-element.305.q_ref, ...), custom_call_target="tpu_custom_call" | custom-call | flops 6499999744 | bytes 8000000 | tf_op jit(solution)/shard_map/mix/pallas_call | solution.py:406
  191.6 24.2 %feed.2 = (f32[1024,768]{1,0:T(8,128)}, f32[1024,768]{1,0:T(8,128)}, bf16[4,1024,768]{2,1,0:T(8,128)(2,1)}, bf16[1024,768]{1,0:T(8,128)(2,1)}, f32[1024,768]{1,0:T(8,128)}, /*index=5*/bf16[1024,768]{1,0:T(8,128)(2,1)}) custom-call(s32[4]{0:T(128)} %pad_add_fusion.place_ref, f32[8,768]{1,0:T(8,128)} %reshape.1011.small_ref, f32[1,3072]{1,0:T(1,128)} %bitcast.256, ...), custom_call_target="tpu_custom_call" | custom-call | flops 10871635968 | bytes 40000000 | tf_op jit(solution)/shard_map/feed/pallas_call | solution.py:614
  234.1 8.4 %project.3 = (bf16[1024,768]{1,0:T(8,128)(2,1)}, bf16[512,768]{1,0:T(8,128)(2,1)}, bf16[512,768]{1,0:T(8,128)(2,1)}, bf16[4,768,768]{2,1,0:T(8,128)(2,1)}) custom-call(s32[4]{0:T(128)} %pad_add_fusion.place_ref, bf16[1024,768]{1,0:T(8,128)(2,1)} %get-tuple-element.237.low_ref, f32[8,768]{1,0:T(8,128)} %reshape.1009.small_ref, ...), custom_call_target="tpu_custom_call" | custom-call | flops 2415919104 | bytes 16000000 | tf_op jit(solution)/shard_map/project/pallas_call | solution.py:295
  249.3 19.4 %mix.3 = (bf16[1024,768]{1,0:T(8,128)(2,1)}, bf16[12,512,1024]{2,1,0:T(8,128)(2,1)}, f32[12,1,1024]{2,1,0:T(1,128)}, f32[1,1024]{1,0:T(1,128)}) custom-call(s32[1]{0:T(128)} %copy.406.length_ref, f32[12,2]{1,0:T(8,128)} %pad_maximum_fusion.43.far_ref, bf16[1024,768]{1,0:T(8,128)(2,1)} %get-tuple-element.269.q_ref, ...), custom_call_target="tpu_custom_call" | custom-call | flops 6499999744 | bytes 8000000 | tf_op jit(solution)/shard_map/mix/pallas_call | solution.py:406
  268.8 24.3 %feed.3 = (f32[1024,768]{1,0:T(8,128)}, f32[1024,768]{1,0:T(8,128)}, bf16[4,1024,768]{2,1,0:T(8,128)(2,1)}, bf16[1024,768]{1,0:T(8,128)(2,1)}, f32[1024,768]{1,0:T(8,128)}, /*index=5*/bf16[1024,768]{1,0:T(8,128)(2,1)}) custom-call(s32[4]{0:T(128)} %pad_add_fusion.place_ref, f32[8,768]{1,0:T(8,128)} %reshape.1009.small_ref, f32[1,3072]{1,0:T(1,128)} %bitcast.255, ...), custom_call_target="tpu_custom_call" | custom-call | flops 10871635968 | bytes 40000000 | tf_op jit(solution)/shard_map/feed/pallas_call | solution.py:614
  293.1 40.8 %feed_back.2 = (f32[1024,768]{1,0:T(8,128)}, bf16[1024,768]{1,0:T(8,128)(2,1)}, bf16[768,768]{1,0:T(8,128)(2,1)}, bf16[2,2,4,2,96,768]{5,4,3,2,1,0:T(8,128)(2,1)...) custom-call(s32[4]{0:T(128)} %pad_add_fusion.place_ref, ...), custom_call_target="tpu_custom_call" | custom-call | flops 21743271936 | bytes 60000000 | tf_op jit(solution)/shard_map/feed_back/pallas_call | solution.py:779
  334.1 12.3 %mix_back.4 = (bf16[1024,384]{1,0:T(8,128)(2,1)}, bf16[512,384]{1,0:T(8,128)(2,1)}, bf16[512,384]{1,0:T(8,128)(2,1)}, f32[6,1,768]{2,1,0:T(1,128)}) custom-call(bf16[1024,768]{1,0:T(8,128)(2,1)} %get-tuple-element.269.q_ref, bf16[512,768]{1,0:T(8,128)(2,1)} %get-tuple-element.243.k_ref, bf16[512,768]{1,0:T(8,128)(2,1)} %get-tuple-element.244.v_ref, ...), custom_call_target="tpu_custom_call" | custom-call | flops 8000000000 | bytes 16000000 | tf_op jit(solution)/shard_map/mix_back/pallas_call | solution.py:508
  349.9 12.4 %mix_back.5 = (bf16[1024,384]{1,0:T(8,128)(2,1)}, bf16[512,384]{1,0:T(8,128)(2,1)}, bf16[512,384]{1,0:T(8,128)(2,1)}, f32[6,1,768]{2,1,0:T(1,128)}) custom-call(bf16[1024,768]{1,0:T(8,128)(2,1)} %get-tuple-element.269.q_ref, bf16[512,768]{1,0:T(8,128)(2,1)} %get-tuple-element.243.k_ref, bf16[512,768]{1,0:T(8,128)(2,1)} %get-tuple-element.244.v_ref, ...), custom_call_target="tpu_custom_call" | custom-call | flops 8000000000 | bytes 16000000 | tf_op jit(solution)/shard_map/mix_back/pallas_call | solution.py:508
  364.4 9.0 %weight_back.2 = (bf16[2,2,4,1,96,768]{5,4,3,2,1,0:T(8,128)(2,1)}, bf16[2,2,4,1,96,768]{5,4,3,2,1,0:T(8,128)(2,1)}, f32[2,768]{1,0:T(2,128)}) custom-call(s32[4]{0:T(128)} %pad_add_fusion.place_ref, bf16[1024,768]{1,0:T(8,128)(2,1)} %get-tuple-element.237.low_ref, bf16[1024,384]{1,0:T(8,128)(2,1)} %get-tuple-element.275.dq_a, ...), custom_call_target="tpu_custom_call" | custom-call | flops 2415919104 | bytes 12000000 | tf_op jit(solution)/shard_map/weight_back/pallas_call | solution.py:853
  381.1 9.7 %input_back.2 = (f32[512,768]{1,0:T(8,128)}, f32[512,768]{1,0:T(8,128)}) custom-call(bf16[1024,384]{1,0:T(8,128)(2,1)} %get-tuple-element.275.dq_a, bf16[512,384]{1,0:T(8,128)(2,1)} %get-tuple-element.276.dk_a, bf16[512,384]{1,0:T(8,128)(2,1)} %get-tuple-element.277.dv_a, bf16[1024,384]{1,0:T(8,128)(2,1)} %get-tuple-element.270.dq_b, ...), custom_call_target="tpu_custom_call" | custom-call | flops 2415919104 | bytes 16000000 | tf_op jit(solution)/shard_map/input_back/pallas_call | solution.py:895
  390.9 40.7 %feed_back.3 = (f32[1024,768]{1,0:T(8,128)}, bf16[1024,768]{1,0:T(8,128)(2,1)}, bf16[768,768]{1,0:T(8,128)(2,1)}, bf16[2,2,4,2,96,768]{5,4,3,2,1,0:T(8,128)(2,1)...) custom-call(s32[4]{0:T(128)} %pad_add_fusion.place_ref, ...), custom_call_target="tpu_custom_call" | custom-call | flops 21743271936 | bytes 60000000 | tf_op jit(solution)/shard_map/feed_back/pallas_call | solution.py:779
  455.5 12.3 %mix_back.6 = (bf16[1024,384]{1,0:T(8,128)(2,1)}, bf16[512,384]{1,0:T(8,128)(2,1)}, bf16[512,384]{1,0:T(8,128)(2,1)}, f32[6,1,768]{2,1,0:T(1,128)}) custom-call(bf16[1024,768]{1,0:T(8,128)(2,1)} %get-tuple-element.305.q_ref, bf16[512,768]{1,0:T(8,128)(2,1)} %get-tuple-element.228.k_ref, bf16[512,768]{1,0:T(8,128)(2,1)} %get-tuple-element.229.v_ref, ...), custom_call_target="tpu_custom_call" | custom-call | flops 8000000000 | bytes 16000000 | tf_op jit(solution)/shard_map/mix_back/pallas_call | solution.py:508
  473.1 12.3 %mix_back.7 = (bf16[1024,384]{1,0:T(8,128)(2,1)}, bf16[512,384]{1,0:T(8,128)(2,1)}, bf16[512,384]{1,0:T(8,128)(2,1)}, f32[6,1,768]{2,1,0:T(1,128)}) custom-call(bf16[1024,768]{1,0:T(8,128)(2,1)} %get-tuple-element.305.q_ref, bf16[512,768]{1,0:T(8,128)(2,1)} %get-tuple-element.228.k_ref, bf16[512,768]{1,0:T(8,128)(2,1)} %get-tuple-element.229.v_ref, ...), custom_call_target="tpu_custom_call" | custom-call | flops 8000000000 | bytes 16000000 | tf_op jit(solution)/shard_map/mix_back/pallas_call | solution.py:508
  494.1 9.0 %weight_back.3 = (bf16[2,2,4,1,96,768]{5,4,3,2,1,0:T(8,128)(2,1)}, bf16[2,2,4,1,96,768]{5,4,3,2,1,0:T(8,128)(2,1)}, f32[2,768]{1,0:T(2,128)}) custom-call(s32[4]{0:T(128)} %pad_add_fusion.place_ref, bf16[1024,768]{1,0:T(8,128)(2,1)} %copy-done.2, bf16[1024,384]{1,0:T(8,128)(2,1)} %get-tuple-element.311.dq_a, bf16[512,384]{1,0:T(8,128)(2,1)} %get-tuple-element.312.dk_a, ...), custom_call_target="tpu_custom_call" | custom-call | flops 2415919104 | bytes 12000000 | tf_op jit(solution)/shard_map/weight_back/pallas_call | solution.py:853
  519.9 9.5 %input_back.3 = (f32[512,768]{1,0:T(8,128)}, f32[512,768]{1,0:T(8,128)}) custom-call(bf16[1024,384]{1,0:T(8,128)(2,1)} %get-tuple-element.311.dq_a, bf16[512,384]{1,0:T(8,128)(2,1)} %get-tuple-element.312.dk_a, bf16[512,384]{1,0:T(8,128)(2,1)} %get-tuple-element.313.dv_a, bf16[1024,384]{1,0:T(8,128)(2,1)} %get-tuple-element.306.dq_b, ...), custom_call_target="tpu_custom_call" | custom-call | flops 2415919104 | bytes 16000000 | tf_op jit(solution)/shard_map/input_back/pallas_call | solution.py:895
  530.5 8.7 %collective-permute-done.45 = bf16[4,2,96,768]{3,2,1,0:T(8,128)(2,1)} collective-permute-done((bf16[4,2,96,768]{3,2,1,0:T(8,128)(2,1)}, bf16[4,2,96,768]{3,2,1,0:T(8,128)(2,1)}, u32[]{:S(2)}, u32[]{:S(2)}) %collective-permute-start.45) | collective-permute-done | bytes 1179680 | tf_op jit(solution)/shard_map/ppermute | solution.py:175
  555.8 10.9 %collective-permute-done.56 = bf16[2,96,768]{2,1,0:T(8,128)(2,1)S(1)} collective-permute-done((bf16[2,96,768]{2,1,0:T(8,128)(2,1)S(1)}, bf16[2,96,768]{2,1,0:T(8,128)(2,1)S(1)}, u32[]{:S(2)}, u32[]{:S(2)}) %collective-permute-start.56) | collective-permute-done | bytes 294944 | tf_op jit(solution)/shard_map/ppermute | solution.py:175
  568.4 16.6 %collective-permute-done.59 = bf16[2,1,96,768]{3,2,1,0:T(8,128)(2,1)S(1)} collective-permute-done((bf16[2,1,96,768]{3,2,1,0:T(8,128)(2,1)S(1)}, bf16[2,1,96,768]{3,2,1,0:T(8,128)(2,1)S(1)}, u32[]{:S(2)}, u32[]{:S(2)}) %collective-permute-start.59) | collective-permute-done | bytes 294944 | tf_op jit(solution)/shard_map/ppermute | solution.py:175
  (438 shorter events, 278.1 us)
Async XLA Ops:
  1.9 55.8 %collective-permute-start = (bf16[2,1200]{1,0:T(2,128)(2,1)}, bf16[2,1200]{1,0:T(2,128)(2,1)}, u32[]{:S(2)}, u32[]{:S(2)}) collective-permute-start(bf16[2,1200]{1,0:T(2,128)(2,1)} %convert_element_type.902), channel_id=1, source_target_pairs={{0,2},{1,3},{2,0},{3,1},{4,6},{5,7},{6,4},{7,5},{8,10},{9,11},{10,... | collective-permute-start | bytes 14408 | tf_op jit(solution)/shard_map/ppermute | solution.py:175
  27.1 37.1 %collective-permute-start.9 = (bf16[4,96,768]{2,1,0:T(8,128)(2,1)}, bf16[4,96,768]{2,1,0:T(8,128)(2,1)S(1)}, u32[]{:S(2)}, u32[]{:S(2)}) collective-permute-start(bf16[4,96,768]{2,1,0:T(8,128)(2,1)} %get-tuple-element.447), channel_id=1, source_target_pairs={{0,4},{1,5},{2,6},{3,7},{4,0},{5,1},{6,2},{7,3},{8,12},{9,13},{10,... | collective-permute-start | bytes 1769480 | tf_op jit(solution)/shard_map/ppermute | solution.py:175
  71.1 33.8 %collective-permute-start.12 = (bf16[4,96,768]{2,1,0:T(8,128)(2,1)}, bf16[4,96,768]{2,1,0:T(8,128)(2,1)}, u32[]{:S(2)}, u32[]{:S(2)}) collective-permute-start(bf16[4,96,768]{2,1,0:T(8,128)(2,1)} %get-tuple-element.220), channel_id=1, source_target_pairs={{0,1},{1,0},{2,3},{3,2},{4,5},{5,4},{6,7},{7,6},{8,9},{9,8},{10,11... | collective-permute-start | bytes 1769480 | tf_op jit(solution)/shard_map/ppermute | solution.py:175
  95.3 40.6 %collective-permute-start.14 = (bf16[15,96,768]{2,1,0:T(8,128)(2,1)}, bf16[15,96,768]{2,1,0:T(8,128)(2,1)}, u32[]{:S(2)}, u32[]{:S(2)}) collective-permute-start(bf16[15,96,768]{2,1,0:T(8,128)(2,1)} %constant_dynamic-update-slice_fusion.9.refs_2_.refs_3_), channel_id=1, source_target_pairs={{0,8},{1,9},{2,10},{3,11},{4,12},{5,13},{6,14},{7,15},{8,0},{9,1},... | collective-permute-start | bytes 6635528 | tf_op jit(solution)/shard_map/ppermute | solution.py:175
  131.5 46.2 %collective-permute-start.19 = (bf16[7,96,768]{2,1,0:T(8,128)(2,1)}, bf16[7,96,768]{2,1,0:T(8,128)(2,1)}, u32[]{:S(2)}, u32[]{:S(2)}) collective-permute-start(bf16[7,96,768]{2,1,0:T(8,128)(2,1)} %pad_maximum_fusion.8), channel_id=1, source_target_pairs={{0,16},{1,17},{2,18},{3,19},{4,20},{5,21},{6,22},{7,23},{8,24},{9,... | collective-permute-start | bytes 3096584 | tf_op jit(solution)/shard_map/ppermute | solution.py:175
  133.8 43.9 %collective-permute-start.20 = (bf16[5,96,768]{2,1,0:T(8,128)(2,1)S(1)}, bf16[5,96,768]{2,1,0:T(8,128)(2,1)S(1)}, u32[]{:S(2)}, u32[]{:S(2)}) collective-permute-start(bf16[5,96,768]{2,1,0:T(8,128)(2,1)S(1)} %pad_maximum_fusion.10), channel_id=1, source_target_pairs={{0,1},{1,0},{2,3},{3,2},{4,5},{5,4},{6,7},{7,6},{8,9},{9,8},{10,11... | collective-permute-start | bytes 2211848 | tf_op jit(solution)/shard_map/ppermute | solution.py:175
  134.1 43.5 %collective-permute-start.21 = (bf16[2,96,768]{2,1,0:T(8,128)(2,1)}, bf16[2,96,768]{2,1,0:T(8,128)(2,1)}, u32[]{:S(2)}, u32[]{:S(2)}) collective-permute-start(bf16[2,96,768]{2,1,0:T(8,128)(2,1)} %get-tuple-element.233), channel_id=1, source_target_pairs={{0,1},{1,0},{2,3},{3,2},{4,5},{5,4},{6,7},{7,6},{8,9},{9,8},{10,11... | collective-permute-start | bytes 884744 | tf_op jit(solution)/shard_map/ppermute | solution.py:175
  184.3 37.5 %collective-permute-start.24 = (bf16[9,96,768]{2,1,0:T(8,128)(2,1)}, bf16[9,96,768]{2,1,0:T(8,128)(2,1)}, u32[]{:S(2)}, u32[]{:S(2)}) collective-permute-start(bf16[9,96,768]{2,1,0:T(8,128)(2,1)} %pad_maximum_fusion.1), channel_id=1, source_target_pairs={{0,16},{1,17},{2,18},{3,19},{4,20},{5,21},{6,22},{7,23},{8,24},{9,... | collective-permute-start | bytes 3981320 | tf_op jit(solution)/shard_map/ppermute | solution.py:175
  187.4 34.3 %collective-permute-start.25 = (bf16[6,96,768]{2,1,0:T(8,128)(2,1)S(1)}, bf16[6,96,768]{2,1,0:T(8,128)(2,1)S(1)}, u32[]{:S(2)}, u32[]{:S(2)}) collective-permute-start(bf16[6,96,768]{2,1,0:T(8,128)(2,1)S(1)} %pad_maximum_fusion.9), channel_id=1, source_target_pairs={{0,1},{1,0},{2,3},{3,2},{4,5},{5,4},{6,7},{7,6},{8,9},{9,8},{10,11... | collective-permute-start | bytes 2654216 | tf_op jit(solution)/shard_map/ppermute | solution.py:175
  187.7 34.0 %collective-permute-start.26 = (bf16[4,96,768]{2,1,0:T(8,128)(2,1)}, bf16[4,96,768]{2,1,0:T(8,128)(2,1)S(1)}, u32[]{:S(2)}, u32[]{:S(2)}) collective-permute-start(bf16[4,96,768]{2,1,0:T(8,128)(2,1)} %get-tuple-element.239), channel_id=1, source_target_pairs={{0,1},{1,0},{2,3},{3,2},{4,5},{5,4},{6,7},{7,6},{8,9},{9,8},{10,11... | collective-permute-start | bytes 1769480 | tf_op jit(solution)/shard_map/ppermute | solution.py:175
  377.5 54.2 %collective-permute-start.37 = (bf16[4,2,96,768]{3,2,1,0:T(8,128)(2,1)S(1)}, bf16[4,2,96,768]{3,2,1,0:T(8,128)(2,1)}, u32[]{:S(2)}, u32[]{:S(2)}) collective-permute-start(bf16[4,2,96,768]{3,2,1,0:T(8,128)(2,1)S(1)} %pad_maximum_fusion.3), channel_id=1, source_target_pairs={{0,16},{1,17},{2,18},{3,19},{4,20},{5,21},{6,22},{7,23},{8,24},{9,... | collective-permute-start | bytes 3538952 | tf_op jit(solution)/shard_map/ppermute | solution.py:175
  380.2 51.5 %collective-permute-start.38 = (bf16[4,2,96,768]{3,2,1,0:T(8,128)(2,1)}, bf16[4,2,96,768]{3,2,1,0:T(8,128)(2,1)}, u32[]{:S(2)}, u32[]{:S(2)}) collective-permute-start(bf16[4,2,96,768]{3,2,1,0:T(8,128)(2,1)} %pad_maximum_fusion.4), channel_id=1, source_target_pairs={{0,1},{1,0},{2,3},{3,2},{4,5},{5,4},{6,7},{7,6},{8,9},{9,8},{10,11... | collective-permute-start | bytes 3538952 | tf_op jit(solution)/shard_map/ppermute | solution.py:175
  431.7 36.9 %collective-permute-start.39 = (bf16[2,2,4,2,96,768]{5,4,3,2,1,0:T(8,128)(2,1)}, bf16[2,2,4,2,96,768]{5,4,3,2,1,0:T(8,128)(2,1)}, u32[]{:S(2)}, u32[]{:S(2)}) collective-permute-start(bf16[2,2,4,2,96,768]{5,4,3,2,1,0:T(8,128)(2,1)} %get-tuple-element.300), channel_id=1, source_target_pairs={{0,8},{1,9},{2,10},{3,11},{4,12},{5,13},{6,14},{7,15},{8,0},{9,1},... | collective-permute-start | bytes 14155784 | tf_op jit(solution)/shard_map/ppermute | solution.py:175
  445.3 40.9 %collective-permute-start.53 = (bf16[2,2,96,768]{3,2,1,0:T(8,128)(2,1)}, bf16[2,2,96,768]{3,2,1,0:T(8,128)(2,1)}, u32[]{:S(2)}, u32[]{:S(2)}) collective-permute-start(bf16[2,2,96,768]{3,2,1,0:T(8,128)(2,1)} %pad_maximum_fusion.20), channel_id=1, source_target_pairs={{0,4},{1,5},{2,6},{3,7},{4,0},{5,1},{6,2},{7,3},{8,12},{9,13},{10,... | collective-permute-start | bytes 1769480 | tf_op jit(solution)/shard_map/ppermute | solution.py:175
  452.1 34.1 %collective-permute-start.54 = (bf16[4,1,96,768]{3,2,0,1:T(8,128)(2,1)}, bf16[4,1,96,768]{3,2,0,1:T(8,128)(2,1)}, u32[]{:S(2)}, u32[]{:S(2)}) collective-permute-start(bf16[4,1,96,768]{3,2,0,1:T(8,128)(2,1)} %pad_maximum_fusion.21), channel_id=1, source_target_pairs={{0,16},{1,17},{2,18},{3,19},{4,20},{5,21},{6,22},{7,23},{8,24},{9,... | collective-permute-start | bytes 1769480 | tf_op jit(solution)/shard_map/ppermute | solution.py:175
  454.5 31.7 %collective-permute-start.55 = (bf16[4,1,96,768]{3,2,1,0:T(8,128)(2,1)}, bf16[4,1,96,768]{3,2,1,0:T(8,128)(2,1)}, u32[]{:S(2)}, u32[]{:S(2)}) collective-permute-start(bf16[4,1,96,768]{3,2,1,0:T(8,128)(2,1)} %pad_maximum_fusion.22), channel_id=1, source_target_pairs={{0,1},{1,0},{2,3},{3,2},{4,5},{5,4},{6,7},{7,6},{8,9},{9,8},{10,11... | collective-permute-start | bytes 1769480 | tf_op jit(solution)/shard_map/ppermute | solution.py:175
  518.4 34.2 %collective-permute-start.43 = (bf16[2,1,96,768]{3,2,0,1:T(8,128)(2,1)}, bf16[2,1,96,768]{3,2,0,1:T(8,128)(2,1)S(1)}, u32[]{:S(2)}, u32[]{:S(2)}) collective-permute-start(bf16[2,1,96,768]{3,2,0,1:T(8,128)(2,1)} %get-tuple-element.425), channel_id=1, source_target_pairs={{0,16},{1,17},{2,18},{3,19},{4,20},{5,21},{6,22},{7,23},{8,24},{9,... | collective-permute-start | bytes 884744 | tf_op jit(solution)/shard_map/ppermute | solution.py:175
  518.9 33.6 %collective-permute-start.44 = (bf16[2,1,96,768]{3,2,0,1:T(8,128)(2,1)}, bf16[2,1,96,768]{3,2,0,1:T(8,128)(2,1)}, u32[]{:S(2)}, u32[]{:S(2)}) collective-permute-start(bf16[2,1,96,768]{3,2,0,1:T(8,128)(2,1)} %get-tuple-element.424), channel_id=1, source_target_pairs={{0,1},{1,0},{2,3},{3,2},{4,5},{5,4},{6,7},{7,6},{8,9},{9,8},{10,11... | collective-permute-start | bytes 884744 | tf_op jit(solution)/shard_map/ppermute | solution.py:175
  544.9 40.2 %collective-permute-start.49 = (bf16[2,2,96,768]{3,2,1,0:T(8,128)(2,1)S(1)}, bf16[2,2,96,768]{3,2,1,0:T(8,128)(2,1)S(1)}, u32[]{:S(2)}, u32[]{:S(2)}) collective-permute-start(bf16[2,2,96,768]{3,2,1,0:T(8,128)(2,1)S(1)} %pad_maximum_fusion.19), channel_id=1, source_target_pairs={{0,4},{1,5},{2,6},{3,7},{4,0},{5,1},{6,2},{7,3},{8,12},{9,13},{10,... | collective-permute-start | bytes 1769480 | tf_op jit(solution)/shard_map/ppermute | solution.py:175
  549.9 35.1 %collective-permute-start.59 = (bf16[2,1,96,768]{3,2,1,0:T(8,128)(2,1)S(1)}, bf16[2,1,96,768]{3,2,1,0:T(8,128)(2,1)S(1)}, u32[]{:S(2)}, u32[]{:S(2)}) collective-permute-start(bf16[2,1,96,768]{3,2,1,0:T(8,128)(2,1)S(1)} %pad_maximum_fusion.32), channel_id=1, source_target_pairs={{0,4},{1,5},{2,6},{3,7},{4,0},{5,1},{6,2},{7,3},{8,12},{9,13},{10,... | collective-permute-start | bytes 884744 | tf_op jit(solution)/shard_map/ppermute | solution.py:175
  554.0 33.5 %collective-permute-start.48 = (bf16[4,1,96,768]{3,2,0,1:T(8,128)(2,1)S(1)}, bf16[4,1,96,768]{3,2,0,1:T(8,128)(2,1)S(1)}, u32[]{:S(2)}, u32[]{:S(2)}) collective-permute-start(bf16[4,1,96,768]{3,2,0,1:T(8,128)(2,1)S(1)} %pad_maximum_fusion.18), channel_id=1, source_target_pairs={{0,1},{1,0},{2,3},{3,2},{4,5},{5,4},{6,7},{7,6},{8,9},{9,8},{10,11... | collective-permute-start | bytes 1769480 | tf_op jit(solution)/shard_map/ppermute | solution.py:175
  555.2 32.3 %collective-permute-start.47 = (bf16[4,1,96,768]{3,2,0,1:T(8,128)(2,1)S(1)}, bf16[4,1,96,768]{3,2,0,1:T(8,128)(2,1)S(1)}, u32[]{:S(2)}, u32[]{:S(2)}) collective-permute-start(bf16[4,1,96,768]{3,2,0,1:T(8,128)(2,1)S(1)} %pad_maximum_fusion.17), channel_id=1, source_target_pairs={{0,16},{1,17},{2,18},{3,19},{4,20},{5,21},{6,22},{7,23},{8,24},{9,... | collective-permute-start | bytes 1769480 | tf_op jit(solution)/shard_map/ppermute | solution.py:175
  589.6 46.3 %collective-permute-start.50 = (bf16[1,96,768]{2,1,0:T(8,128)(2,1)}, bf16[1,96,768]{2,1,0:T(8,128)(2,1)S(1)}, u32[]{:S(2)}, u32[]{:S(2)}) collective-permute-start(bf16[1,96,768]{2,1,0:T(8,128)(2,1)} %get-tuple-element.423), channel_id=1, source_target_pairs={{0,2},{1,3},{2,0},{3,1},{4,6},{5,7},{6,4},{7,5},{8,10},{9,11},{10,... | collective-permute-start | bytes 442376 | tf_op jit(solution)/shard_map/ppermute | solution.py:175
  589.7 46.3 %collective-permute-start.51 = (bf16[1,96,768]{2,1,0:T(8,128)(2,1)}, bf16[1,96,768]{2,1,0:T(8,128)(2,1)S(1)}, u32[]{:S(2)}, u32[]{:S(2)}) collective-permute-start(bf16[1,96,768]{2,1,0:T(8,128)(2,1)} %get-tuple-element.422), channel_id=1, source_target_pairs={{0,4},{1,5},{2,6},{3,7},{4,0},{5,1},{6,2},{7,3},{8,12},{9,13},{10,... | collective-permute-start | bytes 442376 | tf_op jit(solution)/shard_map/ppermute | solution.py:175
  (94 other events, 1200.7 us)

commit v5 on v4

--- a/solution.py
+++ b/solution.py
@@ -942,9 +942,15 @@
 def adam_kernel(rate, master_ref, first_ref, second_ref, grad_ref, *refs):
     master_out, first_out, second_out = refs[-3:]
     grad = grad_ref[...].astype(jnp.float32).reshape(master_ref.shape)
-    new = adam_update(master_ref[...], first_ref[...], second_ref[...], grad, rate)
-    for target, value in zip((master_out, first_out, second_out), new):
-        target[...] = value
+    master = master_ref[...]
+    first = BETA_ONE * first_ref[...] + (1.0 - BETA_ONE) * grad
+    second = BETA_TWO * second_ref[...] + (1.0 - BETA_TWO) * grad * grad
+    first_out[...] = first
+    second_out[...] = second
+    first_scale = rate / (1.0 - BETA_ONE**STEP)
+    second_scale = 1.0 / (1.0 - BETA_TWO**STEP)
+    step = (first_scale * first) / (jnp.sqrt(second_scale * second) + ADAM_EPS)
+    master_out[...] = master - (step + (rate * WEIGHT_DECAY) * master)
 
 
 def adam(kind, layer, rate, state, quarters, member, done):
@@ -1289,9 +1295,18 @@
     return lax.optimization_barrier((value, others))[0]
 
 
+def join(*values):
+    return lax.optimization_barrier(values)
+
+
 def own_blocks(kinds, shards, place, side):
     quarter = (place[0] ^ side) * 2 + place[1]
-    return jnp.stack([quarter_of(kind, shard, quarter) for kind, shard in zip(kinds, shards)])
+    return jnp.stack(
+        [
+            quarter_of(kind, shard, quarter).astype(jnp.bfloat16)
+            for kind, shard in zip(kinds, shards)
+        ]
+    )
 
 
 def gather_group(count, shards, plane, column, sides, corners, mine, theirs):
@@ -1332,14 +1347,6 @@
     return pairs.transpose(2, 0, 1, 3).reshape(shard.shape[0], -1)
 
 
-def sum_small(value):
-    value = value + swap_core(value)
-    value = value + swap_x(value)
-    value = value + swap_y(value)
-    value = value + swap_z(value, 1)
-    return value + swap_z(value, 2)
-
-
 def add_low(*values):
     total = values[0].astype(jnp.float32)
     for value in values[1:]:
@@ -1387,13 +1394,12 @@
     return add_low(at_z(column, place, 0), *shifts)
 
 
-def share_quarters(own, place):
+def share_core(pair, place):
     x, c = place[0], place[1]
-    pair = jnp.stack([own, swap_x(own)])
     other = swap_core(pair)
     cores = jnp.where(c == 0, jnp.stack([pair, other], 1), jnp.stack([other, pair], 1))
     sides = jnp.where(x == 0, cores, cores[::-1])
-    return sides.reshape((4,) + own.shape)
+    return sides.reshape((4,) + pair.shape[1:])
 
 
 def small_parts(vectors):
@@ -1427,48 +1433,50 @@
 ):
     place_parts = my_place()
     place = jnp.stack(place_parts).astype(jnp.int32)
-    small_all = gather_small(small_master.astype(jnp.bfloat16), place_parts)
     attn_kinds, feed_kinds = ("attn",), ("inner", "outer")
-    attn_low = [attn_master[layer].astype(jnp.bfloat16) for layer in range(LAYERS)]
-    feed_low = [
-        (inner_master[layer].astype(jnp.bfloat16), outer_master[layer].astype(jnp.bfloat16))
-        for layer in range(LAYERS)
-    ]
-    own_a0, own_a1 = (own_blocks(attn_kinds, (w,), place_parts, 0) for w in attn_low)
-    own_f0, own_f1 = (own_blocks(feed_kinds, w, place_parts, 0) for w in feed_low)
-    oth_a0, oth_a1 = (own_blocks(attn_kinds, (w,), place_parts, 1) for w in attn_low)
-    oth_f0, oth_f1 = (own_blocks(feed_kinds, w, place_parts, 1) for w in feed_low)
-    near_a0 = swap_z(own_a0, 1)
-    far_a0 = swap_z(jnp.concatenate([own_a0, near_a0]), 2)
+    attn_shards = [(attn_master[layer],) for layer in range(LAYERS)]
+    feed_shards = [(inner_master[layer], outer_master[layer]) for layer in range(LAYERS)]
+    own_a0 = own_blocks(attn_kinds, attn_shards[0], place_parts, 0)
+    oth_a0 = own_blocks(attn_kinds, attn_shards[0], place_parts, 1)
+    own_f0 = own_blocks(feed_kinds, feed_shards[0], place_parts, 0)
+    z_a0 = tuple(swap_z(own_a0, apart) for apart in (1, 2, 3))
     plane_a0 = swap_y(jnp.concatenate([own_a0, oth_a0]))
-    near_f0 = swap_z(after(own_f0, near_a0), 1)
-    plane_f0 = swap_y(after(jnp.concatenate([own_f0, oth_f0]), plane_a0))
-    col_a0 = jnp.concatenate([near_a0, far_a0])
+    near_f0 = swap_z(own_f0, 1)
+    z_a0, plane_a0, near_f0 = join(z_a0, plane_a0, near_f0)
+    oth_f0 = own_blocks(feed_kinds, feed_shards[0], place_parts, 1)
+    own_a1 = own_blocks(attn_kinds, attn_shards[1], place_parts, 0)
+    oth_a1 = own_blocks(attn_kinds, attn_shards[1], place_parts, 1)
+    own_f1 = own_blocks(feed_kinds, feed_shards[1], place_parts, 0)
+    oth_f1 = own_blocks(feed_kinds, feed_shards[1], place_parts, 1)
+    attn_low = [tuple(w.astype(jnp.bfloat16) for w in shards) for shards in attn_shards]
+    feed_low = [tuple(w.astype(jnp.bfloat16) for w in shards) for shards in feed_shards]
+    col_a0 = jnp.concatenate(z_a0)
     x0 = swap_x(col_a0)
-    y0 = swap_y(after(col_a0, plane_a0))
+    y0 = swap_y(col_a0)
     far_f0 = swap_z(jnp.concatenate([own_f0, near_f0]), 2)
-    far_f0_in = after(far_f0, x0, y0)
-    near_a1 = swap_z(after(own_a1, near_f0), 1)
-    near_f1 = swap_z(after(own_f1, near_a1), 1)
-    mine_0 = jnp.concatenate([plane_a0, col_a0, x0, y0])
-    theirs_0 = swap_core(after(mine_0, plane_f0))
-    col_f0 = jnp.concatenate([near_f0, far_f0_in])
+    plane_f0 = swap_y(after(jnp.concatenate([own_f0, oth_f0]), z_a0))
+    near_1 = swap_z(after(jnp.concatenate([own_a1, own_f1]), z_a0), 1)
+    x0, y0, far_f0, plane_f0, near_1 = join(x0, y0, far_f0, plane_f0, near_1)
+    col_f0 = jnp.concatenate([near_f0, far_f0])
     x1 = swap_x(jnp.concatenate([col_f0, y0[:2]]))
     y1 = swap_y(jnp.concatenate([col_f0, x0[2:]]))
-    far_a1 = swap_z(after(jnp.concatenate([own_a1, near_a1]), far_f0), 2)
-    col_a1 = jnp.concatenate([near_a1, far_a1])
-    mine_p0 = jnp.concatenate([plane_f0, col_f0])
-    theirs_p0 = swap_core(mine_p0)
+    far_a1 = swap_z(jnp.concatenate([own_a1, near_1[:1]]), 2)
+    mine_0 = jnp.concatenate([plane_a0, col_a0, x0, y0])
+    theirs_0 = swap_core(mine_0)
+    small_all = gather_small(after(small_master.astype(jnp.bfloat16), far_f0), place_parts)
+    x1, y1, far_a1, theirs_0, small_all = join(x1, y1, far_a1, theirs_0, small_all)
+    col_a1 = jnp.concatenate([near_1[:1], far_a1])
+    x2 = swap_x(jnp.concatenate([col_a1, y1[:4]]))
+    y2 = swap_y(jnp.concatenate([col_a1, x1[4:6], own_a1, oth_a1]))
+    far_f1 = swap_z(jnp.concatenate([own_f1, after(near_1[1:], far_a1)]), 2)
     mine_1 = jnp.concatenate([x1, y1])
     theirs_1 = swap_core(mine_1)
+    mine_p0 = jnp.concatenate([plane_f0, col_f0])
+    theirs_p0 = swap_core(after(mine_p0, theirs_1))
     group_a0 = gather_group(
-        1, (attn_low[0],), (0, 0), (0, 2), ((0, 5), (0, 8)), ((1, 6, 2), (1, 14, 1)),
+        1, attn_low[0], (0, 0), (0, 2), ((0, 5), (0, 8)), ((1, 6, 2), (1, 14, 1)),
         (mine_0, mine_1), (theirs_0, theirs_1),
     )
-    x2 = swap_x(jnp.concatenate([after(col_a1, x1, y1), y1[:4]]))
-    y2 = swap_y(jnp.concatenate([after(col_a1, x1, y1), x1[4:6]]))
-    plane_a1 = swap_y(after(jnp.concatenate([own_a1, oth_a1]), x1, y1))
-    far_f1 = swap_z(after(jnp.concatenate([own_f1, near_f1]), far_a1, x1, y1), 2)
     row_flags = predicted.reshape(1, LEN).astype(jnp.float32)
     col_flags = predicted.reshape(LEN, 1).astype(jnp.float32)
     low0 = jnp.concatenate([content, query])
@@ -1478,41 +1486,36 @@
     valid = (jnp.arange(LEN, dtype=jnp.int32) < lengths[0])[:, None].astype(jnp.float32)
     grads = (content_cot.astype(jnp.float32) * valid, query_cot.astype(jnp.float32) * valid)
     q0, k0, v0, attn0 = project(place, low0, small0, group_a0)
-    q0_late = after(q0, far_f1)
-    mixed0, p0, inverse0, dead = mix(
-        lengths, far0, tvec0, q0_late, k0, v0, row_flags, col_flags
-    )
-    x2, y2, plane_a1 = after((x2, y2, plane_a1), mixed0)
-    mine_2 = jnp.concatenate([plane_a1, col_a1, x2, y2])
+    mixed0, p0, inverse0, dead = mix(lengths, far0, tvec0, q0, k0, v0, row_flags, col_flags)
+    x2, y2, far_f1, mixed0, theirs_p0 = join(x2, y2, far_f1, mixed0, theirs_p0)
+    col_f1 = jnp.concatenate([near_1[1:], far_f1])
+    x3 = swap_x(jnp.concatenate([col_f1, y2[:3]]))
+    y3 = swap_y(jnp.concatenate([col_f1, own_f1, oth_f1]))
+    mine_2 = jnp.concatenate([x2, y2, col_a1])
     theirs_2 = swap_core(mine_2)
     group_f0 = gather_group(
-        2, feed_low[0], (0, 0), (0, 4), ((1, 0), (1, 8)), ((2, 8, 4), (2, 15, 2)),
+        2, feed_low[0], (0, 0), (0, 4), ((1, 0), (1, 8)), ((2, 3, 4), (2, 10, 2)),
         (mine_p0, mine_1, mine_2), (theirs_p0, theirs_1, theirs_2),
     )
-    far_f1 = after(far_f1, x2, y2)
-    col_f1 = jnp.concatenate([near_f1, far_f1])
-    x3 = swap_x(jnp.concatenate([col_f1, y2[:3]]))
-    y3 = swap_y(col_f1)
-    plane_f1 = swap_y(after(jnp.concatenate([own_f1, oth_f1]), x2, y2))
     resid0, summed0, pre0, normed0, hidden1, low1 = feed(
         place, small0, hidden_bias0, mixed0, hidden0, attn0, group_f0
     )
-    x3, y3, plane_f1 = after((x3, y3, plane_f1), low1)
+    x3, y3, low1, hidden1 = join(x3, y3, low1, hidden1)
     x4 = swap_x(y3[:3])
     y4 = swap_y(x3[3:6])
-    mine_3 = jnp.concatenate([x3[6:], x3[:6], y3])
+    mine_3 = jnp.concatenate([x3, y3])
     theirs_3 = swap_core(mine_3)
     group_a1 = gather_group(
-        1, (attn_low[1],), (0, 0), (0, 2), ((0, 5), (0, 12)), ((1, 0, 3),),
+        1, attn_low[1], (0, 12), (0, 14), ((0, 0), (0, 7)), ((1, 6, 3),),
         (mine_2, mine_3), (theirs_2, theirs_3),
     )
     q1, k1, v1, attn1 = project(place, low1, small1, group_a1)
-    x4, y4 = after((x4, y4), q1)
-    mine_4 = jnp.concatenate([plane_f1, col_f1, x4, y4])
+    x4, y4, q1 = join(x4, y4, q1)
+    mine_4 = jnp.concatenate([col_f1, x4, y4])
     theirs_4 = swap_core(mine_4)
     group_f1 = gather_group(
-        2, feed_low[1], (0, 0), (0, 4), ((1, 3), (1, 9)), ((0, 10, 3), (0, 13, 3)),
-        (mine_4, mine_3), (theirs_4, theirs_3),
+        2, feed_low[1], (0, 15), (1, 0), ((0, 0), (0, 9)), ((1, 6, 3), (1, 9, 3)),
+        (mine_3, mine_4), (theirs_3, theirs_4),
     )
     mixed1, p1, inverse1, dead = mix(
         lengths, far1, tvec1, q1, k1, v1, row_flags, col_flags
@@ -1539,72 +1542,94 @@
     dresid0, dmix0, dwo0, keep_f0, send_f0, vec_f0, dhidden0 = feed_back(
         place, small0, after(grads, get_a1), summed0, normed0, resid0, pre0, mixed0, attn0, group_f0
     )
-    get_f0 = swap_core(after(send_f0, sides_rf1))
+    get_f0 = swap_core(after(send_f0, sides_rf1, by_a1))
     sides_ra1 = reduce_sides(keep_a1, get_a1, after(by_a1, dmix0))
-    column_f1 = reduce_column(keep_f1, get_f1, after(sides_rf1, dmix0))
-    zfar_f1 = reduce_far(column_f1, place_parts)
     first0 = mix_back(
         0, q0, k0, v0, after(dmix0, by_a1, sides_rf1), mixed0, p0, inverse0, dead
     )
     by_f0 = reduce_corners(keep_f0, after(get_f0, first0[0]))
+    column_f1 = reduce_column(keep_f1, get_f1, after(sides_rf1, first0[0]))
+    zfar_f1 = reduce_far(column_f1, place_parts)
     second0 = mix_back(
         3, after(q0, get_f0, first0[0]), k0, v0, dmix0, mixed0, p0, inverse0, dead
     )
-    zfar_f1, sides_ra1 = after((zfar_f1, sides_ra1), second0[0])
+    by_f0, sides_ra1, zfar_f1, second0_q = join(by_f0, sides_ra1, zfar_f1, second0[0])
+    sides_rf0 = reduce_sides(keep_f0, get_f0, by_f0)
     keep_a0, send_a0, vec_a0 = weight_back(
-        place, low0, after(first0[:3], by_f0), second0[:3], dwo0
-    )
-    sides_rf0 = reduce_sides(keep_f0, get_f0, after(by_f0, second0[0]))
+        place, low0, first0[:3], [second0_q, second0[1], second0[2]], dwo0
+    )
     get_a0 = swap_core(send_a0)
+    znear_f1 = reduce_near(column_f1, zfar_f1, place_parts)
+    column_a1 = reduce_column(keep_a1, get_a1, sides_ra1)
+    zfar_a1 = reduce_far(column_a1, place_parts)
+    small_sum = jnp.stack(
+        [
+            jnp.concatenate(
+                [
+                    attn_vec.reshape(-1),
+                    feed_vec[2:].reshape(-1),
+                    dhidden.reshape(-1),
+                    table_grad(jnp.concatenate([first[3], second[3]]), onehot).reshape(-1),
+                ]
+            )
+            for attn_vec, feed_vec, dhidden, first, second in (
+                (vec_a0, vec_f0, dhidden0, first0, second0),
+                (vec_a1, vec_f1, dhidden1, first1, second1),
+            )
+        ]
+    )
+    small_sum = small_sum + swap_core(small_sum)
+    sides_rf0, get_a0, znear_f1, zfar_a1, small_sum = join(
+        sides_rf0, get_a0, znear_f1, zfar_a1, small_sum
+    )
+    column_f0 = reduce_column(keep_f0, get_f0, sides_rf0)
+    zfar_f0 = reduce_far(column_f0, place_parts)
     by_a0 = reduce_corners(keep_a0, get_a0)
-    znear_f1 = reduce_near(column_f1, after(zfar_f1, get_a0), place_parts)
-    column_a1 = reduce_column(keep_a1, get_a1, after(sides_ra1, get_a0))
-    zfar_a1 = reduce_far(column_a1, place_parts)
-    content_grad, query_grad = input_back(after(first0[:3], get_a0), second0[:3], attn0, dresid0)
-    column_f0 = reduce_column(keep_f0, get_f0, after(sides_rf0, content_grad))
-    zfar_f0 = reduce_far(column_f0, place_parts)
-    sides_ra0 = reduce_sides(keep_a0, get_a0, after(by_a0, column_f0))
-    znear_a1 = reduce_near(column_a1, after(zfar_a1, column_f0), place_parts)
-    four_f1 = share_quarters(
-        reduce_total(column_f1, zfar_f1, after(znear_f1, column_f0), place_parts), place_parts
-    )
-    column_a0 = reduce_column(keep_a0, get_a0, sides_ra0)
-    shifts_a0 = reduce_direct(after(column_a0, zfar_f0), place_parts)
-    znear_f0 = reduce_near(column_f0, zfar_f0, place_parts)
-    four_a1 = share_quarters(
-        reduce_total(column_a1, zfar_a1, after(znear_a1, column_a0), place_parts), place_parts
-    )
-    four_f0 = share_quarters(
-        reduce_total(column_f0, zfar_f0, znear_f0, place_parts), place_parts
-    )
+    own_f1 = reduce_total(column_f1, zfar_f1, znear_f1, place_parts)
+    pair_f1 = jnp.stack([own_f1, swap_x(own_f1)])
+    content_grad, query_grad = input_back(
+        after(first0[:3], sides_rf0), [second0_q, second0[1], second0[2]], attn0, dresid0
+    )
+    by_a0, pair_f1, content_grad = join(by_a0, pair_f1, content_grad)
+    sides_ra0 = reduce_sides(keep_a0, get_a0, by_a0)
+    znear_a1 = reduce_near(column_a1, zfar_a1, place_parts)
+    four_f1 = share_core(pair_f1, place_parts)
     attn_state = (attn_master, attn_first, attn_second)
     inner_state = (inner_master, inner_first, inner_second)
     outer_state = (outer_master, outer_first, outer_second)
     inner_new = adam("inner", 1, FEED_RATE, inner_state, four_f1, 0, None)
     outer_new = adam("outer", 1, FEED_RATE, outer_state, four_f1, 1, None)
+    sides_ra0, zfar_f0, znear_a1, inner_new, outer_new = join(
+        sides_ra0, zfar_f0, znear_a1, inner_new, outer_new
+    )
+    column_a0 = reduce_column(keep_a0, get_a0, sides_ra0)
+    shifts_a0 = reduce_direct(column_a0, place_parts)
+    znear_f0 = reduce_near(column_f0, zfar_f0, place_parts)
+    own_a1 = reduce_total(column_a1, zfar_a1, znear_a1, place_parts)
+    pair_a1 = jnp.stack([own_a1, swap_x(after(own_a1, column_a0))])
+    shifts_a0, znear_f0, pair_a1 = join(shifts_a0, znear_f0, pair_a1)
+    own_0 = jnp.concatenate(
+        [
+            reduce_total(column_f0, zfar_f0, znear_f0, place_parts),
+            direct_total(column_a0, shifts_a0, place_parts),
+        ]
+    )
+    pair_0 = jnp.stack([own_0, swap_x(own_0)])
+    four_a1 = share_core(pair_a1, place_parts)
+    small_sum = small_sum + swap_y(small_sum)
     attn_new = adam("attn", 1, ATTENTION_RATE, attn_state, four_a1, 0, None)
-    shifts_a0 = after(shifts_a0, inner_new, outer_new, attn_new)
-    four_a0 = share_quarters(direct_total(column_a0, shifts_a0, place_parts), place_parts)
-    small_grads = [
-        jnp.concatenate(
-            [
-                attn_vec.reshape(-1),
-                feed_vec[2:].reshape(-1),
-                dhidden.reshape(-1),
-                table_grad(jnp.concatenate([first[3], second[3]]), onehot).reshape(-1),
-            ]
-        )
-        for attn_vec, feed_vec, dhidden, first, second in (
-            (vec_a0, vec_f0, dhidden0, first0, second0),
-            (vec_a1, vec_f1, dhidden1, first1, second1),
-        )
-    ]
-    small_sum = sum_small(after(jnp.stack(small_grads), column_a0))
+    pair_0, attn_new, small_sum = join(pair_0, attn_new, small_sum)
+    four_0 = share_core(pair_0, place_parts)
+    small_sum = small_sum + swap_x(small_sum)
+    four_0, small_sum = join(four_0, small_sum)
+    small_far = swap_z(small_sum, 1)
+    inner_new = adam("inner", 0, FEED_RATE, inner_state, four_0, 0, tuple(inner_new))
+    small_sum = small_sum + small_far
+    outer_new = adam("outer", 0, FEED_RATE, outer_state, four_0, 1, tuple(outer_new))
+    small_sum = small_sum + swap_z(small_sum, 2)
+    attn_new = adam("attn", 0, ATTENTION_RATE, attn_state, four_0, 2, tuple(attn_new))
     size = small_master.shape[1]
     small_own = lax.dynamic_slice_in_dim(small_sum, lax.axis_index("fsdp") * size, size, 1)
-    inner_new = adam("inner", 0, FEED_RATE, inner_state, four_f0, 0, tuple(inner_new))
-    outer_new = adam("outer", 0, FEED_RATE, outer_state, four_f0, 1, tuple(outer_new))
-    attn_new = adam("attn", 0, ATTENTION_RATE, attn_state, four_a0, 0, tuple(attn_new))
     small_new = adam_update(small_master, small_first, small_second, small_own, SMALL_RATE)
     return (
         (low_out[:LEN], low_out[LEN:], content_grad, query_grad)

time: 670 us -> 616 us (0.919)
  waiting for transfers between devices: 156 us -> 83.4 us
  starting transfers between devices: 61.8 us -> 72.3 us
    ppermute x73 -> x69, waiting for transfers between devices: 156 us -> 83.4 us  [move(): return lax.ppermute(value, AXES, pairs)]
    ppermute x73 -> x69, starting transfers between devices: 61.8 us -> 72.3 us  [move(): return lax.ppermute(value, AXES, pairs)]
    unnamed x105 -> x137, local copies, waits for them, and re-layouts: 16.9 us -> 24.3 us
    convert_element_type x24 -> x23, other arithmetic: 32.3 us -> 37.7 us  [add_low(): return total.astype(jnp.bfloat16)]
  transfers between devices with their start and end apart: 73 -> 69, of which waited for: 25 -> 26; matrix products, arithmetic and copies ran while one was open for 18% -> 19% of each run, Pallas kernels for 32% -> 37%
where the time goes in v5:
time: 616 us; the launch traced here: 605 us
  Pallas kernels  299 us (49%)
  waiting for transfers between devices  83.4 us (14%)
  other arithmetic  78.4 us (13%)
  starting transfers between devices  72.3 us (12%)
  local copies, waits for them, and re-layouts  68.4 us (11%)
    ppermute x69, waiting for transfers between devices, move(): return lax.ppermute(value, AXES, pairs)  83.4 us
    pallas_call x2, Pallas kernels, feed_back(): pl.pallas_call(partial(feed_back_kernel, plan), out_shape=[jax.ShapeDtype...  81.2 us
    ppermute x69, starting transfers between devices, move(): return lax.ppermute(value, AXES, pairs)  72.3 us
    pallas_call x4, Pallas kernels, mix_back(): pl.pallas_call(mix_back_kernel, grid=(H // 4,), out_shape=[jax.ShapeDtype...  49.4 us
    pallas_call x2, Pallas kernels, feed(): pl.pallas_call(partial(feed_kernel, plan), out_shape=[jax.ShapeDtypeStruc...  48.2 us
    pallas_call x2, Pallas kernels, mix(): pl.pallas_call(mix_kernel, grid=(H // 2,), out_shape=[jax.ShapeDtypeStruc...  38.8 us
    convert_element_type x23, other arithmetic, add_low(): return total.astype(jnp.bfloat16)  37.7 us
    pallas_call x6, Pallas kernels, adam(): pl.pallas_call(partial(adam_kernel, rate), grid=(4,), out_shape=[jax.Shap...  27.1 us
  transfers between devices with their start and end apart: 69, of which 26 were waited for; matrix products, arithmetic and copies ran while one was open for 19% of the time, Pallas kernels for 37%

profile of v5, /device:TPU:0, one launch (start us, length us, event | category | flops | bytes accessed | tf_op | source)
XLA Modules:
  0.0 605.5 jit_solution(1700418663705319124)
XLA Ops:
  22.5 4.8 collective-permute-done.4
  46.8 8.2 %collective-permute-done.6 = bf16[3,96,768]{2,1,0:T(8,128)(2,1)S(1)} collective-permute-done((bf16[3,96,768]{2,1,0:T(8,128)(2,1)S(1)}, bf16[3,96,768]{2,1,0:T(8,128)(2,1)S(1)}, u32[]{:S(2)}, u32[]{:S(2)}) %collective-permute-start.6) | collective-permute-done | bytes 442400 | tf_op jit(solution)/shard_map/ppermute | solution.py:175
  55.0 5.8 collective-permute-done.9
  107.9 8.3 %project.2 = (bf16[1024,768]{1,0:T(8,128)(2,1)}, bf16[512,768]{1,0:T(8,128)(2,1)}, bf16[512,768]{1,0:T(8,128)(2,1)}, bf16[4,768,768]{2,1,0:T(8,128)(2,1)}) custom-call(s32[4]{0:T(128)} %pad_add_fusion.place_ref, bf16[1024,768]{1,0:T(8,128)(2,1)} %copy-done.3, f32[8,768]{1,0:T(8,128)} %reshape.988.small_ref, bf16[4,96,768]{2,1,0:T(8,128)(2,1)} %get-tuple-element.458.refs_0_, ...), custom_call_target="tpu_custom_call" | custom-call | flops 2415919104 | bytes 16000000 | tf_op jit(solution)/shard_map/project/pallas_call | solution.py:295
  116.2 19.3 %mix.2 = (bf16[1024,768]{1,0:T(8,128)(2,1)}, bf16[12,512,1024]{2,1,0:T(8,128)(2,1)}, f32[12,1,1024]{2,1,0:T(1,128)}, f32[1,1024]{1,0:T(1,128)}) custom-call(s32[1]{0:T(128)} %copy.235.length_ref, f32[12,2]{1,0:T(8,128)} %pad_maximum_fusion.38.far_ref, bf16[1024,768]{1,0:T(8,128)(2,1)} %get-tuple-element.342.q_ref, ...), custom_call_target="tpu_custom_call" | custom-call | flops 6499999744 | bytes 8000000 | tf_op jit(solution)/shard_map/mix/pallas_call | solution.py:406
  150.3 24.2 %feed.2 = (f32[1024,768]{1,0:T(8,128)}, f32[1024,768]{1,0:T(8,128)}, bf16[4,1024,768]{2,1,0:T(8,128)(2,1)}, bf16[1024,768]{1,0:T(8,128)(2,1)}, f32[1024,768]{1,0:T(8,128)}, /*index=5*/bf16[1024,768]{1,0:T(8,128)(2,1)}) custom-call(s32[4]{0:T(128)} %pad_add_fusion.place_ref, f32[8,768]{1,0:T(8,128)} %reshape.988.small_ref, f32[1,3072]{1,0:T(1,128)} %slice.539.hidden_bias_ref, ...), custom_call_target="tpu_custom_call" | custom-call | flops 10871635968 | bytes 40000000 | tf_op jit(solution)/shard_map/feed/pallas_call | solution.py:614
  187.7 8.3 %project.3 = (bf16[1024,768]{1,0:T(8,128)(2,1)}, bf16[512,768]{1,0:T(8,128)(2,1)}, bf16[512,768]{1,0:T(8,128)(2,1)}, bf16[4,768,768]{2,1,0:T(8,128)(2,1)}) custom-call(s32[4]{0:T(128)} %pad_add_fusion.place_ref, bf16[1024,768]{1,0:T(8,128)(2,1)} %get-tuple-element.277.low_ref, f32[8,768]{1,0:T(8,128)} %reshape.987.small_ref, ...), custom_call_target="tpu_custom_call" | custom-call | flops 2415919104 | bytes 16000000 | tf_op jit(solution)/shard_map/project/pallas_call | solution.py:295
  204.8 19.4 %mix.3 = (bf16[1024,768]{1,0:T(8,128)(2,1)}, bf16[12,512,1024]{2,1,0:T(8,128)(2,1)}, f32[12,1,1024]{2,1,0:T(1,128)}, f32[1,1024]{1,0:T(1,128)}) custom-call(s32[1]{0:T(128)} %copy.235.length_ref, f32[12,2]{1,0:T(8,128)} %pad_maximum_fusion.37.far_ref, bf16[1024,768]{1,0:T(8,128)(2,1)} %get-tuple-element.305.q_ref, ...), custom_call_target="tpu_custom_call" | custom-call | flops 6499999744 | bytes 8000000 | tf_op jit(solution)/shard_map/mix/pallas_call | solution.py:406
  224.3 24.1 %feed.3 = (f32[1024,768]{1,0:T(8,128)}, f32[1024,768]{1,0:T(8,128)}, bf16[4,1024,768]{2,1,0:T(8,128)(2,1)}, bf16[1024,768]{1,0:T(8,128)(2,1)}, f32[1024,768]{1,0:T(8,128)}, /*index=5*/bf16[1024,768]{1,0:T(8,128)(2,1)}) custom-call(s32[4]{0:T(128)} %pad_add_fusion.place_ref, f32[8,768]{1,0:T(8,128)} %reshape.987.small_ref, f32[1,3072]{1,0:T(1,128)} %slice.533.hidden_bias_ref, ...), custom_call_target="tpu_custom_call" | custom-call | flops 10871635968 | bytes 40000000 | tf_op jit(solution)/shard_map/feed/pallas_call | solution.py:614
  248.3 40.7 %feed_back.2 = (f32[1024,768]{1,0:T(8,128)}, bf16[1024,768]{1,0:T(8,128)(2,1)}, bf16[768,768]{1,0:T(8,128)(2,1)}, bf16[2,2,4,2,96,768]{5,4,3,2,1,0:T(8,128)(2,1)...) custom-call(s32[4]{0:T(128)} %pad_add_fusion.place_ref, ...), custom_call_target="tpu_custom_call" | custom-call | flops 21743271936 | bytes 60000000 | tf_op jit(solution)/shard_map/feed_back/pallas_call | solution.py:779
  289.5 12.3 %mix_back.4 = (bf16[1024,384]{1,0:T(8,128)(2,1)}, bf16[512,384]{1,0:T(8,128)(2,1)}, bf16[512,384]{1,0:T(8,128)(2,1)}, f32[6,1,768]{2,1,0:T(1,128)}) custom-call(bf16[1024,768]{1,0:T(8,128)(2,1)} %get-tuple-element.305.q_ref, bf16[512,768]{1,0:T(8,128)(2,1)} %get-tuple-element.280.k_ref, bf16[512,768]{1,0:T(8,128)(2,1)} %get-tuple-element.281.v_ref, ...), custom_call_target="tpu_custom_call" | custom-call | flops 8000000000 | bytes 16000000 | tf_op jit(solution)/shard_map/mix_back/pallas_call | solution.py:508
  305.3 12.4 %mix_back.5 = (bf16[1024,384]{1,0:T(8,128)(2,1)}, bf16[512,384]{1,0:T(8,128)(2,1)}, bf16[512,384]{1,0:T(8,128)(2,1)}, f32[6,1,768]{2,1,0:T(1,128)}) custom-call(bf16[1024,768]{1,0:T(8,128)(2,1)} %get-tuple-element.305.q_ref, bf16[512,768]{1,0:T(8,128)(2,1)} %get-tuple-element.280.k_ref, bf16[512,768]{1,0:T(8,128)(2,1)} %get-tuple-element.281.v_ref, ...), custom_call_target="tpu_custom_call" | custom-call | flops 8000000000 | bytes 16000000 | tf_op jit(solution)/shard_map/mix_back/pallas_call | solution.py:508
  319.9 9.0 %weight_back.2 = (bf16[2,2,4,1,96,768]{5,4,3,2,1,0:T(8,128)(2,1)}, bf16[2,2,4,1,96,768]{5,4,3,2,1,0:T(8,128)(2,1)}, f32[2,768]{1,0:T(2,128)}) custom-call(s32[4]{0:T(128)} %pad_add_fusion.place_ref, bf16[1024,768]{1,0:T(8,128)(2,1)} %get-tuple-element.277.low_ref, bf16[1024,384]{1,0:T(8,128)(2,1)} %get-tuple-element.311.dq_a, ...), custom_call_target="tpu_custom_call" | custom-call | flops 2415919104 | bytes 12000000 | tf_op jit(solution)/shard_map/weight_back/pallas_call | solution.py:853
  336.0 9.9 %input_back.2 = (f32[512,768]{1,0:T(8,128)}, f32[512,768]{1,0:T(8,128)}) custom-call(bf16[1024,384]{1,0:T(8,128)(2,1)} %get-tuple-element.311.dq_a, bf16[512,384]{1,0:T(8,128)(2,1)} %get-tuple-element.312.dk_a, bf16[512,384]{1,0:T(8,128)(2,1)} %get-tuple-element.313.dv_a, bf16[1024,384]{1,0:T(8,128)(2,1)} %get-tuple-element.306.dq_b, ...), custom_call_target="tpu_custom_call" | custom-call | flops 2415919104 | bytes 16000000 | tf_op jit(solution)/shard_map/input_back/pallas_call | solution.py:895
  350.1 40.4 %feed_back.3 = (f32[1024,768]{1,0:T(8,128)}, bf16[1024,768]{1,0:T(8,128)(2,1)}, bf16[768,768]{1,0:T(8,128)(2,1)}, bf16[2,2,4,2,96,768]{5,4,3,2,1,0:T(8,128)(2,1)...) custom-call(s32[4]{0:T(128)} %pad_add_fusion.place_ref, ...), custom_call_target="tpu_custom_call" | custom-call | flops 21743271936 | bytes 60000000 | tf_op jit(solution)/shard_map/feed_back/pallas_call | solution.py:779
  404.9 12.3 %mix_back.6 = (bf16[1024,384]{1,0:T(8,128)(2,1)}, bf16[512,384]{1,0:T(8,128)(2,1)}, bf16[512,384]{1,0:T(8,128)(2,1)}, f32[6,1,768]{2,1,0:T(1,128)}) custom-call(bf16[1024,768]{1,0:T(8,128)(2,1)} %get-tuple-element.342.q_ref, bf16[512,768]{1,0:T(8,128)(2,1)} %get-tuple-element.262.k_ref, bf16[512,768]{1,0:T(8,128)(2,1)} %get-tuple-element.263.v_ref, ...), custom_call_target="tpu_custom_call" | custom-call | flops 8000000000 | bytes 16000000 | tf_op jit(solution)/shard_map/mix_back/pallas_call | solution.py:508
  423.4 12.3 %mix_back.7 = (bf16[1024,384]{1,0:T(8,128)(2,1)}, bf16[512,384]{1,0:T(8,128)(2,1)}, bf16[512,384]{1,0:T(8,128)(2,1)}, f32[6,1,768]{2,1,0:T(1,128)}) custom-call(bf16[1024,768]{1,0:T(8,128)(2,1)} %get-tuple-element.342.q_ref, bf16[512,768]{1,0:T(8,128)(2,1)} %get-tuple-element.262.k_ref, bf16[512,768]{1,0:T(8,128)(2,1)} %get-tuple-element.263.v_ref, ...), custom_call_target="tpu_custom_call" | custom-call | flops 8000000000 | bytes 16000000 | tf_op jit(solution)/shard_map/mix_back/pallas_call | solution.py:508
  462.9 9.0 %weight_back.3 = (bf16[2,2,4,1,96,768]{5,4,3,2,1,0:T(8,128)(2,1)}, bf16[2,2,4,1,96,768]{5,4,3,2,1,0:T(8,128)(2,1)}, f32[2,768]{1,0:T(2,128)}) custom-call(s32[4]{0:T(128)} %pad_add_fusion.place_ref, bf16[1024,768]{1,0:T(8,128)(2,1)} %copy-done.3, bf16[1024,384]{1,0:T(8,128)(2,1)} %get-tuple-element.369.dq_a, bf16[512,384]{1,0:T(8,128)(2,1)} %get-tuple-element.370.dk_a, ...), custom_call_target="tpu_custom_call" | custom-call | flops 2415919104 | bytes 12000000 | tf_op jit(solution)/shard_map/weight_back/pallas_call | solution.py:853
  484.8 12.2 %collective-permute-done.47 = bf16[2,1,96,768]{3,2,1,0:T(8,128)(2,1)S(1)} collective-permute-done((bf16[2,1,96,768]{3,2,1,0:T(8,128)(2,1)S(1)}, bf16[2,1,96,768]{3,2,1,0:T(8,128)(2,1)S(1)}, u32[]{:S(2)}, u32[]{:S(2)}) %collective-permute-start.47) | collective-permute-done | bytes 294944 | tf_op jit(solution)/shard_map/ppermute | solution.py:175
  509.9 9.6 %input_back.3 = (f32[512,768]{1,0:T(8,128)}, f32[512,768]{1,0:T(8,128)}) custom-call(bf16[1024,384]{1,0:T(8,128)(2,1)} %get-tuple-element.369.dq_a, bf16[512,384]{1,0:T(8,128)(2,1)} %get-tuple-element.370.dk_a, bf16[512,384]{1,0:T(8,128)(2,1)} %get-tuple-element.371.dv_a, bf16[1024,384]{1,0:T(8,128)(2,1)} %get-tuple-element.344.dq_b, ...), custom_call_target="tpu_custom_call" | custom-call | flops 2415919104 | bytes 16000000 | tf_op jit(solution)/shard_map/input_back/pallas_call | solution.py:895
  557.1 5.1 collective-permute-done.58
  570.5 5.7 collective-permute-done.62
  595.5 4.5 adam.10
  600.0 4.5 adam.11
  (443 shorter events, 280.2 us)
Async XLA Ops:
  29.2 31.6 %collective-permute-start.7 = (bf16[4,96,768]{2,1,0:T(8,128)(2,1)S(1)}, bf16[4,96,768]{2,1,0:T(8,128)(2,1)S(1)}, u32[]{:S(2)}, u32[]{:S(2)}) collective-permute-start(bf16[4,96,768]{2,1,0:T(8,128)(2,1)S(1)} %get-tuple-element.491), channel_id=1, source_target_pairs={{0,4},{1,5},{2,6},{3,7},{4,0},{5,1},{6,2},{7,3},{8,12},{9,13},{10,... | collective-permute-start | bytes 1769480 | tf_op jit(solution)/shard_map/ppermute | solution.py:175
  32.5 28.3 %collective-permute-start.8 = (bf16[4,96,768]{2,1,0:T(8,128)(2,1)S(1)}, bf16[4,96,768]{2,1,0:T(8,128)(2,1)S(1)}, u32[]{:S(2)}, u32[]{:S(2)}) collective-permute-start(bf16[4,96,768]{2,1,0:T(8,128)(2,1)S(1)} %get-tuple-element.247), channel_id=1, source_target_pairs={{0,1},{1,0},{2,3},{3,2},{4,5},{5,4},{6,7},{7,6},{8,9},{9,8},{10,11... | collective-permute-start | bytes 1769480 | tf_op jit(solution)/shard_map/ppermute | solution.py:175
  39.2 21.6 %collective-permute-start.9 = (bf16[3,96,768]{2,1,0:T(8,128)(2,1)S(1)}, bf16[3,96,768]{2,1,0:T(8,128)(2,1)S(1)}, u32[]{:S(2)}, u32[]{:S(2)}) collective-permute-start(bf16[3,96,768]{2,1,0:T(8,128)(2,1)S(1)} %pad_maximum_fusion.22), channel_id=1, source_target_pairs={{0,2},{1,3},{2,0},{3,1},{4,6},{5,7},{6,4},{7,5},{8,10},{9,11},{10,... | collective-permute-start | bytes 1327112 | tf_op jit(solution)/shard_map/ppermute | solution.py:175
  63.4 25.1 %collective-permute-start.10 = (bf16[8,96,768]{2,1,0:T(8,128)(2,1)}, bf16[8,96,768]{2,1,0:T(8,128)(2,1)S(1)}, u32[]{:S(2)}, u32[]{:S(2)}) collective-permute-start(bf16[8,96,768]{2,1,0:T(8,128)(2,1)} %pad_maximum_fusion.3), channel_id=1, source_target_pairs={{0,16},{1,17},{2,18},{3,19},{4,20},{5,21},{6,22},{7,23},{8,24},{9,... | collective-permute-start | bytes 3538952 | tf_op jit(solution)/shard_map/ppermute | solution.py:175
  65.0 22.2 %collective-permute-start.11 = (bf16[7,96,768]{2,1,0:T(8,128)(2,1)}, bf16[7,96,768]{2,1,0:T(8,128)(2,1)S(1)}, u32[]{:S(2)}, u32[]{:S(2)}) collective-permute-start(bf16[7,96,768]{2,1,0:T(8,128)(2,1)} %pad_maximum_fusion.8), channel_id=1, source_target_pairs={{0,1},{1,0},{2,3},{3,2},{4,5},{5,4},{6,7},{7,6},{8,9},{9,8},{10,11... | collective-permute-start | bytes 3096584 | tf_op jit(solution)/shard_map/ppermute | solution.py:175
  90.6 44.9 %collective-permute-start.17 = (bf16[7,96,768]{2,1,0:T(8,128)(2,1)}, bf16[7,96,768]{2,1,0:T(8,128)(2,1)}, u32[]{:S(2)}, u32[]{:S(2)}) collective-permute-start(bf16[7,96,768]{2,1,0:T(8,128)(2,1)} %pad_maximum_fusion.9), channel_id=1, source_target_pairs={{0,16},{1,17},{2,18},{3,19},{4,20},{5,21},{6,22},{7,23},{8,24},{9,... | collective-permute-start | bytes 3096584 | tf_op jit(solution)/shard_map/ppermute | solution.py:175
  96.4 39.2 %collective-permute-start.18 = (bf16[7,96,768]{2,1,0:T(8,128)(2,1)}, bf16[7,96,768]{2,1,0:T(8,128)(2,1)}, u32[]{:S(2)}, u32[]{:S(2)}) collective-permute-start(bf16[7,96,768]{2,1,0:T(8,128)(2,1)} %fusion.38), channel_id=1, source_target_pairs={{0,1},{1,0},{2,3},{3,2},{4,5},{5,4},{6,7},{7,6},{8,9},{9,8},{10,11... | collective-permute-start | bytes 3096584 | tf_op jit(solution)/shard_map/ppermute | solution.py:175
  98.8 36.8 %collective-permute-start.19 = (bf16[4,96,768]{2,1,0:T(8,128)(2,1)}, bf16[4,96,768]{2,1,0:T(8,128)(2,1)S(1)}, u32[]{:S(2)}, u32[]{:S(2)}) collective-permute-start(bf16[4,96,768]{2,1,0:T(8,128)(2,1)} %pad_maximum_fusion.14), channel_id=1, source_target_pairs={{0,4},{1,5},{2,6},{3,7},{4,0},{5,1},{6,2},{7,3},{8,12},{9,13},{10,... | collective-permute-start | bytes 1769480 | tf_op jit(solution)/shard_map/ppermute | solution.py:175
  105.6 30.0 %collective-permute-start.21 = (bf16[10,96,768]{2,1,0:T(8,128)(2,1)}, bf16[10,96,768]{2,1,0:T(8,128)(2,1)}, u32[]{:S(2)}, u32[]{:S(2)}) collective-permute-start(bf16[10,96,768]{2,1,0:T(8,128)(2,1)} %copy-done.45), channel_id=1, source_target_pairs={{0,8},{1,9},{2,10},{3,11},{4,12},{5,13},{6,14},{7,15},{8,0},{9,1},... | collective-permute-start | bytes 4423688 | tf_op jit(solution)/shard_map/ppermute | solution.py:175
  143.7 34.6 %collective-permute-start.23 = (bf16[10,96,768]{2,1,0:T(8,128)(2,1)}, bf16[10,96,768]{2,1,0:T(8,128)(2,1)}, u32[]{:S(2)}, u32[]{:S(2)}) collective-permute-start(bf16[10,96,768]{2,1,0:T(8,128)(2,1)} %fusion.40), channel_id=1, source_target_pairs={{0,1},{1,0},{2,3},{3,2},{4,5},{5,4},{6,7},{7,6},{8,9},{9,8},{10,11... | collective-permute-start | bytes 4423688 | tf_op jit(solution)/shard_map/ppermute | solution.py:175
  145.1 31.1 %collective-permute-start.22 = (bf16[9,96,768]{2,1,0:T(8,128)(2,1)S(1)}, bf16[9,96,768]{2,1,0:T(8,128)(2,1)S(1)}, u32[]{:S(2)}, u32[]{:S(2)}) collective-permute-start(bf16[9,96,768]{2,1,0:T(8,128)(2,1)S(1)} %pad_maximum_fusion.2), channel_id=1, source_target_pairs={{0,16},{1,17},{2,18},{3,19},{4,20},{5,21},{6,22},{7,23},{8,24},{9,... | collective-permute-start | bytes 3981320 | tf_op jit(solution)/shard_map/ppermute | solution.py:175
  200.2 24.0 %collective-permute-start.28 = (bf16[12,96,768]{2,1,0:T(8,128)(2,1)S(1)}, bf16[12,96,768]{2,1,0:T(8,128)(2,1)}, u32[]{:S(2)}, u32[]{:S(2)}) collective-permute-start(bf16[12,96,768]{2,1,0:T(8,128)(2,1)S(1)} %pad_maximum_fusion.1.refs_3_), channel_id=1, source_target_pairs={{0,8},{1,9},{2,10},{3,11},{4,12},{5,13},{6,14},{7,15},{8,0},{9,1},... | collective-permute-start | bytes 5308424 | tf_op jit(solution)/shard_map/ppermute | solution.py:175
  333.0 57.5 %collective-permute-start.35 = (bf16[4,2,96,768]{3,2,1,0:T(8,128)(2,1)S(1)}, bf16[4,2,96,768]{3,2,1,0:T(8,128)(2,1)}, u32[]{:S(2)}, u32[]{:S(2)}) collective-permute-start(bf16[4,2,96,768]{3,2,1,0:T(8,128)(2,1)S(1)} %pad_maximum_fusion.4), channel_id=1, source_target_pairs={{0,16},{1,17},{2,18},{3,19},{4,20},{5,21},{6,22},{7,23},{8,24},{9,... | collective-permute-start | bytes 3538952 | tf_op jit(solution)/shard_map/ppermute | solution.py:175
  335.4 55.2 %collective-permute-start.36 = (bf16[4,2,96,768]{3,2,1,0:T(8,128)(2,1)}, bf16[4,2,96,768]{3,2,1,0:T(8,128)(2,1)}, u32[]{:S(2)}, u32[]{:S(2)}) collective-permute-start(bf16[4,2,96,768]{3,2,1,0:T(8,128)(2,1)} %pad_maximum_fusion.5), channel_id=1, source_target_pairs={{0,1},{1,0},{2,3},{3,2},{4,5},{5,4},{6,7},{7,6},{8,9},{9,8},{10,11... | collective-permute-start | bytes 3538952 | tf_op jit(solution)/shard_map/ppermute | solution.py:175
  347.8 42.7 %collective-permute-start.33 = (bf16[2,1,96,768]{3,2,0,1:T(8,128)(2,1)}, bf16[2,1,96,768]{3,2,0,1:T(8,128)(2,1)}, u32[]{:S(2)}, u32[]{:S(2)}) collective-permute-start(bf16[2,1,96,768]{3,2,0,1:T(8,128)(2,1)} %slice_bitcast_fusion.7), channel_id=1, source_target_pairs={{0,16},{1,17},{2,18},{3,19},{4,20},{5,21},{6,22},{7,23},{8,24},{9,... | collective-permute-start | bytes 884744 | tf_op jit(solution)/shard_map/ppermute | solution.py:175
  348.7 41.9 %collective-permute-start.34 = (bf16[2,1,96,768]{3,2,0,1:T(8,128)(2,1)S(1)}, bf16[2,1,96,768]{3,2,0,1:T(8,128)(2,1)}, u32[]{:S(2)}, u32[]{:S(2)}) collective-permute-start(bf16[2,1,96,768]{3,2,0,1:T(8,128)(2,1)S(1)} %slice_bitcast_fusion.6), channel_id=1, source_target_pairs={{0,1},{1,0},{2,3},{3,2},{4,5},{5,4},{6,7},{7,6},{8,9},{9,8},{10,11... | collective-permute-start | bytes 884744 | tf_op jit(solution)/shard_map/ppermute | solution.py:175
  390.6 32.8 %collective-permute-start.37 = (bf16[2,2,4,2,96,768]{5,4,3,2,1,0:T(8,128)(2,1)}, bf16[2,2,4,2,96,768]{5,4,3,2,1,0:T(8,128)(2,1)}, u32[]{:S(2)}, u32[]{:S(2)}) collective-permute-start(bf16[2,2,4,2,96,768]{5,4,3,2,1,0:T(8,128)(2,1)} %get-tuple-element.336), channel_id=1, source_target_pairs={{0,8},{1,9},{2,10},{3,11},{4,12},{5,13},{6,14},{7,15},{8,0},{9,1},... | collective-permute-start | bytes 14155784 | tf_op jit(solution)/shard_map/ppermute | solution.py:175
  402.2 50.3 %collective-permute-start.40 = (bf16[4,1,96,768]{3,2,0,1:T(8,128)(2,1)}, bf16[4,1,96,768]{3,2,0,1:T(8,128)(2,1)}, u32[]{:S(2)}, u32[]{:S(2)}) collective-permute-start(bf16[4,1,96,768]{3,2,0,1:T(8,128)(2,1)} %pad_maximum_fusion.15), channel_id=1, source_target_pairs={{0,16},{1,17},{2,18},{3,19},{4,20},{5,21},{6,22},{7,23},{8,24},{9,... | collective-permute-start | bytes 1769480 | tf_op jit(solution)/shard_map/ppermute | solution.py:175
  404.3 48.2 %collective-permute-start.41 = (bf16[4,1,96,768]{3,2,0,1:T(8,128)(2,1)}, bf16[4,1,96,768]{3,2,0,1:T(8,128)(2,1)}, u32[]{:S(2)}, u32[]{:S(2)}) collective-permute-start(bf16[4,1,96,768]{3,2,0,1:T(8,128)(2,1)} %pad_maximum_fusion.16), channel_id=1, source_target_pairs={{0,1},{1,0},{2,3},{3,2},{4,5},{5,4},{6,7},{7,6},{8,9},{9,8},{10,11... | collective-permute-start | bytes 1769480 | tf_op jit(solution)/shard_map/ppermute | solution.py:175
  421.1 31.4 %collective-permute-start.42 = (bf16[2,2,96,768]{3,2,1,0:T(8,128)(2,1)}, bf16[2,2,96,768]{3,2,1,0:T(8,128)(2,1)}, u32[]{:S(2)}, u32[]{:S(2)}) collective-permute-start(bf16[2,2,96,768]{3,2,1,0:T(8,128)(2,1)} %pad_maximum_fusion.17), channel_id=1, source_target_pairs={{0,4},{1,5},{2,6},{3,7},{4,0},{5,1},{6,2},{7,3},{8,12},{9,13},{10,... | collective-permute-start | bytes 1769480 | tf_op jit(solution)/shard_map/ppermute | solution.py:175
  459.2 37.9 %collective-permute-start.43 = (bf16[4,2,96,768]{3,2,1,0:T(8,128)(2,1)}, bf16[4,2,96,768]{3,2,1,0:T(8,128)(2,1)}, u32[]{:S(2)}, u32[]{:S(2)}) collective-permute-start(bf16[4,2,96,768]{3,2,1,0:T(8,128)(2,1)} %pad_maximum_fusion.6), channel_id=1, source_target_pairs={{0,16},{1,17},{2,18},{3,19},{4,20},{5,21},{6,22},{7,23},{8,24},{9,... | collective-permute-start | bytes 3538952 | tf_op jit(solution)/shard_map/ppermute | solution.py:175
  461.7 35.3 %collective-permute-start.44 = (bf16[4,2,96,768]{3,2,1,0:T(8,128)(2,1)}, bf16[4,2,96,768]{3,2,1,0:T(8,128)(2,1)}, u32[]{:S(2)}, u32[]{:S(2)}) collective-permute-start(bf16[4,2,96,768]{3,2,1,0:T(8,128)(2,1)} %pad_maximum_fusion.7), channel_id=1, source_target_pairs={{0,1},{1,0},{2,3},{3,2},{4,5},{5,4},{6,7},{7,6},{8,9},{9,8},{10,11... | collective-permute-start | bytes 3538952 | tf_op jit(solution)/shard_map/ppermute | solution.py:175
  471.9 25.1 %collective-permute-start.45 = (bf16[2,2,4,1,96,768]{5,4,3,2,1,0:T(8,128)(2,1)}, bf16[2,2,4,1,96,768]{5,4,3,2,1,0:T(8,128)(2,1)}, u32[]{:S(2)}, u32[]{:S(2)}) collective-permute-start(bf16[2,2,4,1,96,768]{5,4,3,2,1,0:T(8,128)(2,1)} %get-tuple-element.351), channel_id=1, source_target_pairs={{0,8},{1,9},{2,10},{3,11},{4,12},{5,13},{6,14},{7,15},{8,0},{9,1},... | collective-permute-start | bytes 7077896 | tf_op jit(solution)/shard_map/ppermute | solution.py:175
  509.9 30.7 %collective-permute-start.54 = (bf16[2,2,96,768]{3,2,1,0:T(8,128)(2,1)}, bf16[2,2,96,768]{3,2,1,0:T(8,128)(2,1)}, u32[]{:S(2)}, u32[]{:S(2)}) collective-permute-start(bf16[2,2,96,768]{3,2,1,0:T(8,128)(2,1)} %pad_maximum_fusion.21), channel_id=1, source_target_pairs={{0,4},{1,5},{2,6},{3,7},{4,0},{5,1},{6,2},{7,3},{8,12},{9,13},{10,... | collective-permute-start | bytes 1769480 | tf_op jit(solution)/shard_map/ppermute | solution.py:175
  (103 other events, 1120.0 us)

commit v6 on v5

--- a/solution.py
+++ b/solution.py
@@ -272,21 +272,43 @@
     return copies
 
 
-def project_kernel(plan, place_ref, low_ref, small_ref, *refs):
-    pieces = refs[:-7]
-    q_ref, k_ref, v_ref, w_out, w_ref, sems, out_sem = refs[-7:]
-    for copy in start_fetch(("attn",), plan, place_ref, pieces, (w_ref,), sems):
+def project_kernel(plan, place_ref, small_ref, low_any, *refs):
+    pieces = refs[:-14]
+    (
+        q_out, k_out, v_out, w_out, low_ref, q_ref, k_ref, v_ref, w_ref,
+        sems, load_sem, keep_sem, store_sems, unused,
+    ) = refs[-14:]
+    load = pltpu.make_async_copy(low_any, low_ref, load_sem)
+    load.start()
+    fetches = start_fetch(("attn",), plan, place_ref, pieces, (w_ref,), sems)
+    load.wait()
+    for copy in fetches:
         copy.wait()
-    keep = pltpu.make_async_copy(w_ref, w_out, out_sem)
+    keep = pltpu.make_async_copy(w_ref, w_out, keep_sem)
     keep.start()
     bias_q = small_ref[0:1, :]
     bias_v = small_ref[1:2, :]
+    stores = []
+
+    def store(source, target):
+        copy = pltpu.make_async_copy(source, target, store_sems.at[len(stores)])
+        copy.start()
+        stores.append(copy)
+
     for row in range(0, TALL, HALF):
-        rows = low_ref[row : row + HALF, :]
-        q_ref[row : row + HALF, :] = (dot_nn(rows, w_ref[0]) + bias_q).astype(jnp.bfloat16)
+        span = slice(row, row + HALF)
+        rows = low_ref[span, :]
+        q_ref[span, :] = (dot_nn(rows, w_ref[0]) + bias_q).astype(jnp.bfloat16)
         if row < LEN:
-            k_ref[row : row + HALF, :] = dot_nn(rows, w_ref[1]).astype(jnp.bfloat16)
-            v_ref[row : row + HALF, :] = (dot_nn(rows, w_ref[2]) + bias_v).astype(jnp.bfloat16)
+            k_ref[span, :] = dot_nn(rows, w_ref[1]).astype(jnp.bfloat16)
+            v_ref[span, :] = (dot_nn(rows, w_ref[2]) + bias_v).astype(jnp.bfloat16)
+        if row == LEN - HALF:
+            store(k_ref, k_out)
+            store(v_ref, v_out)
+            store(q_ref.at[:LEN, :], q_out.at[:LEN, :])
+    store(q_ref.at[LEN:, :], q_out.at[LEN:, :])
+    for copy in stores:
+        copy.wait()
     keep.wait()
 
 
@@ -300,17 +322,24 @@
             jax.ShapeDtypeStruct((LEN, D), jnp.bfloat16),
             jax.ShapeDtypeStruct((4, D, D), jnp.bfloat16),
         ],
-        in_specs=[SMEM_SPEC, VMEM_SPEC, VMEM_SPEC] + [ANY_SPEC] * len(pieces),
-        out_specs=[VMEM_SPEC] * 3 + [ANY_SPEC],
+        in_specs=[SMEM_SPEC, VMEM_SPEC, ANY_SPEC] + [ANY_SPEC] * len(pieces),
+        out_specs=[ANY_SPEC] * 4,
         scratch_shapes=[
+            pltpu.VMEM((TALL, D), jnp.bfloat16),
+            pltpu.VMEM((TALL, D), jnp.bfloat16),
+            pltpu.VMEM((LEN, D), jnp.bfloat16),
+            pltpu.VMEM((LEN, D), jnp.bfloat16),
             pltpu.VMEM((4, D, D), jnp.bfloat16),
             pltpu.SemaphoreType.DMA((32,)),
+            pltpu.SemaphoreType.DMA,
+            pltpu.SemaphoreType.DMA,
+            pltpu.SemaphoreType.DMA((4,)),
             pltpu.SemaphoreType.DMA,
         ],
         compiler_params=PARAMS,
         cost_estimate=pl.CostEstimate(flops=2 * 2048 * D * D, bytes_accessed=16000000, transcendentals=0),
         name="project",
-    )(place, low, small, *pieces)
+    )(place, small, low, *pieces)
 
 
 def build_masks(length, row_flags, col_flags, mask_ref, alive_ref):
@@ -436,11 +465,10 @@
     )(length, far, q, k, v, row_flags, col_flags, tvec)
 
 
-def mix_back_kernel(
-    q_ref, k_ref, v_ref, da_ref, a_ref, p_ref, inverse_ref, dead_ref,
-    dq_ref, dk_ref, dv_ref, table_ref,
-    s_ref, near_ref, da_t, low_t, q_t, g_ref,
-):
+def mix_back_kernel(q_ref, k_ref, v_ref, da_ref, a_ref, p_ref, inverse_ref, dead_ref, *refs):
+    (
+        dq_ref, dk_ref, dv_ref, table_ref, s_ref, near_ref, da_t, low_t, q_t, g_ref,
+    ) = refs[-10:]
     keys = k_ref[...].astype(jnp.float32) * SCORE_SCALE
     keys_t = keys.T.astype(jnp.bfloat16)
     q_t[...] = q_ref[...].astype(jnp.float32).T.astype(jnp.bfloat16)
@@ -502,16 +530,16 @@
     dq_ref[...] = da_t[...].T.astype(jnp.bfloat16)
 
 
-def mix_back(first, q, k, v, da, a, p, inverse, dead):
+def mix_back(first, q, k, v, da, a, p, inverse, dead, held=()):
     tall = pl.BlockSpec((TALL, 128), lambda i: (0, i + first))
     short = pl.BlockSpec((LEN, 128), lambda i: (0, i + first))
     return pl.pallas_call(
         mix_back_kernel,
         grid=(H // 4,),
         out_shape=[
-            jax.ShapeDtypeStruct((TALL, D // 2), jnp.bfloat16),
-            jax.ShapeDtypeStruct((LEN, D // 2), jnp.bfloat16),
-            jax.ShapeDtypeStruct((LEN, D // 2), jnp.bfloat16),
+            jax.ShapeDtypeStruct((TALL, D), jnp.bfloat16),
+            jax.ShapeDtypeStruct((LEN, D), jnp.bfloat16),
+            jax.ShapeDtypeStruct((LEN, D), jnp.bfloat16),
             jax.ShapeDtypeStruct((H // 2, 1, 768), jnp.float32),
         ],
         in_specs=[
@@ -519,13 +547,10 @@
             pl.BlockSpec((2, LEN, TALL), lambda i: (i + first, 0, 0)),
             pl.BlockSpec((2, 1, TALL), lambda i: (i + first, 0, 0)),
             pl.BlockSpec((1, TALL), lambda i: (0, 0)),
-        ],
-        out_specs=[
-            pl.BlockSpec((TALL, 128), lambda i: (0, i)),
-            pl.BlockSpec((LEN, 128), lambda i: (0, i)),
-            pl.BlockSpec((LEN, 128), lambda i: (0, i)),
-            pl.BlockSpec((2, 1, 768), lambda i: (i, 0, 0)),
-        ],
+        ]
+        + [ANY_SPEC] * len(held),
+        out_specs=[tall, short, short, pl.BlockSpec((2, 1, 768), lambda i: (i, 0, 0))],
+        input_output_aliases={8 + index: index for index in range(len(held))},
         scratch_shapes=[
             pltpu.VMEM((2, LEN, TALL), jnp.bfloat16),
             pltpu.VMEM((2, 128, 512), jnp.float32),
@@ -537,95 +562,120 @@
         compiler_params=PARAMS,
         cost_estimate=pl.CostEstimate(flops=8000000000, bytes_accessed=16000000, transcendentals=0),
         name="mix_back",
-    )(q, k, v, da, a, p, inverse, dead)
+    )(q, k, v, da, a, p, inverse, dead, *held)
 
 
 GELU_SCALE = 0.7978845608028654
 GELU_CUBE = 0.044715
 
 
-def feed_kernel(plan, place_ref, small_ref, hidden_bias_ref, mix_any, hidden_any, attn_any, *refs):
-    pieces = refs[:-20]
+def feed_rows(rows, small_ref, hidden_bias_ref, resid, normed_ref, pre_ref, inner_ref, outer_ref):
+    unit, scale = norm_parts(resid)
+    normed = unit * small_ref[3:4, :] + small_ref[4:5, :]
+    low = normed.astype(jnp.bfloat16)
+    normed_ref[rows, :] = low
+    total = normed + small_ref[5:6, :]
+    for chunk in range(4):
+        pre = dot_nn(low, inner_ref[chunk]) + hidden_bias_ref[:, chunk * D : chunk * D + D]
+        pre_ref[chunk, rows, :] = pre.astype(jnp.bfloat16)
+        tanh = jnp.tanh(GELU_SCALE * (pre + GELU_CUBE * (pre * pre * pre)))
+        active = (pre * (0.5 + 0.5 * tanh)).astype(jnp.bfloat16)
+        total = total + dot_nn(active, outer_ref[chunk])
+    return total
+
+
+def norm_two_back(unit, scale, grad, small_ref, sums):
+    back = norm_back(unit, scale, grad, small_ref[6:7, :])
+    low = back.astype(jnp.bfloat16)
+    parts = (low.astype(jnp.float32), grad * unit, grad)
+    return back, low, [
+        total + jnp.sum(part, axis=0, keepdims=True) for total, part in zip(sums, parts)
+    ]
+
+
+def issue(pairs, sems, first=0):
+    copies = [
+        pltpu.make_async_copy(source, target, sems.at[first + index])
+        for index, (source, target) in enumerate(pairs)
+    ]
+    for copy in copies:
+        copy.start()
+    return copies
+
+
+def finish(copies):
+    for copy in copies:
+        copy.wait()
+
+
+def storer(sems):
+    copies = []
+
+    def store(source, target):
+        copy = pltpu.make_async_copy(source, target, sems.at[len(copies)])
+        copy.start()
+        copies.append(copy)
+
+    return store, copies
+
+
+def feed_kernel(
+    plan, place_ref, small_ref, hidden_bias_ref, mix_any, hidden_any, attn_any, *refs
+):
     (
-        resid_out, summed_out, pre_out, normed_out, next_out, low_out,
+        resid_out, pre_out, normed_out, low_out, summed_out,
         mix_ref, hidden_ref, wo_ref, inner_ref, outer_ref, resid_ref, total_ref, normed_ref,
-        pre_ref, next_ref, low_ref, sems, load_sems, store_sems,
-    ) = refs[-20:]
-    loads = [
-        pltpu.make_async_copy(mix_any, mix_ref, load_sems.at[0]),
-        pltpu.make_async_copy(attn_any.at[3], wo_ref, load_sems.at[1]),
-        pltpu.make_async_copy(hidden_any, hidden_ref, load_sems.at[2]),
-    ]
-    for load in loads:
-        load.start()
-    fetches = start_fetch(("inner", "outer"), plan, place_ref, pieces, (inner_ref, outer_ref), sems)
-    for load in loads:
-        load.wait()
+        pre_ref, low_ref, sems, load_sems, store_sems,
+    ) = refs[-18:]
+    finish(
+        issue(
+            ((mix_any, mix_ref), (attn_any.at[3], wo_ref), (hidden_any, hidden_ref)), load_sems
+        )
+    )
+    fetches = start_fetch(
+        ("inner", "outer"), plan, place_ref, refs[:-18], (inner_ref, outer_ref), sems
+    )
     for row in range(0, TALL, HALF):
         rows = slice(row, row + HALF)
-        resid = hidden_ref[rows, :] + dot_nn(mix_ref[rows, :], wo_ref[...]) + small_ref[2:3, :]
-        resid_ref[rows, :] = resid
-        unit, scale = norm_parts(resid)
-        normed = unit * small_ref[3:4, :] + small_ref[4:5, :]
-        normed_ref[rows, :] = normed.astype(jnp.bfloat16)
-        total_ref[rows, :] = normed + small_ref[5:6, :]
-    stores = [
-        pltpu.make_async_copy(resid_ref, resid_out, store_sems.at[0]),
-        pltpu.make_async_copy(normed_ref, normed_out, store_sems.at[8]),
-    ]
-    for store in stores:
-        store.start()
-    for fetch in fetches:
-        fetch.wait()
-    for chunk in range(4):
-        for row in range(0, TALL, HALF):
-            rows = slice(row, row + HALF)
-            pre = dot_nn(normed_ref[rows, :], inner_ref[chunk]) + hidden_bias_ref[
-                :, chunk * D : chunk * D + D
-            ]
-            pre_ref[chunk, rows, :] = pre.astype(jnp.bfloat16)
-            tanh = jnp.tanh(GELU_SCALE * (pre + GELU_CUBE * (pre * pre * pre)))
-            active = (pre * (0.5 + 0.5 * tanh)).astype(jnp.bfloat16)
-            total_ref[rows, :] += dot_nn(active, outer_ref[chunk])
-        store = pltpu.make_async_copy(
-            pre_ref.at[chunk], pre_out.at[chunk], store_sems.at[1 + chunk]
-        )
-        store.start()
-        stores.append(store)
-    store = pltpu.make_async_copy(total_ref, summed_out, store_sems.at[5])
-    store.start()
-    stores.append(store)
+        resid_ref[rows, :] = (
+            hidden_ref[rows, :].astype(jnp.float32)
+            + dot_nn(mix_ref[rows, :], wo_ref[...])
+            + small_ref[2:3, :]
+        )
+    finish(fetches)
+    store, stores = storer(store_sems)
+    store(resid_ref, resid_out)
     for row in range(0, TALL, HALF):
         rows = slice(row, row + HALF)
-        unit, scale = norm_parts(total_ref[rows, :])
+        total = feed_rows(
+            rows, small_ref, hidden_bias_ref, resid_ref[rows, :], normed_ref, pre_ref, inner_ref,
+            outer_ref,
+        )
+        total_ref[rows, :] = total
+        store(pre_ref.at[:, rows, :], pre_out.at[:, rows, :])
+        store(total_ref.at[rows, :], summed_out.at[rows, :])
+        store(normed_ref.at[rows, :], normed_out.at[rows, :])
+        unit, scale = norm_parts(total)
         following = unit * small_ref[6:7, :] + small_ref[7:8, :]
-        next_ref[rows, :] = following
         low_ref[rows, :] = following.astype(jnp.bfloat16)
-    for index, (source, target) in enumerate(((next_ref, next_out), (low_ref, low_out))):
-        store = pltpu.make_async_copy(source, target, store_sems.at[6 + index])
-        store.start()
-        stores.append(store)
-    for store in stores:
-        store.wait()
+        store(low_ref.at[rows, :], low_out.at[rows, :])
+    finish(stores)
 
 
 def feed(place, small, hidden_bias, mixed, hidden, attn, group):
     plan, pieces = group
+    tall = jax.ShapeDtypeStruct((TALL, D), jnp.float32)
+    tall_low = jax.ShapeDtypeStruct((TALL, D), jnp.bfloat16)
     return pl.pallas_call(
         partial(feed_kernel, plan),
         out_shape=[
-            jax.ShapeDtypeStruct((TALL, D), jnp.float32),
-            jax.ShapeDtypeStruct((TALL, D), jnp.float32),
-            jax.ShapeDtypeStruct((4, TALL, D), jnp.bfloat16),
-            jax.ShapeDtypeStruct((TALL, D), jnp.bfloat16),
-            jax.ShapeDtypeStruct((TALL, D), jnp.float32),
-            jax.ShapeDtypeStruct((TALL, D), jnp.bfloat16),
+            tall, jax.ShapeDtypeStruct((4, TALL, D), jnp.bfloat16), tall_low, tall_low, tall
         ],
         in_specs=[SMEM_SPEC, VMEM_SPEC, VMEM_SPEC] + [ANY_SPEC] * (3 + len(pieces)),
-        out_specs=[ANY_SPEC] * 6,
+        out_specs=[ANY_SPEC] * 5,
         scratch_shapes=[
             pltpu.VMEM((TALL, D), jnp.bfloat16),
-            pltpu.VMEM((TALL, D), jnp.float32),
+            pltpu.VMEM((TALL, D), jnp.bfloat16),
             pltpu.VMEM((D, D), jnp.bfloat16),
             pltpu.VMEM((4, D, D), jnp.bfloat16),
             pltpu.VMEM((4, D, D), jnp.bfloat16),
@@ -633,82 +683,31 @@
             pltpu.VMEM((TALL, D), jnp.float32),
             pltpu.VMEM((TALL, D), jnp.bfloat16),
             pltpu.VMEM((4, TALL, D), jnp.bfloat16),
-            pltpu.VMEM((TALL, D), jnp.float32),
             pltpu.VMEM((TALL, D), jnp.bfloat16),
             pltpu.SemaphoreType.DMA((64,)),
             pltpu.SemaphoreType.DMA((3,)),
-            pltpu.SemaphoreType.DMA((9,)),
+            pltpu.SemaphoreType.DMA((17,)),
         ],
         compiler_params=PARAMS,
-        cost_estimate=pl.CostEstimate(flops=2 * TALL * D * (D + 2 * FF), bytes_accessed=40000000, transcendentals=3000000),
+        cost_estimate=pl.CostEstimate(flops=2 * TALL * D * (D + 2 * FF), bytes_accessed=30000000, transcendentals=3000000),
         name="feed",
     )(place, small, hidden_bias, mixed, hidden, attn, *pieces)
 
 
-def feed_back_kernel(
-    plan, place_ref, small_ref, grad_c_any, grad_q_any, summed_any, normed_any, resid_any, pre_any,
-    mix_any, attn_any, *refs
+def back_steps(
+    place_ref, small_ref, before, store, outs, vec_ref, dhidden_ref, branch_ref, total_ref,
+    normed_ref, resid_ref, pre_ref, mix_ref, wo_ref, inner_ref, outer_ref, active_ref, dpre_ref,
+    dinner_ref, douter_ref, dwo_ref,
 ):
-    pieces = refs[:-26]
-    (
-        dresid_out, dmix_out, dwo_out, keep_out, send_out, vec_ref, dhidden_ref,
-        grad_ref, summed_ref, resid_ref, pre_ref, mix_ref, wo_ref, inner_ref, outer_ref,
-        branch_ref, normed_ref, active_ref, dpre_ref, dinner_ref, douter_ref,
-        dwo_ref, sems, load_sems, store_sems, block_sems,
-    ) = refs[-26:]
+    dresid_out, dmix_out, dwo_out, keep_out, send_out = outs
     x, c, z, y = (place_ref[index] for index in range(4))
-    total_ref = summed_ref
-    load = [
-        pltpu.make_async_copy(source, target, load_sems.at[index])
-        for index, (source, target) in enumerate(
-            (
-                (summed_any, summed_ref),
-                (grad_c_any, grad_ref.at[:LEN, :]),
-                (grad_q_any, grad_ref.at[LEN:, :]),
-                (pre_any, pre_ref),
-                (normed_any, normed_ref),
-                (resid_any, resid_ref),
-                (mix_any, mix_ref),
-                (attn_any.at[3], wo_ref),
-            )
-        )
-    ]
-    for copy in load[:3]:
-        copy.start()
-    fetches = start_fetch(("inner", "outer"), plan, place_ref, pieces, (inner_ref, outer_ref), sems)
-    for copy in load[3:]:
-        copy.start()
-    for copy in load[:3]:
-        copy.wait()
-    gain_two_grad = jnp.zeros((1, D), jnp.float32)
-    shift_two_grad = jnp.zeros((1, D), jnp.float32)
-    bias_two_grad = jnp.zeros((1, D), jnp.float32)
-    for row in range(0, TALL, HALF):
-        rows = slice(row, row + HALF)
-        grad = grad_ref[rows, :]
-        unit, scale = norm_parts(summed_ref[rows, :])
-        gain_two_grad += jnp.sum(grad * unit, axis=0, keepdims=True)
-        shift_two_grad += jnp.sum(grad, axis=0, keepdims=True)
-        back = norm_back(unit, scale, grad, small_ref[6:7, :])
-        total_ref[rows, :] = back
-        low = back.astype(jnp.bfloat16)
-        branch_ref[rows, :] = low
-        bias_two_grad += jnp.sum(low.astype(jnp.float32), axis=0, keepdims=True)
-    vec_ref[5:6, :] = bias_two_grad
-    vec_ref[6:7, :] = gain_two_grad
-    vec_ref[7:8, :] = shift_two_grad
-    for copy in fetches + load[3:]:
-        copy.wait()
-    blocks = []
-
-    def store(source, target):
-        copy = pltpu.make_async_copy(source, target, block_sems.at[len(blocks)])
-        copy.start()
-        blocks.append(copy)
-
+    order = [(1 - step // 2, step % 2) for step in range(4)]
+    chunks = [side * 2 + (c ^ apart) for apart, side in order]
+    sums = [jnp.zeros((1, D), jnp.float32)] * 3
     for step in range(4):
-        apart, side = 1 - step // 2, step % 2
-        chunk = side * 2 + (c ^ apart)
+        apart, side = order[step]
+        chunk = chunks[step]
+        before(step)
         bias_grad = jnp.zeros((1, D), jnp.float32)
         for row in range(0, TALL, HALF):
             rows = slice(row, row + HALF)
@@ -724,8 +723,25 @@
             dpre = (pull * slope).astype(jnp.bfloat16)
             dpre_ref[rows, :] = dpre
             bias_grad += jnp.sum(dpre.astype(jnp.float32), axis=0, keepdims=True)
-            total_ref[rows, :] += dot_nt(dpre, inner_ref[chunk])
+            grad = total_ref[rows, :] + dot_nt(dpre, inner_ref[chunk])
+            if step < 3:
+                total_ref[rows, :] = grad
+            else:
+                unit, scale = norm_parts(resid_ref[rows, :])
+                back = norm_back(unit, scale, grad, small_ref[3:4, :])
+                resid_ref[rows, :] = back
+                low = back.astype(jnp.bfloat16)
+                pre_ref[chunks[0], rows, :] = low
+                pre_ref[chunks[1], rows, :] = dot_nt(low, wo_ref[...]).astype(jnp.bfloat16)
+                parts = (low.astype(jnp.float32), grad * unit, grad)
+                sums = [
+                    value + jnp.sum(part, axis=0, keepdims=True)
+                    for value, part in zip(sums, parts)
+                ]
         dhidden_ref[chunk] = bias_grad
+        if step == 3:
+            store(resid_ref, dresid_out)
+            store(pre_ref.at[chunks[1]], dmix_out)
         douter_ref[step] = (
             dot_tn(active_ref[...], branch_ref[...]).astype(jnp.bfloat16).reshape(2, 2, 2, ROWS, D)
         )
@@ -740,99 +756,243 @@
         target = send_out if apart else keep_out
         for y_block in range(2):
             store(dinner_ref.at[step, :, y_block], target.at[y_block ^ y, side ^ x, :, 0])
-    gain_one_grad = jnp.zeros((1, D), jnp.float32)
-    shift_one_grad = jnp.zeros((1, D), jnp.float32)
-    bias_o_grad = jnp.zeros((1, D), jnp.float32)
+    dwo_ref[...] = dot_tn(mix_ref[...], pre_ref[chunks[0]]).astype(jnp.bfloat16)
+    store(dwo_ref, dwo_out)
+    for index, value in enumerate(sums):
+        vec_ref[index : index + 1, :] = value
+
+
+BACK_SHAPES = [
+    jax.ShapeDtypeStruct((TALL, D), jnp.float32),
+    jax.ShapeDtypeStruct((TALL, D), jnp.bfloat16),
+    jax.ShapeDtypeStruct((D, D), jnp.bfloat16),
+    jax.ShapeDtypeStruct((2, 2, 4, 2, ROWS, D), jnp.bfloat16),
+    jax.ShapeDtypeStruct((2, 2, 4, 2, ROWS, D), jnp.bfloat16),
+    jax.ShapeDtypeStruct((6, D), jnp.float32),
+    jax.ShapeDtypeStruct((4, 1, D), jnp.float32),
+]
+BACK_SCRATCH = [
+    pltpu.VMEM((TALL, D), jnp.bfloat16),
+    pltpu.VMEM((TALL, D), jnp.float32),
+    pltpu.VMEM((TALL, D), jnp.bfloat16),
+    pltpu.VMEM((TALL, D), jnp.float32),
+    pltpu.VMEM((4, TALL, D), jnp.bfloat16),
+    pltpu.VMEM((TALL, D), jnp.bfloat16),
+    pltpu.VMEM((D, D), jnp.bfloat16),
+    pltpu.VMEM((4, D, D), jnp.bfloat16),
+    pltpu.VMEM((4, D, D), jnp.bfloat16),
+    pltpu.VMEM((TALL, D), jnp.bfloat16),
+    pltpu.VMEM((TALL, D), jnp.bfloat16),
+    pltpu.VMEM((4, 4, 2, ROWS, D), jnp.bfloat16),
+    pltpu.VMEM((4, 2, 2, 2, ROWS, D), jnp.bfloat16),
+    pltpu.VMEM((D, D), jnp.bfloat16),
+    pltpu.SemaphoreType.DMA((64,)),
+    pltpu.SemaphoreType.DMA((16,)),
+    pltpu.SemaphoreType.DMA((48,)),
+]
+
+
+def turn_kernel(
+    plan, place_ref, length_ref, small_ref, below_ref, hidden_bias_ref, mix_any, summed_any,
+    attn_any, cot_c_any, cot_q_any, *refs
+):
+    content_out, query_out = refs[-27:-25]
+    outs = refs[-25:-20]
+    vec_ref, dhidden_ref = refs[-20:-18]
+    low_ref = refs[-18]
+    (
+        branch_ref, total_ref, normed_ref, resid_ref, pre_ref, mix_ref, wo_ref, inner_ref,
+        outer_ref, active_ref, dpre_ref, dinner_ref, douter_ref, dwo_ref,
+        sems, load_sems, store_sems,
+    ) = refs[-17:]
+    store, stores = storer(store_sems)
+    finish(
+        issue(
+            ((mix_any, mix_ref), (attn_any.at[3], wo_ref), (summed_any, resid_ref)), load_sems
+        )
+    )
+    fetches = start_fetch(
+        ("inner", "outer"), plan, place_ref, refs[:-27], (inner_ref, outer_ref), sems
+    )
+    fetches += issue(
+        ((cot_c_any, low_ref.at[:LEN, :]), (cot_q_any, low_ref.at[LEN:, :])), load_sems, 3
+    )
     for row in range(0, TALL, HALF):
         rows = slice(row, row + HALF)
-        grad = total_ref[rows, :]
         unit, scale = norm_parts(resid_ref[rows, :])
-        gain_one_grad += jnp.sum(grad * unit, axis=0, keepdims=True)
-        shift_one_grad += jnp.sum(grad, axis=0, keepdims=True)
-        back = norm_back(unit, scale, grad, small_ref[3:4, :])
-        grad_ref[rows, :] = back
-        low = back.astype(jnp.bfloat16)
-        branch_ref[rows, :] = low
-        bias_o_grad += jnp.sum(low.astype(jnp.float32), axis=0, keepdims=True)
-        active_ref[rows, :] = dot_nt(low, wo_ref[...]).astype(jnp.bfloat16)
-    stores = [
-        pltpu.make_async_copy(source, target, store_sems.at[index])
-        for index, (source, target) in enumerate(
-            ((grad_ref, dresid_out), (active_ref, dmix_out), (dwo_ref, dwo_out))
-        )
-    ]
-    stores[0].start()
-    stores[1].start()
-    dwo_ref[...] = dot_tn(mix_ref[...], branch_ref[...]).astype(jnp.bfloat16)
-    stores[2].start()
-    vec_ref[0:2, :] = jnp.zeros((2, D), jnp.float32)
-    vec_ref[2:3, :] = bias_o_grad
-    vec_ref[3:4, :] = gain_one_grad
-    vec_ref[4:5, :] = shift_one_grad
-    for copy in blocks + stores:
-        copy.wait()
-
-
-def feed_back(place, small, grads, summed, normed, resid, pre, mixed, attn, group):
+        resid_ref[rows, :] = (
+            unit * below_ref[6:7, :]
+            + below_ref[7:8, :]
+            + dot_nn(mix_ref[rows, :], wo_ref[...])
+            + small_ref[2:3, :]
+        )
+    finish(fetches)
+    sums = [jnp.zeros((1, D), jnp.float32)] * 3
+    for row in range(0, TALL, HALF):
+        rows = slice(row, row + HALF)
+        total = feed_rows(
+            rows, small_ref, hidden_bias_ref, resid_ref[rows, :], normed_ref, pre_ref, inner_ref,
+            outer_ref,
+        )
+        unit, scale = norm_parts(total)
+        position = lax.broadcasted_iota(jnp.int32, (HALF, 1), 0) + row % LEN
+        valid = (position < length_ref[0]).astype(jnp.float32)
+        grad = low_ref[rows, :].astype(jnp.float32) * valid
+        low_ref[rows, :] = (unit * small_ref[6:7, :] + small_ref[7:8, :]).astype(jnp.bfloat16)
+        total_ref[rows, :], branch_ref[rows, :], sums = norm_two_back(
+            unit, scale, grad, small_ref, sums
+        )
+    store(low_ref.at[:LEN, :], content_out)
+    store(low_ref.at[LEN:, :], query_out)
+    for index, value in enumerate(sums):
+        vec_ref[3 + index : 4 + index, :] = value
+    back_steps(
+        place_ref, small_ref, lambda step: None, store, outs, vec_ref, dhidden_ref, branch_ref,
+        total_ref, normed_ref, resid_ref, pre_ref, mix_ref, wo_ref, inner_ref, outer_ref,
+        active_ref, dpre_ref, dinner_ref, douter_ref, dwo_ref,
+    )
+    finish(stores)
+
+
+def turn(place, length, small, below, hidden_bias, mixed, summed, attn, cots, group):
     plan, pieces = group
-    blocks = jax.ShapeDtypeStruct((2, 2, 4, 2, ROWS, D), jnp.bfloat16)
+    half_low = jax.ShapeDtypeStruct((LEN, D), jnp.bfloat16)
     return pl.pallas_call(
-        partial(feed_back_kernel, plan),
-        out_shape=[
-            jax.ShapeDtypeStruct((TALL, D), jnp.float32),
-            jax.ShapeDtypeStruct((TALL, D), jnp.bfloat16),
-            jax.ShapeDtypeStruct((D, D), jnp.bfloat16),
-            blocks,
-            blocks,
-            jax.ShapeDtypeStruct((8, D), jnp.float32),
-            jax.ShapeDtypeStruct((4, 1, D), jnp.float32),
-        ],
-        in_specs=[SMEM_SPEC, VMEM_SPEC] + [ANY_SPEC] * (8 + len(pieces)),
+        partial(turn_kernel, plan),
+        out_shape=[half_low, half_low] + BACK_SHAPES,
+        in_specs=[SMEM_SPEC] * 2 + [VMEM_SPEC] * 3 + [ANY_SPEC] * (5 + len(pieces)),
+        out_specs=[ANY_SPEC] * 7 + [VMEM_SPEC] * 2,
+        scratch_shapes=[pltpu.VMEM((TALL, D), jnp.bfloat16)] + BACK_SCRATCH,
+        compiler_params=PARAMS,
+        cost_estimate=pl.CostEstimate(flops=6 * TALL * D * (D + 2 * FF), bytes_accessed=60000000, transcendentals=6000000),
+        name="turn",
+    )(place, length, small, below, hidden_bias, mixed, summed, attn, *cots, *pieces)
+
+
+def down_kernel(
+    plan, place_ref, small_ref, dq_any, dk_any, dv_any, w_any, dresid_any, summed_any,
+    normed_any, resid_any, pre_any, mix_any, attn_any, *refs
+):
+    outs = refs[-29:-24]
+    vec_ref, dhidden_ref = refs[-24:-22]
+    dq_ref, dk_ref, dv_ref, w_ref, summed_ref = refs[-22:-17]
+    (
+        branch_ref, total_ref, normed_ref, resid_ref, pre_ref, mix_ref, wo_ref, inner_ref,
+        outer_ref, active_ref, dpre_ref, dinner_ref, douter_ref, dwo_ref,
+        sems, load_sems, store_sems,
+    ) = refs[-17:]
+    x, c, z, y = (place_ref[index] for index in range(4))
+    chunks = [side * 2 + (c ^ apart) for apart in (1, 0) for side in range(2)]
+    store, stores = storer(store_sems)
+    loads = issue(
+        (
+            (w_any.at[0], w_ref.at[0]), (dq_any, dq_ref), (dresid_any, total_ref),
+            (summed_any, summed_ref), (w_any.at[1:3], w_ref.at[1:3]), (dk_any, dk_ref),
+            (dv_any, dv_ref),
+        ),
+        load_sems,
+    )
+    finish(loads[:4])
+    fetches = start_fetch(
+        ("inner", "outer"), plan, place_ref, refs[:-29], (inner_ref, outer_ref), sems
+    )
+    fetches += issue(((pre_any.at[chunks[0]], pre_ref.at[chunks[0]]),), load_sems, 7)
+    sums = [jnp.zeros((1, D), jnp.float32)] * 3
+    for index, row in enumerate((LEN, LEN + HALF, 0, HALF)):
+        rows = slice(row, row + HALF)
+        if index == 2:
+            finish(loads[4:])
+        total = total_ref[rows, :] + dot_nt(dq_ref[rows, :], w_ref[0])
+        if index >= 2:
+            total = total + dot_nt(dk_ref[rows, :], w_ref[1]) + dot_nt(dv_ref[rows, :], w_ref[2])
+        unit, scale = norm_parts(summed_ref[rows, :])
+        total_ref[rows, :], branch_ref[rows, :], sums = norm_two_back(
+            unit, scale, total, small_ref, sums
+        )
+    for index, value in enumerate(sums):
+        vec_ref[3 + index : 4 + index, :] = value
+    finish(fetches)
+    late = []
+
+    def before(step):
+        if step == 0:
+            late.append(issue(((normed_any, normed_ref),), load_sems, 8))
+        else:
+            finish(late.pop())
+        if step < 3:
+            chunk = chunks[step + 1]
+            late.insert(0, issue(((pre_any.at[chunk], pre_ref.at[chunk]),), load_sems, 9 + step))
+        if step == 0:
+            finish(late.pop())
+        if step == 2:
+            late[0].extend(
+                issue(
+                    ((resid_any, resid_ref), (mix_any, mix_ref), (attn_any.at[3], wo_ref)),
+                    load_sems,
+                    12,
+                )
+            )
+
+    back_steps(
+        place_ref, small_ref, before, store, outs, vec_ref, dhidden_ref, branch_ref, total_ref,
+        normed_ref, resid_ref, pre_ref, mix_ref, wo_ref, inner_ref, outer_ref, active_ref,
+        dpre_ref, dinner_ref, douter_ref, dwo_ref,
+    )
+    finish(stores)
+
+
+def down(place, small, dq, dk, dv, w_above, dresid, summed, normed, resid, pre, mixed, attn, group):
+    plan, pieces = group
+    return pl.pallas_call(
+        partial(down_kernel, plan),
+        out_shape=BACK_SHAPES,
+        in_specs=[SMEM_SPEC, VMEM_SPEC] + [ANY_SPEC] * (11 + len(pieces)),
         out_specs=[ANY_SPEC] * 5 + [VMEM_SPEC] * 2,
         scratch_shapes=[
+            pltpu.VMEM((TALL, D), jnp.bfloat16),
+            pltpu.VMEM((LEN, D), jnp.bfloat16),
+            pltpu.VMEM((LEN, D), jnp.bfloat16),
+            pltpu.VMEM((3, D, D), jnp.bfloat16),
             pltpu.VMEM((TALL, D), jnp.float32),
-            pltpu.VMEM((TALL, D), jnp.float32),
-            pltpu.VMEM((TALL, D), jnp.float32),
-            pltpu.VMEM((4, TALL, D), jnp.bfloat16),
-            pltpu.VMEM((TALL, D), jnp.bfloat16),
-            pltpu.VMEM((D, D), jnp.bfloat16),
-            pltpu.VMEM((4, D, D), jnp.bfloat16),
-            pltpu.VMEM((4, D, D), jnp.bfloat16),
-            pltpu.VMEM((TALL, D), jnp.bfloat16),
-            pltpu.VMEM((TALL, D), jnp.bfloat16),
-            pltpu.VMEM((TALL, D), jnp.bfloat16),
-            pltpu.VMEM((TALL, D), jnp.bfloat16),
-            pltpu.VMEM((4, 4, 2, ROWS, D), jnp.bfloat16),
-            pltpu.VMEM((4, 2, 2, 2, ROWS, D), jnp.bfloat16),
-            pltpu.VMEM((D, D), jnp.bfloat16),
-            pltpu.SemaphoreType.DMA((64,)),
-            pltpu.SemaphoreType.DMA((8,)),
-            pltpu.SemaphoreType.DMA((3,)),
-            pltpu.SemaphoreType.DMA((40,)),
-        ],
+        ]
+        + BACK_SCRATCH,
         compiler_params=PARAMS,
-        cost_estimate=pl.CostEstimate(flops=4 * TALL * D * (D + 2 * FF), bytes_accessed=60000000, transcendentals=3000000),
-        name="feed_back",
-    )(place, small, *grads, summed, normed, resid, pre, mixed, attn, *pieces)
+        cost_estimate=pl.CostEstimate(flops=5 * TALL * D * (D + 2 * FF), bytes_accessed=60000000, transcendentals=3000000),
+        name="down",
+    )(place, small, dq, dk, dv, w_above, dresid, summed, normed, resid, pre, mixed, attn, *pieces)
 
 
 def weight_back_kernel(
-    place_ref, low_ref, dq_a, dk_a, dv_a, dq_b, dk_b, dv_b, dwo_ref, keep_out, send_out, vec_ref, grads_ref, sems
+    place_ref, low_any, dq_any, dk_any, dv_any, dwo_any, keep_out, send_out, vec_ref,
+    low_ref, dq_ref, dk_ref, dv_ref, dwo_ref, grads_ref, load_sems, sems,
 ):
     x, c, z, y = (place_ref[index] for index in range(4))
+    load = [
+        pltpu.make_async_copy(source, target, load_sems.at[index])
+        for index, (source, target) in enumerate(
+            (
+                (low_any.at[:LEN, :], low_ref.at[:LEN, :]), (dk_any, dk_ref), (dv_any, dv_ref),
+                (low_any.at[LEN:, :], low_ref.at[LEN:, :]), (dq_any, dq_ref), (dwo_any, dwo_ref),
+            )
+        )
+    ]
+    for copy in load:
+        copy.start()
+    load[0].wait()
+    load[1].wait()
+    grads_ref[1] = (
+        dot_tn(low_ref[:LEN, :], dk_ref[...]).astype(jnp.bfloat16).reshape(4, 2, ROWS, D)
+    )
+    load[2].wait()
+    grads_ref[2] = (
+        dot_tn(low_ref[:LEN, :], dv_ref[...]).astype(jnp.bfloat16).reshape(4, 2, ROWS, D)
+    )
+    vec_ref[1:2, :] = jnp.sum(dv_ref[...].astype(jnp.float32), axis=0, keepdims=True)
+    for copy in load[3:]:
+        copy.wait()
     grads_ref[3] = dwo_ref[...].reshape(4, 2, ROWS, D)
-    for matrix, halves in enumerate(((dq_a, dq_b), (dk_a, dk_b), (dv_a, dv_b))):
-        for half, grad in enumerate(halves):
-            cols = slice(half * 384, half * 384 + 384)
-            grads_ref[matrix, :, :, :, cols] = (
-                dot_tn(low_ref[: grad.shape[0], :], grad[...])
-                .astype(jnp.bfloat16)
-                .reshape(4, 2, ROWS, 384)
-            )
-            if matrix != 1:
-                vec_ref[matrix // 2 : matrix // 2 + 1, cols] = jnp.sum(
-                    grad[...].astype(jnp.float32), axis=0, keepdims=True
-                )
+    grads_ref[0] = dot_tn(low_ref[...], dq_ref[...]).astype(jnp.bfloat16).reshape(4, 2, ROWS, D)
+    vec_ref[0:1, :] = jnp.sum(dq_ref[...].astype(jnp.float32), axis=0, keepdims=True)
     blocks = []
     for apart, target in ((1, send_out), (0, keep_out)):
         for side in range(2):
@@ -848,67 +1008,75 @@
         block.wait()
 
 
-def weight_back(place, low, first, second, dwo):
+def weight_back(place, low, dq, dk, dv, dwo):
     blocks = jax.ShapeDtypeStruct((2, 2, 4, 1, ROWS, D), jnp.bfloat16)
     return pl.pallas_call(
         weight_back_kernel,
         out_shape=[blocks, blocks, jax.ShapeDtypeStruct((2, D), jnp.float32)],
-        in_specs=[SMEM_SPEC] + [VMEM_SPEC] * 8,
+        in_specs=[SMEM_SPEC] + [ANY_SPEC] * 5,
         out_specs=[ANY_SPEC] * 2 + [VMEM_SPEC],
         scratch_shapes=[
+            pltpu.VMEM((TALL, D), jnp.bfloat16),
+            pltpu.VMEM((TALL, D), jnp.bfloat16),
+            pltpu.VMEM((LEN, D), jnp.bfloat16),
+            pltpu.VMEM((LEN, D), jnp.bfloat16),
+            pltpu.VMEM((D, D), jnp.bfloat16),
             pltpu.VMEM((4, 4, 2, ROWS, D), jnp.bfloat16),
+            pltpu.SemaphoreType.DMA((6,)),
             pltpu.SemaphoreType.DMA((8,)),
         ],
         compiler_params=PARAMS,
         cost_estimate=pl.CostEstimate(flops=2 * 2048 * D * D, bytes_accessed=12000000, transcendentals=0),
         name="weight_back",
-    )(place, low, *first, *second, dwo)
+    )(place, low, dq, dk, dv, dwo)
 
 
 def input_back_kernel(
-    dq_a, dk_a, dv_a, dq_b, dk_b, dv_b, w_ref, dresid_ref, first_ref, second_ref
+    dq_any, dk_any, dv_any, w_any, dresid_any, first_out, second_out,
+    dq_ref, dk_ref, dv_ref, w_ref, dresid_ref, load_sems, store_sems,
 ):
-    step = pl.program_id(0)
-    total = (
-        dresid_ref[...]
-        + dot_nt(dq_a[...], w_ref[0, :, :384])
-        + dot_nt(dq_b[...], w_ref[0, :, 384:])
-    )
-
-    @pl.when(step < 2)
-    def _():
-        content = total
-        for matrix, halves in ((1, (dk_a, dk_b)), (2, (dv_a, dv_b))):
-            for half, grad in enumerate(halves):
-                content += dot_nt(grad[...], w_ref[matrix, :, half * 384 : half * 384 + 384])
-        first_ref[...] = content
-
-    @pl.when(step >= 2)
-    def _():
-        second_ref[...] = total
-
-
-def input_back(first, second, attn, dresid):
+    loads = issue(
+        (
+            (w_any.at[0], w_ref.at[0]), (dq_any, dq_ref), (dresid_any, dresid_ref),
+            (w_any.at[1:3], w_ref.at[1:3]), (dk_any, dk_ref), (dv_any, dv_ref),
+        ),
+        load_sems,
+    )
+    finish(loads[:3])
+    store, stores = storer(store_sems)
+    for index, row in enumerate((LEN, LEN + HALF, 0, HALF)):
+        rows = slice(row, row + HALF)
+        if index == 2:
+            finish(loads[3:])
+        total = dresid_ref[rows, :] + dot_nt(dq_ref[rows, :], w_ref[0])
+        if index >= 2:
+            total = total + dot_nt(dk_ref[rows, :], w_ref[1]) + dot_nt(dv_ref[rows, :], w_ref[2])
+        dresid_ref[rows, :] = total
+        target = first_out if index >= 2 else second_out
+        store(dresid_ref.at[rows, :], target.at[row % LEN : row % LEN + HALF, :])
+    finish(stores)
+
+
+def input_back(dq, dk, dv, attn, dresid):
     half = jax.ShapeDtypeStruct((LEN, D), jnp.float32)
-    tall = pl.BlockSpec((HALF, D // 2), lambda i: (i, 0))
-    short = pl.BlockSpec((HALF, D // 2), lambda i: (jnp.minimum(i, 1), 0))
     return pl.pallas_call(
         input_back_kernel,
-        grid=(4,),
         out_shape=[half, half],
-        in_specs=[
-            tall, short, short, tall, short, short,
-            pl.BlockSpec((3, D, D), lambda i: (0, 0, 0)),
-            pl.BlockSpec((HALF, D), lambda i: (i, 0)),
-        ],
-        out_specs=[
-            pl.BlockSpec((HALF, D), lambda i: (jnp.minimum(i, 1), 0)),
-            pl.BlockSpec((HALF, D), lambda i: (jnp.maximum(i - 2, 0), 0)),
+        in_specs=[ANY_SPEC] * 5,
+        out_specs=[ANY_SPEC] * 2,
+        scratch_shapes=[
+            pltpu.VMEM((TALL, D), jnp.bfloat16),
+            pltpu.VMEM((LEN, D), jnp.bfloat16),
+            pltpu.VMEM((LEN, D), jnp.bfloat16),
+            pltpu.VMEM((3, D, D), jnp.bfloat16),
+            pltpu.VMEM((TALL, D), jnp.float32),
+            pltpu.SemaphoreType.DMA((6,)),
+            pltpu.SemaphoreType.DMA((4,)),
         ],
         compiler_params=PARAMS,
         cost_estimate=pl.CostEstimate(flops=2 * 2048 * D * D, bytes_accessed=16000000, transcendentals=0),
         name="input_back",
-    )(*first, *second, attn, dresid)
+    )(dq, dk, dv, attn, dresid)
 
 
 def bias_vectors(table):
@@ -929,14 +1097,13 @@
 
 
 def table_grad(sums, onehot):
-    near = jnp.dot(
-        sums[:, 0, :512],
-        jnp.roll(onehot.astype(jnp.float32), 127, axis=0),
+    near = jnp.roll(onehot.astype(jnp.float32), 127, axis=0)
+    far = jnp.arange(NB, dtype=jnp.int32)[None, :] == jnp.repeat(jnp.array([15, 31]), 128)[:, None]
+    return jnp.dot(
+        sums[:, 0, :],
+        jnp.concatenate([near, far.astype(jnp.float32)]),
         precision=lax.Precision.HIGHEST,
     )
-    low = jnp.sum(sums[:, 0, 512:640], axis=1)
-    high = jnp.sum(sums[:, 0, 640:], axis=1)
-    return near.at[:, 15].add(low).at[:, 31].add(high)
 
 
 def adam_kernel(rate, master_ref, first_ref, second_ref, grad_ref, *refs):
@@ -1480,11 +1647,8 @@
     row_flags = predicted.reshape(1, LEN).astype(jnp.float32)
     col_flags = predicted.reshape(LEN, 1).astype(jnp.float32)
     low0 = jnp.concatenate([content, query])
-    hidden0 = low0.astype(jnp.float32)
     small0, hidden_bias0, (tvec0, far0, onehot) = small_parts(small_all[0])
     small1, hidden_bias1, (tvec1, far1, onehot) = small_parts(small_all[1])
-    valid = (jnp.arange(LEN, dtype=jnp.int32) < lengths[0])[:, None].astype(jnp.float32)
-    grads = (content_cot.astype(jnp.float32) * valid, query_cot.astype(jnp.float32) * valid)
     q0, k0, v0, attn0 = project(place, low0, small0, group_a0)
     mixed0, p0, inverse0, dead = mix(lengths, far0, tvec0, q0, k0, v0, row_flags, col_flags)
     x2, y2, far_f1, mixed0, theirs_p0 = join(x2, y2, far_f1, mixed0, theirs_p0)
@@ -1497,10 +1661,10 @@
         2, feed_low[0], (0, 0), (0, 4), ((1, 0), (1, 8)), ((2, 3, 4), (2, 10, 2)),
         (mine_p0, mine_1, mine_2), (theirs_p0, theirs_1, theirs_2),
     )
-    resid0, summed0, pre0, normed0, hidden1, low1 = feed(
-        place, small0, hidden_bias0, mixed0, hidden0, attn0, group_f0
-    )
-    x3, y3, low1, hidden1 = join(x3, y3, low1, hidden1)
+    resid0, pre0, normed0, low1, summed0 = feed(
+        place, small0, hidden_bias0, mixed0, low0, attn0, group_f0
+    )
+    x3, y3, low1 = join(x3, y3, low1)
     x4 = swap_x(y3[:3])
     y4 = swap_y(x3[3:6])
     mine_3 = jnp.concatenate([x3, y3])
@@ -1520,77 +1684,63 @@
     mixed1, p1, inverse1, dead = mix(
         lengths, far1, tvec1, q1, k1, v1, row_flags, col_flags
     )
-    resid1, summed1, pre1, normed1, unused, low_out = feed(
-        place, small1, hidden_bias1, mixed1, hidden1, attn1, group_f1
-    )
-    dresid1, dmix1, dwo1, keep_f1, send_f1, vec_f1, dhidden1 = feed_back(
-        place, small1, grads, summed1, normed1, resid1, pre1, mixed1, attn1, group_f1
+    content_out, query_out, dresid1, dmix1, dwo1, keep_f1, send_f1, vec_f1, dhidden1 = turn(
+        place, lengths, small1, small0, hidden_bias1, mixed1, summed0, attn1,
+        (content_cot, query_cot), group_f1
     )
     get_f1 = swap_core(send_f1)
-    first1 = mix_back(0, q1, k1, v1, dmix1, mixed1, p1, inverse1, dead)
-    by_f1 = reduce_corners(keep_f1, after(get_f1, first1[0]))
-    second1 = mix_back(
-        3, after(q1, get_f1, first1[0]), k1, v1, dmix1, mixed1, p1, inverse1, dead
-    )
-    sides_rf1 = reduce_sides(keep_f1, get_f1, after(by_f1, second1[0]))
-    keep_a1, send_a1, vec_a1 = weight_back(
-        place, low1, after(first1[:3], by_f1), second1[:3], dwo1
-    )
+    *first1, table1_a = mix_back(0, q1, k1, v1, dmix1, mixed1, p1, inverse1, dead)
+    by_f1 = reduce_corners(keep_f1, after(get_f1, table1_a))
+    dq1, dk1, dv1, table1_b = mix_back(
+        3, after(q1, get_f1, table1_a), k1, v1, dmix1, mixed1, p1, inverse1, dead, tuple(first1)
+    )
+    sides_rf1 = reduce_sides(keep_f1, get_f1, after(by_f1, table1_b))
+    keep_a1, send_a1, vec_a1 = weight_back(place, after(low1, by_f1), dq1, dk1, dv1, dwo1)
     get_a1 = swap_core(send_a1)
-    grads = input_back(after(first1[:3], keep_a1), second1[:3], attn1, dresid1)
-    by_a1 = reduce_corners(keep_a1, after(get_a1, grads[0]))
-    dresid0, dmix0, dwo0, keep_f0, send_f0, vec_f0, dhidden0 = feed_back(
-        place, small0, after(grads, get_a1), summed0, normed0, resid0, pre0, mixed0, attn0, group_f0
+    by_a1 = reduce_corners(keep_a1, get_a1)
+    dresid0, dmix0, dwo0, keep_f0, send_f0, vec_f0, dhidden0 = down(
+        place, small0, dq1, dk1, dv1, after(attn1, get_a1), dresid1, summed0, normed0, resid0,
+        pre0, mixed0, attn0, group_f0
     )
     get_f0 = swap_core(after(send_f0, sides_rf1, by_a1))
     sides_ra1 = reduce_sides(keep_a1, get_a1, after(by_a1, dmix0))
-    first0 = mix_back(
-        0, q0, k0, v0, after(dmix0, by_a1, sides_rf1), mixed0, p0, inverse0, dead
-    )
-    by_f0 = reduce_corners(keep_f0, after(get_f0, first0[0]))
-    column_f1 = reduce_column(keep_f1, get_f1, after(sides_rf1, first0[0]))
+    column_f1 = reduce_column(keep_f1, get_f1, after(sides_rf1, dmix0))
     zfar_f1 = reduce_far(column_f1, place_parts)
-    second0 = mix_back(
-        3, after(q0, get_f0, first0[0]), k0, v0, dmix0, mixed0, p0, inverse0, dead
-    )
-    by_f0, sides_ra1, zfar_f1, second0_q = join(by_f0, sides_ra1, zfar_f1, second0[0])
+    *first0, table0_a = mix_back(
+        0, after(q0, by_a1, sides_rf1), k0, v0, dmix0, mixed0, p0, inverse0, dead
+    )
+    by_f0 = reduce_corners(keep_f0, after(get_f0, table0_a))
+    zfar_f1 = after(zfar_f1, table0_a)
+    znear_f1 = reduce_near(column_f1, zfar_f1, place_parts)
+    dq0, dk0, dv0, table0_b = mix_back(
+        3, after(q0, get_f0, zfar_f1), k0, v0, dmix0, mixed0, p0, inverse0, dead, tuple(first0)
+    )
+    by_f0, sides_ra1, znear_f1, table0_b = join(by_f0, sides_ra1, znear_f1, table0_b)
     sides_rf0 = reduce_sides(keep_f0, get_f0, by_f0)
-    keep_a0, send_a0, vec_a0 = weight_back(
-        place, low0, first0[:3], [second0_q, second0[1], second0[2]], dwo0
-    )
+    keep_a0, send_a0, vec_a0 = weight_back(place, after(low0, table0_b), dq0, dk0, dv0, dwo0)
     get_a0 = swap_core(send_a0)
-    znear_f1 = reduce_near(column_f1, zfar_f1, place_parts)
     column_a1 = reduce_column(keep_a1, get_a1, sides_ra1)
     zfar_a1 = reduce_far(column_a1, place_parts)
-    small_sum = jnp.stack(
-        [
-            jnp.concatenate(
-                [
-                    attn_vec.reshape(-1),
-                    feed_vec[2:].reshape(-1),
-                    dhidden.reshape(-1),
-                    table_grad(jnp.concatenate([first[3], second[3]]), onehot).reshape(-1),
-                ]
-            )
-            for attn_vec, feed_vec, dhidden, first, second in (
-                (vec_a0, vec_f0, dhidden0, first0, second0),
-                (vec_a1, vec_f1, dhidden1, first1, second1),
-            )
-        ]
-    )
-    small_sum = small_sum + swap_core(small_sum)
-    sides_rf0, get_a0, znear_f1, zfar_a1, small_sum = join(
-        sides_rf0, get_a0, znear_f1, zfar_a1, small_sum
-    )
+    sides_rf0, get_a0, zfar_a1, vec_a0 = join(sides_rf0, get_a0, zfar_a1, vec_a0)
     column_f0 = reduce_column(keep_f0, get_f0, sides_rf0)
     zfar_f0 = reduce_far(column_f0, place_parts)
     by_a0 = reduce_corners(keep_a0, get_a0)
     own_f1 = reduce_total(column_f1, zfar_f1, znear_f1, place_parts)
     pair_f1 = jnp.stack([own_f1, swap_x(own_f1)])
-    content_grad, query_grad = input_back(
-        after(first0[:3], sides_rf0), [second0_q, second0[1], second0[2]], attn0, dresid0
-    )
-    by_a0, pair_f1, content_grad = join(by_a0, pair_f1, content_grad)
+    content_grad, query_grad = input_back(after(dq0, sides_rf0), dk0, dv0, attn0, dresid0)
+    small_sum = jnp.concatenate(
+        [
+            jnp.stack([vec_a0, vec_a1]).reshape(LAYERS, -1),
+            jnp.stack([vec_f0, vec_f1]).reshape(LAYERS, -1),
+            jnp.stack([dhidden0, dhidden1]).reshape(LAYERS, -1),
+            table_grad(
+                jnp.concatenate([table0_a, table0_b, table1_a, table1_b]), onehot
+            ).reshape(LAYERS, -1),
+        ],
+        axis=1,
+    )
+    small_sum = small_sum + swap_core(small_sum)
+    by_a0, pair_f1, content_grad, small_sum = join(by_a0, pair_f1, content_grad, small_sum)
     sides_ra0 = reduce_sides(keep_a0, get_a0, by_a0)
     znear_a1 = reduce_near(column_a1, zfar_a1, place_parts)
     four_f1 = share_core(pair_f1, place_parts)
@@ -1632,7 +1782,7 @@
     small_own = lax.dynamic_slice_in_dim(small_sum, lax.axis_index("fsdp") * size, size, 1)
     small_new = adam_update(small_master, small_first, small_second, small_own, SMALL_RATE)
     return (
-        (low_out[:LEN], low_out[LEN:], content_grad, query_grad)
+        (content_out, query_out, content_grad, query_grad)
         + tuple(attn_new)
         + tuple(inner_new)
         + tuple(outer_new)

time: 616 us -> 613 us (level)
  waiting for transfers between devices: 83.4 us -> 121 us
  Pallas kernels: 299 us -> 280 us
  other arithmetic: 78.4 us -> 66.2 us
    ppermute x69, waiting for transfers between devices: 83.4 us -> 121 us  [move(): return lax.ppermute(value, AXES, pairs)]
    pallas_call x6 -> x4, Pallas kernels: 149 us -> 131 us  [the longest x1 55.5 us: turn(): pl.pallas_call(partial(turn_kernel, plan), out_shape=[half_low, half_low]...]
    unnamed x137 -> x149, local copies, waits for them, and re-layouts: 24.3 us -> 26.3 us
  transfers between devices with their start and end apart: 69 -> 69, of which waited for: 26 -> 22; matrix products, arithmetic and copies ran while one was open for 19% -> 16% of each run, Pallas kernels for 37% -> 34%
where the time goes in v6:
time: 613 us; the launch traced here: 603 us
  Pallas kernels  280 us (46%)
  waiting for transfers between devices  121 us (20%)
  starting transfers between devices  68.8 us (11%)
  other arithmetic  66.2 us (11%)
  local copies, waits for them, and re-layouts  63.2 us (10%)
    ppermute x69, waiting for transfers between devices, move(): return lax.ppermute(value, AXES, pairs)  121 us
    ppermute x69, starting transfers between devices, move(): return lax.ppermute(value, AXES, pairs)  68.8 us
    pallas_call x1, Pallas kernels, turn(): pl.pallas_call(partial(turn_kernel, plan), out_shape=[half_low, half_low]...  55.5 us
    pallas_call x4, Pallas kernels, mix_back(): pl.pallas_call(mix_back_kernel, grid=(H // 4,), out_shape=[jax.ShapeDtype...  49.5 us
    pallas_call x1, Pallas kernels, down(): pl.pallas_call(partial(down_kernel, plan), out_shape=BACK_SHAPES, in_spec...  46 us
    pallas_call x2, Pallas kernels, mix(): pl.pallas_call(mix_kernel, grid=(H // 2,), out_shape=[jax.ShapeDtypeStruc...  38.8 us
    convert_element_type x23, other arithmetic, add_low(): return total.astype(jnp.bfloat16)  35.5 us
    pallas_call x6, Pallas kernels, adam(): pl.pallas_call(partial(adam_kernel, rate), grid=(4,), out_shape=[jax.Shap...  27.3 us
  transfers between devices with their start and end apart: 69, of which 22 were waited for; matrix products, arithmetic and copies ran while one was open for 16% of the time, Pallas kernels for 34%

profile of v6, /device:TPU:0, one launch (start us, length us, event | category | flops | bytes accessed | tf_op | source)
XLA Modules:
  0.0 602.9 jit_solution(10077763817454836765)
XLA Ops:
  37.9 19.4 %collective-permute-done.9 = bf16[3,96,768]{2,1,0:T(8,128)(2,1)S(1)} collective-permute-done((bf16[3,96,768]{2,1,0:T(8,128)(2,1)S(1)}, bf16[3,96,768]{2,1,0:T(8,128)(2,1)S(1)}, u32[]{:S(2)}, u32[]{:S(2)}) %collective-permute-start.9) | collective-permute-done | bytes 442400 | tf_op jit(solution)/shard_map/ppermute | solution.py:175
  70.5 11.8 %collective-permute-done.15 = bf16[2,2,1200]{2,1,0:T(2,128)(2,1)S(1)} collective-permute-done((bf16[2,2,1200]{2,1,0:T(2,128)(2,1)S(1)}, bf16[2,2,1200]{2,1,0:T(2,128)(2,1)S(1)}, u32[]{:S(2)}, u32[]{:S(2)}) %collective-permute-start.15) | collective-permute-done | bytes 9632 | tf_op jit(solution)/shard_map/ppermute | solution.py:175
  89.0 8.4 %collective-permute-done.10 = bf16[8,96,768]{2,1,0:T(8,128)(2,1)} collective-permute-done((bf16[8,96,768]{2,1,0:T(8,128)(2,1)}, bf16[8,96,768]{2,1,0:T(8,128)(2,1)}, u32[]{:S(2)}, u32[]{:S(2)}) %collective-permute-start.10) | collective-permute-done | bytes 1179680 | tf_op jit(solution)/shard_map/ppermute | solution.py:175
  118.2 7.5 %project.2 = (bf16[1024,768]{1,0:T(8,128)(2,1)}, bf16[512,768]{1,0:T(8,128)(2,1)}, bf16[512,768]{1,0:T(8,128)(2,1)}, bf16[4,768,768]{2,1,0:T(8,128)(2,1)}) custom-call(s32[4]{0:T(128)} %pad_add_fusion.place_ref, f32[8,768]{1,0:T(8,128)} %reshape.878.small_ref.below_ref, bf16[1024,768]{1,0:T(8,128)(2,1)} %copy-done.7, ...), custom_call_target="tpu_custom_call" | custom-call | flops 2415919104 | bytes 16000000 | tf_op jit(solution)/shard_map/project/pallas_call | solution.py:317
  125.7 19.3 %mix.2 = (bf16[1024,768]{1,0:T(8,128)(2,1)}, bf16[12,512,1024]{2,1,0:T(8,128)(2,1)}, f32[12,1,1024]{2,1,0:T(1,128)}, f32[1,1024]{1,0:T(1,128)}) custom-call(s32[1]{0:T(128)S(6)} %copy.221.length_ref, f32[12,2]{1,0:T(8,128)} %pad_maximum_fusion.34.far_ref, bf16[1024,768]{1,0:T(8,128)(2,1)} %get-tuple-element.267.q_ref, ...), custom_call_target="tpu_custom_call" | custom-call | flops 6499999744 | bytes 8000000 | tf_op jit(solution)/shard_map/mix/pallas_call | solution.py:435
  160.5 21.9 %feed.1 = (f32[1024,768]{1,0:T(8,128)}, bf16[4,1024,768]{2,1,0:T(8,128)(2,1)}, bf16[1024,768]{1,0:T(8,128)(2,1)}, bf16[1024,768]{1,0:T(8,128)(2,1)}, f32[1024,768]{1,0:T(8,128)}) custom-call(s32[4]{0:T(128)} %pad_add_fusion.place_ref, f32[8,768]{1,0:T(8,128)} %reshape.878.small_ref.below_ref, f32[1,3072]{1,0:T(1,128)} %slice.425.hidden_bias_ref, ...), custom_call_target="tpu_custom_call" | custom-call | flops 10871635968 | bytes 30000000 | tf_op jit(solution)/shard_map/feed/pallas_call | solution.py:669
  182.4 5.3 collective-permute-done.22
  199.1 7.6 %project.3 = (bf16[1024,768]{1,0:T(8,128)(2,1)}, bf16[512,768]{1,0:T(8,128)(2,1)}, bf16[512,768]{1,0:T(8,128)(2,1)}, bf16[4,768,768]{2,1,0:T(8,128)(2,1)}) custom-call(s32[4]{0:T(128)} %pad_add_fusion.place_ref, f32[8,768]{1,0:T(8,128)} %reshape.877.small_ref, bf16[1024,768]{1,0:T(8,128)(2,1)} %get-tuple-element.241.low_any, ...), custom_call_target="tpu_custom_call" | custom-call | flops 2415919104 | bytes 16000000 | tf_op jit(solution)/shard_map/project/pallas_call | solution.py:317
  213.4 19.4 %mix.3 = (bf16[1024,768]{1,0:T(8,128)(2,1)}, bf16[12,512,1024]{2,1,0:T(8,128)(2,1)}, f32[12,1,1024]{2,1,0:T(1,128)}, f32[1,1024]{1,0:T(1,128)}) custom-call(s32[1]{0:T(128)S(6)} %copy.221.length_ref, f32[12,2]{1,0:T(8,128)} %pad_maximum_fusion.33.far_ref, bf16[1024,768]{1,0:T(8,128)(2,1)} %get-tuple-element.232.q_ref, ...), custom_call_target="tpu_custom_call" | custom-call | flops 6499999744 | bytes 8000000 | tf_op jit(solution)/shard_map/mix/pallas_call | solution.py:435
  232.8 55.5 %turn.1 = (bf16[512,768]{1,0:T(8,128)(2,1)}, bf16[512,768]{1,0:T(8,128)(2,1)}, f32[1024,768]{1,0:T(8,128)}, bf16[1024,768]{1,0:T(8,128)(2,1)}, bf16[768,768]{1,0...) custom-call(s32[4]{0:T(128)} %pad_add_fusion.place_ref, ...), custom_call_target="tpu_custom_call" | custom-call | flops 32614907904 | bytes 60000000 | tf_op jit(solution)/shard_map/turn/pallas_call | solution.py:860
  288.8 12.3 %mix_back.4 = (bf16[1024,768]{1,0:T(8,128)(2,1)}, bf16[512,768]{1,0:T(8,128)(2,1)}, bf16[512,768]{1,0:T(8,128)(2,1)}, f32[6,1,768]{2,1,0:T(1,128)}) custom-call(bf16[1024,768]{1,0:T(8,128)(2,1)} %get-tuple-element.232.q_ref, bf16[512,768]{1,0:T(8,128)(2,1)} %get-tuple-element.217.k_ref, bf16[512,768]{1,0:T(8,128)(2,1)} %get-tuple-element.218.v_ref, ...), custom_call_target="tpu_custom_call" | custom-call | flops 8000000000 | bytes 16000000 | tf_op jit(solution)/shard_map/mix_back/pallas_call | solution.py:536
  305.0 12.5 %mix_back.5 = (bf16[1024,768]{1,0:T(8,128)(2,1)}, bf16[512,768]{1,0:T(8,128)(2,1)}, bf16[512,768]{1,0:T(8,128)(2,1)}, f32[6,1,768]{2,1,0:T(1,128)}) custom-call(bf16[1024,768]{1,0:T(8,128)(2,1)} %get-tuple-element.232.q_ref, bf16[512,768]{1,0:T(8,128)(2,1)} %get-tuple-element.217.k_ref, ...), custom_call_target="tpu_custom_call", output_to_operand_aliasing={{0}: (8, {}), {1}: (9, {}), {2}: (10, {})} | custom-call | flops 8000000000 | bytes 16000000 | tf_op jit(solution)/shard_map/mix_back/pallas_call | solution.py:536
  318.8 8.8 %weight_back.2 = (bf16[2,2,4,1,96,768]{5,4,3,2,1,0:T(8,128)(2,1)}, bf16[2,2,4,1,96,768]{5,4,3,2,1,0:T(8,128)(2,1)}, f32[2,768]{1,0:T(2,128)}) custom-call(s32[4]{0:T(128)} %pad_add_fusion.place_ref, bf16[1024,768]{1,0:T(8,128)(2,1)} %get-tuple-element.241.low_any, bf16[1024,768]{1,0:T(8,128)(2,1)} %get-tuple-element.236.dq_any, ...), custom_call_target="tpu_custom_call" | custom-call | flops 2415919104 | bytes 12000000 | tf_op jit(solution)/shard_map/weight_back/pallas_call | solution.py:1013
  338.6 46.0 %down.1 = (f32[1024,768]{1,0:T(8,128)}, bf16[1024,768]{1,0:T(8,128)(2,1)}, bf16[768,768]{1,0:T(8,128)(2,1)}, bf16[2,2,4,2,96,768]{5,4,3,2,1,0:T(8,128)(2,1)}, bf...) custom-call(s32[4]{0:T(128)} %pad_add_fusion.place_ref, ...), custom_call_target="tpu_custom_call" | custom-call | flops 27179089920 | bytes 60000000 | tf_op jit(solution)/shard_map/down/pallas_call | solution.py:946
  396.4 12.3 %mix_back.6 = (bf16[1024,768]{1,0:T(8,128)(2,1)}, bf16[512,768]{1,0:T(8,128)(2,1)}, bf16[512,768]{1,0:T(8,128)(2,1)}, f32[6,1,768]{2,1,0:T(1,128)}) custom-call(bf16[1024,768]{1,0:T(8,128)(2,1)} %get-tuple-element.267.q_ref, bf16[512,768]{1,0:T(8,128)(2,1)} %get-tuple-element.200.k_ref, bf16[512,768]{1,0:T(8,128)(2,1)} %get-tuple-element.201.v_ref, ...), custom_call_target="tpu_custom_call" | custom-call | flops 8000000000 | bytes 16000000 | tf_op jit(solution)/shard_map/mix_back/pallas_call | solution.py:536
  408.7 9.6 %collective-permute-done.42 = bf16[2,2,96,768]{3,2,1,0:T(8,128)(2,1)} collective-permute-done((bf16[2,2,96,768]{3,2,1,0:T(8,128)(2,1)}, bf16[2,2,96,768]{3,2,1,0:T(8,128)(2,1)}, u32[]{:S(2)}, u32[]{:S(2)}) %collective-permute-start.42) | collective-permute-done | bytes 589856 | tf_op jit(solution)/shard_map/ppermute | solution.py:175
  425.2 12.3 %mix_back.7 = (bf16[1024,768]{1,0:T(8,128)(2,1)}, bf16[512,768]{1,0:T(8,128)(2,1)}, bf16[512,768]{1,0:T(8,128)(2,1)}, f32[6,1,768]{2,1,0:T(1,128)}) custom-call(bf16[1024,768]{1,0:T(8,128)(2,1)} %get-tuple-element.267.q_ref, bf16[512,768]{1,0:T(8,128)(2,1)} %get-tuple-element.200.k_ref, ...), custom_call_target="tpu_custom_call", output_to_operand_aliasing={{0}: (8, {}), {1}: (9, {}), {2}: (10, {})} | custom-call | flops 8000000000 | bytes 16000000 | tf_op jit(solution)/shard_map/mix_back/pallas_call | solution.py:536
  439.3 8.9 %weight_back.3 = (bf16[2,2,4,1,96,768]{5,4,3,2,1,0:T(8,128)(2,1)}, bf16[2,2,4,1,96,768]{5,4,3,2,1,0:T(8,128)(2,1)}, f32[2,768]{1,0:T(2,128)}) custom-call(s32[4]{0:T(128)} %pad_add_fusion.place_ref, bf16[1024,768]{1,0:T(8,128)(2,1)} %copy-done.7, bf16[1024,768]{1,0:T(8,128)(2,1)} %get-tuple-element.289.dq_any, bf16[512,768]{1,0:T(8,128)(2,1)} %get-tuple-element.275.dk_any, ...), custom_call_target="tpu_custom_call" | custom-call | flops 2415919104 | bytes 12000000 | tf_op jit(solution)/shard_map/weight_back/pallas_call | solution.py:1013
  469.8 25.7 %collective-permute-done.50 = bf16[2,96,768]{2,1,0:T(8,128)(2,1)S(1)} collective-permute-done((bf16[2,96,768]{2,1,0:T(8,128)(2,1)}, bf16[2,96,768]{2,1,0:T(8,128)(2,1)S(1)}, u32[]{:S(2)}, u32[]{:S(2)}) %collective-permute-start.50) | collective-permute-done | bytes 294944 | tf_op jit(solution)/shard_map/ppermute | solution.py:175
  508.7 7.7 %input_back.1 = (f32[512,768]{1,0:T(8,128)}, f32[512,768]{1,0:T(8,128)}) custom-call(bf16[1024,768]{1,0:T(8,128)(2,1)} %get-tuple-element.289.dq_any, bf16[512,768]{1,0:T(8,128)(2,1)} %get-tuple-element.275.dk_any, bf16[512,768]{1,0:T(8,128)(2,1)} %get-tuple-element.276.dv_any, bf16[4,768,768]{2,1,0:T(8,128)(2,1)} %get-tuple-element.208.attn_any.w_any, ...), custom_call_target="tpu_custom_call" | custom-call | flops 2415919104 | bytes 16000000 | tf_op jit(solution)/shard_map/input_back/pallas_call | solution.py:1062
  532.2 4.7 adam.7
  554.2 6.1 %collective-permute-done.58 = bf16[1,96,768]{2,1,0:T(8,128)(2,1)S(1)} collective-permute-done((bf16[1,96,768]{2,1,0:T(8,128)(2,1)S(1)}, bf16[1,96,768]{2,1,0:T(8,128)(2,1)S(1)}, u32[]{:S(2)}, u32[]{:S(2)}) %collective-permute-start.58) | collective-permute-done | bytes 147488 | tf_op jit(solution)/shard_map/ppermute | solution.py:175
  567.8 6.5 %collective-permute-done.62 = bf16[3,96,768]{2,1,0:T(8,128)(2,1)S(1)} collective-permute-done((bf16[3,96,768]{2,1,0:T(8,128)(2,1)S(1)}, bf16[3,96,768]{2,1,0:T(8,128)(2,1)S(1)}, u32[]{:S(2)}, u32[]{:S(2)}) %collective-permute-start.62) | collective-permute-done | bytes 442400 | tf_op jit(solution)/shard_map/ppermute | solution.py:175
  597.1 4.5 adam.9
  (423 shorter events, 245.2 us)
Async XLA Ops:
  25.5 31.9 %collective-permute-start.8 = (bf16[4,96,768]{2,1,0:T(8,128)(2,1)S(1)}, bf16[4,96,768]{2,1,0:T(8,128)(2,1)S(1)}, u32[]{:S(2)}, u32[]{:S(2)}) collective-permute-start(bf16[4,96,768]{2,1,0:T(8,128)(2,1)S(1)} %get-tuple-element.185), channel_id=1, source_target_pairs={{0,1},{1,0},{2,3},{3,2},{4,5},{5,4},{6,7},{7,6},{8,9},{9,8},{10,11... | collective-permute-start | bytes 1769480 | tf_op jit(solution)/shard_map/ppermute | solution.py:175
  27.0 30.3 %collective-permute-start.7 = (bf16[4,96,768]{2,1,0:T(8,128)(2,1)S(1)}, bf16[4,96,768]{2,1,0:T(8,128)(2,1)S(1)}, u32[]{:S(2)}, u32[]{:S(2)}) collective-permute-start(bf16[4,96,768]{2,1,0:T(8,128)(2,1)S(1)} %get-tuple-element.411), channel_id=1, source_target_pairs={{0,4},{1,5},{2,6},{3,7},{4,0},{5,1},{6,2},{7,3},{8,12},{9,13},{10,... | collective-permute-start | bytes 1769480 | tf_op jit(solution)/shard_map/ppermute | solution.py:175
  61.6 35.7 %collective-permute-start.13 = (bf16[11,96,768]{2,1,0:T(8,128)(2,1)S(1)}, bf16[11,96,768]{2,1,0:T(8,128)(2,1)}, u32[]{:S(2)}, u32[]{:S(2)}) collective-permute-start(bf16[11,96,768]{2,1,0:T(8,128)(2,1)S(1)} %constant_dynamic-update-slice_fusion.3.refs_1_), channel_id=1, source_target_pairs={{0,8},{1,9},{2,10},{3,11},{4,12},{5,13},{6,14},{7,15},{8,0},{9,1},... | collective-permute-start | bytes 4866056 | tf_op jit(solution)/shard_map/ppermute | solution.py:175
  69.9 27.4 %collective-permute-start.10 = (bf16[8,96,768]{2,1,0:T(8,128)(2,1)}, bf16[8,96,768]{2,1,0:T(8,128)(2,1)}, u32[]{:S(2)}, u32[]{:S(2)}) collective-permute-start(bf16[8,96,768]{2,1,0:T(8,128)(2,1)} %pad_maximum_fusion.3), channel_id=1, source_target_pairs={{0,16},{1,17},{2,18},{3,19},{4,20},{5,21},{6,22},{7,23},{8,24},{9,... | collective-permute-start | bytes 3538952 | tf_op jit(solution)/shard_map/ppermute | solution.py:175
  107.6 37.5 %collective-permute-start.21 = (bf16[10,96,768]{2,1,0:T(8,128)(2,1)}, bf16[10,96,768]{2,1,0:T(8,128)(2,1)}, u32[]{:S(2)}, u32[]{:S(2)}) collective-permute-start(bf16[10,96,768]{2,1,0:T(8,128)(2,1)} %constant_dynamic-update-slice_fusion.16.refs_2_), channel_id=1, source_target_pairs={{0,8},{1,9},{2,10},{3,11},{4,12},{5,13},{6,14},{7,15},{8,0},{9,1},... | collective-permute-start | bytes 4423688 | tf_op jit(solution)/shard_map/ppermute | solution.py:175
  111.2 33.8 %collective-permute-start.18 = (bf16[7,96,768]{2,1,0:T(8,128)(2,1)}, bf16[7,96,768]{2,1,0:T(8,128)(2,1)S(1)}, u32[]{:S(2)}, u32[]{:S(2)}) collective-permute-start(bf16[7,96,768]{2,1,0:T(8,128)(2,1)} %fusion.38), channel_id=1, source_target_pairs={{0,1},{1,0},{2,3},{3,2},{4,5},{5,4},{6,7},{7,6},{8,9},{9,8},{10,11... | collective-permute-start | bytes 3096584 | tf_op jit(solution)/shard_map/ppermute | solution.py:175
  114.1 30.9 %collective-permute-start.17 = (bf16[7,96,768]{2,1,0:T(8,128)(2,1)}, bf16[7,96,768]{2,1,0:T(8,128)(2,1)S(1)}, u32[]{:S(2)}, u32[]{:S(2)}) collective-permute-start(bf16[7,96,768]{2,1,0:T(8,128)(2,1)} %pad_maximum_fusion.9), channel_id=1, source_target_pairs={{0,16},{1,17},{2,18},{3,19},{4,20},{5,21},{6,22},{7,23},{8,24},{9,... | collective-permute-start | bytes 3096584 | tf_op jit(solution)/shard_map/ppermute | solution.py:175
  114.8 30.2 %collective-permute-start.19 = (bf16[4,96,768]{2,1,0:T(8,128)(2,1)S(1)}, bf16[4,96,768]{2,1,0:T(8,128)(2,1)S(1)}, u32[]{:S(2)}, u32[]{:S(2)}) collective-permute-start(bf16[4,96,768]{2,1,0:T(8,128)(2,1)S(1)} %pad_maximum_fusion.14), channel_id=1, source_target_pairs={{0,4},{1,5},{2,6},{3,7},{4,0},{5,1},{6,2},{7,3},{8,12},{9,13},{10,... | collective-permute-start | bytes 1769480 | tf_op jit(solution)/shard_map/ppermute | solution.py:175
  153.8 35.0 %collective-permute-start.23 = (bf16[10,96,768]{2,1,0:T(8,128)(2,1)}, bf16[10,96,768]{2,1,0:T(8,128)(2,1)}, u32[]{:S(2)}, u32[]{:S(2)}) collective-permute-start(bf16[10,96,768]{2,1,0:T(8,128)(2,1)} %fusion.40), channel_id=1, source_target_pairs={{0,1},{1,0},{2,3},{3,2},{4,5},{5,4},{6,7},{7,6},{8,9},{9,8},{10,11... | collective-permute-start | bytes 4423688 | tf_op jit(solution)/shard_map/ppermute | solution.py:175
  156.3 31.5 %collective-permute-start.22 = (bf16[9,96,768]{2,1,0:T(8,128)(2,1)}, bf16[9,96,768]{2,1,0:T(8,128)(2,1)}, u32[]{:S(2)}, u32[]{:S(2)}) collective-permute-start(bf16[9,96,768]{2,1,0:T(8,128)(2,1)} %pad_maximum_fusion.2), channel_id=1, source_target_pairs={{0,16},{1,17},{2,18},{3,19},{4,20},{5,21},{6,22},{7,23},{8,24},{9,... | collective-permute-start | bytes 3981320 | tf_op jit(solution)/shard_map/ppermute | solution.py:175
  331.8 52.9 %collective-permute-start.34 = (bf16[4,2,96,768]{3,2,1,0:T(8,128)(2,1)S(1)}, bf16[4,2,96,768]{3,2,1,0:T(8,128)(2,1)}, u32[]{:S(2)}, u32[]{:S(2)}) collective-permute-start(bf16[4,2,96,768]{3,2,1,0:T(8,128)(2,1)S(1)} %pad_maximum_fusion.5), channel_id=1, source_target_pairs={{0,1},{1,0},{2,3},{3,2},{4,5},{5,4},{6,7},{7,6},{8,9},{9,8},{10,11... | collective-permute-start | bytes 3538952 | tf_op jit(solution)/shard_map/ppermute | solution.py:175
  334.2 50.4 %collective-permute-start.33 = (bf16[4,2,96,768]{3,2,1,0:T(8,128)(2,1)}, bf16[4,2,96,768]{3,2,1,0:T(8,128)(2,1)}, u32[]{:S(2)}, u32[]{:S(2)}) collective-permute-start(bf16[4,2,96,768]{3,2,1,0:T(8,128)(2,1)} %pad_maximum_fusion.4), channel_id=1, source_target_pairs={{0,16},{1,17},{2,18},{3,19},{4,20},{5,21},{6,22},{7,23},{8,24},{9,... | collective-permute-start | bytes 3538952 | tf_op jit(solution)/shard_map/ppermute | solution.py:175
  337.3 47.3 %collective-permute-start.35 = (bf16[2,1,96,768]{3,2,0,1:T(8,128)(2,1)}, bf16[2,1,96,768]{3,2,0,1:T(8,128)(2,1)S(1)}, u32[]{:S(2)}, u32[]{:S(2)}) collective-permute-start(bf16[2,1,96,768]{3,2,0,1:T(8,128)(2,1)} %get-tuple-element.397), channel_id=1, source_target_pairs={{0,16},{1,17},{2,18},{3,19},{4,20},{5,21},{6,22},{7,23},{8,24},{9,... | collective-permute-start | bytes 884744 | tf_op jit(solution)/shard_map/ppermute | solution.py:175
  337.8 46.8 %collective-permute-start.36 = (bf16[2,1,96,768]{3,2,0,1:T(8,128)(2,1)}, bf16[2,1,96,768]{3,2,0,1:T(8,128)(2,1)}, u32[]{:S(2)}, u32[]{:S(2)}) collective-permute-start(bf16[2,1,96,768]{3,2,0,1:T(8,128)(2,1)} %get-tuple-element.396), channel_id=1, source_target_pairs={{0,1},{1,0},{2,3},{3,2},{4,5},{5,4},{6,7},{7,6},{8,9},{9,8},{10,11... | collective-permute-start | bytes 884744 | tf_op jit(solution)/shard_map/ppermute | solution.py:175
  384.7 34.7 %collective-permute-start.37 = (bf16[2,2,4,2,96,768]{5,4,3,2,1,0:T(8,128)(2,1)}, bf16[2,2,4,2,96,768]{5,4,3,2,1,0:T(8,128)(2,1)}, u32[]{:S(2)}, u32[]{:S(2)}) collective-permute-start(bf16[2,2,4,2,96,768]{5,4,3,2,1,0:T(8,128)(2,1)} %get-tuple-element.255), channel_id=1, source_target_pairs={{0,8},{1,9},{2,10},{3,11},{4,12},{5,13},{6,14},{7,15},{8,0},{9,1},... | collective-permute-start | bytes 14155784 | tf_op jit(solution)/shard_map/ppermute | solution.py:175
  389.3 29.0 %collective-permute-start.42 = (bf16[2,2,96,768]{3,2,1,0:T(8,128)(2,1)}, bf16[2,2,96,768]{3,2,1,0:T(8,128)(2,1)}, u32[]{:S(2)}, u32[]{:S(2)}) collective-permute-start(bf16[2,2,96,768]{3,2,1,0:T(8,128)(2,1)} %pad_maximum_fusion.17), channel_id=1, source_target_pairs={{0,4},{1,5},{2,6},{3,7},{4,0},{5,1},{6,2},{7,3},{8,12},{9,13},{10,... | collective-permute-start | bytes 1769480 | tf_op jit(solution)/shard_map/ppermute | solution.py:175
  392.7 44.9 %collective-permute-start.41 = (bf16[4,1,96,768]{3,2,0,1:T(8,128)(2,1)}, bf16[4,1,96,768]{3,2,0,1:T(8,128)(2,1)}, u32[]{:S(2)}, u32[]{:S(2)}) collective-permute-start(bf16[4,1,96,768]{3,2,0,1:T(8,128)(2,1)} %pad_maximum_fusion.16), channel_id=1, source_target_pairs={{0,1},{1,0},{2,3},{3,2},{4,5},{5,4},{6,7},{7,6},{8,9},{9,8},{10,11... | collective-permute-start | bytes 1769480 | tf_op jit(solution)/shard_map/ppermute | solution.py:175
  394.8 42.8 %collective-permute-start.40 = (bf16[4,1,96,768]{3,2,0,1:T(8,128)(2,1)}, bf16[4,1,96,768]{3,2,0,1:T(8,128)(2,1)}, u32[]{:S(2)}, u32[]{:S(2)}) collective-permute-start(bf16[4,1,96,768]{3,2,0,1:T(8,128)(2,1)} %pad_maximum_fusion.15), channel_id=1, source_target_pairs={{0,16},{1,17},{2,18},{3,19},{4,20},{5,21},{6,22},{7,23},{8,24},{9,... | collective-permute-start | bytes 1769480 | tf_op jit(solution)/shard_map/ppermute | solution.py:175
  448.2 48.3 %collective-permute-start.46 = (bf16[2,2,4,1,96,768]{5,4,3,2,1,0:T(8,128)(2,1)}, bf16[2,2,4,1,96,768]{5,4,3,2,1,0:T(8,128)(2,1)}, u32[]{:S(2)}, u32[]{:S(2)}) collective-permute-start(bf16[2,2,4,1,96,768]{5,4,3,2,1,0:T(8,128)(2,1)} %get-tuple-element.281), channel_id=1, source_target_pairs={{0,8},{1,9},{2,10},{3,11},{4,12},{5,13},{6,14},{7,15},{8,0},{9,1},... | collective-permute-start | bytes 7077896 | tf_op jit(solution)/shard_map/ppermute | solution.py:175
  458.5 38.0 %collective-permute-start.45 = (bf16[4,2,96,768]{3,2,1,0:T(8,128)(2,1)}, bf16[4,2,96,768]{3,2,1,0:T(8,128)(2,1)}, u32[]{:S(2)}, u32[]{:S(2)}) collective-permute-start(bf16[4,2,96,768]{3,2,1,0:T(8,128)(2,1)} %pad_maximum_fusion.7), channel_id=1, source_target_pairs={{0,1},{1,0},{2,3},{3,2},{4,5},{5,4},{6,7},{7,6},{8,9},{9,8},{10,11... | collective-permute-start | bytes 3538952 | tf_op jit(solution)/shard_map/ppermute | solution.py:175
  460.9 35.7 %collective-permute-start.44 = (bf16[4,2,96,768]{3,2,1,0:T(8,128)(2,1)}, bf16[4,2,96,768]{3,2,1,0:T(8,128)(2,1)}, u32[]{:S(2)}, u32[]{:S(2)}) collective-permute-start(bf16[4,2,96,768]{3,2,1,0:T(8,128)(2,1)} %pad_maximum_fusion.6), channel_id=1, source_target_pairs={{0,16},{1,17},{2,18},{3,19},{4,20},{5,21},{6,22},{7,23},{8,24},{9,... | collective-permute-start | bytes 3538952 | tf_op jit(solution)/shard_map/ppermute | solution.py:175
  464.0 32.6 %collective-permute-start.47 = (bf16[2,1,96,768]{3,2,1,0:T(8,128)(2,1)}, bf16[2,1,96,768]{3,2,1,0:T(8,128)(2,1)}, u32[]{:S(2)}, u32[]{:S(2)}) collective-permute-start(bf16[2,1,96,768]{3,2,1,0:T(8,128)(2,1)} %pad_maximum_fusion.27), channel_id=1, source_target_pairs={{0,4},{1,5},{2,6},{3,7},{4,0},{5,1},{6,2},{7,3},{8,12},{9,13},{10,... | collective-permute-start | bytes 884744 | tf_op jit(solution)/shard_map/ppermute | solution.py:175
  467.8 27.7 %collective-permute-start.50 = (bf16[2,96,768]{2,1,0:T(8,128)(2,1)}, bf16[2,96,768]{2,1,0:T(8,128)(2,1)S(1)}, u32[]{:S(2)}, u32[]{:S(2)}) collective-permute-start(bf16[2,96,768]{2,1,0:T(8,128)(2,1)} %fusion.19), channel_id=1, source_target_pairs={{0,16},{1,17},{2,18},{3,19},{4,20},{5,21},{6,22},{7,23},{8,24},{9,... | collective-permute-start | bytes 884744 | tf_op jit(solution)/shard_map/ppermute | solution.py:175
  506.7 32.2 %collective-permute-start.54 = (bf16[2,2,96,768]{3,2,1,0:T(8,128)(2,1)}, bf16[2,2,96,768]{3,2,1,0:T(8,128)(2,1)}, u32[]{:S(2)}, u32[]{:S(2)}) collective-permute-start(bf16[2,2,96,768]{3,2,1,0:T(8,128)(2,1)} %pad_maximum_fusion.21), channel_id=1, source_target_pairs={{0,4},{1,5},{2,6},{3,7},{4,0},{5,1},{6,2},{7,3},{8,12},{9,13},{10,... | collective-permute-start | bytes 1769480 | tf_op jit(solution)/shard_map/ppermute | solution.py:175
  (111 other events, 1354.4 us)

commit v7 on v6

--- a/solution.py
+++ b/solution.py
@@ -395,37 +395,54 @@
 
     keys = k_ref[...].astype(jnp.float32) * SCORE_SCALE
     values_t = v_ref[...].astype(jnp.float32).T.astype(jnp.bfloat16)
+    keys_own = [
+        jnp.where(head_lanes(keys.shape, head), keys, 0.0).astype(jnp.bfloat16) for head in range(2)
+    ]
     for head in range(2):
         build_tiles(t_ref[head], tile_ref.at[head])
-        keys_own = jnp.where(head_lanes(keys.shape, head), keys, 0.0).astype(jnp.bfloat16)
-        for chunk in range(4):
-            at = chunk * HALF
-            scores = dot_nt(keys_own, q_ref[at : at + HALF, :])
-            for side in range(2):
-                lanes = slice(at + side * 128, at + side * 128 + 128)
-                blocks = []
-                peak = None
-                for key_block in range(4):
-                    rows = slice(key_block * 128, key_block * 128 + 128)
-                    block = scores[rows, side * 128 : side * 128 + 128] + position_bias(
-                        tile_ref.at[head], far_ref, pair * 2 + head, (chunk % 2) * 2 + side, key_block
-                    )
-                    block = jnp.where(mask_ref[rows, lanes] > 0.0, block, MASKED)
-                    blocks.append(block)
-                    high = jnp.max(block, axis=0, keepdims=True)
-                    peak = high if peak is None else jnp.maximum(peak, high)
-                total = None
-                for key_block in range(4):
-                    rows = slice(key_block * 128, key_block * 128 + 128)
-                    expo = jnp.exp(blocks[key_block] - peak)
-                    part = jnp.sum(expo, axis=0, keepdims=True)
-                    total = part if total is None else total + part
-                    p_ref[head, rows, lanes] = expo.astype(jnp.bfloat16)
-                inverse = 1.0 / total
-                inverse_ref[head, :, lanes] = inverse * alive_ref[:, lanes]
-                o_ref[head : head + 1, lanes] = inverse
-        mixed = dot_nn(values_t[head * 64 : head * 64 + 64, :], p_ref[head])
-        o_ref[8 + head * 64 : 8 + head * 64 + 64, :] = mixed * o_ref[head : head + 1, :]
+    work = [(head, chunk) for head in range(2) for chunk in range(4)]
+
+    def score(head, chunk):
+        return dot_nt(keys_own[head], q_ref[chunk * HALF : chunk * HALF + HALF, :])
+
+    def mixture(head, chunk):
+        span = slice(chunk * HALF, chunk * HALF + HALF)
+        own = slice(8 + head * 64, 8 + head * 64 + 64)
+        mixed = dot_nn(values_t[head * 64 : head * 64 + 64, :], p_ref[head, :, span])
+        o_ref[own, span] = mixed * o_ref[head : head + 1, span]
+
+    following = score(*work[0])
+    for index, (head, chunk) in enumerate(work):
+        scores = following
+        if index + 1 < len(work):
+            following = score(*work[index + 1])
+        at = chunk * HALF
+        for side in range(2):
+            lanes = slice(at + side * 128, at + side * 128 + 128)
+            blocks = []
+            peak = None
+            for key_block in range(4):
+                rows = slice(key_block * 128, key_block * 128 + 128)
+                block = scores[rows, side * 128 : side * 128 + 128] + position_bias(
+                    tile_ref.at[head], far_ref, pair * 2 + head, (chunk % 2) * 2 + side, key_block
+                )
+                block = jnp.where(mask_ref[rows, lanes] > 0.0, block, MASKED)
+                blocks.append(block)
+                high = jnp.max(block, axis=0, keepdims=True)
+                peak = high if peak is None else jnp.maximum(peak, high)
+            total = None
+            for key_block in range(4):
+                rows = slice(key_block * 128, key_block * 128 + 128)
+                expo = jnp.exp(blocks[key_block] - peak)
+                part = jnp.sum(expo, axis=0, keepdims=True)
+                total = part if total is None else total + part
+                p_ref[head, rows, lanes] = expo.astype(jnp.bfloat16)
+            inverse = 1.0 / total
+            inverse_ref[head, :, lanes] = inverse * alive_ref[:, lanes]
+            o_ref[head : head + 1, lanes] = inverse
+        if index:
+            mixture(*work[index - 1])
+    mixture(*work[-1])
     a_ref[...] = o_ref[8:, :].T.astype(jnp.bfloat16)
 
 
@@ -1106,41 +1123,48 @@
     )
 
 
-def adam_kernel(rate, master_ref, first_ref, second_ref, grad_ref, *refs):
-    master_out, first_out, second_out = refs[-3:]
-    grad = grad_ref[...].astype(jnp.float32).reshape(master_ref.shape)
-    master = master_ref[...]
-    first = BETA_ONE * first_ref[...] + (1.0 - BETA_ONE) * grad
-    second = BETA_TWO * second_ref[...] + (1.0 - BETA_TWO) * grad * grad
-    first_out[...] = first
-    second_out[...] = second
-    first_scale = rate / (1.0 - BETA_ONE**STEP)
-    second_scale = 1.0 / (1.0 - BETA_TWO**STEP)
-    step = (first_scale * first) / (jnp.sqrt(second_scale * second) + ADAM_EPS)
-    master_out[...] = master - (step + (rate * WEIGHT_DECAY) * master)
-
-
-def adam(kind, layer, rate, state, quarters, member, done):
-    if kind == "attn":
-        block = pl.BlockSpec((1, 1, ROWS, D), lambda i: (layer, i, 0, 0))
-    elif kind == "inner":
-        block = pl.BlockSpec((1, ROWS, D), lambda i: (layer, 0, i))
-    else:
-        block = pl.BlockSpec((1, ROWS, D), lambda i: (layer, i, 0))
-    held = done or ()
+RATES = (ATTENTION_RATE, FEED_RATE, FEED_RATE)
+
+
+def adam_kernel(*refs):
+    states, grads, outs = refs[:9], refs[9:12], refs[-9:]
+    for kind, rate in enumerate(RATES):
+        master_ref, first_ref, second_ref = states[3 * kind : 3 * kind + 3]
+        master_out, first_out, second_out = outs[3 * kind : 3 * kind + 3]
+        grad = grads[kind][...].astype(jnp.float32).reshape(master_ref.shape)
+        master = master_ref[...]
+        first = BETA_ONE * first_ref[...] + (1.0 - BETA_ONE) * grad
+        second = BETA_TWO * second_ref[...] + (1.0 - BETA_TWO) * grad * grad
+        first_out[...] = first
+        second_out[...] = second
+        first_scale = rate / (1.0 - BETA_ONE**STEP)
+        second_scale = 1.0 / (1.0 - BETA_TWO**STEP)
+        step = (first_scale * first) / (jnp.sqrt(second_scale * second) + ADAM_EPS)
+        master_out[...] = master - (step + (rate * WEIGHT_DECAY) * master)
+
+
+def adam(layer, state, quarters, held):
+    half = ROWS // 2
+    blocks = (
+        [pl.BlockSpec((1, 1, half, D), lambda i: (layer, i // 2, i % 2, 0))] * 3
+        + [pl.BlockSpec((1, half, D), lambda i: (layer, i % 2, i // 2))] * 3
+        + [pl.BlockSpec((1, half, D), lambda i: (layer, i, 0))] * 3
+    )
+    grads = [
+        pl.BlockSpec((1, 1, half, D), partial(lambda member, i: (i // 2, member, i % 2, 0), member))
+        for member in (2, 0, 1)
+    ]
     return pl.pallas_call(
-        partial(adam_kernel, rate),
-        grid=(4,),
+        adam_kernel,
+        grid=(8,),
         out_shape=[jax.ShapeDtypeStruct(array.shape, jnp.float32) for array in state],
-        in_specs=[block] * 3
-        + [pl.BlockSpec((1, 1, ROWS, D), lambda i: (i, member, 0, 0))]
-        + [ANY_SPEC] * len(held),
-        out_specs=[block] * 3,
-        input_output_aliases={4 + index: index for index in range(len(held))},
-        compiler_params=PARAMS,
-        cost_estimate=pl.CostEstimate(flops=5000000, bytes_accessed=8000000, transcendentals=0),
+        in_specs=blocks + grads + [ANY_SPEC] * len(held),
+        out_specs=blocks,
+        input_output_aliases={12 + index: index for index in range(len(held))},
+        compiler_params=pltpu.CompilerParams(vmem_limit_bytes=16 * 1024 * 1024),
+        cost_estimate=pl.CostEstimate(flops=20000000, bytes_accessed=22000000, transcendentals=0),
         name="adam",
-    )(*state, quarters, *held)
+    )(*state, quarters, quarters, quarters, *held)
 
 
 def fetch_forward(shards):
@@ -1502,16 +1526,14 @@
     return (tuple(plan), tuple(shards) + tuple(mine) + tuple(theirs))
 
 
-def gather_small(shard, place):
+def gather_small(blocks, place):
     z, y = place[2], place[3]
-    pair = jnp.stack([shard, swap_z(shard, 1)])
-    blocks = jnp.concatenate([pair, swap_z(pair, 2)])
     low, high = z % 2, z // 2
     blocks = jnp.where(low == 0, blocks, blocks[jnp.array([1, 0, 3, 2])])
     blocks = jnp.where(high == 0, blocks, blocks[jnp.array([2, 3, 0, 1])])
     other = swap_y(blocks)
     pairs = jnp.where(y == 0, jnp.stack([blocks, other], 1), jnp.stack([other, blocks], 1))
-    return pairs.transpose(2, 0, 1, 3).reshape(shard.shape[0], -1)
+    return pairs.transpose(2, 0, 1, 3).reshape(blocks.shape[1], -1)
 
 
 def add_low(*values):
@@ -1526,39 +1548,49 @@
     return (swap_x(corner[:2]), swap_y(corner[2:]))
 
 
-def reduce_sides(keep, get, corners):
+def side_payloads(keep, get, corners):
     by_x, by_y = corners
-    for_y = jnp.concatenate([add_low(keep[1, 0, :2], get[1, 0, :2], by_x), add_low(keep[1, 0, 2:], get[1, 0, 2:])])
-    for_x = jnp.concatenate([add_low(keep[0, 1, :2], get[0, 1, :2]), add_low(keep[0, 1, 2:], get[0, 1, 2:], by_y)])
-    return (swap_x(for_x), swap_y(for_y))
-
-
-def reduce_column(keep, get, sides):
-    return add_low(keep[0, 0], get[0, 0], *sides)
-
-
-def at_z(column, place, apart):
-    return lax.dynamic_index_in_dim(column, place[2] ^ apart, 0, keepdims=False)
-
-
-def reduce_far(column, place):
-    return swap_z(jnp.stack([at_z(column, place, 2), at_z(column, place, 3)]), 2)
-
-
-def reduce_near(column, far, place):
-    return swap_z(add_low(at_z(column, place, 1), far[1]), 1)
-
-
-def reduce_total(column, far, near, place):
-    return add_low(at_z(column, place, 0), far[0], near)
+    pad = ((0, 0),) * 3
+    for_x = add_low(keep[0, 1], get[0, 1], jnp.pad(by_y, ((2, 0),) + pad))
+    for_y = add_low(keep[1, 0], get[1, 0], jnp.pad(by_x, ((0, 2),) + pad))
+    return (for_x, for_y)
+
+
+def reduce_sides(payloads):
+    return (swap_x(payloads[0]), swap_y(payloads[1]))
+
+
+def z_pair(values, half):
+    return add_low(*(lax.dynamic_slice_in_dim(value, 2 * half, 2, 0) for value in values))
+
+
+def far_payload(keep, get, sides, place):
+    return z_pair((keep[0, 0], get[0, 0]) + tuple(sides), 1 - place[2] // 2)
+
+
+def own_pair(keep, get, sides, far, place):
+    half = place[2] // 2
+    pair = (
+        lax.dynamic_slice_in_dim(value, 2 * half, 2, 0)
+        for value in (keep[0, 0], get[0, 0]) + tuple(sides)
+    )
+    return add_low(*pair, far)
+
+
+def pick(pair, index):
+    return lax.dynamic_index_in_dim(pair, index, 0, keepdims=False)
+
+
+def reduce_near(pair, place):
+    return swap_z(pick(pair, 1 - place[2] % 2), 1)
+
+
+def reduce_total(pair, near, place):
+    return add_low(pick(pair, place[2] % 2), near)
 
 
 def reduce_direct(column, place):
-    return tuple(swap_z(at_z(column, place, apart), apart) for apart in (1, 2, 3))
-
-
-def direct_total(column, shifts, place):
-    return add_low(at_z(column, place, 0), *shifts)
+    return tuple(swap_z(pick(column, place[2] ^ apart), apart) for apart in (1, 2, 3))
 
 
 def share_core(pair, place):
@@ -1619,30 +1651,30 @@
     feed_low = [tuple(w.astype(jnp.bfloat16) for w in shards) for shards in feed_shards]
     col_a0 = jnp.concatenate(z_a0)
     x0 = swap_x(col_a0)
-    y0 = swap_y(col_a0)
+    y0 = swap_y(jnp.concatenate([col_a0, own_f0, oth_f0]))
     far_f0 = swap_z(jnp.concatenate([own_f0, near_f0]), 2)
-    plane_f0 = swap_y(after(jnp.concatenate([own_f0, oth_f0]), z_a0))
     near_1 = swap_z(after(jnp.concatenate([own_a1, own_f1]), z_a0), 1)
-    x0, y0, far_f0, plane_f0, near_1 = join(x0, y0, far_f0, plane_f0, near_1)
+    small_low = small_master.astype(jnp.bfloat16)
+    small_near = swap_z(after(small_low, z_a0), 1)
+    x0, y0, far_f0, near_1, small_near = join(x0, y0, far_f0, near_1, small_near)
     col_f0 = jnp.concatenate([near_f0, far_f0])
     x1 = swap_x(jnp.concatenate([col_f0, y0[:2]]))
     y1 = swap_y(jnp.concatenate([col_f0, x0[2:]]))
     far_a1 = swap_z(jnp.concatenate([own_a1, near_1[:1]]), 2)
-    mine_0 = jnp.concatenate([plane_a0, col_a0, x0, y0])
+    mine_0 = jnp.concatenate([plane_a0, col_a0, x0, y0, col_f0])
     theirs_0 = swap_core(mine_0)
-    small_all = gather_small(after(small_master.astype(jnp.bfloat16), far_f0), place_parts)
+    small_pair = jnp.stack([small_low, small_near])
+    small_far = swap_z(small_pair, 2)
+    small_all = gather_small(jnp.concatenate([small_pair, small_far]), place_parts)
     x1, y1, far_a1, theirs_0, small_all = join(x1, y1, far_a1, theirs_0, small_all)
     col_a1 = jnp.concatenate([near_1[:1], far_a1])
     x2 = swap_x(jnp.concatenate([col_a1, y1[:4]]))
     y2 = swap_y(jnp.concatenate([col_a1, x1[4:6], own_a1, oth_a1]))
     far_f1 = swap_z(jnp.concatenate([own_f1, after(near_1[1:], far_a1)]), 2)
-    mine_1 = jnp.concatenate([x1, y1])
-    theirs_1 = swap_core(mine_1)
-    mine_p0 = jnp.concatenate([plane_f0, col_f0])
-    theirs_p0 = swap_core(after(mine_p0, theirs_1))
+    their_x1, their_y1 = swap_core(x1), swap_core(y1)
     group_a0 = gather_group(
-        1, attn_low[0], (0, 0), (0, 2), ((0, 5), (0, 8)), ((1, 6, 2), (1, 14, 1)),
-        (mine_0, mine_1), (theirs_0, theirs_1),
+        1, attn_low[0], (0, 0), (0, 2), ((0, 5), (0, 8)), ((1, 6, 2), (2, 6, 1)),
+        (mine_0, x1, y1), (theirs_0, their_x1, their_y1),
     )
     row_flags = predicted.reshape(1, LEN).astype(jnp.float32)
     col_flags = predicted.reshape(LEN, 1).astype(jnp.float32)
@@ -1651,15 +1683,14 @@
     small1, hidden_bias1, (tvec1, far1, onehot) = small_parts(small_all[1])
     q0, k0, v0, attn0 = project(place, low0, small0, group_a0)
     mixed0, p0, inverse0, dead = mix(lengths, far0, tvec0, q0, k0, v0, row_flags, col_flags)
-    x2, y2, far_f1, mixed0, theirs_p0 = join(x2, y2, far_f1, mixed0, theirs_p0)
+    x2, y2, far_f1, mixed0 = join(x2, y2, far_f1, mixed0)
     col_f1 = jnp.concatenate([near_1[1:], far_f1])
     x3 = swap_x(jnp.concatenate([col_f1, y2[:3]]))
     y3 = swap_y(jnp.concatenate([col_f1, own_f1, oth_f1]))
-    mine_2 = jnp.concatenate([x2, y2, col_a1])
-    theirs_2 = swap_core(mine_2)
+    their_x2, their_y2, their_a1 = swap_core(x2), swap_core(y2), swap_core(after(col_a1, x2))
     group_f0 = gather_group(
-        2, feed_low[0], (0, 0), (0, 4), ((1, 0), (1, 8)), ((2, 3, 4), (2, 10, 2)),
-        (mine_p0, mine_1, mine_2), (theirs_p0, theirs_1, theirs_2),
+        2, feed_low[0], (0, 11), (0, 15), ((1, 0), (2, 0)), ((3, 3, 4), (4, 3, 2)),
+        (mine_0, x1, y1, x2, y2), (theirs_0, their_x1, their_y1, their_x2, their_y2),
     )
     resid0, pre0, normed0, low1, summed0 = feed(
         place, small0, hidden_bias0, mixed0, low0, attn0, group_f0
@@ -1667,19 +1698,17 @@
     x3, y3, low1 = join(x3, y3, low1)
     x4 = swap_x(y3[:3])
     y4 = swap_y(x3[3:6])
-    mine_3 = jnp.concatenate([x3, y3])
-    theirs_3 = swap_core(mine_3)
+    their_x3, their_y3 = swap_core(x3), swap_core(y3)
     group_a1 = gather_group(
-        1, attn_low[1], (0, 12), (0, 14), ((0, 0), (0, 7)), ((1, 6, 3),),
-        (mine_2, mine_3), (theirs_2, theirs_3),
+        1, attn_low[1], (1, 5), (2, 0), ((0, 0), (1, 0)), ((3, 6, 3),),
+        (x2, y2, col_a1, x3), (their_x2, their_y2, their_a1, their_x3),
     )
     q1, k1, v1, attn1 = project(place, low1, small1, group_a1)
     x4, y4, q1 = join(x4, y4, q1)
-    mine_4 = jnp.concatenate([col_f1, x4, y4])
-    theirs_4 = swap_core(mine_4)
+    their_x4, their_y4, their_f1 = swap_core(x4), swap_core(y4), swap_core(after(col_f1, q1))
     group_f1 = gather_group(
-        2, feed_low[1], (0, 15), (1, 0), ((0, 0), (0, 9)), ((1, 6, 3), (1, 9, 3)),
-        (mine_3, mine_4), (theirs_3, theirs_4),
+        2, feed_low[1], (1, 6), (4, 0), ((0, 0), (1, 0)), ((2, 0, 3), (3, 0, 3)),
+        (x3, y3, x4, y4, col_f1), (their_x3, their_y3, their_x4, their_y4, their_f1),
     )
     mixed1, p1, inverse1, dead = mix(
         lengths, far1, tvec1, q1, k1, v1, row_flags, col_flags
@@ -1694,7 +1723,7 @@
     dq1, dk1, dv1, table1_b = mix_back(
         3, after(q1, get_f1, table1_a), k1, v1, dmix1, mixed1, p1, inverse1, dead, tuple(first1)
     )
-    sides_rf1 = reduce_sides(keep_f1, get_f1, after(by_f1, table1_b))
+    sides_rf1 = reduce_sides(side_payloads(keep_f1, get_f1, after(by_f1, table1_b)))
     keep_a1, send_a1, vec_a1 = weight_back(place, after(low1, by_f1), dq1, dk1, dv1, dwo1)
     get_a1 = swap_core(send_a1)
     by_a1 = reduce_corners(keep_a1, get_a1)
@@ -1703,30 +1732,32 @@
         pre0, mixed0, attn0, group_f0
     )
     get_f0 = swap_core(after(send_f0, sides_rf1, by_a1))
-    sides_ra1 = reduce_sides(keep_a1, get_a1, after(by_a1, dmix0))
-    column_f1 = reduce_column(keep_f1, get_f1, after(sides_rf1, dmix0))
-    zfar_f1 = reduce_far(column_f1, place_parts)
+    sides_ra1 = reduce_sides(side_payloads(keep_a1, get_a1, after(by_a1, dmix0)))
+    sides_rf1 = after(sides_rf1, dmix0)
+    zfar_f1 = swap_z(far_payload(keep_f1, get_f1, sides_rf1, place_parts), 2)
     *first0, table0_a = mix_back(
         0, after(q0, by_a1, sides_rf1), k0, v0, dmix0, mixed0, p0, inverse0, dead
     )
     by_f0 = reduce_corners(keep_f0, after(get_f0, table0_a))
-    zfar_f1 = after(zfar_f1, table0_a)
-    znear_f1 = reduce_near(column_f1, zfar_f1, place_parts)
+    pair_f1 = own_pair(keep_f1, get_f1, sides_rf1, after(zfar_f1, table0_a), place_parts)
+    znear_f1 = reduce_near(pair_f1, place_parts)
     dq0, dk0, dv0, table0_b = mix_back(
         3, after(q0, get_f0, zfar_f1), k0, v0, dmix0, mixed0, p0, inverse0, dead, tuple(first0)
     )
     by_f0, sides_ra1, znear_f1, table0_b = join(by_f0, sides_ra1, znear_f1, table0_b)
-    sides_rf0 = reduce_sides(keep_f0, get_f0, by_f0)
-    keep_a0, send_a0, vec_a0 = weight_back(place, after(low0, table0_b), dq0, dk0, dv0, dwo0)
+    payloads_f0 = side_payloads(keep_f0, get_f0, by_f0)
+    sides_rf0 = reduce_sides(payloads_f0)
+    keep_a0, send_a0, vec_a0 = weight_back(
+        place, after(low0, payloads_f0, table0_b), dq0, dk0, dv0, dwo0
+    )
     get_a0 = swap_core(send_a0)
-    column_a1 = reduce_column(keep_a1, get_a1, sides_ra1)
-    zfar_a1 = reduce_far(column_a1, place_parts)
+    zfar_a1 = swap_z(far_payload(keep_a1, get_a1, sides_ra1, place_parts), 2)
     sides_rf0, get_a0, zfar_a1, vec_a0 = join(sides_rf0, get_a0, zfar_a1, vec_a0)
-    column_f0 = reduce_column(keep_f0, get_f0, sides_rf0)
-    zfar_f0 = reduce_far(column_f0, place_parts)
-    by_a0 = reduce_corners(keep_a0, get_a0)
-    own_f1 = reduce_total(column_f1, zfar_f1, znear_f1, place_parts)
-    pair_f1 = jnp.stack([own_f1, swap_x(own_f1)])
+    payload_f0 = far_payload(keep_f0, get_f0, sides_rf0, place_parts)
+    zfar_f0 = swap_z(payload_f0, 2)
+    by_a0 = reduce_corners(keep_a0, after(get_a0, payload_f0))
+    pair_a1 = own_pair(keep_a1, get_a1, sides_ra1, zfar_a1, place_parts)
+    znear_a1 = reduce_near(after(pair_a1, payload_f0), place_parts)
     content_grad, query_grad = input_back(after(dq0, sides_rf0), dk0, dv0, attn0, dresid0)
     small_sum = jnp.concatenate(
         [
@@ -1739,53 +1770,50 @@
         ],
         axis=1,
     )
-    small_sum = small_sum + swap_core(small_sum)
-    by_a0, pair_f1, content_grad, small_sum = join(by_a0, pair_f1, content_grad, small_sum)
-    sides_ra0 = reduce_sides(keep_a0, get_a0, by_a0)
-    znear_a1 = reduce_near(column_a1, zfar_a1, place_parts)
-    four_f1 = share_core(pair_f1, place_parts)
-    attn_state = (attn_master, attn_first, attn_second)
-    inner_state = (inner_master, inner_first, inner_second)
-    outer_state = (outer_master, outer_first, outer_second)
-    inner_new = adam("inner", 1, FEED_RATE, inner_state, four_f1, 0, None)
-    outer_new = adam("outer", 1, FEED_RATE, outer_state, four_f1, 1, None)
-    sides_ra0, zfar_f0, znear_a1, inner_new, outer_new = join(
-        sides_ra0, zfar_f0, znear_a1, inner_new, outer_new
-    )
-    column_a0 = reduce_column(keep_a0, get_a0, sides_ra0)
+    by_a0, content_grad, znear_a1 = join(by_a0, content_grad, znear_a1)
+    payloads_a0 = side_payloads(keep_a0, get_a0, by_a0)
+    sides_ra0 = reduce_sides(payloads_a0)
+    own_1 = jnp.concatenate(
+        [
+            reduce_total(pair_f1, znear_f1, place_parts),
+            reduce_total(pair_a1, znear_a1, place_parts),
+        ]
+    )
+    across_1 = swap_x(after(own_1, payloads_a0))
+    small_sum = small_sum + swap_core(after(small_sum, payloads_a0))
+    sides_ra0, zfar_f0, small_sum = join(sides_ra0, zfar_f0, small_sum)
+    column_a0 = add_low(keep_a0[0, 0], get_a0[0, 0], *sides_ra0)
     shifts_a0 = reduce_direct(column_a0, place_parts)
-    znear_f0 = reduce_near(column_f0, zfar_f0, place_parts)
-    own_a1 = reduce_total(column_a1, zfar_a1, znear_a1, place_parts)
-    pair_a1 = jnp.stack([own_a1, swap_x(after(own_a1, column_a0))])
-    shifts_a0, znear_f0, pair_a1 = join(shifts_a0, znear_f0, pair_a1)
+    pair_f0 = own_pair(keep_f0, get_f0, sides_rf0, zfar_f0, place_parts)
+    znear_f0 = reduce_near(after(pair_f0, column_a0), place_parts)
+    small_sum = small_sum + swap_y(after(small_sum, column_a0))
+    shifts_a0, znear_f0, across_1, small_sum = join(shifts_a0, znear_f0, across_1, small_sum)
     own_0 = jnp.concatenate(
         [
-            reduce_total(column_f0, zfar_f0, znear_f0, place_parts),
-            direct_total(column_a0, shifts_a0, place_parts),
+            reduce_total(pair_f0, znear_f0, place_parts),
+            add_low(pick(column_a0, place_parts[2]), *shifts_a0),
         ]
     )
-    pair_0 = jnp.stack([own_0, swap_x(own_0)])
-    four_a1 = share_core(pair_a1, place_parts)
-    small_sum = small_sum + swap_y(small_sum)
-    attn_new = adam("attn", 1, ATTENTION_RATE, attn_state, four_a1, 0, None)
-    pair_0, attn_new, small_sum = join(pair_0, attn_new, small_sum)
-    four_0 = share_core(pair_0, place_parts)
-    small_sum = small_sum + swap_x(small_sum)
-    four_0, small_sum = join(four_0, small_sum)
-    small_far = swap_z(small_sum, 1)
-    inner_new = adam("inner", 0, FEED_RATE, inner_state, four_0, 0, tuple(inner_new))
-    small_sum = small_sum + small_far
-    outer_new = adam("outer", 0, FEED_RATE, outer_state, four_0, 1, tuple(outer_new))
+    across_0 = swap_x(own_0)
+    four_1 = share_core(jnp.stack([own_1, after(across_1, own_0)]), place_parts)
+    state = (
+        attn_master, attn_first, attn_second, inner_master, inner_first, inner_second,
+        outer_master, outer_first, outer_second,
+    )
+    new_1 = adam(1, state, four_1, ())
+    small_sum = small_sum + swap_z(after(small_sum, own_0), 1)
     small_sum = small_sum + swap_z(small_sum, 2)
-    attn_new = adam("attn", 0, ATTENTION_RATE, attn_state, four_0, 2, tuple(attn_new))
+    across_0, new_1, small_sum = join(across_0, new_1, small_sum)
+    four_0 = share_core(jnp.stack([own_0, across_0]), place_parts)
+    small_x = swap_x(small_sum)
+    new_0 = adam(0, state, four_0, tuple(new_1))
+    small_sum = small_sum + small_x
     size = small_master.shape[1]
     small_own = lax.dynamic_slice_in_dim(small_sum, lax.axis_index("fsdp") * size, size, 1)
     small_new = adam_update(small_master, small_first, small_second, small_own, SMALL_RATE)
     return (
         (content_out, query_out, content_grad, query_grad)
-        + tuple(attn_new)
-        + tuple(inner_new)
-        + tuple(outer_new)
+        + tuple(new_0)
         + small_new
     )
 

time: 613 us -> 609 us (level)
  local copies, waits for them, and re-layouts: 63.2 us -> 86.3 us
  Pallas kernels: 280 us -> 263 us
  other arithmetic: 66.2 us -> 59.8 us
    unnamed x149 -> x178, local copies, waits for them, and re-layouts: 26.3 us -> 50.4 us
    pallas_call x6 -> x2, Pallas kernels: 27.3 us -> 12.6 us  [adam(): pl.pallas_call(adam_kernel, grid=(8,), out_shape=[jax.ShapeDtypeStruct(ar...]
    slice x0 -> x6, local copies, waits for them, and re-layouts: none -> 7.85 us  [the longest x4 5 us: far_payload(): return z_pair((keep[0, 0], get[0, 0]) + tuple(sides), 1 - place[2] // 2)]
    concatenate x12 -> x6, other arithmetic: 10.5 us -> 3.81 us  [the longest x1 1.86 us: per_device_fast(): col_a0 = jnp.concatenate(z_a0)]
    ppermute x69 -> x71, starting transfers between devices: 68.8 us -> 62.9 us  [move(): return lax.ppermute(value, AXES, pairs)]
    convert_element_type x23 -> x19, other arithmetic: 35.5 us -> 32.6 us  [add_low(): return total.astype(jnp.bfloat16)]
    ppermute x69 -> x71, waiting for transfers between devices: 121 us -> 124 us  [move(): return lax.ppermute(value, AXES, pairs)]
  transfers between devices with their start and end apart: 69 -> 71, of which waited for: 22 -> 28; matrix products, arithmetic and copies ran while one was open for 16% -> 15% of each run, Pallas kernels for 34% -> 31%
where the time goes in v7:
time: 609 us; the launch traced here: 600 us
  Pallas kernels  263 us (43%)
  waiting for transfers between devices  124 us (20%)
  local copies, waits for them, and re-layouts  86.3 us (14%)
  starting transfers between devices  62.9 us (10%)
  other arithmetic  59.8 us (10%)
    ppermute x71, waiting for transfers between devices, move(): return lax.ppermute(value, AXES, pairs)  124 us
    ppermute x71, starting transfers between devices, move(): return lax.ppermute(value, AXES, pairs)  62.9 us
    pallas_call x1, Pallas kernels, turn(): pl.pallas_call(partial(turn_kernel, plan), out_shape=[half_low, half_low]...  55.5 us
    unnamed x178, local copies, waits for them, and re-layouts  50.4 us
    pallas_call x4, Pallas kernels, mix_back(): pl.pallas_call(mix_back_kernel, grid=(H // 4,), out_shape=[jax.ShapeDtype...  49.8 us
    pallas_call x1, Pallas kernels, down(): pl.pallas_call(partial(down_kernel, plan), out_shape=BACK_SHAPES, in_spec...  46.2 us
    pallas_call x2, Pallas kernels, mix(): pl.pallas_call(mix_kernel, grid=(H // 2,), out_shape=[jax.ShapeDtypeStruc...  36.8 us
    convert_element_type x19, other arithmetic, add_low(): return total.astype(jnp.bfloat16)  32.6 us
  transfers between devices with their start and end apart: 71, of which 28 were waited for; matrix products, arithmetic and copies ran while one was open for 15% of the time, Pallas kernels for 31%

profile of v7, /device:TPU:0, one launch (start us, length us, event | category | flops | bytes accessed | tf_op | source)
XLA Modules:
  0.0 600.0 jit_solution(9911257238466103806)
XLA Ops:
  47.4 14.7 %collective-permute-done.9 = bf16[2,1200]{1,0:T(2,128)(2,1)S(1)} collective-permute-done((bf16[2,1200]{1,0:T(2,128)(2,1)S(1)}, bf16[2,1200]{1,0:T(2,128)(2,1)S(1)}, u32[]{:S(2)}, u32[]{:S(2)}) %collective-permute-start.9) | collective-permute-done | bytes 4832 | tf_op jit(solution)/shard_map/ppermute | solution.py:175
  62.2 5.2 collective-permute-done.7
  90.4 13.5 %collective-permute-done.15 = bf16[4,2,1200]{2,1,0:T(2,128)(2,1)S(1)} collective-permute-done((bf16[4,2,1200]{2,1,0:T(2,128)(2,1)S(1)}, bf16[4,2,1200]{2,1,0:T(2,128)(2,1)S(1)}, u32[]{:S(2)}, u32[]{:S(2)}) %collective-permute-start.15) | collective-permute-done | bytes 19232 | tf_op jit(solution)/shard_map/ppermute | solution.py:175
  104.1 9.6 %collective-permute-done.10.refs_2_.refs_3_ = bf16[8,96,768]{2,1,0:T(8,128)(2,1)S(1)} collective-permute-done((bf16[8,96,768]{2,1,0:T(8,128)(2,1)}, bf16[8,96,768]{2,1,0:T(8,128)(2,1)S(1)}, u32[]{:S(2)}, u32[]{:S(2)}) %collective-permute-start.10) | collective-permute-done | bytes 1179680 | tf_op jit(solution)/shard_map/ppermute | solution.py:175
  128.0 7.5 %project.2 = (bf16[1024,768]{1,0:T(8,128)(2,1)}, bf16[512,768]{1,0:T(8,128)(2,1)}, bf16[512,768]{1,0:T(8,128)(2,1)}, bf16[4,768,768]{2,1,0:T(8,128)(2,1)}) custom-call(s32[4]{0:T(128)} %pad_add_fusion.place_ref, f32[8,768]{1,0:T(8,128)} %reshape.633.small_ref.below_ref, bf16[1024,768]{1,0:T(8,128)(2,1)} %copy-done.19, ...), custom_call_target="tpu_custom_call" | custom-call | flops 2415919104 | bytes 16000000 | tf_op jit(solution)/shard_map/project/pallas_call | solution.py:317
  135.4 18.4 %mix.2 = (bf16[1024,768]{1,0:T(8,128)(2,1)}, bf16[12,512,1024]{2,1,0:T(8,128)(2,1)}, f32[12,1,1024]{2,1,0:T(1,128)}, f32[1,1024]{1,0:T(1,128)}) custom-call(s32[1]{0:T(128)S(6)} %copy.183.length_ref, f32[12,2]{1,0:T(8,128)} %pad_maximum_fusion.22.far_ref, bf16[1024,768]{1,0:T(8,128)(2,1)} %get-tuple-element.270.q_ref, ...), custom_call_target="tpu_custom_call" | custom-call | flops 6499999744 | bytes 8000000 | tf_op jit(solution)/shard_map/mix/pallas_call | solution.py:452
  164.6 21.9 %feed.1 = (f32[1024,768]{1,0:T(8,128)}, bf16[4,1024,768]{2,1,0:T(8,128)(2,1)}, bf16[1024,768]{1,0:T(8,128)(2,1)}, bf16[1024,768]{1,0:T(8,128)(2,1)}, f32[1024,768]{1,0:T(8,128)}) custom-call(s32[4]{0:T(128)} %pad_add_fusion.place_ref, f32[8,768]{1,0:T(8,128)} %reshape.633.small_ref.below_ref, f32[1,3072]{1,0:T(1,128)} %slice.343.hidden_bias_ref, ...), custom_call_target="tpu_custom_call" | custom-call | flops 10871635968 | bytes 30000000 | tf_op jit(solution)/shard_map/feed/pallas_call | solution.py:686
  186.5 8.0 %collective-permute-done.21.refs_4_.refs_2_ = bf16[9,96,768]{2,1,0:T(8,128)(2,1)S(1)} collective-permute-done((bf16[9,96,768]{2,1,0:T(8,128)(2,1)}, bf16[9,96,768]{2,1,0:T(8,128)(2,1)S(1)}, u32[]{:S(2)}, u32[]{:S(2)}) %collective-permute-start.21) | collective-permute-done | bytes 1327136 | tf_op jit(solution)/shard_map/ppermute | solution.py:175
  202.4 7.6 %project.3 = (bf16[1024,768]{1,0:T(8,128)(2,1)}, bf16[512,768]{1,0:T(8,128)(2,1)}, bf16[512,768]{1,0:T(8,128)(2,1)}, bf16[4,768,768]{2,1,0:T(8,128)(2,1)}) custom-call(s32[4]{0:T(128)} %pad_add_fusion.place_ref, f32[8,768]{1,0:T(8,128)} %reshape.632.small_ref, bf16[1024,768]{1,0:T(8,128)(2,1)} %get-tuple-element.244.low_any, ...), custom_call_target="tpu_custom_call" | custom-call | flops 2415919104 | bytes 16000000 | tf_op jit(solution)/shard_map/project/pallas_call | solution.py:317
  212.9 18.4 %mix.3 = (bf16[1024,768]{1,0:T(8,128)(2,1)}, bf16[12,512,1024]{2,1,0:T(8,128)(2,1)}, f32[12,1,1024]{2,1,0:T(1,128)}, f32[1,1024]{1,0:T(1,128)}) custom-call(s32[1]{0:T(128)S(6)} %copy.183.length_ref, f32[12,2]{1,0:T(8,128)} %pad_maximum_fusion.21.far_ref, bf16[1024,768]{1,0:T(8,128)(2,1)} %get-tuple-element.235.q_ref, ...), custom_call_target="tpu_custom_call" | custom-call | flops 6499999744 | bytes 8000000 | tf_op jit(solution)/shard_map/mix/pallas_call | solution.py:452
  232.5 55.5 %turn.1 = (bf16[512,768]{1,0:T(8,128)(2,1)}, bf16[512,768]{1,0:T(8,128)(2,1)}, f32[1024,768]{1,0:T(8,128)}, bf16[1024,768]{1,0:T(8,128)(2,1)}, bf16[768,768]{1,0...) custom-call(s32[4]{0:T(128)} %pad_add_fusion.place_ref, ...), custom_call_target="tpu_custom_call" | custom-call | flops 32614907904 | bytes 60000000 | tf_op jit(solution)/shard_map/turn/pallas_call | solution.py:877
  288.5 12.3 %mix_back.4 = (bf16[1024,768]{1,0:T(8,128)(2,1)}, bf16[512,768]{1,0:T(8,128)(2,1)}, bf16[512,768]{1,0:T(8,128)(2,1)}, f32[6,1,768]{2,1,0:T(1,128)}) custom-call(bf16[1024,768]{1,0:T(8,128)(2,1)} %get-tuple-element.235.q_ref, bf16[512,768]{1,0:T(8,128)(2,1)} %get-tuple-element.219.k_ref, bf16[512,768]{1,0:T(8,128)(2,1)} %get-tuple-element.220.v_ref, ...), custom_call_target="tpu_custom_call" | custom-call | flops 8000000000 | bytes 16000000 | tf_op jit(solution)/shard_map/mix_back/pallas_call | solution.py:553
  305.2 12.6 %mix_back.5 = (bf16[1024,768]{1,0:T(8,128)(2,1)}, bf16[512,768]{1,0:T(8,128)(2,1)}, bf16[512,768]{1,0:T(8,128)(2,1)}, f32[6,1,768]{2,1,0:T(1,128)}) custom-call(bf16[1024,768]{1,0:T(8,128)(2,1)} %get-tuple-element.235.q_ref, bf16[512,768]{1,0:T(8,128)(2,1)} %get-tuple-element.219.k_ref, ...), custom_call_target="tpu_custom_call", output_to_operand_aliasing={{0}: (8, {}), {1}: (9, {}), {2}: (10, {})} | custom-call | flops 8000000000 | bytes 16000000 | tf_op jit(solution)/shard_map/mix_back/pallas_call | solution.py:553
  319.4 8.8 %weight_back.2 = (bf16[2,2,4,1,96,768]{5,4,3,2,1,0:T(8,128)(2,1)}, bf16[2,2,4,1,96,768]{5,4,3,2,1,0:T(8,128)(2,1)}, f32[2,768]{1,0:T(2,128)}) custom-call(s32[4]{0:T(128)} %pad_add_fusion.place_ref, bf16[1024,768]{1,0:T(8,128)(2,1)} %get-tuple-element.244.low_any, bf16[1024,768]{1,0:T(8,128)(2,1)} %get-tuple-element.239.dq_any, ...), custom_call_target="tpu_custom_call" | custom-call | flops 2415919104 | bytes 12000000 | tf_op jit(solution)/shard_map/weight_back/pallas_call | solution.py:1030
  338.1 46.2 %down.1 = (f32[1024,768]{1,0:T(8,128)}, bf16[1024,768]{1,0:T(8,128)(2,1)}, bf16[768,768]{1,0:T(8,128)(2,1)}, bf16[2,2,4,2,96,768]{5,4,3,2,1,0:T(8,128)(2,1)}, bf...) custom-call(s32[4]{0:T(128)} %pad_add_fusion.place_ref, ...), custom_call_target="tpu_custom_call" | custom-call | flops 27179089920 | bytes 60000000 | tf_op jit(solution)/shard_map/down/pallas_call | solution.py:963
  394.3 12.4 %mix_back.6 = (bf16[1024,768]{1,0:T(8,128)(2,1)}, bf16[512,768]{1,0:T(8,128)(2,1)}, bf16[512,768]{1,0:T(8,128)(2,1)}, f32[6,1,768]{2,1,0:T(1,128)}) custom-call(bf16[1024,768]{1,0:T(8,128)(2,1)} %get-tuple-element.270.q_ref, bf16[512,768]{1,0:T(8,128)(2,1)} %get-tuple-element.204.k_ref, bf16[512,768]{1,0:T(8,128)(2,1)} %get-tuple-element.205.v_ref, ...), custom_call_target="tpu_custom_call" | custom-call | flops 8000000000 | bytes 16000000 | tf_op jit(solution)/shard_map/mix_back/pallas_call | solution.py:553
  406.7 12.6 %collective-permute-done.46 = bf16[2,2,96,768]{3,2,1,0:T(8,128)(2,1)} collective-permute-done((bf16[2,2,96,768]{3,2,1,0:T(8,128)(2,1)}, bf16[2,2,96,768]{3,2,1,0:T(8,128)(2,1)}, u32[]{:S(2)}, u32[]{:S(2)}) %collective-permute-start.46) | collective-permute-done | bytes 589856 | tf_op jit(solution)/shard_map/ppermute | solution.py:175
  425.1 12.5 %mix_back.7 = (bf16[1024,768]{1,0:T(8,128)(2,1)}, bf16[512,768]{1,0:T(8,128)(2,1)}, bf16[512,768]{1,0:T(8,128)(2,1)}, f32[6,1,768]{2,1,0:T(1,128)}) custom-call(bf16[1024,768]{1,0:T(8,128)(2,1)} %get-tuple-element.270.q_ref, bf16[512,768]{1,0:T(8,128)(2,1)} %get-tuple-element.204.k_ref, ...), custom_call_target="tpu_custom_call", output_to_operand_aliasing={{0}: (8, {}), {1}: (9, {}), {2}: (10, {})} | custom-call | flops 8000000000 | bytes 16000000 | tf_op jit(solution)/shard_map/mix_back/pallas_call | solution.py:553
  443.5 8.9 %weight_back.3 = (bf16[2,2,4,1,96,768]{5,4,3,2,1,0:T(8,128)(2,1)}, bf16[2,2,4,1,96,768]{5,4,3,2,1,0:T(8,128)(2,1)}, f32[2,768]{1,0:T(2,128)}) custom-call(s32[4]{0:T(128)} %pad_add_fusion.place_ref, bf16[1024,768]{1,0:T(8,128)(2,1)} %copy-done.19, bf16[1024,768]{1,0:T(8,128)(2,1)} %get-tuple-element.292.dq_any, bf16[512,768]{1,0:T(8,128)(2,1)} %get-tuple-element.280.dk_any, ...), custom_call_target="tpu_custom_call" | custom-call | flops 2415919104 | bytes 12000000 | tf_op jit(solution)/shard_map/weight_back/pallas_call | solution.py:1030
  468.2 12.0 %collective-permute-done.51 = bf16[2,1,96,768]{3,2,1,0:T(8,128)(2,1)} collective-permute-done((bf16[2,1,96,768]{3,2,1,0:T(8,128)(2,1)}, bf16[2,1,96,768]{3,2,1,0:T(8,128)(2,1)}, u32[]{:S(2)}, u32[]{:S(2)}) %collective-permute-start.51) | collective-permute-done | bytes 294944 | tf_op jit(solution)/shard_map/ppermute | solution.py:175
  493.8 7.7 %input_back.1 = (f32[512,768]{1,0:T(8,128)}, f32[512,768]{1,0:T(8,128)}) custom-call(bf16[1024,768]{1,0:T(8,128)(2,1)} %get-tuple-element.292.dq_any, bf16[512,768]{1,0:T(8,128)(2,1)} %get-tuple-element.280.dk_any, bf16[512,768]{1,0:T(8,128)(2,1)} %get-tuple-element.281.dv_any, bf16[4,768,768]{2,1,0:T(8,128)(2,1)} %get-tuple-element.210.attn_any.w_any, ...), custom_call_target="tpu_custom_call" | custom-call | flops 2415919104 | bytes 16000000 | tf_op jit(solution)/shard_map/input_back/pallas_call | solution.py:1079
  514.4 7.1 %collective-permute-done.55 = bf16[4,1,96,768]{3,2,0,1:T(8,128)(2,1)S(1)} collective-permute-done((bf16[4,1,96,768]{3,2,0,1:T(8,128)(2,1)S(1)}, bf16[4,1,96,768]{3,2,0,1:T(8,128)(2,1)S(1)}, u32[]{:S(2)}, u32[]{:S(2)}) %collective-permute-start.55) | collective-permute-done | bytes 589856 | tf_op jit(solution)/shard_map/ppermute | solution.py:175
  567.7 6.3 %adam.2 = (f32[2,4,96,768]{3,2,1,0:T(8,128)}, f32[2,4,96,768]{3,2,1,0:T(8,128)}, f32[2,4,96,768]{3,2,1,0:T(8,128)}, f32[2,96,3072]{2,1,0:T(8,128)}, f32[2,96,307...) custom-call(f32[2,4,96,768]{3,2,1,0:T(8,128)S(1)} %copy-done, ...), custom_call_target="tpu_custom_call" | custom-call | flops 20000000 | bytes 22000000 | tf_op jit(solution)/shard_map/adam/pallas_call | solution.py:1157
  593.2 6.3 %adam.3 = (f32[2,4,96,768]{3,2,1,0:T(8,128)}, f32[2,4,96,768]{3,2,1,0:T(8,128)}, f32[2,4,96,768]{3,2,1,0:T(8,128)}, f32[2,96,3072]{2,1,0:T(8,128)}, f32[2,96,307...) custom-call(f32[2,4,96,768]{3,2,1,0:T(8,128)S(1)} %copy-done, ...), custom_call_target="tpu_custom_call", output_to_operand_aliasing={{0}: (12, {}), {1}: (13, {}), {2}: (14, {}), {3}: (15, {}),... | custom-call | flops 20000000 | bytes 22000000 | tf_op jit(solution)/shard_map/adam/pallas_call | solution.py:1157
  (439 shorter events, 250.9 us)
Async XLA Ops:
  37.1 30.3 %collective-permute-start.6 = (bf16[7,96,768]{2,1,0:T(8,128)(2,1)}, bf16[7,96,768]{2,1,0:T(8,128)(2,1)}, u32[]{:S(2)}, u32[]{:S(2)}) collective-permute-start(bf16[7,96,768]{2,1,0:T(8,128)(2,1)} %fusion.36), channel_id=1, source_target_pairs={{0,1},{1,0},{2,3},{3,2},{4,5},{5,4},{6,7},{7,6},{8,9},{9,8},{10,11... | collective-permute-start | bytes 3096584 | tf_op jit(solution)/shard_map/ppermute | solution.py:175
  39.6 27.8 %collective-permute-start.7 = (bf16[4,96,768]{2,1,0:T(8,128)(2,1)}, bf16[4,96,768]{2,1,0:T(8,128)(2,1)S(1)}, u32[]{:S(2)}, u32[]{:S(2)}) collective-permute-start(bf16[4,96,768]{2,1,0:T(8,128)(2,1)} %pad_maximum_fusion.7), channel_id=1, source_target_pairs={{0,4},{1,5},{2,6},{3,7},{4,0},{5,1},{6,2},{7,3},{8,12},{9,13},{10,... | collective-permute-start | bytes 1769480 | tf_op jit(solution)/shard_map/ppermute | solution.py:175
  72.1 41.6 %collective-permute-start.13 = (bf16[21,96,768]{2,1,0:T(8,128)(2,1)}, bf16[21,96,768]{2,1,0:T(8,128)(2,1)}, u32[]{:S(2)}, u32[]{:S(2)}) collective-permute-start(bf16[21,96,768]{2,1,0:T(8,128)(2,1)} %constant_dynamic-update-slice_fusion.5.refs_1_.refs_2_), channel_id=1, source_target_pairs={{0,8},{1,9},{2,10},{3,11},{4,12},{5,13},{6,14},{7,15},{8,0},{9,1},... | collective-permute-start | bytes 9289736 | tf_op jit(solution)/shard_map/ppermute | solution.py:175
  78.0 26.1 %collective-permute-start.11 = (bf16[7,96,768]{2,1,0:T(8,128)(2,1)}, bf16[7,96,768]{2,1,0:T(8,128)(2,1)}, u32[]{:S(2)}, u32[]{:S(2)}) collective-permute-start(bf16[7,96,768]{2,1,0:T(8,128)(2,1)} %pad_maximum_fusion.2), channel_id=1, source_target_pairs={{0,1},{1,0},{2,3},{3,2},{4,5},{5,4},{6,7},{7,6},{8,9},{9,8},{10,11... | collective-permute-start | bytes 3096584 | tf_op jit(solution)/shard_map/ppermute | solution.py:175
  86.0 27.7 %collective-permute-start.10 = (bf16[8,96,768]{2,1,0:T(8,128)(2,1)}, bf16[8,96,768]{2,1,0:T(8,128)(2,1)S(1)}, u32[]{:S(2)}, u32[]{:S(2)}) collective-permute-start(bf16[8,96,768]{2,1,0:T(8,128)(2,1)} %pad_maximum_fusion.1), channel_id=1, source_target_pairs={{0,16},{1,17},{2,18},{3,19},{4,20},{5,21},{6,22},{7,23},{8,24},{9,... | collective-permute-start | bytes 3538952 | tf_op jit(solution)/shard_map/ppermute | solution.py:175
  122.0 32.9 %collective-permute-start.17 = (bf16[7,96,768]{2,1,0:T(8,128)(2,1)}, bf16[7,96,768]{2,1,0:T(8,128)(2,1)}, u32[]{:S(2)}, u32[]{:S(2)}) collective-permute-start(bf16[7,96,768]{2,1,0:T(8,128)(2,1)} %fusion.39), channel_id=1, source_target_pairs={{0,1},{1,0},{2,3},{3,2},{4,5},{5,4},{6,7},{7,6},{8,9},{9,8},{10,11... | collective-permute-start | bytes 3096584 | tf_op jit(solution)/shard_map/ppermute | solution.py:175
  124.6 30.3 %collective-permute-start.16 = (bf16[7,96,768]{2,1,0:T(8,128)(2,1)}, bf16[7,96,768]{2,1,0:T(8,128)(2,1)}, u32[]{:S(2)}, u32[]{:S(2)}) collective-permute-start(bf16[7,96,768]{2,1,0:T(8,128)(2,1)} %pad_maximum_fusion.3), channel_id=1, source_target_pairs={{0,16},{1,17},{2,18},{3,19},{4,20},{5,21},{6,22},{7,23},{8,24},{9,... | collective-permute-start | bytes 3096584 | tf_op jit(solution)/shard_map/ppermute | solution.py:175
  127.0 27.8 %collective-permute-start.18 = (bf16[4,96,768]{2,1,0:T(8,128)(2,1)}, bf16[4,96,768]{2,1,0:T(8,128)(2,1)S(1)}, u32[]{:S(2)}, u32[]{:S(2)}) collective-permute-start(bf16[4,96,768]{2,1,0:T(8,128)(2,1)} %pad_maximum_fusion.8), channel_id=1, source_target_pairs={{0,4},{1,5},{2,6},{3,7},{4,0},{5,1},{6,2},{7,3},{8,12},{9,13},{10,... | collective-permute-start | bytes 1769480 | tf_op jit(solution)/shard_map/ppermute | solution.py:175
  160.7 34.6 %collective-permute-start.22 = (bf16[10,96,768]{2,1,0:T(8,128)(2,1)}, bf16[10,96,768]{2,1,0:T(8,128)(2,1)}, u32[]{:S(2)}, u32[]{:S(2)}) collective-permute-start(bf16[10,96,768]{2,1,0:T(8,128)(2,1)} %fusion.41), channel_id=1, source_target_pairs={{0,1},{1,0},{2,3},{3,2},{4,5},{5,4},{6,7},{7,6},{8,9},{9,8},{10,11... | collective-permute-start | bytes 4423688 | tf_op jit(solution)/shard_map/ppermute | solution.py:175
  163.5 31.0 %collective-permute-start.21 = (bf16[9,96,768]{2,1,0:T(8,128)(2,1)}, bf16[9,96,768]{2,1,0:T(8,128)(2,1)S(1)}, u32[]{:S(2)}, u32[]{:S(2)}) collective-permute-start(bf16[9,96,768]{2,1,0:T(8,128)(2,1)} %pad_maximum_fusion), channel_id=1, source_target_pairs={{0,16},{1,17},{2,18},{3,19},{4,20},{5,21},{6,22},{7,23},{8,24},{9,... | collective-permute-start | bytes 3981320 | tf_op jit(solution)/shard_map/ppermute | solution.py:175
  196.0 35.3 %collective-permute-start.29 = (bf16[10,96,768]{2,1,0:T(8,128)(2,1)}, bf16[10,96,768]{2,1,0:T(8,128)(2,1)}, u32[]{:S(2)}, u32[]{:S(2)}) collective-permute-start(bf16[10,96,768]{2,1,0:T(8,128)(2,1)} %collective-permute-done.22.refs_3_), channel_id=1, source_target_pairs={{0,8},{1,9},{2,10},{3,11},{4,12},{5,13},{6,14},{7,15},{8,0},{9,1},... | collective-permute-start | bytes 4423688 | tf_op jit(solution)/shard_map/ppermute | solution.py:175
  331.5 52.8 %collective-permute-start.37 = (bf16[4,2,96,768]{3,2,1,0:T(8,128)(2,1)S(1)}, bf16[4,2,96,768]{3,2,1,0:T(8,128)(2,1)S(1)}, u32[]{:S(2)}, u32[]{:S(2)}) collective-permute-start(bf16[4,2,96,768]{3,2,1,0:T(8,128)(2,1)S(1)} %get-tuple-element.364), channel_id=1, source_target_pairs={{0,16},{1,17},{2,18},{3,19},{4,20},{5,21},{6,22},{7,23},{8,24},{9,... | collective-permute-start | bytes 3538952 | tf_op jit(solution)/shard_map/ppermute | solution.py:175
  332.1 52.2 %collective-permute-start.38 = (bf16[4,2,96,768]{3,2,1,0:T(8,128)(2,1)S(1)}, bf16[4,2,96,768]{3,2,1,0:T(8,128)(2,1)}, u32[]{:S(2)}, u32[]{:S(2)}) collective-permute-start(bf16[4,2,96,768]{3,2,1,0:T(8,128)(2,1)S(1)} %get-tuple-element.363), channel_id=1, source_target_pairs={{0,1},{1,0},{2,3},{3,2},{4,5},{5,4},{6,7},{7,6},{8,9},{9,8},{10,11... | collective-permute-start | bytes 3538952 | tf_op jit(solution)/shard_map/ppermute | solution.py:175
  335.5 48.8 %collective-permute-start.39 = (bf16[2,1,96,768]{3,2,0,1:T(8,128)(2,1)}, bf16[2,1,96,768]{3,2,0,1:T(8,128)(2,1)S(1)}, u32[]{:S(2)}, u32[]{:S(2)}) collective-permute-start(bf16[2,1,96,768]{3,2,0,1:T(8,128)(2,1)} %get-tuple-element.393), channel_id=1, source_target_pairs={{0,16},{1,17},{2,18},{3,19},{4,20},{5,21},{6,22},{7,23},{8,24},{9,... | collective-permute-start | bytes 884744 | tf_op jit(solution)/shard_map/ppermute | solution.py:175
  336.8 47.5 %collective-permute-start.40 = (bf16[2,1,96,768]{3,2,0,1:T(8,128)(2,1)}, bf16[2,1,96,768]{3,2,0,1:T(8,128)(2,1)S(1)}, u32[]{:S(2)}, u32[]{:S(2)}) collective-permute-start(bf16[2,1,96,768]{3,2,0,1:T(8,128)(2,1)} %get-tuple-element.392), channel_id=1, source_target_pairs={{0,1},{1,0},{2,3},{3,2},{4,5},{5,4},{6,7},{7,6},{8,9},{9,8},{10,11... | collective-permute-start | bytes 884744 | tf_op jit(solution)/shard_map/ppermute | solution.py:175
  384.3 36.7 %collective-permute-start.41 = (bf16[2,2,4,2,96,768]{5,4,3,2,1,0:T(8,128)(2,1)}, bf16[2,2,4,2,96,768]{5,4,3,2,1,0:T(8,128)(2,1)}, u32[]{:S(2)}, u32[]{:S(2)}) collective-permute-start(bf16[2,2,4,2,96,768]{5,4,3,2,1,0:T(8,128)(2,1)} %get-tuple-element.258), channel_id=1, source_target_pairs={{0,8},{1,9},{2,10},{3,11},{4,12},{5,13},{6,14},{7,15},{8,0},{9,1},... | collective-permute-start | bytes 14155784 | tf_op jit(solution)/shard_map/ppermute | solution.py:175
  389.7 29.6 %collective-permute-start.46 = (bf16[2,2,96,768]{3,2,1,0:T(8,128)(2,1)}, bf16[2,2,96,768]{3,2,1,0:T(8,128)(2,1)}, u32[]{:S(2)}, u32[]{:S(2)}) collective-permute-start(bf16[2,2,96,768]{3,2,1,0:T(8,128)(2,1)} %fusion.14), channel_id=1, source_target_pairs={{0,4},{1,5},{2,6},{3,7},{4,0},{5,1},{6,2},{7,3},{8,12},{9,13},{10,... | collective-permute-start | bytes 1769480 | tf_op jit(solution)/shard_map/ppermute | solution.py:175
  392.9 44.8 %collective-permute-start.44 = (bf16[4,1,96,768]{3,2,1,0:T(8,128)(2,1)}, bf16[4,1,96,768]{3,2,1,0:T(8,128)(2,1)S(1)}, u32[]{:S(2)}, u32[]{:S(2)}) collective-permute-start(bf16[4,1,96,768]{3,2,1,0:T(8,128)(2,1)} %get-tuple-element.368), channel_id=1, source_target_pairs={{0,16},{1,17},{2,18},{3,19},{4,20},{5,21},{6,22},{7,23},{8,24},{9,... | collective-permute-start | bytes 1769480 | tf_op jit(solution)/shard_map/ppermute | solution.py:175
  393.4 44.4 %collective-permute-start.45 = (bf16[4,1,96,768]{3,2,1,0:T(8,128)(2,1)}, bf16[4,1,96,768]{3,2,1,0:T(8,128)(2,1)}, u32[]{:S(2)}, u32[]{:S(2)}) collective-permute-start(bf16[4,1,96,768]{3,2,1,0:T(8,128)(2,1)} %get-tuple-element.367), channel_id=1, source_target_pairs={{0,1},{1,0},{2,3},{3,2},{4,5},{5,4},{6,7},{7,6},{8,9},{9,8},{10,11... | collective-permute-start | bytes 1769480 | tf_op jit(solution)/shard_map/ppermute | solution.py:175
  452.4 30.1 %collective-permute-start.50 = (bf16[2,2,4,1,96,768]{5,4,3,2,1,0:T(8,128)(2,1)}, bf16[2,2,4,1,96,768]{5,4,3,2,1,0:T(8,128)(2,1)}, u32[]{:S(2)}, u32[]{:S(2)}) collective-permute-start(bf16[2,2,4,1,96,768]{5,4,3,2,1,0:T(8,128)(2,1)} %get-tuple-element.284), channel_id=1, source_target_pairs={{0,8},{1,9},{2,10},{3,11},{4,12},{5,13},{6,14},{7,15},{8,0},{9,1},... | collective-permute-start | bytes 7077896 | tf_op jit(solution)/shard_map/ppermute | solution.py:175
  452.5 28.7 %collective-permute-start.48 = (bf16[4,2,96,768]{3,2,1,0:T(8,128)(2,1)}, bf16[4,2,96,768]{3,2,1,0:T(8,128)(2,1)}, u32[]{:S(2)}, u32[]{:S(2)}) collective-permute-start(bf16[4,2,96,768]{3,2,1,0:T(8,128)(2,1)} %get-tuple-element.362), channel_id=1, source_target_pairs={{0,16},{1,17},{2,18},{3,19},{4,20},{5,21},{6,22},{7,23},{8,24},{9,... | collective-permute-start | bytes 3538952 | tf_op jit(solution)/shard_map/ppermute | solution.py:175
  454.2 28.4 %collective-permute-start.49 = (bf16[4,2,96,768]{3,2,1,0:T(8,128)(2,1)}, bf16[4,2,96,768]{3,2,1,0:T(8,128)(2,1)}, u32[]{:S(2)}, u32[]{:S(2)}) collective-permute-start(bf16[4,2,96,768]{3,2,1,0:T(8,128)(2,1)} %get-tuple-element.361), channel_id=1, source_target_pairs={{0,1},{1,0},{2,3},{3,2},{4,5},{5,4},{6,7},{7,6},{8,9},{9,8},{10,11... | collective-permute-start | bytes 3538952 | tf_op jit(solution)/shard_map/ppermute | solution.py:175
  486.3 28.2 %collective-permute-start.57 = (bf16[2,2,96,768]{3,2,1,0:T(8,128)(2,1)S(1)}, bf16[2,2,96,768]{3,2,1,0:T(8,128)(2,1)S(1)}, u32[]{:S(2)}, u32[]{:S(2)}) collective-permute-start(bf16[2,2,96,768]{3,2,1,0:T(8,128)(2,1)S(1)} %fusion.12), channel_id=1, source_target_pairs={{0,4},{1,5},{2,6},{3,7},{4,0},{5,1},{6,2},{7,3},{8,12},{9,13},{10,... | collective-permute-start | bytes 1769480 | tf_op jit(solution)/shard_map/ppermute | solution.py:175
  508.6 26.6 %collective-permute-start.63 = (bf16[3,96,768]{2,1,0:T(8,128)(2,1)}, bf16[3,96,768]{2,1,0:T(8,128)(2,1)}, u32[]{:S(2)}, u32[]{:S(2)}) collective-permute-start(bf16[3,96,768]{2,1,0:T(8,128)(2,1)} %get-tuple-element.314), channel_id=1, source_target_pairs={{0,16},{1,17},{2,18},{3,19},{4,20},{5,21},{6,22},{7,23},{8,24},{9,... | collective-permute-start | bytes 1327112 | tf_op jit(solution)/shard_map/ppermute | solution.py:175
  (124 other events, 1160.0 us)

commit v8 on v7

--- a/solution.py
+++ b/solution.py
@@ -270,6 +270,85 @@
             targets[member].at[lead, pl.ds(pl.multiple_of(row, ROWS), ROWS), :],
         )
     return copies
+
+
+def quarter_spans(place_ref, side):
+    quarter = (place_ref[0] ^ side) * 2 + place_ref[1]
+    return (
+        quarter,
+        pl.ds(pl.multiple_of(quarter * D, D), D),
+        pl.ds(pl.multiple_of(quarter * ROWS, ROWS), ROWS),
+    )
+
+
+def cast_first_kernel(
+    place_ref, attn_any, inner_any, outer_any, own_a0, plane_a0, own_f0, hold_ref, sems
+):
+    index, cols, rows = quarter_spans(place_ref, 0)
+    other = quarter_spans(place_ref, 1)[0]
+    finish(
+        issue(
+            (
+                (attn_any.at[0, index], hold_ref.at[0]),
+                (attn_any.at[0, other], hold_ref.at[1]),
+                (inner_any.at[0, :, cols], hold_ref.at[2]),
+                (outer_any.at[0, rows, :], hold_ref.at[3]),
+            ),
+            sems,
+        )
+    )
+    own_a0[...] = hold_ref[0:1].astype(jnp.bfloat16)
+    plane_a0[...] = hold_ref[0:2].astype(jnp.bfloat16)
+    own_f0[...] = hold_ref[2:4].astype(jnp.bfloat16)
+
+
+def cast_first(place, attn, inner, outer):
+    return pl.pallas_call(
+        cast_first_kernel,
+        out_shape=[jax.ShapeDtypeStruct((count, ROWS, D), jnp.bfloat16) for count in (1, 2, 2)],
+        in_specs=[SMEM_SPEC] + [ANY_SPEC] * 3,
+        out_specs=[VMEM_SPEC] * 3,
+        scratch_shapes=[pltpu.VMEM((4, ROWS, D), jnp.float32), pltpu.SemaphoreType.DMA((4,))],
+        compiler_params=PARAMS,
+        cost_estimate=pl.CostEstimate(flops=1000000, bytes_accessed=2000000, transcendentals=0),
+        name="cast_first",
+    )(place, attn, inner, outer)
+
+
+def cast_rest_kernel(
+    place_ref, attn_ref, inner_ref, outer_ref, attn_0, attn_1, inner_0, inner_1, outer_0, outer_1,
+    plane_f0, own_1, oth_1,
+):
+    for layer, (attn_low, inner_low, outer_low) in enumerate(
+        ((attn_0, inner_0, outer_0), (attn_1, inner_1, outer_1))
+    ):
+        attn_low[...] = attn_ref[layer].astype(jnp.bfloat16)
+        inner_low[...] = inner_ref[layer].astype(jnp.bfloat16)
+        outer_low[...] = outer_ref[layer].astype(jnp.bfloat16)
+    for side, (target, first) in enumerate(((own_1, 0), (oth_1, 0))):
+        index, cols, rows = quarter_spans(place_ref, side)
+        plane_f0[2 * side] = inner_ref[0, :, cols].astype(jnp.bfloat16)
+        plane_f0[2 * side + 1] = outer_ref[0, rows, :].astype(jnp.bfloat16)
+        target[0] = attn_ref[1, index].astype(jnp.bfloat16)
+        target[1] = inner_ref[1, :, cols].astype(jnp.bfloat16)
+        target[2] = outer_ref[1, rows, :].astype(jnp.bfloat16)
+
+
+def cast_rest(place, attn, inner, outer):
+    low = [
+        jax.ShapeDtypeStruct(array.shape[1:], jnp.bfloat16)
+        for array in (attn, attn, inner, inner, outer, outer)
+    ]
+    return pl.pallas_call(
+        cast_rest_kernel,
+        out_shape=low
+        + [jax.ShapeDtypeStruct((count, ROWS, D), jnp.bfloat16) for count in (4, 3, 3)],
+        in_specs=[SMEM_SPEC] + [VMEM_SPEC] * 3,
+        out_specs=[VMEM_SPEC] * 9,
+        compiler_params=PARAMS,
+        cost_estimate=pl.CostEstimate(flops=10000000, bytes_accessed=12000000, transcendentals=0),
+        name="cast_rest",
+    )(place, attn, inner, outer)
 
 
 def project_kernel(plan, place_ref, small_ref, low_any, *refs):
@@ -1161,7 +1240,7 @@
         in_specs=blocks + grads + [ANY_SPEC] * len(held),
         out_specs=blocks,
         input_output_aliases={12 + index: index for index in range(len(held))},
-        compiler_params=pltpu.CompilerParams(vmem_limit_bytes=16 * 1024 * 1024),
+        compiler_params=PARAMS,
         cost_estimate=pl.CostEstimate(flops=20000000, bytes_accessed=22000000, transcendentals=0),
         name="adam",
     )(*state, quarters, quarters, quarters, *held)
@@ -1474,30 +1553,12 @@
     )
 
 
-def quarter_of(kind, shard, quarter):
-    if kind == "attn":
-        return lax.dynamic_index_in_dim(shard, quarter, 0, keepdims=False)
-    if kind == "inner":
-        return lax.dynamic_slice_in_dim(shard, quarter * D, D, 1)
-    return lax.dynamic_slice_in_dim(shard, quarter * ROWS, ROWS, 0)
-
-
 def after(value, *others):
     return lax.optimization_barrier((value, others))[0]
 
 
 def join(*values):
     return lax.optimization_barrier(values)
-
-
-def own_blocks(kinds, shards, place, side):
-    quarter = (place[0] ^ side) * 2 + place[1]
-    return jnp.stack(
-        [
-            quarter_of(kind, shard, quarter).astype(jnp.bfloat16)
-            for kind, shard in zip(kinds, shards)
-        ]
-    )
 
 
 def gather_group(count, shards, plane, column, sides, corners, mine, theirs):
@@ -1632,36 +1693,38 @@
 ):
     place_parts = my_place()
     place = jnp.stack(place_parts).astype(jnp.int32)
-    attn_kinds, feed_kinds = ("attn",), ("inner", "outer")
-    attn_shards = [(attn_master[layer],) for layer in range(LAYERS)]
-    feed_shards = [(inner_master[layer], outer_master[layer]) for layer in range(LAYERS)]
-    own_a0 = own_blocks(attn_kinds, attn_shards[0], place_parts, 0)
-    oth_a0 = own_blocks(attn_kinds, attn_shards[0], place_parts, 1)
-    own_f0 = own_blocks(feed_kinds, feed_shards[0], place_parts, 0)
+    own_a0, plane_a0, own_f0 = cast_first(place, attn_master, inner_master, outer_master)
     z_a0 = tuple(swap_z(own_a0, apart) for apart in (1, 2, 3))
-    plane_a0 = swap_y(jnp.concatenate([own_a0, oth_a0]))
+    plane_a0 = swap_y(plane_a0)
     near_f0 = swap_z(own_f0, 1)
-    z_a0, plane_a0, near_f0 = join(z_a0, plane_a0, near_f0)
-    oth_f0 = own_blocks(feed_kinds, feed_shards[0], place_parts, 1)
-    own_a1 = own_blocks(attn_kinds, attn_shards[1], place_parts, 0)
-    oth_a1 = own_blocks(attn_kinds, attn_shards[1], place_parts, 1)
-    own_f1 = own_blocks(feed_kinds, feed_shards[1], place_parts, 0)
-    oth_f1 = own_blocks(feed_kinds, feed_shards[1], place_parts, 1)
-    attn_low = [tuple(w.astype(jnp.bfloat16) for w in shards) for shards in attn_shards]
-    feed_low = [tuple(w.astype(jnp.bfloat16) for w in shards) for shards in feed_shards]
+    attn_low0, attn_low1, inner_low0, inner_low1, outer_low0, outer_low1, plane_f0, own_1, oth_1 = (
+        cast_rest(place, attn_master, inner_master, outer_master)
+    )
+    low0 = jnp.concatenate([content, query])
+    row_flags = predicted.reshape(1, LEN).astype(jnp.float32)
+    col_flags = predicted.reshape(LEN, 1).astype(jnp.float32)
+    small_low = small_master.astype(jnp.bfloat16)
+    z_a0, plane_a0, near_f0, plane_f0, own_1, oth_1, low0, row_flags, col_flags, small_low = join(
+        z_a0, plane_a0, near_f0, plane_f0, own_1, oth_1, low0, row_flags, col_flags, small_low
+    )
     col_a0 = jnp.concatenate(z_a0)
     x0 = swap_x(col_a0)
-    y0 = swap_y(jnp.concatenate([col_a0, own_f0, oth_f0]))
+    y0 = swap_y(col_a0)
     far_f0 = swap_z(jnp.concatenate([own_f0, near_f0]), 2)
-    near_1 = swap_z(after(jnp.concatenate([own_a1, own_f1]), z_a0), 1)
-    small_low = small_master.astype(jnp.bfloat16)
-    small_near = swap_z(after(small_low, z_a0), 1)
-    x0, y0, far_f0, near_1, small_near = join(x0, y0, far_f0, near_1, small_near)
+    plane_f0 = swap_y(after(plane_f0, col_a0))
+    near_1 = swap_z(after(own_1, col_a0), 1)
+    small_near = swap_z(small_low, 1)
+    x0, y0, far_f0, plane_f0, near_1, small_near = join(
+        x0, y0, far_f0, plane_f0, near_1, small_near
+    )
     col_f0 = jnp.concatenate([near_f0, far_f0])
-    x1 = swap_x(jnp.concatenate([col_f0, y0[:2]]))
-    y1 = swap_y(jnp.concatenate([col_f0, x0[2:]]))
-    far_a1 = swap_z(jnp.concatenate([own_a1, near_1[:1]]), 2)
-    mine_0 = jnp.concatenate([plane_a0, col_a0, x0, y0, col_f0])
+    to_x1 = jnp.concatenate([col_f0, y0[:2]])
+    to_y1 = jnp.concatenate([col_f0, x0[2:]])
+    x1 = swap_x(to_x1)
+    y1 = swap_y(to_y1)
+    far_a1 = swap_z(jnp.concatenate([own_1[:1], near_1[:1]]), 2)
+    held = after((plane_a0, col_a0, x0, y0, plane_f0, col_f0), to_x1, to_y1)
+    mine_0 = jnp.concatenate(held)
     theirs_0 = swap_core(mine_0)
     small_pair = jnp.stack([small_low, small_near])
     small_far = swap_z(small_pair, 2)
@@ -1669,16 +1732,13 @@
     x1, y1, far_a1, theirs_0, small_all = join(x1, y1, far_a1, theirs_0, small_all)
     col_a1 = jnp.concatenate([near_1[:1], far_a1])
     x2 = swap_x(jnp.concatenate([col_a1, y1[:4]]))
-    y2 = swap_y(jnp.concatenate([col_a1, x1[4:6], own_a1, oth_a1]))
-    far_f1 = swap_z(jnp.concatenate([own_f1, after(near_1[1:], far_a1)]), 2)
+    y2 = swap_y(jnp.concatenate([col_a1, x1[4:6], own_1[:1], oth_1[:1]]))
+    far_f1 = swap_z(jnp.concatenate([own_1[1:], after(near_1[1:], far_a1)]), 2)
     their_x1, their_y1 = swap_core(x1), swap_core(y1)
     group_a0 = gather_group(
-        1, attn_low[0], (0, 0), (0, 2), ((0, 5), (0, 8)), ((1, 6, 2), (2, 6, 1)),
+        1, (attn_low0,), (0, 0), (0, 2), ((0, 5), (0, 8)), ((1, 6, 2), (2, 6, 1)),
         (mine_0, x1, y1), (theirs_0, their_x1, their_y1),
     )
-    row_flags = predicted.reshape(1, LEN).astype(jnp.float32)
-    col_flags = predicted.reshape(LEN, 1).astype(jnp.float32)
-    low0 = jnp.concatenate([content, query])
     small0, hidden_bias0, (tvec0, far0, onehot) = small_parts(small_all[0])
     small1, hidden_bias1, (tvec1, far1, onehot) = small_parts(small_all[1])
     q0, k0, v0, attn0 = project(place, low0, small0, group_a0)
@@ -1686,10 +1746,10 @@
     x2, y2, far_f1, mixed0 = join(x2, y2, far_f1, mixed0)
     col_f1 = jnp.concatenate([near_1[1:], far_f1])
     x3 = swap_x(jnp.concatenate([col_f1, y2[:3]]))
-    y3 = swap_y(jnp.concatenate([col_f1, own_f1, oth_f1]))
+    y3 = swap_y(jnp.concatenate([col_f1, own_1[1:], oth_1[1:]]))
     their_x2, their_y2, their_a1 = swap_core(x2), swap_core(y2), swap_core(after(col_a1, x2))
     group_f0 = gather_group(
-        2, feed_low[0], (0, 11), (0, 15), ((1, 0), (2, 0)), ((3, 3, 4), (4, 3, 2)),
+        2, (inner_low0, outer_low0), (0, 11), (0, 15), ((1, 0), (2, 0)), ((3, 3, 4), (4, 3, 2)),
         (mine_0, x1, y1, x2, y2), (theirs_0, their_x1, their_y1, their_x2, their_y2),
     )
     resid0, pre0, normed0, low1, summed0 = feed(
@@ -1700,14 +1760,14 @@
     y4 = swap_y(x3[3:6])
     their_x3, their_y3 = swap_core(x3), swap_core(y3)
     group_a1 = gather_group(
-        1, attn_low[1], (1, 5), (2, 0), ((0, 0), (1, 0)), ((3, 6, 3),),
+        1, (attn_low1,), (1, 5), (2, 0), ((0, 0), (1, 0)), ((3, 6, 3),),
         (x2, y2, col_a1, x3), (their_x2, their_y2, their_a1, their_x3),
     )
     q1, k1, v1, attn1 = project(place, low1, small1, group_a1)
     x4, y4, q1 = join(x4, y4, q1)
     their_x4, their_y4, their_f1 = swap_core(x4), swap_core(y4), swap_core(after(col_f1, q1))
     group_f1 = gather_group(
-        2, feed_low[1], (1, 6), (4, 0), ((0, 0), (1, 0)), ((2, 0, 3), (3, 0, 3)),
+        2, (inner_low1, outer_low1), (1, 6), (4, 0), ((0, 0), (1, 0)), ((2, 0, 3), (3, 0, 3)),
         (x3, y3, x4, y4, col_f1), (their_x3, their_y3, their_x4, their_y4, their_f1),
     )
     mixed1, p1, inverse1, dead = mix(
@@ -1739,12 +1799,10 @@
         0, after(q0, by_a1, sides_rf1), k0, v0, dmix0, mixed0, p0, inverse0, dead
     )
     by_f0 = reduce_corners(keep_f0, after(get_f0, table0_a))
-    pair_f1 = own_pair(keep_f1, get_f1, sides_rf1, after(zfar_f1, table0_a), place_parts)
-    znear_f1 = reduce_near(pair_f1, place_parts)
     dq0, dk0, dv0, table0_b = mix_back(
-        3, after(q0, get_f0, zfar_f1), k0, v0, dmix0, mixed0, p0, inverse0, dead, tuple(first0)
-    )
-    by_f0, sides_ra1, znear_f1, table0_b = join(by_f0, sides_ra1, znear_f1, table0_b)
+        3, after(q0, get_f0, table0_a), k0, v0, dmix0, mixed0, p0, inverse0, dead, tuple(first0)
+    )
+    by_f0, sides_ra1, zfar_f1, table0_b = join(by_f0, sides_ra1, zfar_f1, table0_b)
     payloads_f0 = side_payloads(keep_f0, get_f0, by_f0)
     sides_rf0 = reduce_sides(payloads_f0)
     keep_a0, send_a0, vec_a0 = weight_back(
@@ -1752,7 +1810,11 @@
     )
     get_a0 = swap_core(send_a0)
     zfar_a1 = swap_z(far_payload(keep_a1, get_a1, sides_ra1, place_parts), 2)
-    sides_rf0, get_a0, zfar_a1, vec_a0 = join(sides_rf0, get_a0, zfar_a1, vec_a0)
+    pair_f1 = own_pair(keep_f1, get_f1, sides_rf1, after(zfar_f1, get_a0), place_parts)
+    znear_f1 = reduce_near(pair_f1, place_parts)
+    sides_rf0, get_a0, zfar_a1, znear_f1, vec_a0 = join(
+        sides_rf0, get_a0, zfar_a1, znear_f1, vec_a0
+    )
     payload_f0 = far_payload(keep_f0, get_f0, sides_rf0, place_parts)
     zfar_f0 = swap_z(payload_f0, 2)
     by_a0 = reduce_corners(keep_a0, after(get_a0, payload_f0))
@@ -1801,10 +1863,11 @@
         outer_master, outer_first, outer_second,
     )
     new_1 = adam(1, state, four_1, ())
-    small_sum = small_sum + swap_z(after(small_sum, own_0), 1)
+    small_z = swap_z(after(small_sum, own_0), 1)
+    across_0, new_1, small_z = join(across_0, new_1, small_z)
+    small_sum = small_sum + small_z
+    four_0 = share_core(jnp.stack([own_0, across_0]), place_parts)
     small_sum = small_sum + swap_z(small_sum, 2)
-    across_0, new_1, small_sum = join(across_0, new_1, small_sum)
-    four_0 = share_core(jnp.stack([own_0, across_0]), place_parts)
     small_x = swap_x(small_sum)
     new_0 = adam(0, state, four_0, tuple(new_1))
     small_sum = small_sum + small_x

time: 609 us -> 570 us (0.936)
  waiting for transfers between devices: 124 us -> 86.1 us
  local copies, waits for them, and re-layouts: 86.3 us -> 53.8 us
  Pallas kernels: 263 us -> 282 us
  other arithmetic: 59.8 us -> 65.9 us
    ppermute x71 -> x72, waiting for transfers between devices: 124 us -> 86.1 us  [move(): return lax.ppermute(value, AXES, pairs)]
    unnamed x178 -> x149, local copies, waits for them, and re-layouts: 50.4 us -> 18.7 us
    pallas_call x2, Pallas kernels: 12.6 us -> 23.2 us  [adam(): pl.pallas_call(adam_kernel, grid=(8,), out_shape=[jax.ShapeDtypeStruct(ar...]
    pallas_call x0 -> x2, Pallas kernels: none -> 8.63 us  [the longest x1 5.69 us: cast_rest(): pl.pallas_call(cast_rest_kernel, out_shape=low + [jax.ShapeDtypeStruct((c...]
    convert_element_type x8 -> x0, local copies, waits for them, and re-layouts: 7.36 us -> none  [the longest x3 5.67 us: per_device_fast(): w.astype(jnp.bfloat16)]
    ppermute x71 -> x72, starting transfers between devices: 62.9 us -> 68.6 us  [move(): return lax.ppermute(value, AXES, pairs)]
  transfers between devices with their start and end apart: 71 -> 72, of which waited for: 28 -> 27; matrix products, arithmetic and copies ran while one was open for 15% -> 16% of each run, Pallas kernels for 31% -> 35%
where the time goes in v8:
time: 570 us; the launch traced here: 560 us
  Pallas kernels  282 us (49%)
  waiting for transfers between devices  86.1 us (15%)
  starting transfers between devices  68.6 us (12%)
  other arithmetic  65.9 us (12%)
  local copies, waits for them, and re-layouts  53.8 us (9%)
    ppermute x72, waiting for transfers between devices, move(): return lax.ppermute(value, AXES, pairs)  86.1 us
    ppermute x72, starting transfers between devices, move(): return lax.ppermute(value, AXES, pairs)  68.6 us
    pallas_call x1, Pallas kernels, turn(): pl.pallas_call(partial(turn_kernel, plan), out_shape=[half_low, half_low]...  55.5 us
    pallas_call x4, Pallas kernels, mix_back(): pl.pallas_call(mix_back_kernel, grid=(H // 4,), out_shape=[jax.ShapeDtype...  49.7 us
    pallas_call x1, Pallas kernels, down(): pl.pallas_call(partial(down_kernel, plan), out_shape=BACK_SHAPES, in_spec...  46 us
    pallas_call x2, Pallas kernels, mix(): pl.pallas_call(mix_kernel, grid=(H // 2,), out_shape=[jax.ShapeDtypeStruc...  36.9 us
    convert_element_type x19, other arithmetic, add_low(): return total.astype(jnp.bfloat16)  33.3 us
    pallas_call x2, Pallas kernels, adam(): pl.pallas_call(adam_kernel, grid=(8,), out_shape=[jax.ShapeDtypeStruct(ar...  23.2 us
  transfers between devices with their start and end apart: 72, of which 27 were waited for; matrix products, arithmetic and copies ran while one was open for 16% of the time, Pallas kernels for 35%

profile of v8, /device:TPU:0, one launch (start us, length us, event | category | flops | bytes accessed | tf_op | source)
XLA Modules:
  0.0 560.4 jit_solution(13377329915234810310)
XLA Ops:
  13.9 5.7 %cast_rest.1 = (bf16[4,96,768]{2,1,0:T(8,128)(2,1)}, bf16[4,96,768]{2,1,0:T(8,128)(2,1)}, bf16[96,3072]{1,0:T(8,128)(2,1)}, bf16[96,3072]{1,0:T(8,128)(2,1)}, bf...) custom-call(s32[4]{0:T(128)} %pad_add_fusion.place_ref, ...), custom_call_target="tpu_custom_call" | custom-call | flops 10000000 | bytes 12000000 | tf_op jit(solution)/shard_map/cast_rest/pallas_call | solution.py:342
  31.7 10.2 %collective-permute-done.10 = bf16[2,1200]{1,0:T(2,128)(2,1)S(1)} collective-permute-done((bf16[2,1200]{1,0:T(2,128)(2,1)S(1)}, bf16[2,1200]{1,0:T(2,128)(2,1)S(1)}, u32[]{:S(2)}, u32[]{:S(2)}) %collective-permute-start.10) | collective-permute-done | bytes 4832 | tf_op jit(solution)/shard_map/ppermute | solution.py:175
  43.6 5.8 %collective-permute-done.9 = bf16[3,96,768]{2,1,0:T(8,128)(2,1)S(1)} collective-permute-done((bf16[3,96,768]{2,1,0:T(8,128)(2,1)S(1)}, bf16[3,96,768]{2,1,0:T(8,128)(2,1)S(1)}, u32[]{:S(2)}, u32[]{:S(2)}) %collective-permute-start.9) | collective-permute-done | bytes 442400 | tf_op jit(solution)/shard_map/ppermute | solution.py:175
  81.7 6.6 %collective-permute-done.16 = bf16[4,2,1200]{2,1,0:T(2,128)(2,1)S(1)} collective-permute-done((bf16[4,2,1200]{2,1,0:T(2,128)(2,1)S(1)}, bf16[4,2,1200]{2,1,0:T(2,128)(2,1)S(1)}, u32[]{:S(2)}, u32[]{:S(2)}) %collective-permute-start.16) | collective-permute-done | bytes 19232 | tf_op jit(solution)/shard_map/ppermute | solution.py:175
  113.0 7.5 %project.2 = (bf16[1024,768]{1,0:T(8,128)(2,1)}, bf16[512,768]{1,0:T(8,128)(2,1)}, bf16[512,768]{1,0:T(8,128)(2,1)}, bf16[4,768,768]{2,1,0:T(8,128)(2,1)}) custom-call(s32[4]{0:T(128)} %pad_add_fusion.place_ref, f32[8,768]{1,0:T(8,128)} %reshape.567.small_ref.below_ref, bf16[1024,768]{1,0:T(8,128)(2,1)} %pad_maximum_fusion.low_any.hidden_any, ...), custom_call_target="tpu_custom_call" | custom-call | flops 2415919104 | bytes 16000000 | tf_op jit(solution)/shard_map/project/pallas_call | solution.py:396
  120.4 18.5 %mix.2 = (bf16[1024,768]{1,0:T(8,128)(2,1)}, bf16[12,512,1024]{2,1,0:T(8,128)(2,1)}, f32[12,1,1024]{2,1,0:T(1,128)}, f32[1,1024]{1,0:T(1,128)}) custom-call(s32[1]{0:T(128)S(6)} %copy.171.length_ref, f32[12,2]{1,0:T(8,128)} %pad_maximum_fusion.21.far_ref, bf16[1024,768]{1,0:T(8,128)(2,1)} %get-tuple-element.322.q_ref, ...), custom_call_target="tpu_custom_call" | custom-call | flops 6499999744 | bytes 8000000 | tf_op jit(solution)/shard_map/mix/pallas_call | solution.py:531
  147.1 22.0 %feed.1 = (f32[1024,768]{1,0:T(8,128)}, bf16[4,1024,768]{2,1,0:T(8,128)(2,1)}, bf16[1024,768]{1,0:T(8,128)(2,1)}, bf16[1024,768]{1,0:T(8,128)(2,1)}, f32[1024,768]{1,0:T(8,128)}) custom-call(s32[4]{0:T(128)} %pad_add_fusion.place_ref, f32[8,768]{1,0:T(8,128)} %reshape.567.small_ref.below_ref, f32[1,3072]{1,0:T(1,128)} %slice.337.hidden_bias_ref, ...), custom_call_target="tpu_custom_call" | custom-call | flops 10871635968 | bytes 30000000 | tf_op jit(solution)/shard_map/feed/pallas_call | solution.py:765
  169.1 5.1 collective-permute-done.22.refs_4_.refs_2_
  183.9 7.6 %project.3 = (bf16[1024,768]{1,0:T(8,128)(2,1)}, bf16[512,768]{1,0:T(8,128)(2,1)}, bf16[512,768]{1,0:T(8,128)(2,1)}, bf16[4,768,768]{2,1,0:T(8,128)(2,1)}) custom-call(s32[4]{0:T(128)} %pad_add_fusion.place_ref, f32[8,768]{1,0:T(8,128)} %reshape.566.small_ref, bf16[1024,768]{1,0:T(8,128)(2,1)} %get-tuple-element.297.low_any, ...), custom_call_target="tpu_custom_call" | custom-call | flops 2415919104 | bytes 16000000 | tf_op jit(solution)/shard_map/project/pallas_call | solution.py:396
  194.6 18.4 %mix.3 = (bf16[1024,768]{1,0:T(8,128)(2,1)}, bf16[12,512,1024]{2,1,0:T(8,128)(2,1)}, f32[12,1,1024]{2,1,0:T(1,128)}, f32[1,1024]{1,0:T(1,128)}) custom-call(s32[1]{0:T(128)S(6)} %copy.171.length_ref, f32[12,2]{1,0:T(8,128)} %pad_maximum_fusion.20.far_ref, bf16[1024,768]{1,0:T(8,128)(2,1)} %get-tuple-element.288.q_ref, ...), custom_call_target="tpu_custom_call" | custom-call | flops 6499999744 | bytes 8000000 | tf_op jit(solution)/shard_map/mix/pallas_call | solution.py:531
  214.3 55.5 %turn.1 = (bf16[512,768]{1,0:T(8,128)(2,1)}, bf16[512,768]{1,0:T(8,128)(2,1)}, f32[1024,768]{1,0:T(8,128)}, bf16[1024,768]{1,0:T(8,128)(2,1)}, bf16[768,768]{1,0...) custom-call(s32[4]{0:T(128)} %pad_add_fusion.place_ref, ...), custom_call_target="tpu_custom_call" | custom-call | flops 32614907904 | bytes 60000000 | tf_op jit(solution)/shard_map/turn/pallas_call | solution.py:956
  270.3 12.3 %mix_back.4 = (bf16[1024,768]{1,0:T(8,128)(2,1)}, bf16[512,768]{1,0:T(8,128)(2,1)}, bf16[512,768]{1,0:T(8,128)(2,1)}, f32[6,1,768]{2,1,0:T(1,128)}) custom-call(bf16[1024,768]{1,0:T(8,128)(2,1)} %get-tuple-element.288.q_ref, bf16[512,768]{1,0:T(8,128)(2,1)} %get-tuple-element.270.k_ref, bf16[512,768]{1,0:T(8,128)(2,1)} %get-tuple-element.271.v_ref, ...), custom_call_target="tpu_custom_call" | custom-call | flops 8000000000 | bytes 16000000 | tf_op jit(solution)/shard_map/mix_back/pallas_call | solution.py:632
  286.8 12.5 %mix_back.5 = (bf16[1024,768]{1,0:T(8,128)(2,1)}, bf16[512,768]{1,0:T(8,128)(2,1)}, bf16[512,768]{1,0:T(8,128)(2,1)}, f32[6,1,768]{2,1,0:T(1,128)}) custom-call(bf16[1024,768]{1,0:T(8,128)(2,1)} %get-tuple-element.288.q_ref, bf16[512,768]{1,0:T(8,128)(2,1)} %get-tuple-element.270.k_ref, ...), custom_call_target="tpu_custom_call", output_to_operand_aliasing={{0}: (8, {}), {1}: (9, {}), {2}: (10, {})} | custom-call | flops 8000000000 | bytes 16000000 | tf_op jit(solution)/shard_map/mix_back/pallas_call | solution.py:632
  301.2 8.8 %weight_back.2 = (bf16[2,2,4,1,96,768]{5,4,3,2,1,0:T(8,128)(2,1)}, bf16[2,2,4,1,96,768]{5,4,3,2,1,0:T(8,128)(2,1)}, f32[2,768]{1,0:T(2,128)}) custom-call(s32[4]{0:T(128)} %pad_add_fusion.place_ref, bf16[1024,768]{1,0:T(8,128)(2,1)} %get-tuple-element.297.low_any, bf16[1024,768]{1,0:T(8,128)(2,1)} %get-tuple-element.292.dq_any, ...), custom_call_target="tpu_custom_call" | custom-call | flops 2415919104 | bytes 12000000 | tf_op jit(solution)/shard_map/weight_back/pallas_call | solution.py:1109
  321.2 46.0 %down.1 = (f32[1024,768]{1,0:T(8,128)}, bf16[1024,768]{1,0:T(8,128)(2,1)}, bf16[768,768]{1,0:T(8,128)(2,1)}, bf16[2,2,4,2,96,768]{5,4,3,2,1,0:T(8,128)(2,1)}, bf...) custom-call(s32[4]{0:T(128)} %pad_add_fusion.place_ref, ...), custom_call_target="tpu_custom_call" | custom-call | flops 27179089920 | bytes 60000000 | tf_op jit(solution)/shard_map/down/pallas_call | solution.py:1042
  380.2 12.5 %mix_back.6 = (bf16[1024,768]{1,0:T(8,128)(2,1)}, bf16[512,768]{1,0:T(8,128)(2,1)}, bf16[512,768]{1,0:T(8,128)(2,1)}, f32[6,1,768]{2,1,0:T(1,128)}) custom-call(bf16[1024,768]{1,0:T(8,128)(2,1)} %get-tuple-element.322.q_ref, bf16[512,768]{1,0:T(8,128)(2,1)} %get-tuple-element.250.k_ref, bf16[512,768]{1,0:T(8,128)(2,1)} %get-tuple-element.251.v_ref, ...), custom_call_target="tpu_custom_call" | custom-call | flops 8000000000 | bytes 16000000 | tf_op jit(solution)/shard_map/mix_back/pallas_call | solution.py:632
  398.6 12.3 %mix_back.7 = (bf16[1024,768]{1,0:T(8,128)(2,1)}, bf16[512,768]{1,0:T(8,128)(2,1)}, bf16[512,768]{1,0:T(8,128)(2,1)}, f32[6,1,768]{2,1,0:T(1,128)}) custom-call(bf16[1024,768]{1,0:T(8,128)(2,1)} %get-tuple-element.322.q_ref, bf16[512,768]{1,0:T(8,128)(2,1)} %get-tuple-element.250.k_ref, ...), custom_call_target="tpu_custom_call", output_to_operand_aliasing={{0}: (8, {}), {1}: (9, {}), {2}: (10, {})} | custom-call | flops 8000000000 | bytes 16000000 | tf_op jit(solution)/shard_map/mix_back/pallas_call | solution.py:632
  416.0 8.9 %weight_back.3 = (bf16[2,2,4,1,96,768]{5,4,3,2,1,0:T(8,128)(2,1)}, bf16[2,2,4,1,96,768]{5,4,3,2,1,0:T(8,128)(2,1)}, f32[2,768]{1,0:T(2,128)}) custom-call(s32[4]{0:T(128)} %pad_add_fusion.place_ref, bf16[1024,768]{1,0:T(8,128)(2,1)} %pad_maximum_fusion.low_any.hidden_any, bf16[1024,768]{1,0:T(8,128)(2,1)} %get-tuple-element.346.dq_any, ...), custom_call_target="tpu_custom_call" | custom-call | flops 2415919104 | bytes 12000000 | tf_op jit(solution)/shard_map/weight_back/pallas_call | solution.py:1109
  442.3 10.1 %collective-permute-done.51 = bf16[2,1,96,768]{3,2,1,0:T(8,128)(2,1)} collective-permute-done((bf16[2,1,96,768]{3,2,1,0:T(8,128)(2,1)}, bf16[2,1,96,768]{3,2,1,0:T(8,128)(2,1)}, u32[]{:S(2)}, u32[]{:S(2)}) %collective-permute-start.51) | collective-permute-done | bytes 294944 | tf_op jit(solution)/shard_map/ppermute | solution.py:175
  468.4 7.7 %input_back.1 = (f32[512,768]{1,0:T(8,128)}, f32[512,768]{1,0:T(8,128)}) custom-call(bf16[1024,768]{1,0:T(8,128)(2,1)} %get-tuple-element.346.dq_any, bf16[512,768]{1,0:T(8,128)(2,1)} %get-tuple-element.332.dk_any, bf16[512,768]{1,0:T(8,128)(2,1)} %get-tuple-element.333.dv_any, bf16[4,768,768]{2,1,0:T(8,128)(2,1)} %get-tuple-element.258.attn_any.w_any, ...), custom_call_target="tpu_custom_call" | custom-call | flops 2415919104 | bytes 16000000 | tf_op jit(solution)/shard_map/input_back/pallas_call | solution.py:1158
  487.4 7.1 %collective-permute-done.56 = bf16[4,1,96,768]{3,2,0,1:T(8,128)(2,1)S(1)} collective-permute-done((bf16[4,1,96,768]{3,2,0,1:T(8,128)(2,1)S(1)}, bf16[4,1,96,768]{3,2,0,1:T(8,128)(2,1)S(1)}, u32[]{:S(2)}, u32[]{:S(2)}) %collective-permute-start.56) | collective-permute-done | bytes 589856 | tf_op jit(solution)/shard_map/ppermute | solution.py:175
  520.0 11.6 %adam.2 = (f32[2,4,96,768]{3,2,1,0:T(8,128)}, f32[2,4,96,768]{3,2,1,0:T(8,128)}, f32[2,4,96,768]{3,2,1,0:T(8,128)}, f32[2,96,3072]{2,1,0:T(8,128)}, f32[2,96,307...) custom-call(f32[2,4,96,768]{3,2,1,0:T(8,128)} %refs_0_.3, ...), custom_call_target="tpu_custom_call" | custom-call | flops 20000000 | bytes 22000000 | tf_op jit(solution)/shard_map/adam/pallas_call | solution.py:1236
  534.4 5.9 %collective-permute-done.70 = f32[2,9600]{1,0:T(2,128)S(1)} collective-permute-done((f32[2,9600]{1,0:T(2,128)S(1)}, f32[2,9600]{1,0:T(2,128)S(1)}, u32[]{:S(2)}, u32[]{:S(2)}) %collective-permute-start.70) | collective-permute-done | bytes 76832 | tf_op jit(solution)/shard_map/ppermute | solution.py:175
  548.3 11.6 %adam.3 = (f32[2,4,96,768]{3,2,1,0:T(8,128)}, f32[2,4,96,768]{3,2,1,0:T(8,128)}, f32[2,4,96,768]{3,2,1,0:T(8,128)}, f32[2,96,3072]{2,1,0:T(8,128)}, f32[2,96,307...) custom-call(f32[2,4,96,768]{3,2,1,0:T(8,128)} %refs_0_.3, ...), custom_call_target="tpu_custom_call", output_to_operand_aliasing={{0}: (12, {}), {1}: (13, {}), {2}: (14, {}), {3}: (15, {}),... | custom-call | flops 20000000 | bytes 22000000 | tf_op jit(solution)/shard_map/adam/pallas_call | solution.py:1236
  (406 shorter events, 226.8 us)
Async XLA Ops:
  4.3 22.0 %collective-permute-start.4 = (bf16[2,96,768]{2,1,0:T(8,128)(2,1)}, bf16[2,96,768]{2,1,0:T(8,128)(2,1)S(1)}, u32[]{:S(2)}, u32[]{:S(2)}) collective-permute-start(bf16[2,96,768]{2,1,0:T(8,128)(2,1)} %get-tuple-element.214), channel_id=1, source_target_pairs={{0,2},{1,3},{2,0},{3,1},{4,6},{5,7},{6,4},{7,5},{8,10},{9,11},{10,... | collective-permute-start | bytes 884744 | tf_op jit(solution)/shard_map/ppermute | solution.py:175
  26.3 23.9 %collective-permute-start.8 = (bf16[4,96,768]{2,1,0:T(8,128)(2,1)S(1)}, bf16[4,96,768]{2,1,0:T(8,128)(2,1)S(1)}, u32[]{:S(2)}, u32[]{:S(2)}) collective-permute-start(bf16[4,96,768]{2,1,0:T(8,128)(2,1)S(1)} %copy-done.63), channel_id=1, source_target_pairs={{0,1},{1,0},{2,3},{3,2},{4,5},{5,4},{6,7},{7,6},{8,9},{9,8},{10,11... | collective-permute-start | bytes 1769480 | tf_op jit(solution)/shard_map/ppermute | solution.py:175
  28.0 26.2 %collective-permute-start.7 = (bf16[4,96,768]{2,1,0:T(8,128)(2,1)S(1)}, bf16[4,96,768]{2,1,0:T(8,128)(2,1)S(1)}, u32[]{:S(2)}, u32[]{:S(2)}) collective-permute-start(bf16[4,96,768]{2,1,0:T(8,128)(2,1)S(1)} %pad_maximum_fusion.10), channel_id=1, source_target_pairs={{0,4},{1,5},{2,6},{3,7},{4,0},{5,1},{6,2},{7,3},{8,12},{9,13},{10,... | collective-permute-start | bytes 1769480 | tf_op jit(solution)/shard_map/ppermute | solution.py:175
  56.9 34.5 %collective-permute-start.14 = (bf16[21,96,768]{2,1,0:T(8,128)(2,1)S(1)}, bf16[21,96,768]{2,1,0:T(8,128)(2,1)}, u32[]{:S(2)}, u32[]{:S(2)}) collective-permute-start(bf16[21,96,768]{2,1,0:T(8,128)(2,1)S(1)} %constant_dynamic-update-slice_fusion.3.refs_1_.refs_2_), channel_id=1, source_target_pairs={{0,8},{1,9},{2,10},{3,11},{4,12},{5,13},{6,14},{7,15},{8,0},{9,1},... | collective-permute-start | bytes 9289736 | tf_op jit(solution)/shard_map/ppermute | solution.py:175
  62.6 27.9 %collective-permute-start.12 = (bf16[7,96,768]{2,1,0:T(8,128)(2,1)}, bf16[7,96,768]{2,1,0:T(8,128)(2,1)}, u32[]{:S(2)}, u32[]{:S(2)}) collective-permute-start(bf16[7,96,768]{2,1,0:T(8,128)(2,1)} %pad_maximum_fusion.4), channel_id=1, source_target_pairs={{0,1},{1,0},{2,3},{3,2},{4,5},{5,4},{6,7},{7,6},{8,9},{9,8},{10,11... | collective-permute-start | bytes 3096584 | tf_op jit(solution)/shard_map/ppermute | solution.py:175
  63.2 28.2 %collective-permute-start.11 = (bf16[8,96,768]{2,1,0:T(8,128)(2,1)}, bf16[8,96,768]{2,1,0:T(8,128)(2,1)}, u32[]{:S(2)}, u32[]{:S(2)}) collective-permute-start(bf16[8,96,768]{2,1,0:T(8,128)(2,1)} %pad_maximum_fusion.3), channel_id=1, source_target_pairs={{0,16},{1,17},{2,18},{3,19},{4,20},{5,21},{6,22},{7,23},{8,24},{9,... | collective-permute-start | bytes 3538952 | tf_op jit(solution)/shard_map/ppermute | solution.py:175
  105.3 34.2 %collective-permute-start.18 = (bf16[7,96,768]{2,1,0:T(8,128)(2,1)}, bf16[7,96,768]{2,1,0:T(8,128)(2,1)S(1)}, u32[]{:S(2)}, u32[]{:S(2)}) collective-permute-start(bf16[7,96,768]{2,1,0:T(8,128)(2,1)} %slice_dynamic-update-slice_fusion.1), channel_id=1, source_target_pairs={{0,1},{1,0},{2,3},{3,2},{4,5},{5,4},{6,7},{7,6},{8,9},{9,8},{10,11... | collective-permute-start | bytes 3096584 | tf_op jit(solution)/shard_map/ppermute | solution.py:175
  108.8 30.7 %collective-permute-start.17 = (bf16[7,96,768]{2,1,0:T(8,128)(2,1)}, bf16[7,96,768]{2,1,0:T(8,128)(2,1)}, u32[]{:S(2)}, u32[]{:S(2)}) collective-permute-start(bf16[7,96,768]{2,1,0:T(8,128)(2,1)} %pad_maximum_fusion.5), channel_id=1, source_target_pairs={{0,16},{1,17},{2,18},{3,19},{4,20},{5,21},{6,22},{7,23},{8,24},{9,... | collective-permute-start | bytes 3096584 | tf_op jit(solution)/shard_map/ppermute | solution.py:175
  111.3 28.3 %collective-permute-start.19 = (bf16[4,96,768]{2,1,0:T(8,128)(2,1)}, bf16[4,96,768]{2,1,0:T(8,128)(2,1)S(1)}, u32[]{:S(2)}, u32[]{:S(2)}) collective-permute-start(bf16[4,96,768]{2,1,0:T(8,128)(2,1)} %pad_maximum_fusion.11), channel_id=1, source_target_pairs={{0,4},{1,5},{2,6},{3,7},{4,0},{5,1},{6,2},{7,3},{8,12},{9,13},{10,... | collective-permute-start | bytes 1769480 | tf_op jit(solution)/shard_map/ppermute | solution.py:175
  141.5 34.6 %collective-permute-start.23 = (bf16[10,96,768]{2,1,0:T(8,128)(2,1)}, bf16[10,96,768]{2,1,0:T(8,128)(2,1)}, u32[]{:S(2)}, u32[]{:S(2)}) collective-permute-start(bf16[10,96,768]{2,1,0:T(8,128)(2,1)} %pad_maximum_fusion.1), channel_id=1, source_target_pairs={{0,1},{1,0},{2,3},{3,2},{4,5},{5,4},{6,7},{7,6},{8,9},{9,8},{10,11... | collective-permute-start | bytes 4423688 | tf_op jit(solution)/shard_map/ppermute | solution.py:175
  143.2 31.0 %collective-permute-start.22 = (bf16[9,96,768]{2,1,0:T(8,128)(2,1)}, bf16[9,96,768]{2,1,0:T(8,128)(2,1)S(1)}, u32[]{:S(2)}, u32[]{:S(2)}) collective-permute-start(bf16[9,96,768]{2,1,0:T(8,128)(2,1)} %pad_maximum_fusion.2), channel_id=1, source_target_pairs={{0,16},{1,17},{2,18},{3,19},{4,20},{5,21},{6,22},{7,23},{8,24},{9,... | collective-permute-start | bytes 3981320 | tf_op jit(solution)/shard_map/ppermute | solution.py:175
  177.7 35.3 %collective-permute-start.30 = (bf16[10,96,768]{2,1,0:T(8,128)(2,1)}, bf16[10,96,768]{2,1,0:T(8,128)(2,1)}, u32[]{:S(2)}, u32[]{:S(2)}) collective-permute-start(bf16[10,96,768]{2,1,0:T(8,128)(2,1)} %collective-permute-done.23.refs_3_), channel_id=1, source_target_pairs={{0,8},{1,9},{2,10},{3,11},{4,12},{5,13},{6,14},{7,15},{8,0},{9,1},... | collective-permute-start | bytes 4423688 | tf_op jit(solution)/shard_map/ppermute | solution.py:175
  314.7 52.6 %collective-permute-start.38 = (bf16[4,2,96,768]{3,2,1,0:T(8,128)(2,1)}, bf16[4,2,96,768]{3,2,1,0:T(8,128)(2,1)}, u32[]{:S(2)}, u32[]{:S(2)}) collective-permute-start(bf16[4,2,96,768]{3,2,1,0:T(8,128)(2,1)} %get-tuple-element.418), channel_id=1, source_target_pairs={{0,16},{1,17},{2,18},{3,19},{4,20},{5,21},{6,22},{7,23},{8,24},{9,... | collective-permute-start | bytes 3538952 | tf_op jit(solution)/shard_map/ppermute | solution.py:175
  315.2 52.1 %collective-permute-start.39 = (bf16[4,2,96,768]{3,2,1,0:T(8,128)(2,1)S(1)}, bf16[4,2,96,768]{3,2,1,0:T(8,128)(2,1)}, u32[]{:S(2)}, u32[]{:S(2)}) collective-permute-start(bf16[4,2,96,768]{3,2,1,0:T(8,128)(2,1)S(1)} %get-tuple-element.417), channel_id=1, source_target_pairs={{0,1},{1,0},{2,3},{3,2},{4,5},{5,4},{6,7},{7,6},{8,9},{9,8},{10,11... | collective-permute-start | bytes 3538952 | tf_op jit(solution)/shard_map/ppermute | solution.py:175
  318.2 49.1 %collective-permute-start.40 = (bf16[2,1,96,768]{3,2,0,1:T(8,128)(2,1)}, bf16[2,1,96,768]{3,2,0,1:T(8,128)(2,1)S(1)}, u32[]{:S(2)}, u32[]{:S(2)}) collective-permute-start(bf16[2,1,96,768]{3,2,0,1:T(8,128)(2,1)} %get-tuple-element.435), channel_id=1, source_target_pairs={{0,16},{1,17},{2,18},{3,19},{4,20},{5,21},{6,22},{7,23},{8,24},{9,... | collective-permute-start | bytes 884744 | tf_op jit(solution)/shard_map/ppermute | solution.py:175
  319.7 47.6 %collective-permute-start.41 = (bf16[2,1,96,768]{3,2,0,1:T(8,128)(2,1)}, bf16[2,1,96,768]{3,2,0,1:T(8,128)(2,1)}, u32[]{:S(2)}, u32[]{:S(2)}) collective-permute-start(bf16[2,1,96,768]{3,2,0,1:T(8,128)(2,1)} %get-tuple-element.434), channel_id=1, source_target_pairs={{0,1},{1,0},{2,3},{3,2},{4,5},{5,4},{6,7},{7,6},{8,9},{9,8},{10,11... | collective-permute-start | bytes 884744 | tf_op jit(solution)/shard_map/ppermute | solution.py:175
  367.3 25.4 %collective-permute-start.42 = (bf16[2,2,4,2,96,768]{5,4,3,2,1,0:T(8,128)(2,1)}, bf16[2,2,4,2,96,768]{5,4,3,2,1,0:T(8,128)(2,1)}, u32[]{:S(2)}, u32[]{:S(2)}) collective-permute-start(bf16[2,2,4,2,96,768]{5,4,3,2,1,0:T(8,128)(2,1)} %get-tuple-element.311), channel_id=1, source_target_pairs={{0,8},{1,9},{2,10},{3,11},{4,12},{5,13},{6,14},{7,15},{8,0},{9,1},... | collective-permute-start | bytes 14155784 | tf_op jit(solution)/shard_map/ppermute | solution.py:175
  374.3 36.6 %collective-permute-start.47 = (bf16[2,2,96,768]{3,2,1,0:T(8,128)(2,1)}, bf16[2,2,96,768]{3,2,1,0:T(8,128)(2,1)}, u32[]{:S(2)}, u32[]{:S(2)}) collective-permute-start(bf16[2,2,96,768]{3,2,1,0:T(8,128)(2,1)} %fusion.17), channel_id=1, source_target_pairs={{0,4},{1,5},{2,6},{3,7},{4,0},{5,1},{6,2},{7,3},{8,12},{9,13},{10,... | collective-permute-start | bytes 1769480 | tf_op jit(solution)/shard_map/ppermute | solution.py:175
  379.0 31.9 %collective-permute-start.45 = (bf16[4,1,96,768]{3,2,1,0:T(8,128)(2,1)}, bf16[4,1,96,768]{3,2,1,0:T(8,128)(2,1)S(1)}, u32[]{:S(2)}, u32[]{:S(2)}) collective-permute-start(bf16[4,1,96,768]{3,2,1,0:T(8,128)(2,1)} %get-tuple-element.422), channel_id=1, source_target_pairs={{0,16},{1,17},{2,18},{3,19},{4,20},{5,21},{6,22},{7,23},{8,24},{9,... | collective-permute-start | bytes 1769480 | tf_op jit(solution)/shard_map/ppermute | solution.py:175
  379.6 31.4 %collective-permute-start.46 = (bf16[4,1,96,768]{3,2,1,0:T(8,128)(2,1)}, bf16[4,1,96,768]{3,2,1,0:T(8,128)(2,1)S(1)}, u32[]{:S(2)}, u32[]{:S(2)}) collective-permute-start(bf16[4,1,96,768]{3,2,1,0:T(8,128)(2,1)} %get-tuple-element.421), channel_id=1, source_target_pairs={{0,1},{1,0},{2,3},{3,2},{4,5},{5,4},{6,7},{7,6},{8,9},{9,8},{10,11... | collective-permute-start | bytes 1769480 | tf_op jit(solution)/shard_map/ppermute | solution.py:175
  425.7 28.7 %collective-permute-start.48 = (bf16[4,2,96,768]{3,2,1,0:T(8,128)(2,1)}, bf16[4,2,96,768]{3,2,1,0:T(8,128)(2,1)}, u32[]{:S(2)}, u32[]{:S(2)}) collective-permute-start(bf16[4,2,96,768]{3,2,1,0:T(8,128)(2,1)} %get-tuple-element.416), channel_id=1, source_target_pairs={{0,16},{1,17},{2,18},{3,19},{4,20},{5,21},{6,22},{7,23},{8,24},{9,... | collective-permute-start | bytes 3538952 | tf_op jit(solution)/shard_map/ppermute | solution.py:175
  426.3 28.4 %collective-permute-start.49 = (bf16[4,2,96,768]{3,2,1,0:T(8,128)(2,1)}, bf16[4,2,96,768]{3,2,1,0:T(8,128)(2,1)}, u32[]{:S(2)}, u32[]{:S(2)}) collective-permute-start(bf16[4,2,96,768]{3,2,1,0:T(8,128)(2,1)} %get-tuple-element.415), channel_id=1, source_target_pairs={{0,1},{1,0},{2,3},{3,2},{4,5},{5,4},{6,7},{7,6},{8,9},{9,8},{10,11... | collective-permute-start | bytes 3538952 | tf_op jit(solution)/shard_map/ppermute | solution.py:175
  459.4 28.1 %collective-permute-start.58 = (bf16[2,2,96,768]{3,2,1,0:T(8,128)(2,1)S(1)}, bf16[2,2,96,768]{3,2,1,0:T(8,128)(2,1)}, u32[]{:S(2)}, u32[]{:S(2)}) collective-permute-start(bf16[2,2,96,768]{3,2,1,0:T(8,128)(2,1)S(1)} %fusion.12), channel_id=1, source_target_pairs={{0,4},{1,5},{2,6},{3,7},{4,0},{5,1},{6,2},{7,3},{8,12},{9,13},{10,... | collective-permute-start | bytes 1769480 | tf_op jit(solution)/shard_map/ppermute | solution.py:175
  482.2 25.8 %collective-permute-start.64 = (bf16[3,96,768]{2,1,0:T(8,128)(2,1)}, bf16[3,96,768]{2,1,0:T(8,128)(2,1)}, u32[]{:S(2)}, u32[]{:S(2)}) collective-permute-start(bf16[3,96,768]{2,1,0:T(8,128)(2,1)} %get-tuple-element.368), channel_id=1, source_target_pairs={{0,16},{1,17},{2,18},{3,19},{4,20},{5,21},{6,22},{7,23},{8,24},{9,... | collective-permute-start | bytes 1327112 | tf_op jit(solution)/shard_map/ppermute | solution.py:175
  (115 other events, 1126.2 us)

commit v9 on v8

--- a/solution.py
+++ b/solution.py
@@ -270,6 +270,32 @@
             targets[member].at[lead, pl.ds(pl.multiple_of(row, ROWS), ROWS), :],
         )
     return copies
+
+
+def pack_kernel(outputs, count, *refs):
+    sources, targets, sems = refs[:count], refs[count:-1], refs[-1]
+    pairs = []
+    for target, parts in zip(targets, outputs):
+        at = 0
+        for source, first, held in parts:
+            pairs.append((sources[source].at[first : first + held], target.at[at : at + held]))
+            at += held
+    finish(issue(pairs, sems))
+
+
+def pack(outputs, sources):
+    total = sum(len(parts) for parts in outputs)
+    counts = [sum(held for unused, unused_first, held in parts) for parts in outputs]
+    return pl.pallas_call(
+        partial(pack_kernel, outputs, len(sources)),
+        out_shape=[jax.ShapeDtypeStruct((count, ROWS, D), jnp.bfloat16) for count in counts],
+        in_specs=[ANY_SPEC] * len(sources),
+        out_specs=[VMEM_SPEC] * len(outputs),
+        scratch_shapes=[pltpu.SemaphoreType.DMA((total,))],
+        compiler_params=pltpu.CompilerParams(vmem_limit_bytes=16 * 1024 * 1024),
+        cost_estimate=pl.CostEstimate(flops=0, bytes_accessed=300000 * sum(counts), transcendentals=0),
+        name="pack",
+    )(*sources)
 
 
 def quarter_spans(place_ref, side):
@@ -1588,13 +1614,10 @@
 
 
 def gather_small(blocks, place):
-    z, y = place[2], place[3]
-    low, high = z % 2, z // 2
+    low, high = place[2] % 2, place[2] // 2
     blocks = jnp.where(low == 0, blocks, blocks[jnp.array([1, 0, 3, 2])])
     blocks = jnp.where(high == 0, blocks, blocks[jnp.array([2, 3, 0, 1])])
-    other = swap_y(blocks)
-    pairs = jnp.where(y == 0, jnp.stack([blocks, other], 1), jnp.stack([other, blocks], 1))
-    return pairs.transpose(2, 0, 1, 3).reshape(blocks.shape[1], -1)
+    return blocks.transpose(2, 0, 1, 3).reshape(blocks.shape[2], -1)
 
 
 def add_low(*values):
@@ -1704,36 +1727,60 @@
     row_flags = predicted.reshape(1, LEN).astype(jnp.float32)
     col_flags = predicted.reshape(LEN, 1).astype(jnp.float32)
     small_low = small_master.astype(jnp.bfloat16)
-    z_a0, plane_a0, near_f0, plane_f0, own_1, oth_1, low0, row_flags, col_flags, small_low = join(
-        z_a0, plane_a0, near_f0, plane_f0, own_1, oth_1, low0, row_flags, col_flags, small_low
-    )
-    col_a0 = jnp.concatenate(z_a0)
+    small_y = swap_y(small_low)
+    z_a0, plane_a0, near_f0, plane_f0, own_1, oth_1, low0, row_flags, col_flags, small_y = join(
+        z_a0, plane_a0, near_f0, plane_f0, own_1, oth_1, low0, row_flags, col_flags, small_y
+    )
+    col_a0, to_far_f0 = pack(
+        ([(0, 0, 1), (1, 0, 1), (2, 0, 1)], [(3, 0, 2), (4, 0, 2)]), (*z_a0, own_f0, near_f0)
+    )
     x0 = swap_x(col_a0)
     y0 = swap_y(col_a0)
-    far_f0 = swap_z(jnp.concatenate([own_f0, near_f0]), 2)
+    far_f0 = swap_z(to_far_f0, 2)
     plane_f0 = swap_y(after(plane_f0, col_a0))
     near_1 = swap_z(after(own_1, col_a0), 1)
-    small_near = swap_z(small_low, 1)
+    odd = place_parts[3] == 1
+    small_pair = jnp.stack(
+        [jnp.where(odd, small_y, small_low), jnp.where(odd, small_low, small_y)]
+    )
+    small_near = swap_z(small_pair, 1)
     x0, y0, far_f0, plane_f0, near_1, small_near = join(
         x0, y0, far_f0, plane_f0, near_1, small_near
     )
-    col_f0 = jnp.concatenate([near_f0, far_f0])
-    to_x1 = jnp.concatenate([col_f0, y0[:2]])
-    to_y1 = jnp.concatenate([col_f0, x0[2:]])
+    to_x1, to_y1, to_far_a1 = pack(
+        (
+            [(0, 0, 2), (1, 0, 4), (2, 0, 2)],
+            [(0, 0, 2), (1, 0, 4), (3, 2, 1)],
+            [(4, 0, 1), (5, 0, 1)],
+        ),
+        (near_f0, far_f0, y0, x0, own_1, near_1),
+    )
     x1 = swap_x(to_x1)
     y1 = swap_y(to_y1)
-    far_a1 = swap_z(jnp.concatenate([own_1[:1], near_1[:1]]), 2)
-    held = after((plane_a0, col_a0, x0, y0, plane_f0, col_f0), to_x1, to_y1)
-    mine_0 = jnp.concatenate(held)
+    far_a1 = swap_z(to_far_a1, 2)
+    (mine_0,) = pack(
+        (
+            [(0, 0, 2), (1, 0, 3), (2, 0, 3), (3, 0, 3), (4, 0, 4), (5, 0, 2), (6, 0, 4)],
+        ),
+        after((plane_a0, col_a0, x0, y0, plane_f0, near_f0, far_f0), far_a1),
+    )
     theirs_0 = swap_core(mine_0)
-    small_pair = jnp.stack([small_low, small_near])
-    small_far = swap_z(small_pair, 2)
-    small_all = gather_small(jnp.concatenate([small_pair, small_far]), place_parts)
+    small_four = jnp.stack([small_pair, small_near])
+    small_far = swap_z(small_four, 2)
+    small_all = gather_small(jnp.concatenate([small_four, small_far]), place_parts)
     x1, y1, far_a1, theirs_0, small_all = join(x1, y1, far_a1, theirs_0, small_all)
-    col_a1 = jnp.concatenate([near_1[:1], far_a1])
-    x2 = swap_x(jnp.concatenate([col_a1, y1[:4]]))
-    y2 = swap_y(jnp.concatenate([col_a1, x1[4:6], own_1[:1], oth_1[:1]]))
-    far_f1 = swap_z(jnp.concatenate([own_1[1:], after(near_1[1:], far_a1)]), 2)
+    to_x2, to_y2, to_far_f1, col_a1 = pack(
+        (
+            [(0, 0, 1), (1, 0, 2), (2, 0, 4)],
+            [(0, 0, 1), (1, 0, 2), (3, 4, 2), (4, 0, 1), (5, 0, 1)],
+            [(4, 1, 2), (0, 1, 2)],
+            [(0, 0, 1), (1, 0, 2)],
+        ),
+        (near_1, far_a1, y1, x1, own_1, oth_1),
+    )
+    x2 = swap_x(to_x2)
+    y2 = swap_y(to_y2)
+    far_f1 = swap_z(to_far_f1, 2)
     their_x1, their_y1 = swap_core(x1), swap_core(y1)
     group_a0 = gather_group(
         1, (attn_low0,), (0, 0), (0, 2), ((0, 5), (0, 8)), ((1, 6, 2), (2, 6, 1)),
@@ -1744,9 +1791,16 @@
     q0, k0, v0, attn0 = project(place, low0, small0, group_a0)
     mixed0, p0, inverse0, dead = mix(lengths, far0, tvec0, q0, k0, v0, row_flags, col_flags)
     x2, y2, far_f1, mixed0 = join(x2, y2, far_f1, mixed0)
-    col_f1 = jnp.concatenate([near_1[1:], far_f1])
-    x3 = swap_x(jnp.concatenate([col_f1, y2[:3]]))
-    y3 = swap_y(jnp.concatenate([col_f1, own_1[1:], oth_1[1:]]))
+    to_x3, to_y3, col_f1 = pack(
+        (
+            [(0, 1, 2), (1, 0, 4), (2, 0, 3)],
+            [(0, 1, 2), (1, 0, 4), (3, 1, 2), (4, 1, 2)],
+            [(0, 1, 2), (1, 0, 4)],
+        ),
+        (near_1, far_f1, y2, own_1, oth_1),
+    )
+    x3 = swap_x(to_x3)
+    y3 = swap_y(to_y3)
     their_x2, their_y2, their_a1 = swap_core(x2), swap_core(y2), swap_core(after(col_a1, x2))
     group_f0 = gather_group(
         2, (inner_low0, outer_low0), (0, 11), (0, 15), ((1, 0), (2, 0)), ((3, 3, 4), (4, 3, 2)),
@@ -1756,8 +1810,9 @@
         place, small0, hidden_bias0, mixed0, low0, attn0, group_f0
     )
     x3, y3, low1 = join(x3, y3, low1)
-    x4 = swap_x(y3[:3])
-    y4 = swap_y(x3[3:6])
+    to_x4, to_y4 = pack(([(0, 0, 3)], [(1, 3, 3)]), (y3, x3))
+    x4 = swap_x(to_x4)
+    y4 = swap_y(to_y4)
     their_x3, their_y3 = swap_core(x3), swap_core(y3)
     group_a1 = gather_group(
         1, (attn_low1,), (1, 5), (2, 0), ((0, 0), (1, 0)), ((3, 6, 3),),
@@ -1810,17 +1865,6 @@
     )
     get_a0 = swap_core(send_a0)
     zfar_a1 = swap_z(far_payload(keep_a1, get_a1, sides_ra1, place_parts), 2)
-    pair_f1 = own_pair(keep_f1, get_f1, sides_rf1, after(zfar_f1, get_a0), place_parts)
-    znear_f1 = reduce_near(pair_f1, place_parts)
-    sides_rf0, get_a0, zfar_a1, znear_f1, vec_a0 = join(
-        sides_rf0, get_a0, zfar_a1, znear_f1, vec_a0
-    )
-    payload_f0 = far_payload(keep_f0, get_f0, sides_rf0, place_parts)
-    zfar_f0 = swap_z(payload_f0, 2)
-    by_a0 = reduce_corners(keep_a0, after(get_a0, payload_f0))
-    pair_a1 = own_pair(keep_a1, get_a1, sides_ra1, zfar_a1, place_parts)
-    znear_a1 = reduce_near(after(pair_a1, payload_f0), place_parts)
-    content_grad, query_grad = input_back(after(dq0, sides_rf0), dk0, dv0, attn0, dresid0)
     small_sum = jnp.concatenate(
         [
             jnp.stack([vec_a0, vec_a1]).reshape(LAYERS, -1),
@@ -1832,7 +1876,19 @@
         ],
         axis=1,
     )
-    by_a0, content_grad, znear_a1 = join(by_a0, content_grad, znear_a1)
+    pair_f1 = own_pair(keep_f1, get_f1, sides_rf1, after(zfar_f1, get_a0), place_parts)
+    znear_f1 = reduce_near(pair_f1, place_parts)
+    sides_rf0, get_a0, zfar_a1, znear_f1, small_sum = join(
+        sides_rf0, get_a0, zfar_a1, znear_f1, small_sum
+    )
+    payload_f0 = far_payload(keep_f0, get_f0, sides_rf0, place_parts)
+    zfar_f0 = swap_z(payload_f0, 2)
+    by_a0 = reduce_corners(keep_a0, after(get_a0, payload_f0))
+    pair_a1 = own_pair(keep_a1, get_a1, sides_ra1, zfar_a1, place_parts)
+    znear_a1 = reduce_near(after(pair_a1, payload_f0), place_parts)
+    content_grad, query_grad = input_back(after(dq0, sides_rf0), dk0, dv0, attn0, dresid0)
+    small_c = swap_core(after(small_sum, payload_f0))
+    by_a0, content_grad, znear_a1, small_c = join(by_a0, content_grad, znear_a1, small_c)
     payloads_a0 = side_payloads(keep_a0, get_a0, by_a0)
     sides_ra0 = reduce_sides(payloads_a0)
     own_1 = jnp.concatenate(
@@ -1842,14 +1898,16 @@
         ]
     )
     across_1 = swap_x(after(own_1, payloads_a0))
-    small_sum = small_sum + swap_core(after(small_sum, payloads_a0))
-    sides_ra0, zfar_f0, small_sum = join(sides_ra0, zfar_f0, small_sum)
+    small_sum = after(small_sum, payloads_a0) + small_c
+    small_y = swap_y(small_sum)
+    sides_ra0, zfar_f0, small_y = join(sides_ra0, zfar_f0, small_y)
     column_a0 = add_low(keep_a0[0, 0], get_a0[0, 0], *sides_ra0)
     shifts_a0 = reduce_direct(column_a0, place_parts)
     pair_f0 = own_pair(keep_f0, get_f0, sides_rf0, zfar_f0, place_parts)
     znear_f0 = reduce_near(after(pair_f0, column_a0), place_parts)
-    small_sum = small_sum + swap_y(after(small_sum, column_a0))
-    shifts_a0, znear_f0, across_1, small_sum = join(shifts_a0, znear_f0, across_1, small_sum)
+    small_sum = after(small_sum, column_a0) + small_y
+    small_z = swap_z(small_sum, 1)
+    shifts_a0, znear_f0, across_1, small_z = join(shifts_a0, znear_f0, across_1, small_z)
     own_0 = jnp.concatenate(
         [
             reduce_total(pair_f0, znear_f0, place_parts),
@@ -1863,11 +1921,11 @@
         outer_master, outer_first, outer_second,
     )
     new_1 = adam(1, state, four_1, ())
-    small_z = swap_z(after(small_sum, own_0), 1)
+    small_sum = after(small_sum, own_0) + small_z
+    small_z = swap_z(small_sum, 2)
     across_0, new_1, small_z = join(across_0, new_1, small_z)
+    four_0 = share_core(jnp.stack([own_0, across_0]), place_parts)
     small_sum = small_sum + small_z
-    four_0 = share_core(jnp.stack([own_0, across_0]), place_parts)
-    small_sum = small_sum + swap_z(small_sum, 2)
     small_x = swap_x(small_sum)
     new_0 = adam(0, state, four_0, tuple(new_1))
     small_sum = small_sum + small_x

time: 570 us -> 593 us (1.040)
  Pallas kernels: 282 us -> 305 us
  waiting for transfers between devices: 86.1 us -> 103 us
  other arithmetic: 65.9 us -> 53.7 us
    ppermute x72, waiting for transfers between devices: 86.1 us -> 103 us  [move(): return lax.ppermute(value, AXES, pairs)]
    pallas_call x1, Pallas kernels: 22 us -> 34.4 us  [feed(): pl.pallas_call(partial(feed_kernel, plan), out_shape=[tall, jax.ShapeDtyp...]
    pallas_call x0 -> x6, Pallas kernels: none -> 10.7 us  [pack(): pl.pallas_call(partial(pack_kernel, outputs, len(sources)), out_shape=[ja...]
    concatenate x12 -> x1, other arithmetic: 12.1 us -> 1.41 us  [per_device_fast(): jnp.concatenate([small_four, small_far])]
    unnamed x149 -> x164, local copies, waits for them, and re-layouts: 18.7 us -> 17.5 us
  transfers between devices with their start and end apart: 72 -> 72, of which waited for: 27 -> 23; matrix products, arithmetic and copies ran while one was open for 16% -> 13% of each run, Pallas kernels for 35% -> 36%
where the time goes in v9:
time: 593 us; the launch traced here: 586 us
  Pallas kernels  305 us (51%)
  waiting for transfers between devices  103 us (17%)
  starting transfers between devices  69.2 us (12%)
  other arithmetic  53.7 us (9%)
  local copies, waits for them, and re-layouts  49.8 us (8%)
    ppermute x72, waiting for transfers between devices, move(): return lax.ppermute(value, AXES, pairs)  103 us
    ppermute x72, starting transfers between devices, move(): return lax.ppermute(value, AXES, pairs)  69.2 us
    pallas_call x1, Pallas kernels, turn(): pl.pallas_call(partial(turn_kernel, plan), out_shape=[half_low, half_low]...  55.5 us
    pallas_call x4, Pallas kernels, mix_back(): pl.pallas_call(mix_back_kernel, grid=(H // 4,), out_shape=[jax.ShapeDtype...  50 us
    pallas_call x1, Pallas kernels, down(): pl.pallas_call(partial(down_kernel, plan), out_shape=BACK_SHAPES, in_spec...  45.8 us
    pallas_call x2, Pallas kernels, mix(): pl.pallas_call(mix_kernel, grid=(H // 2,), out_shape=[jax.ShapeDtypeStruc...  36.5 us
    pallas_call x1, Pallas kernels, feed(): pl.pallas_call(partial(feed_kernel, plan), out_shape=[tall, jax.ShapeDtyp...  34.4 us
    convert_element_type x19, other arithmetic, add_low(): return total.astype(jnp.bfloat16)  32.7 us
  transfers between devices with their start and end apart: 72, of which 23 were waited for; matrix products, arithmetic and copies ran while one was open for 13% of the time, Pallas kernels for 36%

profile of v9, /device:TPU:0, one launch (start us, length us, event | category | flops | bytes accessed | tf_op | source)
XLA Modules:
  0.0 585.5 jit_solution(11857806282705926259)
XLA Ops:
  35.7 10.4 %collective-permute-done.11 = bf16[2,2,1200]{2,1,0:T(2,128)(2,1)S(1)} collective-permute-done((bf16[2,2,1200]{2,1,0:T(2,128)(2,1)S(1)}, bf16[2,2,1200]{2,1,0:T(2,128)(2,1)S(1)}, u32[]{:S(2)}, u32[]{:S(2)}) %collective-permute-start.11) | collective-permute-done | bytes 9632 | tf_op jit(solution)/shard_map/ppermute | solution.py:175
  46.6 7.6 %collective-permute-done.10.refs_5_.refs_0_ = bf16[3,96,768]{2,1,0:T(8,128)(2,1)S(1)} collective-permute-done((bf16[3,96,768]{2,1,0:T(8,128)(2,1)S(1)}, bf16[3,96,768]{2,1,0:T(8,128)(2,1)S(1)}, u32[]{:S(2)}, u32[]{:S(2)}) %collective-permute-start.10) | collective-permute-done | bytes 442400 | tf_op jit(solution)/shard_map/ppermute | solution.py:175
  62.3 13.7 %collective-permute-done.14.refs_1_ = bf16[2,96,768]{2,1,0:T(8,128)(2,1)S(1)} collective-permute-done((bf16[2,96,768]{2,1,0:T(8,128)(2,1)S(1)}, bf16[2,96,768]{2,1,0:T(8,128)(2,1)S(1)}, u32[]{:S(2)}, u32[]{:S(2)}) %collective-permute-start.14) | collective-permute-done | bytes 294944 | tf_op jit(solution)/shard_map/ppermute | solution.py:175
  97.2 13.8 %collective-permute-done.13.refs_2_.refs_3_.refs_4_ = bf16[7,96,768]{2,1,0:T(8,128)(2,1)} collective-permute-done((bf16[7,96,768]{2,1,0:T(8,128)(2,1)}, bf16[7,96,768]{2,1,0:T(8,128)(2,1)}, u32[]{:S(2)}, u32[]{:S(2)}) %collective-permute-start.13) | collective-permute-done | bytes 1032224 | tf_op jit(solution)/shard_map/ppermute | solution.py:175
  132.0 7.5 %project.2 = (bf16[1024,768]{1,0:T(8,128)(2,1)}, bf16[512,768]{1,0:T(8,128)(2,1)}, bf16[512,768]{1,0:T(8,128)(2,1)}, bf16[4,768,768]{2,1,0:T(8,128)(2,1)}) custom-call(s32[4]{0:T(128)} %pad_add_fusion.place_ref, f32[8,768]{1,0:T(8,128)} %reshape.512.small_ref.below_ref, bf16[1024,768]{1,0:T(8,128)(2,1)} %pad_maximum_fusion.low_any.hidden_any, ...), custom_call_target="tpu_custom_call" | custom-call | flops 2415919104 | bytes 16000000 | tf_op jit(solution)/shard_map/project/pallas_call | solution.py:422
  139.5 18.3 %mix.2 = (bf16[1024,768]{1,0:T(8,128)(2,1)}, bf16[12,512,1024]{2,1,0:T(8,128)(2,1)}, f32[12,1,1024]{2,1,0:T(1,128)}, f32[1,1024]{1,0:T(1,128)}) custom-call(s32[1]{0:T(128)S(6)} %copy.160.length_ref, f32[12,2]{1,0:T(8,128)} %pad_maximum_fusion.11.far_ref, bf16[1024,768]{1,0:T(8,128)(2,1)} %get-tuple-element.352.q_ref, ...), custom_call_target="tpu_custom_call" | custom-call | flops 6499999744 | bytes 8000000 | tf_op jit(solution)/shard_map/mix/pallas_call | solution.py:557
  167.3 34.4 %feed.1 = (f32[1024,768]{1,0:T(8,128)}, bf16[4,1024,768]{2,1,0:T(8,128)(2,1)}, bf16[1024,768]{1,0:T(8,128)(2,1)}, bf16[1024,768]{1,0:T(8,128)(2,1)}, f32[1024,768]{1,0:T(8,128)}) custom-call(s32[4]{0:T(128)} %pad_add_fusion.place_ref, f32[8,768]{1,0:T(8,128)} %reshape.512.small_ref.below_ref, f32[1,3072]{1,0:T(1,128)} %slice.281.hidden_bias_ref, ...), custom_call_target="tpu_custom_call" | custom-call | flops 10871635968 | bytes 30000000 | tf_op jit(solution)/shard_map/feed/pallas_call | solution.py:791
  208.2 7.6 %project.3 = (bf16[1024,768]{1,0:T(8,128)(2,1)}, bf16[512,768]{1,0:T(8,128)(2,1)}, bf16[512,768]{1,0:T(8,128)(2,1)}, bf16[4,768,768]{2,1,0:T(8,128)(2,1)}) custom-call(s32[4]{0:T(128)} %pad_add_fusion.place_ref, f32[8,768]{1,0:T(8,128)} %reshape.511.small_ref, bf16[1024,768]{1,0:T(8,128)(2,1)} %get-tuple-element.327.low_any, ...), custom_call_target="tpu_custom_call" | custom-call | flops 2415919104 | bytes 16000000 | tf_op jit(solution)/shard_map/project/pallas_call | solution.py:422
  219.8 18.2 %mix.3 = (bf16[1024,768]{1,0:T(8,128)(2,1)}, bf16[12,512,1024]{2,1,0:T(8,128)(2,1)}, f32[12,1,1024]{2,1,0:T(1,128)}, f32[1,1024]{1,0:T(1,128)}) custom-call(s32[1]{0:T(128)S(6)} %copy.160.length_ref, f32[12,2]{1,0:T(8,128)} %pad_maximum_fusion.10.far_ref, bf16[1024,768]{1,0:T(8,128)(2,1)} %get-tuple-element.318.q_ref, ...), custom_call_target="tpu_custom_call" | custom-call | flops 6499999744 | bytes 8000000 | tf_op jit(solution)/shard_map/mix/pallas_call | solution.py:557
  239.3 55.5 %turn.1 = (bf16[512,768]{1,0:T(8,128)(2,1)}, bf16[512,768]{1,0:T(8,128)(2,1)}, f32[1024,768]{1,0:T(8,128)}, bf16[1024,768]{1,0:T(8,128)(2,1)}, bf16[768,768]{1,0...) custom-call(s32[4]{0:T(128)} %pad_add_fusion.place_ref, ...), custom_call_target="tpu_custom_call" | custom-call | flops 32614907904 | bytes 60000000 | tf_op jit(solution)/shard_map/turn/pallas_call | solution.py:982
  295.3 12.3 %mix_back.4 = (bf16[1024,768]{1,0:T(8,128)(2,1)}, bf16[512,768]{1,0:T(8,128)(2,1)}, bf16[512,768]{1,0:T(8,128)(2,1)}, f32[6,1,768]{2,1,0:T(1,128)}) custom-call(bf16[1024,768]{1,0:T(8,128)(2,1)} %get-tuple-element.318.q_ref, bf16[512,768]{1,0:T(8,128)(2,1)} %get-tuple-element.299.k_ref, bf16[512,768]{1,0:T(8,128)(2,1)} %get-tuple-element.300.v_ref, ...), custom_call_target="tpu_custom_call" | custom-call | flops 8000000000 | bytes 16000000 | tf_op jit(solution)/shard_map/mix_back/pallas_call | solution.py:658
  311.0 12.8 %mix_back.5 = (bf16[1024,768]{1,0:T(8,128)(2,1)}, bf16[512,768]{1,0:T(8,128)(2,1)}, bf16[512,768]{1,0:T(8,128)(2,1)}, f32[6,1,768]{2,1,0:T(1,128)}) custom-call(bf16[1024,768]{1,0:T(8,128)(2,1)} %get-tuple-element.318.q_ref, bf16[512,768]{1,0:T(8,128)(2,1)} %get-tuple-element.299.k_ref, ...), custom_call_target="tpu_custom_call", output_to_operand_aliasing={{0}: (8, {}), {1}: (9, {}), {2}: (10, {})} | custom-call | flops 8000000000 | bytes 16000000 | tf_op jit(solution)/shard_map/mix_back/pallas_call | solution.py:658
  325.5 8.8 %weight_back.2 = (bf16[2,2,4,1,96,768]{5,4,3,2,1,0:T(8,128)(2,1)}, bf16[2,2,4,1,96,768]{5,4,3,2,1,0:T(8,128)(2,1)}, f32[2,768]{1,0:T(2,128)}) custom-call(s32[4]{0:T(128)} %pad_add_fusion.place_ref, bf16[1024,768]{1,0:T(8,128)(2,1)} %get-tuple-element.327.low_any, bf16[1024,768]{1,0:T(8,128)(2,1)} %get-tuple-element.322.dq_any, ...), custom_call_target="tpu_custom_call" | custom-call | flops 2415919104 | bytes 12000000 | tf_op jit(solution)/shard_map/weight_back/pallas_call | solution.py:1135
  345.4 45.8 %down.1 = (f32[1024,768]{1,0:T(8,128)}, bf16[1024,768]{1,0:T(8,128)(2,1)}, bf16[768,768]{1,0:T(8,128)(2,1)}, bf16[2,2,4,2,96,768]{5,4,3,2,1,0:T(8,128)(2,1)}, bf...) custom-call(s32[4]{0:T(128)} %pad_add_fusion.place_ref, ...), custom_call_target="tpu_custom_call" | custom-call | flops 27179089920 | bytes 60000000 | tf_op jit(solution)/shard_map/down/pallas_call | solution.py:1068
  402.0 12.4 %mix_back.6 = (bf16[1024,768]{1,0:T(8,128)(2,1)}, bf16[512,768]{1,0:T(8,128)(2,1)}, bf16[512,768]{1,0:T(8,128)(2,1)}, f32[6,1,768]{2,1,0:T(1,128)}) custom-call(bf16[1024,768]{1,0:T(8,128)(2,1)} %get-tuple-element.352.q_ref, bf16[512,768]{1,0:T(8,128)(2,1)} %get-tuple-element.274.k_ref, bf16[512,768]{1,0:T(8,128)(2,1)} %get-tuple-element.275.v_ref, ...), custom_call_target="tpu_custom_call" | custom-call | flops 8000000000 | bytes 16000000 | tf_op jit(solution)/shard_map/mix_back/pallas_call | solution.py:658
  419.8 12.5 %mix_back.7 = (bf16[1024,768]{1,0:T(8,128)(2,1)}, bf16[512,768]{1,0:T(8,128)(2,1)}, bf16[512,768]{1,0:T(8,128)(2,1)}, f32[6,1,768]{2,1,0:T(1,128)}) custom-call(bf16[1024,768]{1,0:T(8,128)(2,1)} %get-tuple-element.352.q_ref, bf16[512,768]{1,0:T(8,128)(2,1)} %get-tuple-element.274.k_ref, ...), custom_call_target="tpu_custom_call", output_to_operand_aliasing={{0}: (8, {}), {1}: (9, {}), {2}: (10, {})} | custom-call | flops 8000000000 | bytes 16000000 | tf_op jit(solution)/shard_map/mix_back/pallas_call | solution.py:658
  437.7 8.9 %weight_back.3 = (bf16[2,2,4,1,96,768]{5,4,3,2,1,0:T(8,128)(2,1)}, bf16[2,2,4,1,96,768]{5,4,3,2,1,0:T(8,128)(2,1)}, f32[2,768]{1,0:T(2,128)}) custom-call(s32[4]{0:T(128)} %pad_add_fusion.place_ref, bf16[1024,768]{1,0:T(8,128)(2,1)} %pad_maximum_fusion.low_any.hidden_any, bf16[1024,768]{1,0:T(8,128)(2,1)} %get-tuple-element.381.dq_any, ...), custom_call_target="tpu_custom_call" | custom-call | flops 2415919104 | bytes 12000000 | tf_op jit(solution)/shard_map/weight_back/pallas_call | solution.py:1135
  467.6 11.4 %collective-permute-done.51 = bf16[2,1,96,768]{3,2,1,0:T(8,128)(2,1)S(1)} collective-permute-done((bf16[2,1,96,768]{3,2,1,0:T(8,128)(2,1)S(1)}, bf16[2,1,96,768]{3,2,1,0:T(8,128)(2,1)S(1)}, u32[]{:S(2)}, u32[]{:S(2)}) %collective-permute-start.51) | collective-permute-done | bytes 294944 | tf_op jit(solution)/shard_map/ppermute | solution.py:175
  479.1 5.7 collective-permute-done.48
  495.6 7.7 %input_back.1 = (f32[512,768]{1,0:T(8,128)}, f32[512,768]{1,0:T(8,128)}) custom-call(bf16[1024,768]{1,0:T(8,128)(2,1)} %get-tuple-element.381.dq_any, bf16[512,768]{1,0:T(8,128)(2,1)} %get-tuple-element.362.dk_any, bf16[512,768]{1,0:T(8,128)(2,1)} %get-tuple-element.363.dv_any, bf16[4,768,768]{2,1,0:T(8,128)(2,1)} %get-tuple-element.284.attn_any.w_any, ...), custom_call_target="tpu_custom_call" | custom-call | flops 2415919104 | bytes 16000000 | tf_op jit(solution)/shard_map/input_back/pallas_call | solution.py:1184
  514.8 8.9 %collective-permute-done.60 = f32[2,9600]{1,0:T(2,128)S(1)} collective-permute-done((f32[2,9600]{1,0:T(2,128)S(1)}, f32[2,9600]{1,0:T(2,128)S(1)}, u32[]{:S(2)}, u32[]{:S(2)}) %collective-permute-start.60) | collective-permute-done | bytes 76832 | tf_op jit(solution)/shard_map/ppermute | solution.py:175
  535.8 9.0 %collective-permute-done.66 = f32[2,9600]{1,0:T(2,128)S(1)} collective-permute-done((f32[2,9600]{1,0:T(2,128)S(1)}, f32[2,9600]{1,0:T(2,128)S(1)}, u32[]{:S(2)}, u32[]{:S(2)}) %collective-permute-start.66) | collective-permute-done | bytes 76832 | tf_op jit(solution)/shard_map/ppermute | solution.py:175
  554.2 11.6 %adam.2 = (f32[2,4,96,768]{3,2,1,0:T(8,128)}, f32[2,4,96,768]{3,2,1,0:T(8,128)}, f32[2,4,96,768]{3,2,1,0:T(8,128)}, f32[2,96,3072]{2,1,0:T(8,128)}, f32[2,96,307...) custom-call(f32[2,4,96,768]{3,2,1,0:T(8,128)} %refs_0_.3, ...), custom_call_target="tpu_custom_call" | custom-call | flops 20000000 | bytes 22000000 | tf_op jit(solution)/shard_map/adam/pallas_call | solution.py:1262
  573.7 11.6 %adam.3 = (f32[2,4,96,768]{3,2,1,0:T(8,128)}, f32[2,4,96,768]{3,2,1,0:T(8,128)}, f32[2,4,96,768]{3,2,1,0:T(8,128)}, f32[2,96,3072]{2,1,0:T(8,128)}, f32[2,96,307...) custom-call(f32[2,4,96,768]{3,2,1,0:T(8,128)} %refs_0_.3, ...), custom_call_target="tpu_custom_call", output_to_operand_aliasing={{0}: (12, {}), {1}: (13, {}), {2}: (14, {}), {3}: (15, {}),... | custom-call | flops 20000000 | bytes 22000000 | tf_op jit(solution)/shard_map/adam/pallas_call | solution.py:1262
  (405 shorter events, 216.2 us)
Async XLA Ops:
  4.2 22.1 %collective-permute-start.4 = (bf16[2,96,768]{2,1,0:T(8,128)(2,1)}, bf16[2,96,768]{2,1,0:T(8,128)(2,1)S(1)}, u32[]{:S(2)}, u32[]{:S(2)}) collective-permute-start(bf16[2,96,768]{2,1,0:T(8,128)(2,1)} %get-tuple-element.230.refs_3_), channel_id=1, source_target_pairs={{0,2},{1,3},{2,0},{3,1},{4,6},{5,7},{6,4},{7,5},{8,10},{9,11},{10,... | collective-permute-start | bytes 884744 | tf_op jit(solution)/shard_map/ppermute | solution.py:175
  27.1 28.3 %collective-permute-start.9 = (bf16[4,96,768]{2,1,0:T(8,128)(2,1)S(1)}, bf16[4,96,768]{2,1,0:T(8,128)(2,1)S(1)}, u32[]{:S(2)}, u32[]{:S(2)}) collective-permute-start(bf16[4,96,768]{2,1,0:T(8,128)(2,1)S(1)} %copy-done.75), channel_id=1, source_target_pairs={{0,1},{1,0},{2,3},{3,2},{4,5},{5,4},{6,7},{7,6},{8,9},{9,8},{10,11... | collective-permute-start | bytes 1769480 | tf_op jit(solution)/shard_map/ppermute | solution.py:175
  28.7 29.1 %collective-permute-start.8 = (bf16[4,96,768]{2,1,0:T(8,128)(2,1)S(1)}, bf16[4,96,768]{2,1,0:T(8,128)(2,1)S(1)}, u32[]{:S(2)}, u32[]{:S(2)}) collective-permute-start(bf16[4,96,768]{2,1,0:T(8,128)(2,1)S(1)} %get-tuple-element.239), channel_id=1, source_target_pairs={{0,4},{1,5},{2,6},{3,7},{4,0},{5,1},{6,2},{7,3},{8,12},{9,13},{10,... | collective-permute-start | bytes 1769480 | tf_op jit(solution)/shard_map/ppermute | solution.py:175
  79.8 31.3 %collective-permute-start.15 = (bf16[21,96,768]{2,1,0:T(8,128)(2,1)S(1)}, bf16[21,96,768]{2,1,0:T(8,128)(2,1)}, u32[]{:S(2)}, u32[]{:S(2)}) collective-permute-start(bf16[21,96,768]{2,1,0:T(8,128)(2,1)S(1)} %pack.8.refs_1_.refs_2_), channel_id=1, source_target_pairs={{0,8},{1,9},{2,10},{3,11},{4,12},{5,13},{6,14},{7,15},{8,0},{9,1},... | collective-permute-start | bytes 9289736 | tf_op jit(solution)/shard_map/ppermute | solution.py:175
  82.1 29.0 %collective-permute-start.12 = (bf16[8,96,768]{2,1,0:T(8,128)(2,1)}, bf16[8,96,768]{2,1,0:T(8,128)(2,1)}, u32[]{:S(2)}, u32[]{:S(2)}) collective-permute-start(bf16[8,96,768]{2,1,0:T(8,128)(2,1)} %get-tuple-element.249), channel_id=1, source_target_pairs={{0,16},{1,17},{2,18},{3,19},{4,20},{5,21},{6,22},{7,23},{8,24},{9,... | collective-permute-start | bytes 3538952 | tf_op jit(solution)/shard_map/ppermute | solution.py:175
  85.8 25.2 %collective-permute-start.13 = (bf16[7,96,768]{2,1,0:T(8,128)(2,1)}, bf16[7,96,768]{2,1,0:T(8,128)(2,1)}, u32[]{:S(2)}, u32[]{:S(2)}) collective-permute-start(bf16[7,96,768]{2,1,0:T(8,128)(2,1)} %copy-done.18), channel_id=1, source_target_pairs={{0,1},{1,0},{2,3},{3,2},{4,5},{5,4},{6,7},{7,6},{8,9},{9,8},{10,11... | collective-permute-start | bytes 3096584 | tf_op jit(solution)/shard_map/ppermute | solution.py:175
  124.7 33.1 %collective-permute-start.17 = (bf16[7,96,768]{2,1,0:T(8,128)(2,1)}, bf16[7,96,768]{2,1,0:T(8,128)(2,1)}, u32[]{:S(2)}, u32[]{:S(2)}) collective-permute-start(bf16[7,96,768]{2,1,0:T(8,128)(2,1)} %get-tuple-element.267), channel_id=1, source_target_pairs={{0,16},{1,17},{2,18},{3,19},{4,20},{5,21},{6,22},{7,23},{8,24},{9,... | collective-permute-start | bytes 3096584 | tf_op jit(solution)/shard_map/ppermute | solution.py:175
  125.9 31.9 %collective-permute-start.18 = (bf16[7,96,768]{2,1,0:T(8,128)(2,1)}, bf16[7,96,768]{2,1,0:T(8,128)(2,1)S(1)}, u32[]{:S(2)}, u32[]{:S(2)}) collective-permute-start(bf16[7,96,768]{2,1,0:T(8,128)(2,1)} %get-tuple-element.268), channel_id=1, source_target_pairs={{0,1},{1,0},{2,3},{3,2},{4,5},{5,4},{6,7},{7,6},{8,9},{9,8},{10,11... | collective-permute-start | bytes 3096584 | tf_op jit(solution)/shard_map/ppermute | solution.py:175
  128.7 29.1 %collective-permute-start.19 = (bf16[4,96,768]{2,1,0:T(8,128)(2,1)}, bf16[4,96,768]{2,1,0:T(8,128)(2,1)S(1)}, u32[]{:S(2)}, u32[]{:S(2)}) collective-permute-start(bf16[4,96,768]{2,1,0:T(8,128)(2,1)} %copy-done.21), channel_id=1, source_target_pairs={{0,4},{1,5},{2,6},{3,7},{4,0},{5,1},{6,2},{7,3},{8,12},{9,13},{10,... | collective-permute-start | bytes 1769480 | tf_op jit(solution)/shard_map/ppermute | solution.py:175
  162.1 39.6 %collective-permute-start.23 = (bf16[10,96,768]{2,1,0:T(8,128)(2,1)}, bf16[10,96,768]{2,1,0:T(8,128)(2,1)}, u32[]{:S(2)}, u32[]{:S(2)}) collective-permute-start(bf16[10,96,768]{2,1,0:T(8,128)(2,1)} %get-tuple-element.282), channel_id=1, source_target_pairs={{0,1},{1,0},{2,3},{3,2},{4,5},{5,4},{6,7},{7,6},{8,9},{9,8},{10,11... | collective-permute-start | bytes 4423688 | tf_op jit(solution)/shard_map/ppermute | solution.py:175
  163.6 38.1 %collective-permute-start.22 = (bf16[9,96,768]{2,1,0:T(8,128)(2,1)}, bf16[9,96,768]{2,1,0:T(8,128)(2,1)S(1)}, u32[]{:S(2)}, u32[]{:S(2)}) collective-permute-start(bf16[9,96,768]{2,1,0:T(8,128)(2,1)} %get-tuple-element.281), channel_id=1, source_target_pairs={{0,16},{1,17},{2,18},{3,19},{4,20},{5,21},{6,22},{7,23},{8,24},{9,... | collective-permute-start | bytes 3981320 | tf_op jit(solution)/shard_map/ppermute | solution.py:175
  202.9 35.1 %collective-permute-start.30 = (bf16[10,96,768]{2,1,0:T(8,128)(2,1)}, bf16[10,96,768]{2,1,0:T(8,128)(2,1)}, u32[]{:S(2)}, u32[]{:S(2)}) collective-permute-start(bf16[10,96,768]{2,1,0:T(8,128)(2,1)} %collective-permute-done.23.refs_0_.refs_3_), channel_id=1, source_target_pairs={{0,8},{1,9},{2,10},{3,11},{4,12},{5,13},{6,14},{7,15},{8,0},{9,1},... | collective-permute-start | bytes 4423688 | tf_op jit(solution)/shard_map/ppermute | solution.py:175
  339.0 52.2 %collective-permute-start.38 = (bf16[4,2,96,768]{3,2,1,0:T(8,128)(2,1)}, bf16[4,2,96,768]{3,2,1,0:T(8,128)(2,1)}, u32[]{:S(2)}, u32[]{:S(2)}) collective-permute-start(bf16[4,2,96,768]{3,2,1,0:T(8,128)(2,1)} %get-tuple-element.450), channel_id=1, source_target_pairs={{0,16},{1,17},{2,18},{3,19},{4,20},{5,21},{6,22},{7,23},{8,24},{9,... | collective-permute-start | bytes 3538952 | tf_op jit(solution)/shard_map/ppermute | solution.py:175
  340.2 51.0 %collective-permute-start.39 = (bf16[4,2,96,768]{3,2,1,0:T(8,128)(2,1)S(1)}, bf16[4,2,96,768]{3,2,1,0:T(8,128)(2,1)}, u32[]{:S(2)}, u32[]{:S(2)}) collective-permute-start(bf16[4,2,96,768]{3,2,1,0:T(8,128)(2,1)S(1)} %get-tuple-element.449), channel_id=1, source_target_pairs={{0,1},{1,0},{2,3},{3,2},{4,5},{5,4},{6,7},{7,6},{8,9},{9,8},{10,11... | collective-permute-start | bytes 3538952 | tf_op jit(solution)/shard_map/ppermute | solution.py:175
  343.0 48.2 %collective-permute-start.40 = (bf16[2,1,96,768]{3,2,0,1:T(8,128)(2,1)}, bf16[2,1,96,768]{3,2,0,1:T(8,128)(2,1)}, u32[]{:S(2)}, u32[]{:S(2)}) collective-permute-start(bf16[2,1,96,768]{3,2,0,1:T(8,128)(2,1)} %get-tuple-element.467), channel_id=1, source_target_pairs={{0,16},{1,17},{2,18},{3,19},{4,20},{5,21},{6,22},{7,23},{8,24},{9,... | collective-permute-start | bytes 884744 | tf_op jit(solution)/shard_map/ppermute | solution.py:175
  343.9 47.4 %collective-permute-start.41 = (bf16[2,1,96,768]{3,2,0,1:T(8,128)(2,1)S(1)}, bf16[2,1,96,768]{3,2,0,1:T(8,128)(2,1)}, u32[]{:S(2)}, u32[]{:S(2)}) collective-permute-start(bf16[2,1,96,768]{3,2,0,1:T(8,128)(2,1)S(1)} %get-tuple-element.466), channel_id=1, source_target_pairs={{0,1},{1,0},{2,3},{3,2},{4,5},{5,4},{6,7},{7,6},{8,9},{9,8},{10,11... | collective-permute-start | bytes 884744 | tf_op jit(solution)/shard_map/ppermute | solution.py:175
  391.2 23.2 %collective-permute-start.42 = (bf16[2,2,4,2,96,768]{5,4,3,2,1,0:T(8,128)(2,1)}, bf16[2,2,4,2,96,768]{5,4,3,2,1,0:T(8,128)(2,1)}, u32[]{:S(2)}, u32[]{:S(2)}) collective-permute-start(bf16[2,2,4,2,96,768]{5,4,3,2,1,0:T(8,128)(2,1)} %get-tuple-element.341), channel_id=1, source_target_pairs={{0,8},{1,9},{2,10},{3,11},{4,12},{5,13},{6,14},{7,15},{8,0},{9,1},... | collective-permute-start | bytes 14155784 | tf_op jit(solution)/shard_map/ppermute | solution.py:175
  397.6 34.8 %collective-permute-start.47 = (bf16[2,2,96,768]{3,2,1,0:T(8,128)(2,1)}, bf16[2,2,96,768]{3,2,1,0:T(8,128)(2,1)}, u32[]{:S(2)}, u32[]{:S(2)}) collective-permute-start(bf16[2,2,96,768]{3,2,1,0:T(8,128)(2,1)} %fusion.17), channel_id=1, source_target_pairs={{0,4},{1,5},{2,6},{3,7},{4,0},{5,1},{6,2},{7,3},{8,12},{9,13},{10,... | collective-permute-start | bytes 1769480 | tf_op jit(solution)/shard_map/ppermute | solution.py:175
  400.3 32.0 %collective-permute-start.45 = (bf16[4,1,96,768]{3,2,1,0:T(8,128)(2,1)}, bf16[4,1,96,768]{3,2,1,0:T(8,128)(2,1)S(1)}, u32[]{:S(2)}, u32[]{:S(2)}) collective-permute-start(bf16[4,1,96,768]{3,2,1,0:T(8,128)(2,1)} %get-tuple-element.454), channel_id=1, source_target_pairs={{0,16},{1,17},{2,18},{3,19},{4,20},{5,21},{6,22},{7,23},{8,24},{9,... | collective-permute-start | bytes 1769480 | tf_op jit(solution)/shard_map/ppermute | solution.py:175
  401.5 30.9 %collective-permute-start.46 = (bf16[4,1,96,768]{3,2,1,0:T(8,128)(2,1)}, bf16[4,1,96,768]{3,2,1,0:T(8,128)(2,1)S(1)}, u32[]{:S(2)}, u32[]{:S(2)}) collective-permute-start(bf16[4,1,96,768]{3,2,1,0:T(8,128)(2,1)} %get-tuple-element.453), channel_id=1, source_target_pairs={{0,1},{1,0},{2,3},{3,2},{4,5},{5,4},{6,7},{7,6},{8,9},{9,8},{10,11... | collective-permute-start | bytes 1769480 | tf_op jit(solution)/shard_map/ppermute | solution.py:175
  456.1 28.7 %collective-permute-start.48 = (bf16[4,2,96,768]{3,2,1,0:T(8,128)(2,1)}, bf16[4,2,96,768]{3,2,1,0:T(8,128)(2,1)}, u32[]{:S(2)}, u32[]{:S(2)}) collective-permute-start(bf16[4,2,96,768]{3,2,1,0:T(8,128)(2,1)} %get-tuple-element.448), channel_id=1, source_target_pairs={{0,16},{1,17},{2,18},{3,19},{4,20},{5,21},{6,22},{7,23},{8,24},{9,... | collective-permute-start | bytes 3538952 | tf_op jit(solution)/shard_map/ppermute | solution.py:175
  457.3 28.4 %collective-permute-start.49 = (bf16[4,2,96,768]{3,2,1,0:T(8,128)(2,1)}, bf16[4,2,96,768]{3,2,1,0:T(8,128)(2,1)}, u32[]{:S(2)}, u32[]{:S(2)}) collective-permute-start(bf16[4,2,96,768]{3,2,1,0:T(8,128)(2,1)} %get-tuple-element.447), channel_id=1, source_target_pairs={{0,1},{1,0},{2,3},{3,2},{4,5},{5,4},{6,7},{7,6},{8,9},{9,8},{10,11... | collective-permute-start | bytes 3538952 | tf_op jit(solution)/shard_map/ppermute | solution.py:175
  487.4 36.3 %collective-permute-start.59 = (bf16[2,2,96,768]{3,2,1,0:T(8,128)(2,1)S(1)}, bf16[2,2,96,768]{3,2,1,0:T(8,128)(2,1)S(1)}, u32[]{:S(2)}, u32[]{:S(2)}) collective-permute-start(bf16[2,2,96,768]{3,2,1,0:T(8,128)(2,1)S(1)} %fusion.12), channel_id=1, source_target_pairs={{0,4},{1,5},{2,6},{3,7},{4,0},{5,1},{6,2},{7,3},{8,12},{9,13},{10,... | collective-permute-start | bytes 1769480 | tf_op jit(solution)/shard_map/ppermute | solution.py:175
  513.6 22.1 %collective-permute-start.65 = (bf16[3,96,768]{2,1,0:T(8,128)(2,1)}, bf16[3,96,768]{2,1,0:T(8,128)(2,1)}, u32[]{:S(2)}, u32[]{:S(2)}) collective-permute-start(bf16[3,96,768]{2,1,0:T(8,128)(2,1)} %get-tuple-element.400), channel_id=1, source_target_pairs={{0,16},{1,17},{2,18},{3,19},{4,20},{5,21},{6,22},{7,23},{8,24},{9,... | collective-permute-start | bytes 1327112 | tf_op jit(solution)/shard_map/ppermute | solution.py:175
  (128 other events, 1462.8 us)

commit v10 on v9

--- a/solution.py
+++ b/solution.py
@@ -1644,21 +1644,21 @@
     return (swap_x(payloads[0]), swap_y(payloads[1]))
 
 
-def z_pair(values, half):
-    return add_low(*(lax.dynamic_slice_in_dim(value, 2 * half, 2, 0) for value in values))
+def z_half(value, half):
+    if value.ndim == 4:
+        return lax.dynamic_slice_in_dim(value, 2 * half, 2, 0)
+    part = lax.dynamic_slice(value, (0, 0, 2 * half, 0, 0, 0), (1, 1, 2) + value.shape[3:])
+    return part[0, 0]
 
 
 def far_payload(keep, get, sides, place):
-    return z_pair((keep[0, 0], get[0, 0]) + tuple(sides), 1 - place[2] // 2)
+    half = 1 - place[2] // 2
+    return add_low(*(z_half(value, half) for value in (keep, get) + tuple(sides)))
 
 
 def own_pair(keep, get, sides, far, place):
     half = place[2] // 2
-    pair = (
-        lax.dynamic_slice_in_dim(value, 2 * half, 2, 0)
-        for value in (keep[0, 0], get[0, 0]) + tuple(sides)
-    )
-    return add_low(*pair, far)
+    return add_low(*(z_half(value, half) for value in (keep, get) + tuple(sides)), far)
 
 
 def pick(pair, index):
@@ -1762,7 +1762,7 @@
         (
             [(0, 0, 2), (1, 0, 3), (2, 0, 3), (3, 0, 3), (4, 0, 4), (5, 0, 2), (6, 0, 4)],
         ),
-        after((plane_a0, col_a0, x0, y0, plane_f0, near_f0, far_f0), far_a1),
+        after((plane_a0, col_a0, x0, y0, plane_f0, near_f0, far_f0), to_x1),
     )
     theirs_0 = swap_core(mine_0)
     small_four = jnp.stack([small_pair, small_near])
@@ -1876,10 +1876,11 @@
         ],
         axis=1,
     )
-    pair_f1 = own_pair(keep_f1, get_f1, sides_rf1, after(zfar_f1, get_a0), place_parts)
+    pair_f1 = own_pair(keep_f1, get_f1, sides_rf1, zfar_f1, place_parts)
     znear_f1 = reduce_near(pair_f1, place_parts)
-    sides_rf0, get_a0, zfar_a1, znear_f1, small_sum = join(
-        sides_rf0, get_a0, zfar_a1, znear_f1, small_sum
+    small_c = swap_core(small_sum)
+    sides_rf0, get_a0, zfar_a1, znear_f1, small_c = join(
+        sides_rf0, get_a0, zfar_a1, znear_f1, small_c
     )
     payload_f0 = far_payload(keep_f0, get_f0, sides_rf0, place_parts)
     zfar_f0 = swap_z(payload_f0, 2)
@@ -1887,8 +1888,9 @@
     pair_a1 = own_pair(keep_a1, get_a1, sides_ra1, zfar_a1, place_parts)
     znear_a1 = reduce_near(after(pair_a1, payload_f0), place_parts)
     content_grad, query_grad = input_back(after(dq0, sides_rf0), dk0, dv0, attn0, dresid0)
-    small_c = swap_core(after(small_sum, payload_f0))
-    by_a0, content_grad, znear_a1, small_c = join(by_a0, content_grad, znear_a1, small_c)
+    small_sum = after(small_sum, payload_f0) + small_c
+    small_y = swap_y(small_sum)
+    by_a0, content_grad, znear_a1, small_y = join(by_a0, content_grad, znear_a1, small_y)
     payloads_a0 = side_payloads(keep_a0, get_a0, by_a0)
     sides_ra0 = reduce_sides(payloads_a0)
     own_1 = jnp.concatenate(
@@ -1898,14 +1900,14 @@
         ]
     )
     across_1 = swap_x(after(own_1, payloads_a0))
-    small_sum = after(small_sum, payloads_a0) + small_c
-    small_y = swap_y(small_sum)
-    sides_ra0, zfar_f0, small_y = join(sides_ra0, zfar_f0, small_y)
+    small_sum = after(small_sum, payloads_a0) + small_y
+    small_x = swap_x(small_sum)
+    sides_ra0, zfar_f0, small_x = join(sides_ra0, zfar_f0, small_x)
     column_a0 = add_low(keep_a0[0, 0], get_a0[0, 0], *sides_ra0)
     shifts_a0 = reduce_direct(column_a0, place_parts)
     pair_f0 = own_pair(keep_f0, get_f0, sides_rf0, zfar_f0, place_parts)
     znear_f0 = reduce_near(after(pair_f0, column_a0), place_parts)
-    small_sum = after(small_sum, column_a0) + small_y
+    small_sum = after(small_sum, column_a0) + small_x
     small_z = swap_z(small_sum, 1)
     shifts_a0, znear_f0, across_1, small_z = join(shifts_a0, znear_f0, across_1, small_z)
     own_0 = jnp.concatenate(
@@ -1926,9 +1928,7 @@
     across_0, new_1, small_z = join(across_0, new_1, small_z)
     four_0 = share_core(jnp.stack([own_0, across_0]), place_parts)
     small_sum = small_sum + small_z
-    small_x = swap_x(small_sum)
     new_0 = adam(0, state, four_0, tuple(new_1))
-    small_sum = small_sum + small_x
     size = small_master.shape[1]
     small_own = lax.dynamic_slice_in_dim(small_sum, lax.axis_index("fsdp") * size, size, 1)
     small_new = adam_update(small_master, small_first, small_second, small_own, SMALL_RATE)

time: 593 us -> 562 us (0.948)
  waiting for transfers between devices: 103 us -> 84.1 us
  local copies, waits for them, and re-layouts: 49.8 us -> 37.1 us
    ppermute x72, waiting for transfers between devices: 103 us -> 84.1 us  [move(): return lax.ppermute(value, AXES, pairs)]
    slice x6 -> x0, local copies, waits for them, and re-layouts: 9.29 us -> none  [far_payload(): return z_pair((keep[0, 0], get[0, 0]) + tuple(sides), 1 - place[2] // 2)]
    unnamed x164 -> x130, local copies, waits for them, and re-layouts: 17.5 us -> 13.1 us
  transfers between devices with their start and end apart: 72 -> 72, of which waited for: 23 -> 21; matrix products, arithmetic and copies ran while one was open for 13% -> 12% of each run, Pallas kernels for 36% -> 39%
where the time goes in v10:
time: 562 us; the launch traced here: 554 us
  Pallas kernels  306 us (54%)
  waiting for transfers between devices  84.1 us (15%)
  starting transfers between devices  69.1 us (12%)
  other arithmetic  54.6 us (10%)
  local copies, waits for them, and re-layouts  37.1 us (7%)
    ppermute x72, waiting for transfers between devices, move(): return lax.ppermute(value, AXES, pairs)  84.1 us
    ppermute x72, starting transfers between devices, move(): return lax.ppermute(value, AXES, pairs)  69.1 us
    pallas_call x1, Pallas kernels, turn(): pl.pallas_call(partial(turn_kernel, plan), out_shape=[half_low, half_low]...  55.5 us
    pallas_call x4, Pallas kernels, mix_back(): pl.pallas_call(mix_back_kernel, grid=(H // 4,), out_shape=[jax.ShapeDtype...  50 us
    pallas_call x1, Pallas kernels, down(): pl.pallas_call(partial(down_kernel, plan), out_shape=BACK_SHAPES, in_spec...  45.9 us
    pallas_call x2, Pallas kernels, mix(): pl.pallas_call(mix_kernel, grid=(H // 2,), out_shape=[jax.ShapeDtypeStruc...  36.5 us
    convert_element_type x19, other arithmetic, add_low(): return total.astype(jnp.bfloat16)  34.6 us
    pallas_call x1, Pallas kernels, feed(): pl.pallas_call(partial(feed_kernel, plan), out_shape=[tall, jax.ShapeDtyp...  34.4 us
  transfers between devices with their start and end apart: 72, of which 21 were waited for; matrix products, arithmetic and copies ran while one was open for 12% of the time, Pallas kernels for 39%

profile of v10, /device:TPU:0, one launch (start us, length us, event | category | flops | bytes accessed | tf_op | source)
XLA Modules:
  0.0 554.3 jit_solution(3168110129586738821)
XLA Ops:
  13.1 5.7 %cast_rest.1 = (bf16[4,96,768]{2,1,0:T(8,128)(2,1)}, bf16[4,96,768]{2,1,0:T(8,128)(2,1)}, bf16[96,3072]{1,0:T(8,128)(2,1)}, bf16[96,3072]{1,0:T(8,128)(2,1)}, bf...) custom-call(s32[4]{0:T(128)} %pad_add_fusion.place_ref, ...), custom_call_target="tpu_custom_call" | custom-call | flops 10000000 | bytes 12000000 | tf_op jit(solution)/shard_map/cast_rest/pallas_call | solution.py:368
  35.8 10.4 %collective-permute-done.11 = bf16[2,2,1200]{2,1,0:T(2,128)(2,1)S(1)} collective-permute-done((bf16[2,2,1200]{2,1,0:T(2,128)(2,1)S(1)}, bf16[2,2,1200]{2,1,0:T(2,128)(2,1)S(1)}, u32[]{:S(2)}, u32[]{:S(2)}) %collective-permute-start.11) | collective-permute-done | bytes 9632 | tf_op jit(solution)/shard_map/ppermute | solution.py:175
  46.6 7.6 %collective-permute-done.10.refs_5_.refs_0_ = bf16[3,96,768]{2,1,0:T(8,128)(2,1)S(1)} collective-permute-done((bf16[3,96,768]{2,1,0:T(8,128)(2,1)S(1)}, bf16[3,96,768]{2,1,0:T(8,128)(2,1)S(1)}, u32[]{:S(2)}, u32[]{:S(2)}) %collective-permute-start.10) | collective-permute-done | bytes 442400 | tf_op jit(solution)/shard_map/ppermute | solution.py:175
  87.8 8.4 %collective-permute-done.13.refs_2_.refs_3_.refs_4_ = bf16[7,96,768]{2,1,0:T(8,128)(2,1)} collective-permute-done((bf16[7,96,768]{2,1,0:T(8,128)(2,1)}, bf16[7,96,768]{2,1,0:T(8,128)(2,1)}, u32[]{:S(2)}, u32[]{:S(2)}) %collective-permute-start.13) | collective-permute-done | bytes 1032224 | tf_op jit(solution)/shard_map/ppermute | solution.py:175
  114.9 7.5 %project.2 = (bf16[1024,768]{1,0:T(8,128)(2,1)}, bf16[512,768]{1,0:T(8,128)(2,1)}, bf16[512,768]{1,0:T(8,128)(2,1)}, bf16[4,768,768]{2,1,0:T(8,128)(2,1)}) custom-call(s32[4]{0:T(128)} %pad_add_fusion.place_ref, f32[8,768]{1,0:T(8,128)} %reshape.500.small_ref.below_ref, bf16[1024,768]{1,0:T(8,128)(2,1)} %pad_maximum_fusion.low_any.hidden_any, ...), custom_call_target="tpu_custom_call" | custom-call | flops 2415919104 | bytes 16000000 | tf_op jit(solution)/shard_map/project/pallas_call | solution.py:422
  122.4 18.3 %mix.2 = (bf16[1024,768]{1,0:T(8,128)(2,1)}, bf16[12,512,1024]{2,1,0:T(8,128)(2,1)}, f32[12,1,1024]{2,1,0:T(1,128)}, f32[1,1024]{1,0:T(1,128)}) custom-call(s32[1]{0:T(128)S(6)} %copy.164.length_ref, f32[12,2]{1,0:T(8,128)} %pad_maximum_fusion.11.far_ref, bf16[1024,768]{1,0:T(8,128)(2,1)} %get-tuple-element.351.q_ref, ...), custom_call_target="tpu_custom_call" | custom-call | flops 6499999744 | bytes 8000000 | tf_op jit(solution)/shard_map/mix/pallas_call | solution.py:557
  151.3 34.4 %feed.1 = (f32[1024,768]{1,0:T(8,128)}, bf16[4,1024,768]{2,1,0:T(8,128)(2,1)}, bf16[1024,768]{1,0:T(8,128)(2,1)}, bf16[1024,768]{1,0:T(8,128)(2,1)}, f32[1024,768]{1,0:T(8,128)}) custom-call(s32[4]{0:T(128)} %pad_add_fusion.place_ref, f32[8,768]{1,0:T(8,128)} %reshape.500.small_ref.below_ref, f32[1,3072]{1,0:T(1,128)} %slice.251.hidden_bias_ref, ...), custom_call_target="tpu_custom_call" | custom-call | flops 10871635968 | bytes 30000000 | tf_op jit(solution)/shard_map/feed/pallas_call | solution.py:791
  191.6 7.6 %project.3 = (bf16[1024,768]{1,0:T(8,128)(2,1)}, bf16[512,768]{1,0:T(8,128)(2,1)}, bf16[512,768]{1,0:T(8,128)(2,1)}, bf16[4,768,768]{2,1,0:T(8,128)(2,1)}) custom-call(s32[4]{0:T(128)} %pad_add_fusion.place_ref, f32[8,768]{1,0:T(8,128)} %reshape.499.small_ref, bf16[1024,768]{1,0:T(8,128)(2,1)} %get-tuple-element.326.low_any, ...), custom_call_target="tpu_custom_call" | custom-call | flops 2415919104 | bytes 16000000 | tf_op jit(solution)/shard_map/project/pallas_call | solution.py:422
  203.1 18.2 %mix.3 = (bf16[1024,768]{1,0:T(8,128)(2,1)}, bf16[12,512,1024]{2,1,0:T(8,128)(2,1)}, f32[12,1,1024]{2,1,0:T(1,128)}, f32[1,1024]{1,0:T(1,128)}) custom-call(s32[1]{0:T(128)S(6)} %copy.164.length_ref, f32[12,2]{1,0:T(8,128)} %pad_maximum_fusion.10.far_ref, bf16[1024,768]{1,0:T(8,128)(2,1)} %get-tuple-element.317.q_ref, ...), custom_call_target="tpu_custom_call" | custom-call | flops 6499999744 | bytes 8000000 | tf_op jit(solution)/shard_map/mix/pallas_call | solution.py:557
  222.6 55.5 %turn.1 = (bf16[512,768]{1,0:T(8,128)(2,1)}, bf16[512,768]{1,0:T(8,128)(2,1)}, f32[1024,768]{1,0:T(8,128)}, bf16[1024,768]{1,0:T(8,128)(2,1)}, bf16[768,768]{1,0...) custom-call(s32[4]{0:T(128)} %pad_add_fusion.place_ref, ...), custom_call_target="tpu_custom_call" | custom-call | flops 32614907904 | bytes 60000000 | tf_op jit(solution)/shard_map/turn/pallas_call | solution.py:982
  278.6 12.3 %mix_back.4 = (bf16[1024,768]{1,0:T(8,128)(2,1)}, bf16[512,768]{1,0:T(8,128)(2,1)}, bf16[512,768]{1,0:T(8,128)(2,1)}, f32[6,1,768]{2,1,0:T(1,128)}) custom-call(bf16[1024,768]{1,0:T(8,128)(2,1)} %get-tuple-element.317.q_ref, bf16[512,768]{1,0:T(8,128)(2,1)} %get-tuple-element.298.k_ref, bf16[512,768]{1,0:T(8,128)(2,1)} %get-tuple-element.299.v_ref, ...), custom_call_target="tpu_custom_call" | custom-call | flops 8000000000 | bytes 16000000 | tf_op jit(solution)/shard_map/mix_back/pallas_call | solution.py:658
  295.1 12.7 %mix_back.5 = (bf16[1024,768]{1,0:T(8,128)(2,1)}, bf16[512,768]{1,0:T(8,128)(2,1)}, bf16[512,768]{1,0:T(8,128)(2,1)}, f32[6,1,768]{2,1,0:T(1,128)}) custom-call(bf16[1024,768]{1,0:T(8,128)(2,1)} %get-tuple-element.317.q_ref, bf16[512,768]{1,0:T(8,128)(2,1)} %get-tuple-element.298.k_ref, ...), custom_call_target="tpu_custom_call", output_to_operand_aliasing={{0}: (8, {}), {1}: (9, {}), {2}: (10, {})} | custom-call | flops 8000000000 | bytes 16000000 | tf_op jit(solution)/shard_map/mix_back/pallas_call | solution.py:658
  309.6 8.8 %weight_back.2 = (bf16[2,2,4,1,96,768]{5,4,3,2,1,0:T(8,128)(2,1)}, bf16[2,2,4,1,96,768]{5,4,3,2,1,0:T(8,128)(2,1)}, f32[2,768]{1,0:T(2,128)}) custom-call(s32[4]{0:T(128)} %pad_add_fusion.place_ref, bf16[1024,768]{1,0:T(8,128)(2,1)} %get-tuple-element.326.low_any, bf16[1024,768]{1,0:T(8,128)(2,1)} %get-tuple-element.321.dq_any, ...), custom_call_target="tpu_custom_call" | custom-call | flops 2415919104 | bytes 12000000 | tf_op jit(solution)/shard_map/weight_back/pallas_call | solution.py:1135
  328.7 45.9 %down.1 = (f32[1024,768]{1,0:T(8,128)}, bf16[1024,768]{1,0:T(8,128)(2,1)}, bf16[768,768]{1,0:T(8,128)(2,1)}, bf16[2,2,4,2,96,768]{5,4,3,2,1,0:T(8,128)(2,1)}, bf...) custom-call(s32[4]{0:T(128)} %pad_add_fusion.place_ref, ...), custom_call_target="tpu_custom_call" | custom-call | flops 27179089920 | bytes 60000000 | tf_op jit(solution)/shard_map/down/pallas_call | solution.py:1068
  382.7 12.4 %mix_back.6 = (bf16[1024,768]{1,0:T(8,128)(2,1)}, bf16[512,768]{1,0:T(8,128)(2,1)}, bf16[512,768]{1,0:T(8,128)(2,1)}, f32[6,1,768]{2,1,0:T(1,128)}) custom-call(bf16[1024,768]{1,0:T(8,128)(2,1)} %get-tuple-element.351.q_ref, bf16[512,768]{1,0:T(8,128)(2,1)} %get-tuple-element.273.k_ref, bf16[512,768]{1,0:T(8,128)(2,1)} %get-tuple-element.274.v_ref, ...), custom_call_target="tpu_custom_call" | custom-call | flops 8000000000 | bytes 16000000 | tf_op jit(solution)/shard_map/mix_back/pallas_call | solution.py:658
  401.1 12.5 %mix_back.7 = (bf16[1024,768]{1,0:T(8,128)(2,1)}, bf16[512,768]{1,0:T(8,128)(2,1)}, bf16[512,768]{1,0:T(8,128)(2,1)}, f32[6,1,768]{2,1,0:T(1,128)}) custom-call(bf16[1024,768]{1,0:T(8,128)(2,1)} %get-tuple-element.351.q_ref, bf16[512,768]{1,0:T(8,128)(2,1)} %get-tuple-element.273.k_ref, ...), custom_call_target="tpu_custom_call", output_to_operand_aliasing={{0}: (8, {}), {1}: (9, {}), {2}: (10, {})} | custom-call | flops 8000000000 | bytes 16000000 | tf_op jit(solution)/shard_map/mix_back/pallas_call | solution.py:658
  419.1 8.9 %weight_back.3 = (bf16[2,2,4,1,96,768]{5,4,3,2,1,0:T(8,128)(2,1)}, bf16[2,2,4,1,96,768]{5,4,3,2,1,0:T(8,128)(2,1)}, f32[2,768]{1,0:T(2,128)}) custom-call(s32[4]{0:T(128)} %pad_add_fusion.place_ref, bf16[1024,768]{1,0:T(8,128)(2,1)} %pad_maximum_fusion.low_any.hidden_any, bf16[1024,768]{1,0:T(8,128)(2,1)} %get-tuple-element.379.dq_any, ...), custom_call_target="tpu_custom_call" | custom-call | flops 2415919104 | bytes 12000000 | tf_op jit(solution)/shard_map/weight_back/pallas_call | solution.py:1135
  438.7 8.9 %collective-permute-done.52 = bf16[2,96,768]{2,1,0:T(8,128)(2,1)S(1)} collective-permute-done((bf16[2,96,768]{2,1,0:T(8,128)(2,1)}, bf16[2,96,768]{2,1,0:T(8,128)(2,1)S(1)}, u32[]{:S(2)}, u32[]{:S(2)}) %collective-permute-start.52) | collective-permute-done | bytes 294944 | tf_op jit(solution)/shard_map/ppermute | solution.py:175
  447.6 7.5 %collective-permute-done.51 = bf16[2,1,96,768]{3,2,1,0:T(8,128)(2,1)} collective-permute-done((bf16[2,1,96,768]{3,2,1,0:T(8,128)(2,1)}, bf16[2,1,96,768]{3,2,1,0:T(8,128)(2,1)}, u32[]{:S(2)}, u32[]{:S(2)}) %collective-permute-start.51) | collective-permute-done | bytes 294944 | tf_op jit(solution)/shard_map/ppermute | solution.py:175
  470.0 7.9 %input_back.1 = (f32[512,768]{1,0:T(8,128)}, f32[512,768]{1,0:T(8,128)}) custom-call(bf16[1024,768]{1,0:T(8,128)(2,1)} %get-tuple-element.379.dq_any, bf16[512,768]{1,0:T(8,128)(2,1)} %get-tuple-element.361.dk_any, bf16[512,768]{1,0:T(8,128)(2,1)} %get-tuple-element.362.dv_any, bf16[4,768,768]{2,1,0:T(8,128)(2,1)} %get-tuple-element.283.attn_any.w_any, ...), custom_call_target="tpu_custom_call" | custom-call | flops 2415919104 | bytes 16000000 | tf_op jit(solution)/shard_map/input_back/pallas_call | solution.py:1184
  485.6 12.0 %collective-permute-done.61 = f32[2,9600]{1,0:T(2,128)S(1)} collective-permute-done((f32[2,9600]{1,0:T(2,128)S(1)}, f32[2,9600]{1,0:T(2,128)S(1)}, u32[]{:S(2)}, u32[]{:S(2)}) %collective-permute-start.61) | collective-permute-done | bytes 76832 | tf_op jit(solution)/shard_map/ppermute | solution.py:175
  510.3 6.7 %collective-permute-done.67 = f32[2,9600]{1,0:T(2,128)S(1)} collective-permute-done((f32[2,9600]{1,0:T(2,128)S(1)}, f32[2,9600]{1,0:T(2,128)S(1)}, u32[]{:S(2)}, u32[]{:S(2)}) %collective-permute-start.67) | collective-permute-done | bytes 76832 | tf_op jit(solution)/shard_map/ppermute | solution.py:175
  526.2 11.6 %adam.2 = (f32[2,4,96,768]{3,2,1,0:T(8,128)}, f32[2,4,96,768]{3,2,1,0:T(8,128)}, f32[2,4,96,768]{3,2,1,0:T(8,128)}, f32[2,96,3072]{2,1,0:T(8,128)}, f32[2,96,307...) custom-call(f32[2,4,96,768]{3,2,1,0:T(8,128)} %refs_0_.3, ...), custom_call_target="tpu_custom_call" | custom-call | flops 20000000 | bytes 22000000 | tf_op jit(solution)/shard_map/adam/pallas_call | solution.py:1262
  542.4 11.6 %adam.3 = (f32[2,4,96,768]{3,2,1,0:T(8,128)}, f32[2,4,96,768]{3,2,1,0:T(8,128)}, f32[2,4,96,768]{3,2,1,0:T(8,128)}, f32[2,96,3072]{2,1,0:T(8,128)}, f32[2,96,307...) custom-call(f32[2,4,96,768]{3,2,1,0:T(8,128)} %refs_0_.3, ...), custom_call_target="tpu_custom_call", output_to_operand_aliasing={{0}: (12, {}), {1}: (13, {}), {2}: (14, {}), {3}: (15, {}),... | custom-call | flops 20000000 | bytes 22000000 | tf_op jit(solution)/shard_map/adam/pallas_call | solution.py:1262
  (365 shorter events, 198.3 us)
Async XLA Ops:
  4.3 22.1 %collective-permute-start.4 = (bf16[2,96,768]{2,1,0:T(8,128)(2,1)}, bf16[2,96,768]{2,1,0:T(8,128)(2,1)S(1)}, u32[]{:S(2)}, u32[]{:S(2)}) collective-permute-start(bf16[2,96,768]{2,1,0:T(8,128)(2,1)} %get-tuple-element.229.refs_3_), channel_id=1, source_target_pairs={{0,2},{1,3},{2,0},{3,1},{4,6},{5,7},{6,4},{7,5},{8,10},{9,11},{10,... | collective-permute-start | bytes 884744 | tf_op jit(solution)/shard_map/ppermute | solution.py:175
  27.2 28.4 %collective-permute-start.9 = (bf16[4,96,768]{2,1,0:T(8,128)(2,1)S(1)}, bf16[4,96,768]{2,1,0:T(8,128)(2,1)S(1)}, u32[]{:S(2)}, u32[]{:S(2)}) collective-permute-start(bf16[4,96,768]{2,1,0:T(8,128)(2,1)S(1)} %copy-done.58), channel_id=1, source_target_pairs={{0,1},{1,0},{2,3},{3,2},{4,5},{5,4},{6,7},{7,6},{8,9},{9,8},{10,11... | collective-permute-start | bytes 1769480 | tf_op jit(solution)/shard_map/ppermute | solution.py:175
  28.8 29.1 %collective-permute-start.8 = (bf16[4,96,768]{2,1,0:T(8,128)(2,1)S(1)}, bf16[4,96,768]{2,1,0:T(8,128)(2,1)S(1)}, u32[]{:S(2)}, u32[]{:S(2)}) collective-permute-start(bf16[4,96,768]{2,1,0:T(8,128)(2,1)S(1)} %get-tuple-element.238), channel_id=1, source_target_pairs={{0,4},{1,5},{2,6},{3,7},{4,0},{5,1},{6,2},{7,3},{8,12},{9,13},{10,... | collective-permute-start | bytes 1769480 | tf_op jit(solution)/shard_map/ppermute | solution.py:175
  64.0 32.1 %collective-permute-start.15 = (bf16[21,96,768]{2,1,0:T(8,128)(2,1)S(1)}, bf16[21,96,768]{2,1,0:T(8,128)(2,1)}, u32[]{:S(2)}, u32[]{:S(2)}) collective-permute-start(bf16[21,96,768]{2,1,0:T(8,128)(2,1)S(1)} %pack.8.refs_1_.refs_2_), channel_id=1, source_target_pairs={{0,8},{1,9},{2,10},{3,11},{4,12},{5,13},{6,14},{7,15},{8,0},{9,1},... | collective-permute-start | bytes 9289736 | tf_op jit(solution)/shard_map/ppermute | solution.py:175
  65.6 30.5 %collective-permute-start.12 = (bf16[8,96,768]{2,1,0:T(8,128)(2,1)}, bf16[8,96,768]{2,1,0:T(8,128)(2,1)}, u32[]{:S(2)}, u32[]{:S(2)}) collective-permute-start(bf16[8,96,768]{2,1,0:T(8,128)(2,1)} %get-tuple-element.248), channel_id=1, source_target_pairs={{0,16},{1,17},{2,18},{3,19},{4,20},{5,21},{6,22},{7,23},{8,24},{9,... | collective-permute-start | bytes 3538952 | tf_op jit(solution)/shard_map/ppermute | solution.py:175
  71.5 24.6 %collective-permute-start.13 = (bf16[7,96,768]{2,1,0:T(8,128)(2,1)}, bf16[7,96,768]{2,1,0:T(8,128)(2,1)}, u32[]{:S(2)}, u32[]{:S(2)}) collective-permute-start(bf16[7,96,768]{2,1,0:T(8,128)(2,1)} %copy-done.16), channel_id=1, source_target_pairs={{0,1},{1,0},{2,3},{3,2},{4,5},{5,4},{6,7},{7,6},{8,9},{9,8},{10,11... | collective-permute-start | bytes 3096584 | tf_op jit(solution)/shard_map/ppermute | solution.py:175
  109.4 31.8 %collective-permute-start.17 = (bf16[7,96,768]{2,1,0:T(8,128)(2,1)}, bf16[7,96,768]{2,1,0:T(8,128)(2,1)}, u32[]{:S(2)}, u32[]{:S(2)}) collective-permute-start(bf16[7,96,768]{2,1,0:T(8,128)(2,1)} %get-tuple-element.266), channel_id=1, source_target_pairs={{0,16},{1,17},{2,18},{3,19},{4,20},{5,21},{6,22},{7,23},{8,24},{9,... | collective-permute-start | bytes 3096584 | tf_op jit(solution)/shard_map/ppermute | solution.py:175
  110.0 31.3 %collective-permute-start.18 = (bf16[7,96,768]{2,1,0:T(8,128)(2,1)}, bf16[7,96,768]{2,1,0:T(8,128)(2,1)S(1)}, u32[]{:S(2)}, u32[]{:S(2)}) collective-permute-start(bf16[7,96,768]{2,1,0:T(8,128)(2,1)} %get-tuple-element.267), channel_id=1, source_target_pairs={{0,1},{1,0},{2,3},{3,2},{4,5},{5,4},{6,7},{7,6},{8,9},{9,8},{10,11... | collective-permute-start | bytes 3096584 | tf_op jit(solution)/shard_map/ppermute | solution.py:175
  112.8 28.5 %collective-permute-start.19 = (bf16[4,96,768]{2,1,0:T(8,128)(2,1)}, bf16[4,96,768]{2,1,0:T(8,128)(2,1)S(1)}, u32[]{:S(2)}, u32[]{:S(2)}) collective-permute-start(bf16[4,96,768]{2,1,0:T(8,128)(2,1)} %copy-done.19), channel_id=1, source_target_pairs={{0,4},{1,5},{2,6},{3,7},{4,0},{5,1},{6,2},{7,3},{8,12},{9,13},{10,... | collective-permute-start | bytes 1769480 | tf_op jit(solution)/shard_map/ppermute | solution.py:175
  145.6 40.1 %collective-permute-start.23 = (bf16[10,96,768]{2,1,0:T(8,128)(2,1)}, bf16[10,96,768]{2,1,0:T(8,128)(2,1)}, u32[]{:S(2)}, u32[]{:S(2)}) collective-permute-start(bf16[10,96,768]{2,1,0:T(8,128)(2,1)} %get-tuple-element.281), channel_id=1, source_target_pairs={{0,1},{1,0},{2,3},{3,2},{4,5},{5,4},{6,7},{7,6},{8,9},{9,8},{10,11... | collective-permute-start | bytes 4423688 | tf_op jit(solution)/shard_map/ppermute | solution.py:175
  147.2 38.6 %collective-permute-start.22 = (bf16[9,96,768]{2,1,0:T(8,128)(2,1)}, bf16[9,96,768]{2,1,0:T(8,128)(2,1)S(1)}, u32[]{:S(2)}, u32[]{:S(2)}) collective-permute-start(bf16[9,96,768]{2,1,0:T(8,128)(2,1)} %get-tuple-element.280), channel_id=1, source_target_pairs={{0,16},{1,17},{2,18},{3,19},{4,20},{5,21},{6,22},{7,23},{8,24},{9,... | collective-permute-start | bytes 3981320 | tf_op jit(solution)/shard_map/ppermute | solution.py:175
  186.9 34.4 %collective-permute-start.30 = (bf16[10,96,768]{2,1,0:T(8,128)(2,1)}, bf16[10,96,768]{2,1,0:T(8,128)(2,1)}, u32[]{:S(2)}, u32[]{:S(2)}) collective-permute-start(bf16[10,96,768]{2,1,0:T(8,128)(2,1)} %collective-permute-done.23.refs_0_.refs_3_), channel_id=1, source_target_pairs={{0,8},{1,9},{2,10},{3,11},{4,12},{5,13},{6,14},{7,15},{8,0},{9,1},... | collective-permute-start | bytes 4423688 | tf_op jit(solution)/shard_map/ppermute | solution.py:175
  323.2 51.4 %collective-permute-start.38 = (bf16[4,2,96,768]{3,2,1,0:T(8,128)(2,1)}, bf16[4,2,96,768]{3,2,1,0:T(8,128)(2,1)}, u32[]{:S(2)}, u32[]{:S(2)}) collective-permute-start(bf16[4,2,96,768]{3,2,1,0:T(8,128)(2,1)} %get-tuple-element.448), channel_id=1, source_target_pairs={{0,16},{1,17},{2,18},{3,19},{4,20},{5,21},{6,22},{7,23},{8,24},{9,... | collective-permute-start | bytes 3538952 | tf_op jit(solution)/shard_map/ppermute | solution.py:175
  323.7 51.0 %collective-permute-start.39 = (bf16[4,2,96,768]{3,2,1,0:T(8,128)(2,1)S(1)}, bf16[4,2,96,768]{3,2,1,0:T(8,128)(2,1)}, u32[]{:S(2)}, u32[]{:S(2)}) collective-permute-start(bf16[4,2,96,768]{3,2,1,0:T(8,128)(2,1)S(1)} %get-tuple-element.447), channel_id=1, source_target_pairs={{0,1},{1,0},{2,3},{3,2},{4,5},{5,4},{6,7},{7,6},{8,9},{9,8},{10,11... | collective-permute-start | bytes 3538952 | tf_op jit(solution)/shard_map/ppermute | solution.py:175
  325.7 49.0 %collective-permute-start.40 = (bf16[2,1,96,768]{3,2,0,1:T(8,128)(2,1)}, bf16[2,1,96,768]{3,2,0,1:T(8,128)(2,1)}, u32[]{:S(2)}, u32[]{:S(2)}) collective-permute-start(bf16[2,1,96,768]{3,2,0,1:T(8,128)(2,1)} %get-tuple-element.465), channel_id=1, source_target_pairs={{0,16},{1,17},{2,18},{3,19},{4,20},{5,21},{6,22},{7,23},{8,24},{9,... | collective-permute-start | bytes 884744 | tf_op jit(solution)/shard_map/ppermute | solution.py:175
  327.2 47.4 %collective-permute-start.41 = (bf16[2,1,96,768]{3,2,0,1:T(8,128)(2,1)S(1)}, bf16[2,1,96,768]{3,2,0,1:T(8,128)(2,1)}, u32[]{:S(2)}, u32[]{:S(2)}) collective-permute-start(bf16[2,1,96,768]{3,2,0,1:T(8,128)(2,1)S(1)} %get-tuple-element.464), channel_id=1, source_target_pairs={{0,1},{1,0},{2,3},{3,2},{4,5},{5,4},{6,7},{7,6},{8,9},{9,8},{10,11... | collective-permute-start | bytes 884744 | tf_op jit(solution)/shard_map/ppermute | solution.py:175
  378.2 35.4 %collective-permute-start.47 = (bf16[2,2,96,768]{3,2,1,0:T(8,128)(2,1)}, bf16[2,2,96,768]{3,2,1,0:T(8,128)(2,1)}, u32[]{:S(2)}, u32[]{:S(2)}) collective-permute-start(bf16[2,2,96,768]{3,2,1,0:T(8,128)(2,1)} %fusion.17), channel_id=1, source_target_pairs={{0,4},{1,5},{2,6},{3,7},{4,0},{5,1},{6,2},{7,3},{8,12},{9,13},{10,... | collective-permute-start | bytes 1769480 | tf_op jit(solution)/shard_map/ppermute | solution.py:175
  381.6 32.0 %collective-permute-start.45 = (bf16[4,1,96,768]{3,2,1,0:T(8,128)(2,1)}, bf16[4,1,96,768]{3,2,1,0:T(8,128)(2,1)}, u32[]{:S(2)}, u32[]{:S(2)}) collective-permute-start(bf16[4,1,96,768]{3,2,1,0:T(8,128)(2,1)} %get-tuple-element.452), channel_id=1, source_target_pairs={{0,16},{1,17},{2,18},{3,19},{4,20},{5,21},{6,22},{7,23},{8,24},{9,... | collective-permute-start | bytes 1769480 | tf_op jit(solution)/shard_map/ppermute | solution.py:175
  382.1 31.5 %collective-permute-start.46 = (bf16[4,1,96,768]{3,2,1,0:T(8,128)(2,1)}, bf16[4,1,96,768]{3,2,1,0:T(8,128)(2,1)}, u32[]{:S(2)}, u32[]{:S(2)}) collective-permute-start(bf16[4,1,96,768]{3,2,1,0:T(8,128)(2,1)} %get-tuple-element.451), channel_id=1, source_target_pairs={{0,1},{1,0},{2,3},{3,2},{4,5},{5,4},{6,7},{7,6},{8,9},{9,8},{10,11... | collective-permute-start | bytes 1769480 | tf_op jit(solution)/shard_map/ppermute | solution.py:175
  428.0 29.3 %collective-permute-start.50 = (bf16[2,2,4,1,96,768]{5,4,3,2,1,0:T(8,128)(2,1)}, bf16[2,2,4,1,96,768]{5,4,3,2,1,0:T(8,128)(2,1)}, u32[]{:S(2)}, u32[]{:S(2)}) collective-permute-start(bf16[2,2,4,1,96,768]{5,4,3,2,1,0:T(8,128)(2,1)} %get-tuple-element.365), channel_id=1, source_target_pairs={{0,8},{1,9},{2,10},{3,11},{4,12},{5,13},{6,14},{7,15},{8,0},{9,1},... | collective-permute-start | bytes 7077896 | tf_op jit(solution)/shard_map/ppermute | solution.py:175
  428.3 28.7 %collective-permute-start.48 = (bf16[4,2,96,768]{3,2,1,0:T(8,128)(2,1)}, bf16[4,2,96,768]{3,2,1,0:T(8,128)(2,1)}, u32[]{:S(2)}, u32[]{:S(2)}) collective-permute-start(bf16[4,2,96,768]{3,2,1,0:T(8,128)(2,1)} %get-tuple-element.446), channel_id=1, source_target_pairs={{0,16},{1,17},{2,18},{3,19},{4,20},{5,21},{6,22},{7,23},{8,24},{9,... | collective-permute-start | bytes 3538952 | tf_op jit(solution)/shard_map/ppermute | solution.py:175
  428.9 28.4 %collective-permute-start.49 = (bf16[4,2,96,768]{3,2,1,0:T(8,128)(2,1)}, bf16[4,2,96,768]{3,2,1,0:T(8,128)(2,1)}, u32[]{:S(2)}, u32[]{:S(2)}) collective-permute-start(bf16[4,2,96,768]{3,2,1,0:T(8,128)(2,1)} %get-tuple-element.445), channel_id=1, source_target_pairs={{0,1},{1,0},{2,3},{3,2},{4,5},{5,4},{6,7},{7,6},{8,9},{9,8},{10,11... | collective-permute-start | bytes 3538952 | tf_op jit(solution)/shard_map/ppermute | solution.py:175
  460.0 37.7 %collective-permute-start.60 = (bf16[2,2,96,768]{3,2,1,0:T(8,128)(2,1)}, bf16[2,2,96,768]{3,2,1,0:T(8,128)(2,1)}, u32[]{:S(2)}, u32[]{:S(2)}) collective-permute-start(bf16[2,2,96,768]{3,2,1,0:T(8,128)(2,1)} %fusion.12), channel_id=1, source_target_pairs={{0,4},{1,5},{2,6},{3,7},{4,0},{5,1},{6,2},{7,3},{8,12},{9,13},{10,... | collective-permute-start | bytes 1769480 | tf_op jit(solution)/shard_map/ppermute | solution.py:175
  484.5 25.7 %collective-permute-start.66 = (bf16[3,96,768]{2,1,0:T(8,128)(2,1)S(1)}, bf16[3,96,768]{2,1,0:T(8,128)(2,1)}, u32[]{:S(2)}, u32[]{:S(2)}) collective-permute-start(bf16[3,96,768]{2,1,0:T(8,128)(2,1)S(1)} %get-tuple-element.398), channel_id=1, source_target_pairs={{0,16},{1,17},{2,18},{3,19},{4,20},{5,21},{6,22},{7,23},{8,24},{9,... | collective-permute-start | bytes 1327112 | tf_op jit(solution)/shard_map/ppermute | solution.py:175
  (111 other events, 1250.8 us)

commit v11 on v10

--- a/solution.py
+++ b/solution.py
@@ -1249,19 +1249,18 @@
 
 
 def adam(layer, state, quarters, held):
-    half = ROWS // 2
     blocks = (
-        [pl.BlockSpec((1, 1, half, D), lambda i: (layer, i // 2, i % 2, 0))] * 3
-        + [pl.BlockSpec((1, half, D), lambda i: (layer, i % 2, i // 2))] * 3
-        + [pl.BlockSpec((1, half, D), lambda i: (layer, i, 0))] * 3
+        [pl.BlockSpec((1, 1, ROWS, D), lambda i: (layer, i, 0, 0))] * 3
+        + [pl.BlockSpec((1, ROWS, D), lambda i: (layer, 0, i))] * 3
+        + [pl.BlockSpec((1, ROWS, D), lambda i: (layer, i, 0))] * 3
     )
     grads = [
-        pl.BlockSpec((1, 1, half, D), partial(lambda member, i: (i // 2, member, i % 2, 0), member))
+        pl.BlockSpec((1, 1, ROWS, D), partial(lambda member, i: (i, member, 0, 0), member))
         for member in (2, 0, 1)
     ]
     return pl.pallas_call(
         adam_kernel,
-        grid=(8,),
+        grid=(4,),
         out_shape=[jax.ShapeDtypeStruct(array.shape, jnp.float32) for array in state],
         in_specs=blocks + grads + [ANY_SPEC] * len(held),
         out_specs=blocks,
@@ -1768,7 +1767,11 @@
     small_four = jnp.stack([small_pair, small_near])
     small_far = swap_z(small_four, 2)
     small_all = gather_small(jnp.concatenate([small_four, small_far]), place_parts)
-    x1, y1, far_a1, theirs_0, small_all = join(x1, y1, far_a1, theirs_0, small_all)
+    small0, hidden_bias0, (tvec0, far0, onehot) = small_parts(small_all[0])
+    small1, hidden_bias1, (tvec1, far1, onehot) = small_parts(small_all[1])
+    x1, y1, far_a1, theirs_0, small0, hidden_bias0, tvec0, far0 = join(
+        x1, y1, far_a1, theirs_0, small0, hidden_bias0, tvec0, far0
+    )
     to_x2, to_y2, to_far_f1, col_a1 = pack(
         (
             [(0, 0, 1), (1, 0, 2), (2, 0, 4)],
@@ -1786,8 +1789,6 @@
         1, (attn_low0,), (0, 0), (0, 2), ((0, 5), (0, 8)), ((1, 6, 2), (2, 6, 1)),
         (mine_0, x1, y1), (theirs_0, their_x1, their_y1),
     )
-    small0, hidden_bias0, (tvec0, far0, onehot) = small_parts(small_all[0])
-    small1, hidden_bias1, (tvec1, far1, onehot) = small_parts(small_all[1])
     q0, k0, v0, attn0 = project(place, low0, small0, group_a0)
     mixed0, p0, inverse0, dead = mix(lengths, far0, tvec0, q0, k0, v0, row_flags, col_flags)
     x2, y2, far_f1, mixed0 = join(x2, y2, far_f1, mixed0)
@@ -1879,19 +1880,18 @@
     pair_f1 = own_pair(keep_f1, get_f1, sides_rf1, zfar_f1, place_parts)
     znear_f1 = reduce_near(pair_f1, place_parts)
     small_c = swap_core(small_sum)
-    sides_rf0, get_a0, zfar_a1, znear_f1, small_c = join(
-        sides_rf0, get_a0, zfar_a1, znear_f1, small_c
+    by_a0 = reduce_corners(keep_a0, get_a0)
+    sides_rf0, by_a0, zfar_a1, znear_f1, small_c = join(
+        sides_rf0, by_a0, zfar_a1, znear_f1, small_c
     )
     payload_f0 = far_payload(keep_f0, get_f0, sides_rf0, place_parts)
     zfar_f0 = swap_z(payload_f0, 2)
-    by_a0 = reduce_corners(keep_a0, after(get_a0, payload_f0))
     pair_a1 = own_pair(keep_a1, get_a1, sides_ra1, zfar_a1, place_parts)
     znear_a1 = reduce_near(after(pair_a1, payload_f0), place_parts)
     content_grad, query_grad = input_back(after(dq0, sides_rf0), dk0, dv0, attn0, dresid0)
     small_sum = after(small_sum, payload_f0) + small_c
     small_y = swap_y(small_sum)
-    by_a0, content_grad, znear_a1, small_y = join(by_a0, content_grad, znear_a1, small_y)
-    payloads_a0 = side_payloads(keep_a0, get_a0, by_a0)
+    payloads_a0 = side_payloads(keep_a0, get_a0, after(by_a0, payload_f0))
     sides_ra0 = reduce_sides(payloads_a0)
     own_1 = jnp.concatenate(
         [
@@ -1900,16 +1900,14 @@
         ]
     )
     across_1 = swap_x(after(own_1, payloads_a0))
-    small_sum = after(small_sum, payloads_a0) + small_y
-    small_x = swap_x(small_sum)
-    sides_ra0, zfar_f0, small_x = join(sides_ra0, zfar_f0, small_x)
+    sides_ra0, zfar_f0, small_y, content_grad = join(sides_ra0, zfar_f0, small_y, content_grad)
     column_a0 = add_low(keep_a0[0, 0], get_a0[0, 0], *sides_ra0)
     shifts_a0 = reduce_direct(column_a0, place_parts)
     pair_f0 = own_pair(keep_f0, get_f0, sides_rf0, zfar_f0, place_parts)
     znear_f0 = reduce_near(after(pair_f0, column_a0), place_parts)
-    small_sum = after(small_sum, column_a0) + small_x
-    small_z = swap_z(small_sum, 1)
-    shifts_a0, znear_f0, across_1, small_z = join(shifts_a0, znear_f0, across_1, small_z)
+    small_sum = after(small_sum, column_a0) + small_y
+    small_x = swap_x(small_sum)
+    shifts_a0, znear_f0, across_1, small_x = join(shifts_a0, znear_f0, across_1, small_x)
     own_0 = jnp.concatenate(
         [
             reduce_total(pair_f0, znear_f0, place_parts),
@@ -1923,11 +1921,11 @@
         outer_master, outer_first, outer_second,
     )
     new_1 = adam(1, state, four_1, ())
-    small_sum = after(small_sum, own_0) + small_z
-    small_z = swap_z(small_sum, 2)
+    small_sum = after(small_sum, own_0) + small_x
+    small_z = tuple(swap_z(small_sum, apart) for apart in (1, 2, 3))
     across_0, new_1, small_z = join(across_0, new_1, small_z)
     four_0 = share_core(jnp.stack([own_0, across_0]), place_parts)
-    small_sum = small_sum + small_z
+    small_sum = small_sum + small_z[0] + small_z[1] + small_z[2]
     new_0 = adam(0, state, four_0, tuple(new_1))
     size = small_master.shape[1]
     small_own = lax.dynamic_slice_in_dim(small_sum, lax.axis_index("fsdp") * size, size, 1)

time: 562 us -> 553 us (0.984)
  waiting for transfers between devices: 84.1 us -> 73.3 us
  local copies, waits for them, and re-layouts: 37.1 us -> 43 us
    ppermute x72 -> x73, waiting for transfers between devices: 84.1 us -> 73.3 us  [move(): return lax.ppermute(value, AXES, pairs)]
    unnamed x130 -> x160, local copies, waits for them, and re-layouts: 13.1 us -> 16.2 us
    ppermute x72 -> x73, starting transfers between devices: 69.1 us -> 68.9 us  [move(): return lax.ppermute(value, AXES, pairs)]
  transfers between devices with their start and end apart: 72 -> 73, of which waited for: 21 -> 25; matrix products, arithmetic and copies ran while one was open for 12% -> 13% of each run, Pallas kernels for 39% -> 39%
where the time goes in v11:
time: 553 us; the launch traced here: 545 us
  Pallas kernels  301 us (54%)
  waiting for transfers between devices  73.3 us (13%)
  starting transfers between devices  68.9 us (12%)
  other arithmetic  54.8 us (10%)
  local copies, waits for them, and re-layouts  43 us (8%)
    ppermute x73, waiting for transfers between devices, move(): return lax.ppermute(value, AXES, pairs)  73.3 us
    ppermute x73, starting transfers between devices, move(): return lax.ppermute(value, AXES, pairs)  68.9 us
    pallas_call x1, Pallas kernels, turn(): pl.pallas_call(partial(turn_kernel, plan), out_shape=[half_low, half_low]...  55.5 us
    pallas_call x4, Pallas kernels, mix_back(): pl.pallas_call(mix_back_kernel, grid=(H // 4,), out_shape=[jax.ShapeDtype...  49.9 us
    pallas_call x1, Pallas kernels, down(): pl.pallas_call(partial(down_kernel, plan), out_shape=BACK_SHAPES, in_spec...  45.8 us
    pallas_call x2, Pallas kernels, mix(): pl.pallas_call(mix_kernel, grid=(H // 2,), out_shape=[jax.ShapeDtypeStruc...  36.5 us
    convert_element_type x19, other arithmetic, add_low(): return total.astype(jnp.bfloat16)  36.4 us
    pallas_call x1, Pallas kernels, feed(): pl.pallas_call(partial(feed_kernel, plan), out_shape=[tall, jax.ShapeDtyp...  34.5 us
  transfers between devices with their start and end apart: 73, of which 25 were waited for; matrix products, arithmetic and copies ran while one was open for 13% of the time, Pallas kernels for 39%

profile of v11, /device:TPU:0, one launch (start us, length us, event | category | flops | bytes accessed | tf_op | source)
XLA Modules:
  0.0 544.9 jit_solution(11611634040738346403)
XLA Ops:
  13.1 5.7 %cast_rest.1 = (bf16[4,96,768]{2,1,0:T(8,128)(2,1)}, bf16[4,96,768]{2,1,0:T(8,128)(2,1)}, bf16[96,3072]{1,0:T(8,128)(2,1)}, bf16[96,3072]{1,0:T(8,128)(2,1)}, bf...) custom-call(s32[4]{0:T(128)} %pad_add_fusion.place_ref, ...), custom_call_target="tpu_custom_call" | custom-call | flops 10000000 | bytes 12000000 | tf_op jit(solution)/shard_map/cast_rest/pallas_call | solution.py:368
  21.5 4.9 collective-permute-done.2.refs_2_
  35.7 10.4 %collective-permute-done.11 = bf16[2,2,1200]{2,1,0:T(2,128)(2,1)S(1)} collective-permute-done((bf16[2,2,1200]{2,1,0:T(2,128)(2,1)S(1)}, bf16[2,2,1200]{2,1,0:T(2,128)(2,1)S(1)}, u32[]{:S(2)}, u32[]{:S(2)}) %collective-permute-start.11) | collective-permute-done | bytes 9632 | tf_op jit(solution)/shard_map/ppermute | solution.py:175
  46.6 7.6 %collective-permute-done.10.refs_5_.refs_0_ = bf16[3,96,768]{2,1,0:T(8,128)(2,1)S(1)} collective-permute-done((bf16[3,96,768]{2,1,0:T(8,128)(2,1)S(1)}, bf16[3,96,768]{2,1,0:T(8,128)(2,1)S(1)}, u32[]{:S(2)}, u32[]{:S(2)}) %collective-permute-start.10) | collective-permute-done | bytes 442400 | tf_op jit(solution)/shard_map/ppermute | solution.py:175
  109.2 7.5 %project.2 = (bf16[1024,768]{1,0:T(8,128)(2,1)}, bf16[512,768]{1,0:T(8,128)(2,1)}, bf16[512,768]{1,0:T(8,128)(2,1)}, bf16[4,768,768]{2,1,0:T(8,128)(2,1)}) custom-call(s32[4]{0:T(128)} %pad_add_fusion.place_ref, f32[8,768]{1,0:T(8,128)} %reshape.491.small_ref.below_ref, bf16[1024,768]{1,0:T(8,128)(2,1)} %pad_maximum_fusion.low_any.hidden_any, ...), custom_call_target="tpu_custom_call" | custom-call | flops 2415919104 | bytes 16000000 | tf_op jit(solution)/shard_map/project/pallas_call | solution.py:422
  116.7 18.3 %mix.2 = (bf16[1024,768]{1,0:T(8,128)(2,1)}, bf16[12,512,1024]{2,1,0:T(8,128)(2,1)}, f32[12,1,1024]{2,1,0:T(1,128)}, f32[1,1024]{1,0:T(1,128)}) custom-call(s32[1]{0:T(128)S(6)} %copy.159.length_ref, f32[12,2]{1,0:T(8,128)} %copy.115.far_ref, bf16[1024,768]{1,0:T(8,128)(2,1)} %get-tuple-element.356.q_ref, bf16[512,768]{1,0:T(8,128)(2,1)} %get-tuple-element.276.k_ref, ...), custom_call_target="tpu_custom_call" | custom-call | flops 6499999744 | bytes 8000000 | tf_op jit(solution)/shard_map/mix/pallas_call | solution.py:557
  143.9 34.5 %feed.1 = (f32[1024,768]{1,0:T(8,128)}, bf16[4,1024,768]{2,1,0:T(8,128)(2,1)}, bf16[1024,768]{1,0:T(8,128)(2,1)}, bf16[1024,768]{1,0:T(8,128)(2,1)}, f32[1024,768]{1,0:T(8,128)}) custom-call(s32[4]{0:T(128)} %pad_add_fusion.place_ref, f32[8,768]{1,0:T(8,128)} %reshape.491.small_ref.below_ref, f32[1,3072]{1,0:T(1,128)} %bitcast.220, ...), custom_call_target="tpu_custom_call" | custom-call | flops 10871635968 | bytes 30000000 | tf_op jit(solution)/shard_map/feed/pallas_call | solution.py:791
  185.2 7.6 %project.3 = (bf16[1024,768]{1,0:T(8,128)(2,1)}, bf16[512,768]{1,0:T(8,128)(2,1)}, bf16[512,768]{1,0:T(8,128)(2,1)}, bf16[4,768,768]{2,1,0:T(8,128)(2,1)}) custom-call(s32[4]{0:T(128)} %pad_add_fusion.place_ref, f32[8,768]{1,0:T(8,128)} %reshape.490.small_ref, bf16[1024,768]{1,0:T(8,128)(2,1)} %get-tuple-element.331.low_any, ...), custom_call_target="tpu_custom_call" | custom-call | flops 2415919104 | bytes 16000000 | tf_op jit(solution)/shard_map/project/pallas_call | solution.py:422
  196.7 18.2 %mix.3 = (bf16[1024,768]{1,0:T(8,128)(2,1)}, bf16[12,512,1024]{2,1,0:T(8,128)(2,1)}, f32[12,1,1024]{2,1,0:T(1,128)}, f32[1,1024]{1,0:T(1,128)}) custom-call(s32[1]{0:T(128)S(6)} %copy.159.length_ref, f32[12,2]{1,0:T(8,128)} %pad_maximum_fusion.10.far_ref, bf16[1024,768]{1,0:T(8,128)(2,1)} %get-tuple-element.322.q_ref, ...), custom_call_target="tpu_custom_call" | custom-call | flops 6499999744 | bytes 8000000 | tf_op jit(solution)/shard_map/mix/pallas_call | solution.py:557
  216.3 55.5 %turn.1 = (bf16[512,768]{1,0:T(8,128)(2,1)}, bf16[512,768]{1,0:T(8,128)(2,1)}, f32[1024,768]{1,0:T(8,128)}, bf16[1024,768]{1,0:T(8,128)(2,1)}, bf16[768,768]{1,0...) custom-call(s32[4]{0:T(128)} %pad_add_fusion.place_ref, ...), custom_call_target="tpu_custom_call" | custom-call | flops 32614907904 | bytes 60000000 | tf_op jit(solution)/shard_map/turn/pallas_call | solution.py:982
  272.3 12.3 %mix_back.4 = (bf16[1024,768]{1,0:T(8,128)(2,1)}, bf16[512,768]{1,0:T(8,128)(2,1)}, bf16[512,768]{1,0:T(8,128)(2,1)}, f32[6,1,768]{2,1,0:T(1,128)}) custom-call(bf16[1024,768]{1,0:T(8,128)(2,1)} %get-tuple-element.322.q_ref, bf16[512,768]{1,0:T(8,128)(2,1)} %get-tuple-element.303.k_ref, bf16[512,768]{1,0:T(8,128)(2,1)} %get-tuple-element.304.v_ref, ...), custom_call_target="tpu_custom_call" | custom-call | flops 8000000000 | bytes 16000000 | tf_op jit(solution)/shard_map/mix_back/pallas_call | solution.py:658
  287.8 12.7 %mix_back.5 = (bf16[1024,768]{1,0:T(8,128)(2,1)}, bf16[512,768]{1,0:T(8,128)(2,1)}, bf16[512,768]{1,0:T(8,128)(2,1)}, f32[6,1,768]{2,1,0:T(1,128)}) custom-call(bf16[1024,768]{1,0:T(8,128)(2,1)} %get-tuple-element.322.q_ref, bf16[512,768]{1,0:T(8,128)(2,1)} %get-tuple-element.303.k_ref, ...), custom_call_target="tpu_custom_call", output_to_operand_aliasing={{0}: (8, {}), {1}: (9, {}), {2}: (10, {})} | custom-call | flops 8000000000 | bytes 16000000 | tf_op jit(solution)/shard_map/mix_back/pallas_call | solution.py:658
  302.3 8.8 %weight_back.2 = (bf16[2,2,4,1,96,768]{5,4,3,2,1,0:T(8,128)(2,1)}, bf16[2,2,4,1,96,768]{5,4,3,2,1,0:T(8,128)(2,1)}, f32[2,768]{1,0:T(2,128)}) custom-call(s32[4]{0:T(128)} %pad_add_fusion.place_ref, bf16[1024,768]{1,0:T(8,128)(2,1)} %get-tuple-element.331.low_any, bf16[1024,768]{1,0:T(8,128)(2,1)} %get-tuple-element.326.dq_any, ...), custom_call_target="tpu_custom_call" | custom-call | flops 2415919104 | bytes 12000000 | tf_op jit(solution)/shard_map/weight_back/pallas_call | solution.py:1135
  311.2 4.7 fusion.2
  321.5 45.8 %down.1 = (f32[1024,768]{1,0:T(8,128)}, bf16[1024,768]{1,0:T(8,128)(2,1)}, bf16[768,768]{1,0:T(8,128)(2,1)}, bf16[2,2,4,2,96,768]{5,4,3,2,1,0:T(8,128)(2,1)}, bf...) custom-call(s32[4]{0:T(128)} %pad_add_fusion.place_ref, ...), custom_call_target="tpu_custom_call" | custom-call | flops 27179089920 | bytes 60000000 | tf_op jit(solution)/shard_map/down/pallas_call | solution.py:1068
  375.8 12.3 %mix_back.6 = (bf16[1024,768]{1,0:T(8,128)(2,1)}, bf16[512,768]{1,0:T(8,128)(2,1)}, bf16[512,768]{1,0:T(8,128)(2,1)}, f32[6,1,768]{2,1,0:T(1,128)}) custom-call(bf16[1024,768]{1,0:T(8,128)(2,1)} %get-tuple-element.356.q_ref, bf16[512,768]{1,0:T(8,128)(2,1)} %get-tuple-element.276.k_ref, bf16[512,768]{1,0:T(8,128)(2,1)} %get-tuple-element.277.v_ref, ...), custom_call_target="tpu_custom_call" | custom-call | flops 8000000000 | bytes 16000000 | tf_op jit(solution)/shard_map/mix_back/pallas_call | solution.py:658
  393.2 12.5 %mix_back.7 = (bf16[1024,768]{1,0:T(8,128)(2,1)}, bf16[512,768]{1,0:T(8,128)(2,1)}, bf16[512,768]{1,0:T(8,128)(2,1)}, f32[6,1,768]{2,1,0:T(1,128)}) custom-call(bf16[1024,768]{1,0:T(8,128)(2,1)} %get-tuple-element.356.q_ref, bf16[512,768]{1,0:T(8,128)(2,1)} %get-tuple-element.276.k_ref, ...), custom_call_target="tpu_custom_call", output_to_operand_aliasing={{0}: (8, {}), {1}: (9, {}), {2}: (10, {})} | custom-call | flops 8000000000 | bytes 16000000 | tf_op jit(solution)/shard_map/mix_back/pallas_call | solution.py:658
  411.2 8.9 %weight_back.3 = (bf16[2,2,4,1,96,768]{5,4,3,2,1,0:T(8,128)(2,1)}, bf16[2,2,4,1,96,768]{5,4,3,2,1,0:T(8,128)(2,1)}, f32[2,768]{1,0:T(2,128)}) custom-call(s32[4]{0:T(128)} %pad_add_fusion.place_ref, bf16[1024,768]{1,0:T(8,128)(2,1)} %pad_maximum_fusion.low_any.hidden_any, bf16[1024,768]{1,0:T(8,128)(2,1)} %get-tuple-element.388.dq_any, ...), custom_call_target="tpu_custom_call" | custom-call | flops 2415919104 | bytes 12000000 | tf_op jit(solution)/shard_map/weight_back/pallas_call | solution.py:1135
  435.1 5.3 collective-permute-done.54
  440.9 6.6 %collective-permute-done.53 = bf16[2,1,96,768]{3,2,1,0:T(8,128)(2,1)S(1)} collective-permute-done((bf16[2,1,96,768]{3,2,1,0:T(8,128)(2,1)}, bf16[2,1,96,768]{3,2,1,0:T(8,128)(2,1)S(1)}, u32[]{:S(2)}, u32[]{:S(2)}) %collective-permute-start.53) | collective-permute-done | bytes 294944 | tf_op jit(solution)/shard_map/ppermute | solution.py:175
  470.4 7.7 %input_back.1 = (f32[512,768]{1,0:T(8,128)}, f32[512,768]{1,0:T(8,128)}) custom-call(bf16[1024,768]{1,0:T(8,128)(2,1)} %get-tuple-element.388.dq_any, bf16[512,768]{1,0:T(8,128)(2,1)} %get-tuple-element.366.dk_any, bf16[512,768]{1,0:T(8,128)(2,1)} %get-tuple-element.367.dv_any, bf16[4,768,768]{2,1,0:T(8,128)(2,1)} %get-tuple-element.288.attn_any.w_any, ...), custom_call_target="tpu_custom_call" | custom-call | flops 2415919104 | bytes 16000000 | tf_op jit(solution)/shard_map/input_back/pallas_call | solution.py:1184
  482.0 4.9 collective-permute-done.58
  520.4 9.5 %adam.2 = (f32[2,4,96,768]{3,2,1,0:T(8,128)}, f32[2,4,96,768]{3,2,1,0:T(8,128)}, f32[2,4,96,768]{3,2,1,0:T(8,128)}, f32[2,96,3072]{2,1,0:T(8,128)}, f32[2,96,307...) custom-call(f32[2,4,96,768]{3,2,1,0:T(8,128)} %refs_0_.3, ...), custom_call_target="tpu_custom_call" | custom-call | flops 20000000 | bytes 22000000 | tf_op jit(solution)/shard_map/adam/pallas_call | solution.py:1261
  535.1 9.5 %adam.3 = (f32[2,4,96,768]{3,2,1,0:T(8,128)}, f32[2,4,96,768]{3,2,1,0:T(8,128)}, f32[2,4,96,768]{3,2,1,0:T(8,128)}, f32[2,96,3072]{2,1,0:T(8,128)}, f32[2,96,307...) custom-call(f32[2,4,96,768]{3,2,1,0:T(8,128)} %refs_0_.3, ...), custom_call_target="tpu_custom_call", output_to_operand_aliasing={{0}: (12, {}), {1}: (13, {}), {2}: (14, {}), {3}: (15, {}),... | custom-call | flops 20000000 | bytes 22000000 | tf_op jit(solution)/shard_map/adam/pallas_call | solution.py:1261
  (395 shorter events, 210.3 us)
Async XLA Ops:
  4.3 22.1 %collective-permute-start.4 = (bf16[2,96,768]{2,1,0:T(8,128)(2,1)}, bf16[2,96,768]{2,1,0:T(8,128)(2,1)S(1)}, u32[]{:S(2)}, u32[]{:S(2)}) collective-permute-start(bf16[2,96,768]{2,1,0:T(8,128)(2,1)} %get-tuple-element.231.refs_3_), channel_id=1, source_target_pairs={{0,2},{1,3},{2,0},{3,1},{4,6},{5,7},{6,4},{7,5},{8,10},{9,11},{10,... | collective-permute-start | bytes 884744 | tf_op jit(solution)/shard_map/ppermute | solution.py:175
  27.1 28.3 %collective-permute-start.9 = (bf16[4,96,768]{2,1,0:T(8,128)(2,1)S(1)}, bf16[4,96,768]{2,1,0:T(8,128)(2,1)S(1)}, u32[]{:S(2)}, u32[]{:S(2)}) collective-permute-start(bf16[4,96,768]{2,1,0:T(8,128)(2,1)S(1)} %copy-done.73), channel_id=1, source_target_pairs={{0,1},{1,0},{2,3},{3,2},{4,5},{5,4},{6,7},{7,6},{8,9},{9,8},{10,11... | collective-permute-start | bytes 1769480 | tf_op jit(solution)/shard_map/ppermute | solution.py:175
  28.7 29.1 %collective-permute-start.8 = (bf16[4,96,768]{2,1,0:T(8,128)(2,1)S(1)}, bf16[4,96,768]{2,1,0:T(8,128)(2,1)S(1)}, u32[]{:S(2)}, u32[]{:S(2)}) collective-permute-start(bf16[4,96,768]{2,1,0:T(8,128)(2,1)S(1)} %get-tuple-element.241), channel_id=1, source_target_pairs={{0,4},{1,5},{2,6},{3,7},{4,0},{5,1},{6,2},{7,3},{8,12},{9,13},{10,... | collective-permute-start | bytes 1769480 | tf_op jit(solution)/shard_map/ppermute | solution.py:175
  32.4 21.8 %collective-permute-start.6 = (bf16[3,96,768]{2,1,0:T(8,128)(2,1)S(1)}, bf16[3,96,768]{2,1,0:T(8,128)(2,1)S(1)}, u32[]{:S(2)}, u32[]{:S(2)}) collective-permute-start(bf16[3,96,768]{2,1,0:T(8,128)(2,1)S(1)} %get-tuple-element.257.refs_1_), channel_id=1, source_target_pairs={{0,16},{1,17},{2,18},{3,19},{4,20},{5,21},{6,22},{7,23},{8,24},{9,... | collective-permute-start | bytes 1327112 | tf_op jit(solution)/shard_map/ppermute | solution.py:175
  63.9 31.9 %collective-permute-start.16 = (bf16[21,96,768]{2,1,0:T(8,128)(2,1)S(1)}, bf16[21,96,768]{2,1,0:T(8,128)(2,1)}, u32[]{:S(2)}, u32[]{:S(2)}) collective-permute-start(bf16[21,96,768]{2,1,0:T(8,128)(2,1)S(1)} %pack.8.refs_1_.refs_2_), channel_id=1, source_target_pairs={{0,8},{1,9},{2,10},{3,11},{4,12},{5,13},{6,14},{7,15},{8,0},{9,1},... | collective-permute-start | bytes 9289736 | tf_op jit(solution)/shard_map/ppermute | solution.py:175
  67.7 28.1 %collective-permute-start.13 = (bf16[8,96,768]{2,1,0:T(8,128)(2,1)}, bf16[8,96,768]{2,1,0:T(8,128)(2,1)}, u32[]{:S(2)}, u32[]{:S(2)}) collective-permute-start(bf16[8,96,768]{2,1,0:T(8,128)(2,1)} %copy-done.16), channel_id=1, source_target_pairs={{0,16},{1,17},{2,18},{3,19},{4,20},{5,21},{6,22},{7,23},{8,24},{9,... | collective-permute-start | bytes 3538952 | tf_op jit(solution)/shard_map/ppermute | solution.py:175
  69.3 25.0 %collective-permute-start.14 = (bf16[7,96,768]{2,1,0:T(8,128)(2,1)}, bf16[7,96,768]{2,1,0:T(8,128)(2,1)}, u32[]{:S(2)}, u32[]{:S(2)}) collective-permute-start(bf16[7,96,768]{2,1,0:T(8,128)(2,1)} %copy-done.17), channel_id=1, source_target_pairs={{0,1},{1,0},{2,3},{3,2},{4,5},{5,4},{6,7},{7,6},{8,9},{9,8},{10,11... | collective-permute-start | bytes 3096584 | tf_op jit(solution)/shard_map/ppermute | solution.py:175
  69.8 24.5 %collective-permute-start.15 = (bf16[2,96,768]{2,1,0:T(8,128)(2,1)}, bf16[2,96,768]{2,1,0:T(8,128)(2,1)}, u32[]{:S(2)}, u32[]{:S(2)}) collective-permute-start(bf16[2,96,768]{2,1,0:T(8,128)(2,1)} %copy-done.21), channel_id=1, source_target_pairs={{0,4},{1,5},{2,6},{3,7},{4,0},{5,1},{6,2},{7,3},{8,12},{9,13},{10,... | collective-permute-start | bytes 884744 | tf_op jit(solution)/shard_map/ppermute | solution.py:175
  103.5 32.6 %collective-permute-start.17 = (bf16[7,96,768]{2,1,0:T(8,128)(2,1)}, bf16[7,96,768]{2,1,0:T(8,128)(2,1)}, u32[]{:S(2)}, u32[]{:S(2)}) collective-permute-start(bf16[7,96,768]{2,1,0:T(8,128)(2,1)} %get-tuple-element.268), channel_id=1, source_target_pairs={{0,16},{1,17},{2,18},{3,19},{4,20},{5,21},{6,22},{7,23},{8,24},{9,... | collective-permute-start | bytes 3096584 | tf_op jit(solution)/shard_map/ppermute | solution.py:175
  105.0 31.1 %collective-permute-start.18 = (bf16[7,96,768]{2,1,0:T(8,128)(2,1)}, bf16[7,96,768]{2,1,0:T(8,128)(2,1)S(1)}, u32[]{:S(2)}, u32[]{:S(2)}) collective-permute-start(bf16[7,96,768]{2,1,0:T(8,128)(2,1)} %get-tuple-element.269), channel_id=1, source_target_pairs={{0,1},{1,0},{2,3},{3,2},{4,5},{5,4},{6,7},{7,6},{8,9},{9,8},{10,11... | collective-permute-start | bytes 3096584 | tf_op jit(solution)/shard_map/ppermute | solution.py:175
  107.7 28.4 %collective-permute-start.19 = (bf16[4,96,768]{2,1,0:T(8,128)(2,1)}, bf16[4,96,768]{2,1,0:T(8,128)(2,1)S(1)}, u32[]{:S(2)}, u32[]{:S(2)}) collective-permute-start(bf16[4,96,768]{2,1,0:T(8,128)(2,1)} %copy-done.20), channel_id=1, source_target_pairs={{0,4},{1,5},{2,6},{3,7},{4,0},{5,1},{6,2},{7,3},{8,12},{9,13},{10,... | collective-permute-start | bytes 1769480 | tf_op jit(solution)/shard_map/ppermute | solution.py:175
  140.5 37.9 %collective-permute-start.23 = (bf16[10,96,768]{2,1,0:T(8,128)(2,1)}, bf16[10,96,768]{2,1,0:T(8,128)(2,1)}, u32[]{:S(2)}, u32[]{:S(2)}) collective-permute-start(bf16[10,96,768]{2,1,0:T(8,128)(2,1)} %get-tuple-element.285), channel_id=1, source_target_pairs={{0,1},{1,0},{2,3},{3,2},{4,5},{5,4},{6,7},{7,6},{8,9},{9,8},{10,11... | collective-permute-start | bytes 4423688 | tf_op jit(solution)/shard_map/ppermute | solution.py:175
  142.0 36.3 %collective-permute-start.22 = (bf16[9,96,768]{2,1,0:T(8,128)(2,1)}, bf16[9,96,768]{2,1,0:T(8,128)(2,1)S(1)}, u32[]{:S(2)}, u32[]{:S(2)}) collective-permute-start(bf16[9,96,768]{2,1,0:T(8,128)(2,1)} %get-tuple-element.284), channel_id=1, source_target_pairs={{0,16},{1,17},{2,18},{3,19},{4,20},{5,21},{6,22},{7,23},{8,24},{9,... | collective-permute-start | bytes 3981320 | tf_op jit(solution)/shard_map/ppermute | solution.py:175
  179.0 36.0 %collective-permute-start.30 = (bf16[10,96,768]{2,1,0:T(8,128)(2,1)}, bf16[10,96,768]{2,1,0:T(8,128)(2,1)}, u32[]{:S(2)}, u32[]{:S(2)}) collective-permute-start(bf16[10,96,768]{2,1,0:T(8,128)(2,1)} %collective-permute-done.23.refs_0_.refs_3_), channel_id=1, source_target_pairs={{0,8},{1,9},{2,10},{3,11},{4,12},{5,13},{6,14},{7,15},{8,0},{9,1},... | collective-permute-start | bytes 4423688 | tf_op jit(solution)/shard_map/ppermute | solution.py:175
  315.9 51.4 %collective-permute-start.38 = (bf16[4,2,96,768]{3,2,1,0:T(8,128)(2,1)}, bf16[4,2,96,768]{3,2,1,0:T(8,128)(2,1)}, u32[]{:S(2)}, u32[]{:S(2)}) collective-permute-start(bf16[4,2,96,768]{3,2,1,0:T(8,128)(2,1)} %get-tuple-element.452), channel_id=1, source_target_pairs={{0,16},{1,17},{2,18},{3,19},{4,20},{5,21},{6,22},{7,23},{8,24},{9,... | collective-permute-start | bytes 3538952 | tf_op jit(solution)/shard_map/ppermute | solution.py:175
  317.4 49.9 %collective-permute-start.39 = (bf16[4,2,96,768]{3,2,1,0:T(8,128)(2,1)S(1)}, bf16[4,2,96,768]{3,2,1,0:T(8,128)(2,1)}, u32[]{:S(2)}, u32[]{:S(2)}) collective-permute-start(bf16[4,2,96,768]{3,2,1,0:T(8,128)(2,1)S(1)} %get-tuple-element.451), channel_id=1, source_target_pairs={{0,1},{1,0},{2,3},{3,2},{4,5},{5,4},{6,7},{7,6},{8,9},{9,8},{10,11... | collective-permute-start | bytes 3538952 | tf_op jit(solution)/shard_map/ppermute | solution.py:175
  319.4 47.9 %collective-permute-start.40 = (bf16[2,1,96,768]{3,2,0,1:T(8,128)(2,1)}, bf16[2,1,96,768]{3,2,0,1:T(8,128)(2,1)}, u32[]{:S(2)}, u32[]{:S(2)}) collective-permute-start(bf16[2,1,96,768]{3,2,0,1:T(8,128)(2,1)} %get-tuple-element.471), channel_id=1, source_target_pairs={{0,16},{1,17},{2,18},{3,19},{4,20},{5,21},{6,22},{7,23},{8,24},{9,... | collective-permute-start | bytes 884744 | tf_op jit(solution)/shard_map/ppermute | solution.py:175
  320.0 47.4 %collective-permute-start.41 = (bf16[2,1,96,768]{3,2,0,1:T(8,128)(2,1)S(1)}, bf16[2,1,96,768]{3,2,0,1:T(8,128)(2,1)}, u32[]{:S(2)}, u32[]{:S(2)}) collective-permute-start(bf16[2,1,96,768]{3,2,0,1:T(8,128)(2,1)S(1)} %get-tuple-element.470), channel_id=1, source_target_pairs={{0,1},{1,0},{2,3},{3,2},{4,5},{5,4},{6,7},{7,6},{8,9},{9,8},{10,11... | collective-permute-start | bytes 884744 | tf_op jit(solution)/shard_map/ppermute | solution.py:175
  371.0 34.7 %collective-permute-start.47 = (bf16[2,2,96,768]{3,2,1,0:T(8,128)(2,1)}, bf16[2,2,96,768]{3,2,1,0:T(8,128)(2,1)}, u32[]{:S(2)}, u32[]{:S(2)}) collective-permute-start(bf16[2,2,96,768]{3,2,1,0:T(8,128)(2,1)} %fusion.17), channel_id=1, source_target_pairs={{0,4},{1,5},{2,6},{3,7},{4,0},{5,1},{6,2},{7,3},{8,12},{9,13},{10,... | collective-permute-start | bytes 1769480 | tf_op jit(solution)/shard_map/ppermute | solution.py:175
  373.8 31.9 %collective-permute-start.45 = (bf16[4,1,96,768]{3,2,1,0:T(8,128)(2,1)}, bf16[4,1,96,768]{3,2,1,0:T(8,128)(2,1)}, u32[]{:S(2)}, u32[]{:S(2)}) collective-permute-start(bf16[4,1,96,768]{3,2,1,0:T(8,128)(2,1)} %get-tuple-element.456), channel_id=1, source_target_pairs={{0,16},{1,17},{2,18},{3,19},{4,20},{5,21},{6,22},{7,23},{8,24},{9,... | collective-permute-start | bytes 1769480 | tf_op jit(solution)/shard_map/ppermute | solution.py:175
  375.3 30.5 %collective-permute-start.46 = (bf16[4,1,96,768]{3,2,1,0:T(8,128)(2,1)}, bf16[4,1,96,768]{3,2,1,0:T(8,128)(2,1)}, u32[]{:S(2)}, u32[]{:S(2)}) collective-permute-start(bf16[4,1,96,768]{3,2,1,0:T(8,128)(2,1)} %get-tuple-element.455), channel_id=1, source_target_pairs={{0,1},{1,0},{2,3},{3,2},{4,5},{5,4},{6,7},{7,6},{8,9},{9,8},{10,11... | collective-permute-start | bytes 1769480 | tf_op jit(solution)/shard_map/ppermute | solution.py:175
  420.4 29.1 %collective-permute-start.49 = (bf16[4,2,96,768]{3,2,1,0:T(8,128)(2,1)}, bf16[4,2,96,768]{3,2,1,0:T(8,128)(2,1)}, u32[]{:S(2)}, u32[]{:S(2)}) collective-permute-start(bf16[4,2,96,768]{3,2,1,0:T(8,128)(2,1)} %get-tuple-element.450), channel_id=1, source_target_pairs={{0,16},{1,17},{2,18},{3,19},{4,20},{5,21},{6,22},{7,23},{8,24},{9,... | collective-permute-start | bytes 3538952 | tf_op jit(solution)/shard_map/ppermute | solution.py:175
  421.9 29.1 %collective-permute-start.50 = (bf16[4,2,96,768]{3,2,1,0:T(8,128)(2,1)}, bf16[4,2,96,768]{3,2,1,0:T(8,128)(2,1)}, u32[]{:S(2)}, u32[]{:S(2)}) collective-permute-start(bf16[4,2,96,768]{3,2,1,0:T(8,128)(2,1)} %get-tuple-element.449), channel_id=1, source_target_pairs={{0,1},{1,0},{2,3},{3,2},{4,5},{5,4},{6,7},{7,6},{8,9},{9,8},{10,11... | collective-permute-start | bytes 3538952 | tf_op jit(solution)/shard_map/ppermute | solution.py:175
  458.5 28.3 %collective-permute-start.58 = (bf16[2,2,96,768]{3,2,1,0:T(8,128)(2,1)S(1)}, bf16[2,2,96,768]{3,2,1,0:T(8,128)(2,1)}, u32[]{:S(2)}, u32[]{:S(2)}) collective-permute-start(bf16[2,2,96,768]{3,2,1,0:T(8,128)(2,1)S(1)} %fusion.11), channel_id=1, source_target_pairs={{0,4},{1,5},{2,6},{3,7},{4,0},{5,1},{6,2},{7,3},{8,12},{9,13},{10,... | collective-permute-start | bytes 1769480 | tf_op jit(solution)/shard_map/ppermute | solution.py:175
  (127 other events, 1310.3 us)
